TPU v7x, 32 devices: a whole 2x2x4 slice. The times are simulated.
32 devices in a mesh: groups: 2 (over x), mset: 16 (over z, y, core).
Axes of the slice: x: 2, y: 2, z: 4, core: 2. Of those that a mesh axis runs over, the one named last changes fastest.
Arguments:
- m_list: int32 [16], replicated, may hold values from 1536 to 3071, as said below
- coeff: bfloat16 [32, 32, 1536], P(('groups', 'mset')), parts along dimension 0, may hold values from -6 to 6
- blocks: bfloat16 [32, 1536, 1536], P(('groups', 'mset')), parts along dimension 0, may hold values from -0.15625 to 0.15625
- legendre: bfloat16 [512, 16, 1536], P(('groups', 'mset')), parts along dimension 0, may hold values from -0.15625 to 0.15625
Outputs:
- sky_map: bfloat16 [512, 16, 8192], P(('groups', 'mset')), parts along dimension 0
There are 2 independent parts, one for each index of `groups`. A program takes and returns all parts, laid end to end along the dimension named above; an argument that names none is the same for every part. Nothing has to cross between parts.
Inputs may be any that keep to these rules, and one draw needn't show every extreme that they name: `m_list`: 16 distinct values; the value 3072 - 1536, a block of full order 1536, is always among them.
All inputs are finite; a program needn't handle non-finite values.
Results may differ from a plain program's by a relative error of at most 0.0062.
Values may be sent and summed in bfloat16 or wider, within the bound.
No kernel may reach another device: no remote copies, remote signals or barrier semaphores. Data moves between devices by JAX's collectives and lax.ppermute only.
A program may use at most 64 MiB of HBM per device.

v0:
```python
import math

import jax
import jax.numpy as jnp
from jax import lax
from jax.sharding import PartitionSpec as P

LL = 3072
REAL = 16
NPHI = 8192


def fourier_table(m_values, pixels):
    pixel_index = jnp.arange(pixels, dtype=jnp.int32)
    phases = m_values[:, None] * pixel_index[None, :] % pixels
    angles = phases.astype(jnp.float32) * (2.0 * math.pi / pixels)
    cos_part = jnp.cos(angles).astype(jnp.bfloat16)
    sin_part = jnp.sin(angles).astype(jnp.bfloat16)
    return jnp.concatenate([cos_part, -sin_part], axis=0)


def body(m_list, coeff, blocks, legendre):
    per_device = coeff.shape[0]
    order_max = coeff.shape[2]
    first_slot = lax.axis_index("mset") * per_device
    own_m = lax.dynamic_slice_in_dim(m_list, first_slot, per_device)
    orders = LL - own_m
    valid_mask = jnp.arange(order_max, dtype=jnp.int32)[None, :] < orders[:, None]
    masked = jnp.where(valid_mask[:, None, :], coeff, jnp.zeros_like(coeff))
    products = jnp.einsum("mcj,mjk->mck", masked, blocks, preferred_element_type=jnp.float32)
    filtered = jnp.where(valid_mask[:, None, :], products, jnp.zeros_like(products)).astype(
        jnp.bfloat16
    )
    tables = lax.all_to_all(legendre, "mset", split_axis=1, concat_axis=0, tiled=True)
    local_part = jnp.einsum(
        "rmj,mcj->rmc", tables, filtered, preferred_element_type=jnp.float32
    ).astype(jnp.bfloat16)
    harmonics = lax.all_to_all(local_part, "mset", split_axis=0, concat_axis=1, tiled=True)
    cycle_count = harmonics.shape[0]
    subset_size = m_list.shape[0]
    real_part = harmonics[:, :, :REAL]
    imag_part = harmonics[:, :, REAL:]
    stacked = jnp.concatenate([real_part, imag_part], axis=1)
    flattened = jnp.transpose(stacked, (0, 2, 1)).reshape(cycle_count * REAL, 2 * subset_size)
    trig_table = fourier_table(m_list, NPHI)
    summed_map = jnp.dot(flattened, trig_table, preferred_element_type=jnp.float32)
    scaled = summed_map * (1.0 / math.sqrt(subset_size))
    return scaled.astype(jnp.bfloat16).reshape(cycle_count, REAL, NPHI)


def solution(mesh):
    in_specs = (
        P(),
        P(("groups", "mset"), None, None),
        P(("groups", "mset"), None, None),
        P(("groups", "mset"), None, None),
    )
    out_specs = P(("groups", "mset"), None, None)
    return jax.shard_map(body, mesh=mesh, in_specs=in_specs, out_specs=out_specs, check_vma=False)
```

profile of v0, /device:TPU:0, one launch (start us, length us, event | category | flops | bytes accessed | tf_op | source)
XLA Modules:
  0.0 49.8 jit_solution(17770142422807832663)
XLA Ops:
  0.0 0.0 copy-start
  0.0 2.5 %copy.8 = bf16[16,16,1536]{2,0,1:T(8,128)(2,1)} copy(bf16[16,16,1536]{2,1,0:T(8,128)(2,1)} %param.7) | data formatting | bytes 1572864 | tf_op args[3]
  2.5 7.4 %all-to-all-start = ((bf16[16,16,1536]{2,0,1:T(8,128)(2,1)}), bf16[16,16,1536]{2,0,1:T(8,128)(2,1)S(1)}, u32[]{:S(2)}, u32[]{:S(2)}) async-start(bf16[16,16,1536]{2,0,1:T(8,128)(2,1)} %copy.8), calls=%async_computation | async-start | bytes 1572864 | tf_op jit(solution)/shard_map/all_to_all | solution.py:34
  9.9 1.3 %dynamic_slice.3 = s32[1]{0:T(128)} dynamic-slice(s32[16]{0:T(128)} %param.4, s32[]{:T(128)S(6)} %select_n.19), dynamic_slice_sizes={1} | dynamic-slice | bytes 12 | tf_op jit(solution)/shard_map/dynamic_slice | solution.py:26
  11.8 2.8 %fusion.27 = bf16[16,8192]{1,0:T(8,128)(2,1)S(1)} fusion(s32[16]{0:T(128)} %param.4), kind=kLoop, calls=%fused_computation.23 | loop fusion | flops 2359296 | bytes 262208 | tf_op jit(solution)/shard_map/neg | solution.py:19
  14.6 14.0 %all-to-all-done = bf16[16,16,1536]{2,0,1:T(8,128)(2,1)S(1)} async-done(((bf16[16,16,1536]{2,0,1:T(8,128)(2,1)}), bf16[16,16,1536]{2,0,1:T(8,128)(2,1)S(1)}, u32[]{:S(2)}, u32[]{:S(2)}) %all-to-all-start) | async-done | bytes 786464 | tf_op jit(solution)/shard_map/all_to_all | solution.py:34
  28.6 3.5 %fusion.15 = bf16[256,1,32]{0,2,1:T(8,128)(2,1)S(1)} fusion(bf16[256,1536]{1,0:T(8,128)(2,1)S(1)} %bitcast.38, bf16[1,1536,1536]{2,1,0:T(8,128)(2,1)} %param.6, bf16[1,32,1536]{2,1,0:T(8,128)(2,1)} %param.5, pred[1536]{0:T(1024)(128)(4,1)S(1)} %iota_compare_fusion), kind=kOutput, calls=%fused_computation.8 | convolution fusion | flops 176316416 | bytes 5621248 | tf_op jit(solution)/shard_map/rmj,mcj->rmc/dot_general | solution.py:35
  32.1 0.5 %broadcast.23 = bf16[]{:T(256)} broadcast(bf16[]{:T(256)} %constant.70), dimensions={} | broadcast | bytes 4 | tf_op jit(solution)/shard_map/convert_element_type | solution.py:37
  32.6 0.7 %reduce = bf16[256,32]{0,1:T(8,128)(2,1)S(1)} reduce(bf16[256,1,32]{0,2,1:T(8,128)(2,1)S(1)} %fusion.15, bf16[]{:T(256)} %broadcast.23), dimensions={1}, to_apply=%copy.9.reduce_sub_computation | reduce | bytes 32770 | tf_op jit(solution)/shard_map/convert_element_type | solution.py:37
  33.3 0.1 copy.12
  33.4 0.7 %reshape.40 = bf16[16,2,256]{2,1,0:T(2,128)(2,1)} reshape(bf16[256,32]{1,0:T(8,128)(2,1)S(1)} %copy.12) | data formatting | bytes 32768
  34.1 5.5 %all-to-all-start.1 = ((bf16[16,2,256]{2,1,0:T(2,128)(2,1)}), bf16[16,2,256]{2,1,0:T(2,128)(2,1)S(1)}, u32[]{:S(2)}, u32[]{:S(2)}) async-start(bf16[16,2,256]{2,1,0:T(2,128)(2,1)} %reshape.40), calls=%async_computation.1 | async-start | bytes 32768 | tf_op jit(solution)/shard_map/all_to_all | solution.py:38
  39.6 0.0 copy-done
  39.6 2.1 %cosine_convert_fusion = bf16[16,8192]{1,0:T(8,128)(2,1)S(1)} fusion(s32[16]{0:T(128)S(1)} %copy-done), kind=kLoop, calls=%fused_computation.19 | loop fusion | flops 1966080 | bytes 262208 | tf_op jit(solution)/shard_map/convert_element_type | solution.py:17
  41.7 4.4 %all-to-all-done.1 = bf16[16,2,256]{2,1,0:T(2,128)(2,1)S(1)} async-done(((bf16[16,2,256]{2,1,0:T(2,128)(2,1)}), bf16[16,2,256]{2,1,0:T(2,128)(2,1)S(1)}, u32[]{:S(2)}, u32[]{:S(2)}) %all-to-all-start.1) | async-done | bytes 16416 | tf_op jit(solution)/shard_map/all_to_all | solution.py:38
  46.1 0.1 reshape.41
  46.2 0.1 fusion.42
  46.4 0.2 copy.10
  46.5 3.2 %fusion = bf16[256,8192]{1,0:T(8,128)(2,1)} fusion(bf16[256,32]{1,0:T(8,128)(2,1)S(1)} %bitcast.40, bf16[16,8192]{1,0:T(8,128)(2,1)S(1)} %fusion.27, bf16[16,8192]{1,0:T(8,128)(2,1)S(1)} %cosine_convert_fusion), kind=kOutput, calls=%fused_computation.1 | convolution fusion | flops 139460608 | bytes 4734976 | tf_op jit(solution)/shard_map/dot_general | solution.py:46
  (3 shorter events, 0.0 us)
Async XLA Ops:
  0.0 39.6 %copy-start = (s32[16]{0:T(128)S(1)}, s32[16]{0:T(128)}, u32[]{:S(2)}) copy-start(s32[16]{0:T(128)} %param.4) | copy-start | bytes 196
  2.5 26.1 %all-to-all-start = ((bf16[16,16,1536]{2,0,1:T(8,128)(2,1)}), bf16[16,16,1536]{2,0,1:T(8,128)(2,1)S(1)}, u32[]{:S(2)}, u32[]{:S(2)}) async-start(bf16[16,16,1536]{2,0,1:T(8,128)(2,1)} %copy.8), calls=%async_computation | async-start | bytes 1572864 | tf_op jit(solution)/shard_map/all_to_all | solution.py:34
  34.1 12.0 %all-to-all-start.1 = ((bf16[16,2,256]{2,1,0:T(2,128)(2,1)}), bf16[16,2,256]{2,1,0:T(2,128)(2,1)S(1)}, u32[]{:S(2)}, u32[]{:S(2)}) async-start(bf16[16,2,256]{2,1,0:T(2,128)(2,1)} %reshape.40), calls=%async_computation.1 | async-start | bytes 32768 | tf_op jit(solution)/shard_map/all_to_all | solution.py:38
where the time goes:
time: 50.1 us; the launch traced here: 49.8 us
  waiting for transfers between devices  18.4 us (37%)
  starting transfers between devices  12.9 us (26%)
  matrix products  6.75 us (13%)
  other arithmetic  5.6 us (11%)
  local copies, waits for them, and re-layouts  5.49 us (11%)
  between operations  0.71 us (1%)
    all_to_all x1, waiting for transfers between devices, body(): lax.all_to_all(legendre, 'mset', split_axis=1, concat_axis=0, tiled=True)  14 us
    all_to_all x1, starting transfers between devices, body(): lax.all_to_all(legendre, 'mset', split_axis=1, concat_axis=0, tiled=True)  7.39 us
    all_to_all x1, starting transfers between devices, body(): lax.all_to_all(local_part, 'mset', split_axis=0, concat_axis=1, tiled=True)  5.47 us
    all_to_all x1, waiting for transfers between devices, body(): lax.all_to_all(local_part, 'mset', split_axis=0, concat_axis=1, tiled=True)  4.37 us
    dot_general x1, matrix products, body(): jnp.einsum('rmj,mcj->rmc', tables, filtered, preferred_element_type=jnp.f...  3.51 us
    unnamed x7, local copies, waits for them, and re-layouts  3.42 us
    dot_general x1, matrix products, body(): jnp.dot(flattened, trig_table, preferred_element_type=jnp.float32)  3.24 us
    neg x1, other arithmetic, fourier_table(): return jnp.concatenate([cos_part, -sin_part], axis=0)  2.81 us
  transfers between devices with their start and end apart: 2, of which 2 were waited for; matrix products, arithmetic and copies ran while one was open for 12% of the time, Pallas kernels for 0%

commit v1 on v0

--- a/solution.py
+++ b/solution.py
@@ -31,17 +31,13 @@
     filtered = jnp.where(valid_mask[:, None, :], products, jnp.zeros_like(products)).astype(
         jnp.bfloat16
     )
-    tables = lax.all_to_all(legendre, "mset", split_axis=1, concat_axis=0, tiled=True)
-    local_part = jnp.einsum(
-        "rmj,mcj->rmc", tables, filtered, preferred_element_type=jnp.float32
+    gathered = lax.all_gather(filtered, "mset", axis=0, tiled=True)
+    harmonics = jnp.einsum(
+        "rij,icj->irc", legendre, gathered, preferred_element_type=jnp.float32
     ).astype(jnp.bfloat16)
-    harmonics = lax.all_to_all(local_part, "mset", split_axis=0, concat_axis=1, tiled=True)
-    cycle_count = harmonics.shape[0]
-    subset_size = m_list.shape[0]
-    real_part = harmonics[:, :, :REAL]
-    imag_part = harmonics[:, :, REAL:]
-    stacked = jnp.concatenate([real_part, imag_part], axis=1)
-    flattened = jnp.transpose(stacked, (0, 2, 1)).reshape(cycle_count * REAL, 2 * subset_size)
+    subset_size, cycle_count, _ = harmonics.shape
+    parts = harmonics.reshape(subset_size, cycle_count, 2, REAL)
+    flattened = jnp.transpose(parts, (1, 3, 2, 0)).reshape(cycle_count * REAL, 2 * subset_size)
     trig_table = fourier_table(m_list, NPHI)
     summed_map = jnp.dot(flattened, trig_table, preferred_element_type=jnp.float32)
     scaled = summed_map * (1.0 / math.sqrt(subset_size))

time: 50.1 us -> 67.7 us (1.35)
  waiting for transfers between devices: 18.4 us -> 38.3 us
  between operations: 0.71 us -> 14.1 us
  starting transfers between devices: 12.9 us -> 0.01 us
  local copies, waits for them, and re-layouts: 5.49 us -> 1.61 us
  matrix products: 6.75 us -> 9.27 us
  other arithmetic: 5.6 us -> 4.26 us
    all_gather x0 -> x1, waiting for transfers between devices: none -> 38.3 us  [body(): gathered = lax.all_gather(filtered, 'mset', axis=0, tiled=True)]
    all_to_all x2 -> x0, waiting for transfers between devices: 18.4 us -> none  [the longest x1 14 us: body(): lax.all_to_all(legendre, 'mset', split_axis=1, concat_axis=0, tiled=True)]
    all_to_all x2 -> x0, starting transfers between devices: 12.9 us -> none  [the longest x1 7.39 us: body(): lax.all_to_all(legendre, 'mset', split_axis=1, concat_axis=0, tiled=True)]
    unnamed x7 -> x4, local copies, waits for them, and re-layouts: 3.42 us -> 0.01 us
    dot_general x1 -> x2, matrix products: 3.51 us -> 5.98 us  [the longest x1 3.95 us: body(): jnp.einsum('mcj,mjk->mck', masked, blocks, preferred_element_type=jnp.flo...]
  transfers between devices with their start and end apart: 2 -> 1, of which waited for: 2 -> 1; matrix products, arithmetic and copies ran while one was open for 12% -> 6% of each run, Pallas kernels for 0% -> 0%
where the time goes in v1:
time: 67.7 us; the launch traced here: 67.5 us
  waiting for transfers between devices  38.3 us (57%)
  between operations  14.1 us (21%)
  matrix products  9.27 us (14%)
  other arithmetic  4.26 us (6%)
  local copies, waits for them, and re-layouts  1.61 us (2%)
    all_gather x1, waiting for transfers between devices, body(): gathered = lax.all_gather(filtered, 'mset', axis=0, tiled=True)  38.3 us
    dot_general x1, matrix products, body(): jnp.einsum('mcj,mjk->mck', masked, blocks, preferred_element_type=jnp.flo...  3.95 us
    dot_general x1, matrix products, body(): jnp.dot(flattened, trig_table, preferred_element_type=jnp.float32)  3.29 us
    neg x1, other arithmetic, fourier_table(): return jnp.concatenate([cos_part, -sin_part], axis=0)  2.14 us
    convert_element_type x1, other arithmetic, fourier_table(): cos_part = jnp.cos(angles).astype(jnp.bfloat16)  2.11 us
    dot_general x1, matrix products, body(): jnp.einsum('rij,icj->irc', legendre, gathered, preferred_element_type=jnp...  2.03 us
  transfers between devices with their start and end apart: 1, of which 1 were waited for; matrix products, arithmetic and copies ran while one was open for 6% of the time, Pallas kernels for 0%

profile of v1, /device:TPU:0, one launch (start us, length us, event | category | flops | bytes accessed | tf_op | source)
XLA Modules:
  0.0 67.5 jit_solution(16040673148380894235)
XLA Ops:
  6.5 0.0 copy-start
  6.5 0.0 copy-start.1
  6.5 0.0 all-gather.3.cloned.1.call-start
  6.5 1.3 %dynamic_slice.3 = s32[1]{0:T(128)} dynamic-slice(s32[16]{0:T(128)} %param.4, s32[]{:T(128)S(6)} %select_n.19), dynamic_slice_sizes={1} | dynamic-slice | bytes 12 | tf_op jit(solution)/shard_map/dynamic_slice | solution.py:26
  8.5 3.9 %fusion.6 = bf16[32,1536]{1,0:T(8,128)(2,1)} fusion(bf16[1,1536,1536]{2,1,0:T(8,128)(2,1)} %param.6, bf16[1,32,1536]{2,1,0:T(8,128)(2,1)} %param.5, pred[1536]{0:T(1024)(128)(4,1)S(1)} %iota_compare_fusion), kind=kOutput, calls=%fused_computation.5 | convolution fusion | flops 151142400 | bytes 4916736 | tf_op jit(solution)/shard_map/mcj,mjk->mck/dot_general | solution.py:30
  12.5 0.0 all-gather.3.cloned.1.call-update
  12.5 0.0 copy-done.1
  12.5 2.1 %fusion.20 = bf16[16,8192]{1,0:T(8,128)(2,1)S(1)} fusion(s32[16]{0:T(128)S(1)} %copy-done.1), kind=kLoop, calls=%fused_computation.23 | loop fusion | flops 2359296 | bytes 262208 | tf_op jit(solution)/shard_map/neg | solution.py:19
  14.7 2.1 %cosine_convert_fusion = bf16[16,8192]{1,0:T(8,128)(2,1)S(1)} fusion(s32[16]{0:T(128)S(1)} %copy-done.1), kind=kLoop, calls=%fused_computation.19 | loop fusion | flops 1966080 | bytes 262208 | tf_op jit(solution)/shard_map/convert_element_type | solution.py:17
  16.8 38.3 %all-gather.3.cloned.1.call-done = bf16[512,1536]{1,0:T(8,128)(2,1)} async-done(((bf16[32,1536]{1,0:T(8,128)(2,1)}), bf16[512,1536]{1,0:T(8,128)(2,1)}) %all-gather.3.cloned.1.call-update) | async-done | bytes 1572880 | tf_op jit(solution)/shard_map/all_gather | solution.py:34
  55.0 0.0 copy-done
  55.0 2.0 %fusion.9 = bf16[16,16,32]{2,1,0:T(8,128)(2,1)S(1)} fusion(bf16[16,32,1536]{2,1,0:T(8,128)(2,1)} %bitcast.25, bf16[16,16,1536]{2,1,0:T(8,128)(2,1)S(1)} %copy-done), kind=kOutput, calls=%fused_computation.7 | convolution fusion | flops 25174016 | bytes 2375680 | tf_op jit(solution)/shard_map/rij,icj->irc/dot_general | solution.py:35
  57.1 0.1 reshape.32
  57.2 0.2 reshape.33
  57.4 3.3 %fusion = bf16[256,8192]{1,0:T(8,128)(2,1)} fusion(bf16[256,32]{0,1:T(8,128)(2,1)S(1)} %reshape.33, bf16[16,8192]{1,0:T(8,128)(2,1)S(1)} %fusion.20, bf16[16,8192]{1,0:T(8,128)(2,1)S(1)} %cosine_convert_fusion), kind=kOutput, calls=%fused_computation.1 | convolution fusion | flops 139460608 | bytes 4734976 | tf_op jit(solution)/shard_map/dot_general | solution.py:42
  (2 shorter events, 0.0 us)
Async XLA Ops:
  6.5 48.5 %copy-start = (bf16[16,16,1536]{2,1,0:T(8,128)(2,1)S(1)}, bf16[16,16,1536]{2,1,0:T(8,128)(2,1)}, u32[]{:S(2)}) copy-start(bf16[16,16,1536]{2,1,0:T(8,128)(2,1)} %param.7) | copy-start | bytes 2359300
  6.5 6.0 %copy-start.1 = (s32[16]{0:T(128)S(1)}, s32[16]{0:T(128)}, u32[]{:S(2)}) copy-start(s32[16]{0:T(128)} %param.4) | copy-start | bytes 196
  6.5 48.5 %all-gather.3.cloned.1.call-start = ((), (), s32[]{:S(2)}) async-start(), calls=%async_computation | async-start | bytes 1671168 | tf_op jit(solution)/shard_map/all_gather | solution.py:34
Sparse Core Ops, SparseCore 0:
  12.6 42.3 all-gather.2

commit v2 on v1

v2 whole, which is shorter than its diff:
```python
import functools
import math

import jax
import jax.numpy as jnp
from jax import lax
from jax.experimental import pallas as pl
from jax.experimental.pallas import tpu as pltpu
from jax.sharding import PartitionSpec as P

LL = 3072
REAL = 16
NPHI = 8192
LANES = 128
BF16 = jnp.bfloat16
F32 = jnp.float32


def filter_kernel(per_device, m_ref, coeff_ref, block_ref, out_ref):
    slot, tile = pl.program_id(0), pl.program_id(1)
    order = LL - m_ref[lax.axis_index("mset") * per_device + slot]
    coeff = coeff_ref[...]
    rows = lax.broadcasted_iota(jnp.int32, coeff.shape, 1)
    masked = jnp.where(rows < order, coeff, jnp.zeros_like(coeff))
    product = jnp.dot(masked, block_ref[...], preferred_element_type=F32)
    width = product.shape[1]
    cols = lax.broadcasted_iota(jnp.int32, product.shape, 1) + tile * width
    out_ref[...] = jnp.where(cols < order, product, 0.0).astype(BF16)


def filter_blocks(m_list, coeff, blocks):
    per_device, columns, order_max = coeff.shape
    width = min(256, order_max)
    return pl.pallas_call(
        functools.partial(filter_kernel, per_device),
        out_shape=jax.ShapeDtypeStruct(coeff.shape, BF16),
        grid=(per_device, order_max // width),
        in_specs=[
            pl.BlockSpec(memory_space=pltpu.SMEM),
            pl.BlockSpec((None, columns, order_max), lambda s, t: (s, 0, 0)),
            pl.BlockSpec((None, order_max, width), lambda s, t: (s, 0, t)),
        ],
        out_specs=pl.BlockSpec((None, columns, width), lambda s, t: (s, 0, t)),
        compiler_params=pltpu.CompilerParams(vmem_limit_bytes=16 << 20),
        cost_estimate=pl.CostEstimate(
            flops=2 * coeff.size * order_max,
            bytes_accessed=2 * (blocks.size + 2 * coeff.size),
            transcendentals=0,
        ),
        name="filter_blocks",
    )(m_list, coeff, blocks)


def trig_kernel(m_ref, out_ref):
    n = out_ref.shape[0] // 2
    me = lax.axis_index("mset")
    per_device = n // lax.axis_size("mset")
    steps = NPHI // LANES

    def m_columns(width):
        index = lax.broadcasted_iota(jnp.int32, (n, width), 0)
        values = jnp.zeros((n, width), jnp.int32)
        for k in range(n):
            source = (me ^ (k // per_device)) * per_device + k % per_device
            values = jnp.where(index == k, m_ref[source], values)
        return values

    def angle(phase):
        phase = phase & (NPHI - 1)
        phase = jnp.where(phase >= NPHI // 2, phase - NPHI, phase)
        return phase.astype(F32) * (2.0 * math.pi / NPHI)

    values = m_columns(LANES)
    lane = lax.broadcasted_iota(jnp.int32, (n, LANES), 1)
    fine = angle(values * lane)
    coarse = angle(values * lane * LANES)
    cos_f, sin_f = jnp.cos(fine), jnp.sin(fine)
    cos_c, sin_c = jnp.cos(coarse), jnp.sin(coarse)
    for a in range(steps):
        ca, sa = cos_c[:, a : a + 1], sin_c[:, a : a + 1]
        span = slice(a * LANES, (a + 1) * LANES)
        out_ref[:n, span] = (ca * cos_f - sa * sin_f).astype(BF16)
        out_ref[n:, span] = (-(sa * cos_f + ca * sin_f)).astype(BF16)


def trig_table(m_list):
    rows = 2 * m_list.shape[0]
    return pl.pallas_call(
        trig_kernel,
        out_shape=jax.ShapeDtypeStruct((rows, NPHI), BF16),
        in_specs=[pl.BlockSpec(memory_space=pltpu.SMEM)],
        out_specs=pl.BlockSpec(memory_space=pltpu.VMEM),
        compiler_params=pltpu.CompilerParams(vmem_limit_bytes=16 << 20),
        cost_estimate=pl.CostEstimate(
            flops=8 * rows * NPHI, bytes_accessed=2 * rows * NPHI, transcendentals=0
        ),
        name="trig_table",
    )(m_list)


def synthesis_kernel(shards, chunk, tiles, *refs):
    leg_ref, table_ref = refs[0], refs[1]
    shard_refs = refs[2 : 2 + shards]
    out_ref, held, sems = refs[2 + shards :]
    me = lax.axis_index("mset")
    rows = leg_ref.shape[0]
    per_device, columns, _ = shard_refs[0].shape
    n = shards * per_device
    cycles = rows // n
    out_rows = cycles * REAL
    wide = chunk * per_device * columns
    legendre = leg_ref[...]

    row_m = lax.rem(lax.broadcasted_iota(jnp.int32, (rows, wide), 0), n)
    local = lax.broadcasted_iota(jnp.int32, (rows, wide), 1) // columns
    same_cycle = (
        lax.broadcasted_iota(jnp.int32, (out_rows, rows), 0) // REAL
        == lax.broadcasted_iota(jnp.int32, (out_rows, rows), 1) // n
    ).astype(BF16)
    same_real = lax.rem(lax.broadcasted_iota(jnp.int32, (out_rows, wide), 0), REAL) == lax.rem(
        lax.broadcasted_iota(jnp.int32, (out_rows, wide), 1), REAL
    )
    pick_row = lax.broadcasted_iota(jnp.int32, (wide, 2 * n), 0)
    pick_col = lax.broadcasted_iota(jnp.int32, (wide, 2 * n), 1)
    part = lax.rem(pick_row, columns) // REAL

    flat = jnp.zeros((out_rows, 2 * n), F32)
    for q in range(shards // chunk):
        piece = jnp.concatenate(
            [shard_refs[q * chunk + k][...].reshape(per_device * columns, -1) for k in range(chunk)],
            axis=0,
        )
        cross = lax.dot_general(
            legendre, piece, (((1,), (1,)), ((), ())), preferred_element_type=F32
        )
        slot = q * chunk + local // per_device
        source = (me ^ slot) * per_device + lax.rem(local, per_device)
        own = jnp.where(row_m == source, cross, 0.0).astype(BF16)
        spread = jnp.dot(same_cycle, own, preferred_element_type=F32)
        chosen = jnp.where(same_real, spread, 0.0).astype(BF16)
        pick = (part * n + q * chunk * per_device + pick_row // columns == pick_col).astype(BF16)
        flat += jnp.dot(chosen, pick, preferred_element_type=F32)
    flat = flat.astype(BF16)

    width = NPHI // tiles
    copies = []
    for t in range(tiles):
        span = pl.ds(t * width, width)
        summed = jnp.dot(flat, table_ref[:, span], preferred_element_type=F32)
        held[:, span] = (summed * (1.0 / math.sqrt(n))).astype(BF16)
        copy = pltpu.make_async_copy(held.at[:, span], out_ref.at[:, span], sems.at[t])
        copy.start()
        copies.append(copy)
    for copy in copies:
        copy.wait()


def synthesize(legendre, table, shards):
    cycles, n, order_max = legendre.shape
    count = len(shards)
    chunk = min(8, count)
    tiles = 8
    out_rows = cycles * REAL
    return pl.pallas_call(
        functools.partial(synthesis_kernel, count, chunk, tiles),
        out_shape=jax.ShapeDtypeStruct((out_rows, NPHI), BF16),
        in_specs=[pl.BlockSpec(memory_space=pltpu.VMEM)] * (2 + count),
        out_specs=pl.BlockSpec(memory_space=pl.ANY),
        scratch_shapes=[pltpu.VMEM((out_rows, NPHI), BF16), pltpu.SemaphoreType.DMA((tiles,))],
        compiler_params=pltpu.CompilerParams(vmem_limit_bytes=48 << 20),
        cost_estimate=pl.CostEstimate(
            flops=4 * out_rows * n * NPHI,
            bytes_accessed=2 * (out_rows * NPHI + legendre.size + table.size),
            transcendentals=0,
        ),
        name="legendre_synthesis",
    )(legendre.reshape(cycles * n, order_max), table, *shards)


def exchange(value, size, mask):
    return lax.ppermute(value, "mset", [(d, d ^ mask) for d in range(size)])


def gather_xor(value):
    size = lax.axis_size("mset")
    shards = {0: value}
    bits = size.bit_length() - 1
    stages = [[1 << b] for b in range(min(2, bits))]
    rest = list(range(2, bits))
    for low in range(0, len(rest), 2):
        pair = [1 << b for b in rest[low : low + 2]]
        masks = pair if len(pair) == 1 else [pair[0], pair[1], pair[0] | pair[1]]
        stages.append(masks)
    for masks in reversed(stages):
        fresh = {}
        for mask in masks:
            for k, shard in shards.items():
                fresh[k | mask] = exchange(shard, size, mask)
        shards.update(fresh)
    return [shards[k] for k in range(size)]


def body(m_list, coeff, blocks, legendre):
    filtered = filter_blocks(m_list, coeff, blocks)
    shards = gather_xor(filtered)
    table = trig_table(m_list)
    sky_map = synthesize(legendre, table, shards)
    return sky_map.reshape(legendre.shape[0], REAL, NPHI)


def solution(mesh):
    in_specs = (
        P(),
        P(("groups", "mset"), None, None),
        P(("groups", "mset"), None, None),
        P(("groups", "mset"), None, None),
    )
    out_specs = P(("groups", "mset"), None, None)
    return jax.shard_map(body, mesh=mesh, in_specs=in_specs, out_specs=out_specs, check_vma=False)
```

time: 67.7 us -> 32.3 us (0.48)
  waiting for transfers between devices: 38.3 us -> 8.68 us
  between operations: 14.1 us -> 0.06 us
  starting transfers between devices: 0.01 us -> 12.2 us
  matrix products: 9.27 us -> 0 us
  Pallas kernels: 0 us -> 7.27 us
  other arithmetic: 4.26 us -> 0 us
  local copies, waits for them, and re-layouts: 1.61 us -> 3.89 us
    all_gather x1 -> x0, waiting for transfers between devices: 38.3 us -> none  [body(): gathered = lax.all_gather(filtered, 'mset', axis=0, tiled=True)]
    ppermute x0 -> x15, starting transfers between devices: none -> 12.2 us  [exchange(): return lax.ppermute(value, 'mset', [(d, d ^ mask) for d in range(size)])]
    dot_general x3 -> x0, matrix products: 9.27 us -> none  [the longest x1 3.95 us: body(): jnp.einsum('mcj,mjk->mck', masked, blocks, preferred_element_type=jnp.flo...]
    ppermute x0 -> x15, waiting for transfers between devices: none -> 8.68 us  [exchange(): return lax.ppermute(value, 'mset', [(d, d ^ mask) for d in range(size)])]
    pallas_call x0 -> x3, Pallas kernels: none -> 7.27 us  [the longest x1 3.78 us: synthesize(): pl.pallas_call(functools.partial(synthesis_kernel, count, chunk, tiles),...]
    unnamed x4 -> x8, local copies, waits for them, and re-layouts: 0.01 us -> 3.89 us
    neg x1 -> x0, other arithmetic: 2.14 us -> none  [fourier_table(): return jnp.concatenate([cos_part, -sin_part], axis=0)]
    convert_element_type x1 -> x0, other arithmetic: 2.11 us -> none  [fourier_table(): cos_part = jnp.cos(angles).astype(jnp.bfloat16)]
  transfers between devices with their start and end apart: 1 -> 15, of which waited for: 1 -> 5; matrix products, arithmetic and copies ran while one was open for 6% -> 0% of each run, Pallas kernels for 0% -> 3%
where the time goes in v2:
time: 32.3 us; the launch traced here: 32.1 us
  starting transfers between devices  12.2 us (38%)
  waiting for transfers between devices  8.68 us (27%)
  Pallas kernels  7.27 us (23%)
  local copies, waits for them, and re-layouts  3.89 us (12%)
    ppermute x15, starting transfers between devices, exchange(): return lax.ppermute(value, 'mset', [(d, d ^ mask) for d in range(size)])  12.2 us
    ppermute x15, waiting for transfers between devices, exchange(): return lax.ppermute(value, 'mset', [(d, d ^ mask) for d in range(size)])  8.68 us
    unnamed x8, local copies, waits for them, and re-layouts  3.89 us
    pallas_call x1, Pallas kernels, synthesize(): pl.pallas_call(functools.partial(synthesis_kernel, count, chunk, tiles),...  3.78 us
    pallas_call x1, Pallas kernels, filter_blocks(): pl.pallas_call(functools.partial(filter_kernel, per_device), out_shape=ja...  2.44 us
    pallas_call x1, Pallas kernels, trig_table(): pl.pallas_call(trig_kernel, out_shape=jax.ShapeDtypeStruct((rows, NPHI),...  1.05 us
  transfers between devices with their start and end apart: 15, of which 5 were waited for; matrix products, arithmetic and copies ran while one was open for 0% of the time, Pallas kernels for 3%

profile of v2, /device:TPU:0, one launch (start us, length us, event | category | flops | bytes accessed | tf_op | source)
XLA Modules:
  0.0 32.1 jit_solution(11522320636211375458)
XLA Ops:
  0.0 2.3 %copy-done = bf16[1,1536,1536]{2,1,0:T(8,128)(2,1)S(1)} copy-done((bf16[1,1536,1536]{2,1,0:T(8,128)(2,1)S(1)}, bf16[1,1536,1536]{2,1,0:T(8,128)(2,1)}, u32[]{:S(2)}) %copy-start) | copy-done | bytes 4718616
  2.3 0.9 %copy-done.2 = bf16[1,32,1536]{2,1,0:T(8,128)(2,1)S(1)} copy-done((bf16[1,32,1536]{2,1,0:T(8,128)(2,1)S(1)}, bf16[1,32,1536]{2,1,0:T(8,128)(2,1)}, u32[]{:S(2)}) %copy-start.2) | copy-done | bytes 98328
  3.2 0.7 %copy-done.3 = s32[16]{0:T(128)S(1)} copy-done((s32[16]{0:T(128)S(1)}, s32[16]{0:T(128)}, u32[]{:S(2)}) %copy-start.3) | copy-done | bytes 88
  3.9 2.4 %filter_blocks.1.refs_2_ = bf16[1,32,1536]{2,1,0:T(8,128)(2,1)S(1)} custom-call(s32[16]{0:T(128)S(1)} %copy-done.3, bf16[1,32,1536]{2,1,0:T(8,128)(2,1)S(1)} %copy-done.2, bf16[1,1536,1536]{2,1,0:T(8,128)(2,1)S(1)} %copy-done), custom_call_target="tpu_custom_call" | custom-call | flops 150994944 | bytes 4915200 | tf_op jit(solution)/shard_map/filter_blocks/pallas_call | solution.py:34
  6.3 5.1 %collective-permute-start.11 = (bf16[1,32,1536]{2,1,0:T(8,128)(2,1)S(1)}, bf16[1,32,1536]{2,1,0:T(8,128)(2,1)S(1)}, u32[]{:S(2)}, u32[]{:S(2)}) collective-permute-start(bf16[1,32,1536]{2,1,0:T(8,128)(2,1)S(1)} %filter_blocks.1.refs_2_), channel_id=1, source_target_pairs={{0,12},{1,13},{2,14},{3,15},{4,8},{5,9},{6,10},{7,11},{8,4},{9,5},... | collective-permute-start | bytes 294920 | tf_op jit(solution)/shard_map/ppermute | solution.py:181
  11.5 0.0 collective-permute-start.7
  11.5 0.6 %collective-permute-start.3 = (bf16[1,32,1536]{2,1,0:T(8,128)(2,1)S(1)}, bf16[1,32,1536]{2,1,0:T(8,128)(2,1)S(1)}, u32[]{:S(2)}, u32[]{:S(2)}) collective-permute-start(bf16[1,32,1536]{2,1,0:T(8,128)(2,1)S(1)} %filter_blocks.1.refs_2_), channel_id=1, source_target_pairs={{0,4},{1,5},{2,6},{3,7},{4,0},{5,1},{6,2},{7,3},{8,12},{9,13},{10,... | collective-permute-start | bytes 294920 | tf_op jit(solution)/shard_map/ppermute | solution.py:181
  12.1 1.7 %collective-permute-start.1 = (bf16[1,32,1536]{2,1,0:T(8,128)(2,1)S(1)}, bf16[1,32,1536]{2,1,0:T(8,128)(2,1)S(1)}, u32[]{:S(2)}, u32[]{:S(2)}) collective-permute-start(bf16[1,32,1536]{2,1,0:T(8,128)(2,1)S(1)} %filter_blocks.1.refs_2_), channel_id=1, source_target_pairs={{0,2},{1,3},{2,0},{3,1},{4,6},{5,7},{6,4},{7,5},{8,10},{9,11},{10,... | collective-permute-start | bytes 294920 | tf_op jit(solution)/shard_map/ppermute | solution.py:181
  13.8 0.0 collective-permute-start
  13.8 1.4 %collective-permute-done.11.refs_14_ = bf16[1,32,1536]{2,1,0:T(8,128)(2,1)S(1)} collective-permute-done((bf16[1,32,1536]{2,1,0:T(8,128)(2,1)S(1)}, bf16[1,32,1536]{2,1,0:T(8,128)(2,1)S(1)}, u32[]{:S(2)}, u32[]{:S(2)}) %collective-permute-start.11) | collective-permute-done | bytes 98336 | tf_op jit(solution)/shard_map/ppermute | solution.py:181
  15.2 1.5 %collective-permute-start.13 = (bf16[1,32,1536]{2,1,0:T(8,128)(2,1)S(1)}, bf16[1,32,1536]{2,1,0:T(8,128)(2,1)S(1)}, u32[]{:S(2)}, u32[]{:S(2)}) collective-permute-start(bf16[1,32,1536]{2,1,0:T(8,128)(2,1)S(1)} %collective-permute-done.11.refs_14_), channel_id=1, source_target_pairs={{0,2},{1,3},{2,0},{3,1},{4,6},{5,7},{6,4},{7,5},{8,10},{9,11},{10,... | collective-permute-start | bytes 294920 | tf_op jit(solution)/shard_map/ppermute | solution.py:181
  16.7 3.0 %collective-permute-done.7.refs_10_ = bf16[1,32,1536]{2,1,0:T(8,128)(2,1)S(1)} collective-permute-done((bf16[1,32,1536]{2,1,0:T(8,128)(2,1)S(1)}, bf16[1,32,1536]{2,1,0:T(8,128)(2,1)S(1)}, u32[]{:S(2)}, u32[]{:S(2)}) %collective-permute-start.7) | collective-permute-done | bytes 98336 | tf_op jit(solution)/shard_map/ppermute | solution.py:181
  19.7 0.0 collective-permute-start.12
  19.7 0.0 collective-permute-done.3.refs_6_
  19.7 1.5 %collective-permute-start.9 = (bf16[1,32,1536]{2,1,0:T(8,128)(2,1)S(1)}, bf16[1,32,1536]{2,1,0:T(8,128)(2,1)S(1)}, u32[]{:S(2)}, u32[]{:S(2)}) collective-permute-start(bf16[1,32,1536]{2,1,0:T(8,128)(2,1)S(1)} %collective-permute-done.7.refs_10_), channel_id=1, source_target_pairs={{0,2},{1,3},{2,0},{3,1},{4,6},{5,7},{6,4},{7,5},{8,10},{9,11},{10,... | collective-permute-start | bytes 294920 | tf_op jit(solution)/shard_map/ppermute | solution.py:181
  21.2 0.0 collective-permute-done.1.refs_4_
  21.2 0.2 collective-permute-start.8
  21.5 0.0 collective-permute-done.refs_3_
  21.5 0.5 %collective-permute-start.5 = (bf16[1,32,1536]{2,1,0:T(8,128)(2,1)S(1)}, bf16[1,32,1536]{2,1,0:T(8,128)(2,1)S(1)}, u32[]{:S(2)}, u32[]{:S(2)}) collective-permute-start(bf16[1,32,1536]{2,1,0:T(8,128)(2,1)S(1)} %collective-permute-done.3.refs_6_), channel_id=1, source_target_pairs={{0,2},{1,3},{2,0},{3,1},{4,6},{5,7},{6,4},{7,5},{8,10},{9,11},{10,... | collective-permute-start | bytes 294920 | tf_op jit(solution)/shard_map/ppermute | solution.py:181
  22.0 0.0 collective-permute-done.13.refs_16_
  22.0 0.0 collective-permute-start.4
  22.0 0.5 %collective-permute-start.2 = (bf16[1,32,1536]{2,1,0:T(8,128)(2,1)S(1)}, bf16[1,32,1536]{2,1,0:T(8,128)(2,1)S(1)}, u32[]{:S(2)}, u32[]{:S(2)}) collective-permute-start(bf16[1,32,1536]{2,1,0:T(8,128)(2,1)S(1)} %collective-permute-done.1.refs_4_), channel_id=1, source_target_pairs={{0,1},{1,0},{2,3},{3,2},{4,5},{5,4},{6,7},{7,6},{8,9},{9,8},{10,11... | collective-permute-start | bytes 294920 | tf_op jit(solution)/shard_map/ppermute | solution.py:181
  22.5 2.8 %collective-permute-done.9.refs_12_ = bf16[1,32,1536]{2,1,0:T(8,128)(2,1)S(1)} collective-permute-done((bf16[1,32,1536]{2,1,0:T(8,128)(2,1)S(1)}, bf16[1,32,1536]{2,1,0:T(8,128)(2,1)S(1)}, u32[]{:S(2)}, u32[]{:S(2)}) %collective-permute-start.9) | collective-permute-done | bytes 98336 | tf_op jit(solution)/shard_map/ppermute | solution.py:181
  25.3 0.0 collective-permute-start.14
  25.3 0.0 collective-permute-done.8.refs_11_
  25.3 0.5 %collective-permute-start.10 = (bf16[1,32,1536]{2,1,0:T(8,128)(2,1)S(1)}, bf16[1,32,1536]{2,1,0:T(8,128)(2,1)S(1)}, u32[]{:S(2)}, u32[]{:S(2)}) collective-permute-start(bf16[1,32,1536]{2,1,0:T(8,128)(2,1)S(1)} %collective-permute-done.9.refs_12_), channel_id=1, source_target_pairs={{0,1},{1,0},{2,3},{3,2},{4,5},{5,4},{6,7},{7,6},{8,9},{9,8},{10,11... | collective-permute-start | bytes 294920 | tf_op jit(solution)/shard_map/ppermute | solution.py:181
  25.8 1.2 %collective-permute-done.5.refs_8_ = bf16[1,32,1536]{2,1,0:T(8,128)(2,1)S(1)} collective-permute-done((bf16[1,32,1536]{2,1,0:T(8,128)(2,1)S(1)}, bf16[1,32,1536]{2,1,0:T(8,128)(2,1)S(1)}, u32[]{:S(2)}, u32[]{:S(2)}) %collective-permute-start.5) | collective-permute-done | bytes 98336 | tf_op jit(solution)/shard_map/ppermute | solution.py:181
  27.0 1.1 %trig_table.1.refs_1_ = bf16[32,8192]{1,0:T(8,128)(2,1)S(1)} custom-call(s32[16]{0:T(128)S(1)} %copy-done.3), custom_call_target="tpu_custom_call" | custom-call | flops 2097152 | bytes 524288 | tf_op jit(solution)/shard_map/trig_table/pallas_call | solution.py:88
  28.1 0.0 collective-permute-done.2.refs_5_
  28.1 0.0 collective-permute-done.14.refs_17_
  28.1 0.2 collective-permute-done.6.refs_9_
  28.3 3.8 %legendre_synthesis.1 = bf16[256,8192]{1,0:T(8,128)(2,1)} custom-call(bf16[256,1536]{1,0:T(8,128)(2,1)S(1)} %bitcast.2, bf16[32,8192]{1,0:T(8,128)(2,1)S(1)} %trig_table.1.refs_1_, bf16[1,32,1536]{2,1,0:T(8,128)(2,1)S(1)} %filter_blocks.1.refs_2_, bf16[1,32,1536]{2,1,0:T(8,128)(2,1)S(1)} %collective-permute-done.refs_3_, ...), custom_call_target="tpu_custom_call" | custom-call | flops 134217728 | bytes 5505024 | tf_op jit(solution)/shard_map/legendre_synthesis/pallas_call | solution.py:164
  (9 shorter events, 0.0 us)
Async XLA Ops:
  0.0 2.3 %copy-start = (bf16[1,1536,1536]{2,1,0:T(8,128)(2,1)S(1)}, bf16[1,1536,1536]{2,1,0:T(8,128)(2,1)}, u32[]{:S(2)}) copy-start(bf16[1,1536,1536]{2,1,0:T(8,128)(2,1)} %block_ref.1) | copy-start | bytes 14155780
  2.3 0.9 %copy-start.2 = (bf16[1,32,1536]{2,1,0:T(8,128)(2,1)S(1)}, bf16[1,32,1536]{2,1,0:T(8,128)(2,1)}, u32[]{:S(2)}) copy-start(bf16[1,32,1536]{2,1,0:T(8,128)(2,1)} %coeff_ref.1) | copy-start | bytes 294916
  3.2 0.7 %copy-start.3 = (s32[16]{0:T(128)S(1)}, s32[16]{0:T(128)}, u32[]{:S(2)}) copy-start(s32[16]{0:T(128)} %m_ref.3) | copy-start | bytes 196
  3.9 24.5 %copy-start.1 = (bf16[16,16,1536]{2,1,0:T(8,128)(2,1)S(1)}, bf16[16,16,1536]{2,1,0:T(8,128)(2,1)}, u32[]{:S(2)}) copy-start(bf16[16,16,1536]{2,1,0:T(8,128)(2,1)} %param.7) | copy-start | bytes 2359300
  6.3 8.8 %collective-permute-start.11 = (bf16[1,32,1536]{2,1,0:T(8,128)(2,1)S(1)}, bf16[1,32,1536]{2,1,0:T(8,128)(2,1)S(1)}, u32[]{:S(2)}, u32[]{:S(2)}) collective-permute-start(bf16[1,32,1536]{2,1,0:T(8,128)(2,1)S(1)} %filter_blocks.1.refs_2_), channel_id=1, source_target_pairs={{0,12},{1,13},{2,14},{3,15},{4,8},{5,9},{6,10},{7,11},{8,4},{9,5},... | collective-permute-start | bytes 294920 | tf_op jit(solution)/shard_map/ppermute | solution.py:181
  11.5 8.3 %collective-permute-start.7 = (bf16[1,32,1536]{2,1,0:T(8,128)(2,1)S(1)}, bf16[1,32,1536]{2,1,0:T(8,128)(2,1)S(1)}, u32[]{:S(2)}, u32[]{:S(2)}) collective-permute-start(bf16[1,32,1536]{2,1,0:T(8,128)(2,1)S(1)} %filter_blocks.1.refs_2_), channel_id=1, source_target_pairs={{0,8},{1,9},{2,10},{3,11},{4,12},{5,13},{6,14},{7,15},{8,0},{9,1},... | collective-permute-start | bytes 294920 | tf_op jit(solution)/shard_map/ppermute | solution.py:181
  11.5 8.3 %collective-permute-start.3 = (bf16[1,32,1536]{2,1,0:T(8,128)(2,1)S(1)}, bf16[1,32,1536]{2,1,0:T(8,128)(2,1)S(1)}, u32[]{:S(2)}, u32[]{:S(2)}) collective-permute-start(bf16[1,32,1536]{2,1,0:T(8,128)(2,1)S(1)} %filter_blocks.1.refs_2_), channel_id=1, source_target_pairs={{0,4},{1,5},{2,6},{3,7},{4,0},{5,1},{6,2},{7,3},{8,12},{9,13},{10,... | collective-permute-start | bytes 294920 | tf_op jit(solution)/shard_map/ppermute | solution.py:181
  12.1 9.2 %collective-permute-start.1 = (bf16[1,32,1536]{2,1,0:T(8,128)(2,1)S(1)}, bf16[1,32,1536]{2,1,0:T(8,128)(2,1)S(1)}, u32[]{:S(2)}, u32[]{:S(2)}) collective-permute-start(bf16[1,32,1536]{2,1,0:T(8,128)(2,1)S(1)} %filter_blocks.1.refs_2_), channel_id=1, source_target_pairs={{0,2},{1,3},{2,0},{3,1},{4,6},{5,7},{6,4},{7,5},{8,10},{9,11},{10,... | collective-permute-start | bytes 294920 | tf_op jit(solution)/shard_map/ppermute | solution.py:181
  13.8 7.7 %collective-permute-start = (bf16[1,32,1536]{2,1,0:T(8,128)(2,1)S(1)}, bf16[1,32,1536]{2,1,0:T(8,128)(2,1)S(1)}, u32[]{:S(2)}, u32[]{:S(2)}) collective-permute-start(bf16[1,32,1536]{2,1,0:T(8,128)(2,1)S(1)} %filter_blocks.1.refs_2_), channel_id=1, source_target_pairs={{0,1},{1,0},{2,3},{3,2},{4,5},{5,4},{6,7},{7,6},{8,9},{9,8},{10,11... | collective-permute-start | bytes 294920 | tf_op jit(solution)/shard_map/ppermute | solution.py:181
  15.2 6.8 %collective-permute-start.13 = (bf16[1,32,1536]{2,1,0:T(8,128)(2,1)S(1)}, bf16[1,32,1536]{2,1,0:T(8,128)(2,1)S(1)}, u32[]{:S(2)}, u32[]{:S(2)}) collective-permute-start(bf16[1,32,1536]{2,1,0:T(8,128)(2,1)S(1)} %collective-permute-done.11.refs_14_), channel_id=1, source_target_pairs={{0,2},{1,3},{2,0},{3,1},{4,6},{5,7},{6,4},{7,5},{8,10},{9,11},{10,... | collective-permute-start | bytes 294920 | tf_op jit(solution)/shard_map/ppermute | solution.py:181
  19.7 2.3 %collective-permute-start.12 = (bf16[1,32,1536]{2,1,0:T(8,128)(2,1)S(1)}, bf16[1,32,1536]{2,1,0:T(8,128)(2,1)S(1)}, u32[]{:S(2)}, u32[]{:S(2)}) collective-permute-start(bf16[1,32,1536]{2,1,0:T(8,128)(2,1)S(1)} %collective-permute-done.11.refs_14_), channel_id=1, source_target_pairs={{0,1},{1,0},{2,3},{3,2},{4,5},{5,4},{6,7},{7,6},{8,9},{9,8},{10,11... | collective-permute-start | bytes 294920 | tf_op jit(solution)/shard_map/ppermute | solution.py:181
  19.7 5.6 %collective-permute-start.9 = (bf16[1,32,1536]{2,1,0:T(8,128)(2,1)S(1)}, bf16[1,32,1536]{2,1,0:T(8,128)(2,1)S(1)}, u32[]{:S(2)}, u32[]{:S(2)}) collective-permute-start(bf16[1,32,1536]{2,1,0:T(8,128)(2,1)S(1)} %collective-permute-done.7.refs_10_), channel_id=1, source_target_pairs={{0,2},{1,3},{2,0},{3,1},{4,6},{5,7},{6,4},{7,5},{8,10},{9,11},{10,... | collective-permute-start | bytes 294920 | tf_op jit(solution)/shard_map/ppermute | solution.py:181
  21.2 4.1 %collective-permute-start.8 = (bf16[1,32,1536]{2,1,0:T(8,128)(2,1)S(1)}, bf16[1,32,1536]{2,1,0:T(8,128)(2,1)S(1)}, u32[]{:S(2)}, u32[]{:S(2)}) collective-permute-start(bf16[1,32,1536]{2,1,0:T(8,128)(2,1)S(1)} %collective-permute-done.7.refs_10_), channel_id=1, source_target_pairs={{0,1},{1,0},{2,3},{3,2},{4,5},{5,4},{6,7},{7,6},{8,9},{9,8},{10,11... | collective-permute-start | bytes 294920 | tf_op jit(solution)/shard_map/ppermute | solution.py:181
  21.5 5.6 %collective-permute-start.5 = (bf16[1,32,1536]{2,1,0:T(8,128)(2,1)S(1)}, bf16[1,32,1536]{2,1,0:T(8,128)(2,1)S(1)}, u32[]{:S(2)}, u32[]{:S(2)}) collective-permute-start(bf16[1,32,1536]{2,1,0:T(8,128)(2,1)S(1)} %collective-permute-done.3.refs_6_), channel_id=1, source_target_pairs={{0,2},{1,3},{2,0},{3,1},{4,6},{5,7},{6,4},{7,5},{8,10},{9,11},{10,... | collective-permute-start | bytes 294920 | tf_op jit(solution)/shard_map/ppermute | solution.py:181
  22.0 6.1 %collective-permute-start.4 = (bf16[1,32,1536]{2,1,0:T(8,128)(2,1)S(1)}, bf16[1,32,1536]{2,1,0:T(8,128)(2,1)S(1)}, u32[]{:S(2)}, u32[]{:S(2)}) collective-permute-start(bf16[1,32,1536]{2,1,0:T(8,128)(2,1)S(1)} %collective-permute-done.3.refs_6_), channel_id=1, source_target_pairs={{0,1},{1,0},{2,3},{3,2},{4,5},{5,4},{6,7},{7,6},{8,9},{9,8},{10,11... | collective-permute-start | bytes 294920 | tf_op jit(solution)/shard_map/ppermute | solution.py:181
  22.0 6.1 %collective-permute-start.2 = (bf16[1,32,1536]{2,1,0:T(8,128)(2,1)S(1)}, bf16[1,32,1536]{2,1,0:T(8,128)(2,1)S(1)}, u32[]{:S(2)}, u32[]{:S(2)}) collective-permute-start(bf16[1,32,1536]{2,1,0:T(8,128)(2,1)S(1)} %collective-permute-done.1.refs_4_), channel_id=1, source_target_pairs={{0,1},{1,0},{2,3},{3,2},{4,5},{5,4},{6,7},{7,6},{8,9},{9,8},{10,11... | collective-permute-start | bytes 294920 | tf_op jit(solution)/shard_map/ppermute | solution.py:181
  25.3 2.8 %collective-permute-start.14 = (bf16[1,32,1536]{2,1,0:T(8,128)(2,1)S(1)}, bf16[1,32,1536]{2,1,0:T(8,128)(2,1)S(1)}, u32[]{:S(2)}, u32[]{:S(2)}) collective-permute-start(bf16[1,32,1536]{2,1,0:T(8,128)(2,1)S(1)} %collective-permute-done.13.refs_16_), channel_id=1, source_target_pairs={{0,1},{1,0},{2,3},{3,2},{4,5},{5,4},{6,7},{7,6},{8,9},{9,8},{10,11... | collective-permute-start | bytes 294920 | tf_op jit(solution)/shard_map/ppermute | solution.py:181
  25.3 2.8 %collective-permute-start.10 = (bf16[1,32,1536]{2,1,0:T(8,128)(2,1)S(1)}, bf16[1,32,1536]{2,1,0:T(8,128)(2,1)S(1)}, u32[]{:S(2)}, u32[]{:S(2)}) collective-permute-start(bf16[1,32,1536]{2,1,0:T(8,128)(2,1)S(1)} %collective-permute-done.9.refs_12_), channel_id=1, source_target_pairs={{0,1},{1,0},{2,3},{3,2},{4,5},{5,4},{6,7},{7,6},{8,9},{9,8},{10,11... | collective-permute-start | bytes 294920 | tf_op jit(solution)/shard_map/ppermute | solution.py:181
  27.0 1.3 %collective-permute-start.6 = (bf16[1,32,1536]{2,1,0:T(8,128)(2,1)S(1)}, bf16[1,32,1536]{2,1,0:T(8,128)(2,1)S(1)}, u32[]{:S(2)}, u32[]{:S(2)}) collective-permute-start(bf16[1,32,1536]{2,1,0:T(8,128)(2,1)S(1)} %collective-permute-done.5.refs_8_), channel_id=1, source_target_pairs={{0,1},{1,0},{2,3},{3,2},{4,5},{5,4},{6,7},{7,6},{8,9},{9,8},{10,11... | collective-permute-start | bytes 294920 | tf_op jit(solution)/shard_map/ppermute | solution.py:181

commit v3 on v1

v3 whole, which is shorter than its diff:
```python
import functools
import math

import jax
import jax.numpy as jnp
from jax import lax
from jax.experimental import pallas as pl
from jax.experimental.pallas import tpu as pltpu
from jax.sharding import PartitionSpec as P

LL = 3072
REAL = 16
NPHI = 8192
LANES = 128
BF16 = jnp.bfloat16
F32 = jnp.float32
VMEM = pl.BlockSpec(memory_space=pltpu.VMEM)
HBM = pl.BlockSpec(memory_space=pltpu.HBM)


def iota(shape, dim):
    return lax.broadcasted_iota(jnp.int32, shape, dim)


def insert_bit(value, bit, at):
    low = (1 << at) - 1
    return (value & low) | (bit << at) | ((value >> at) << (at + 1))


def remove_bit(value, at):
    low = (1 << at) - 1
    return (value & low) | ((value >> (at + 1)) << at)


def angle(phase):
    phase = phase & (NPHI - 1)
    phase = jnp.where(phase >= NPHI // 2, phase - NPHI, phase)
    return phase.astype(F32) * (2.0 * math.pi / NPHI)


def write_table(table_ref, m_smem, me, at):
    n = table_ref.shape[0] // 2
    index = iota((n, LANES), 0)
    lane = iota((n, LANES), 1)
    values = jnp.zeros((n, LANES), jnp.int32)
    for j in range(n):
        source = me ^ insert_bit(j % (n // 2), j // (n // 2), at)
        values = jnp.where(index == j, m_smem[source], values)
    fine = angle(values * lane)
    coarse = angle(values * lane * LANES)
    cos_f, sin_f = jnp.cos(fine), jnp.sin(fine)
    cos_c, sin_c = jnp.cos(coarse), jnp.sin(coarse)
    for a in range(NPHI // LANES):
        ca, sa = cos_c[:, a : a + 1], sin_c[:, a : a + 1]
        span = slice(a * LANES, (a + 1) * LANES)
        table_ref[:n, span] = (ca * cos_f - sa * sin_f).astype(BF16)
        table_ref[n:, span] = (-(sa * cos_f + ca * sin_f)).astype(BF16)


def prepare_kernel(
    at, m_ref, coeff_ref, block_ref, leg_ref, filtered_ref, keep_ref, send_ref, table_ref,
    m_smem, coeff_vmem, block_vmem, leg_vmem, sems,
):
    me = lax.axis_index("mset")
    columns, order_max = coeff_ref.shape
    pieces = block_vmem.shape[0]
    depth = order_max // pieces
    copy_m = pltpu.make_async_copy(m_ref, m_smem, sems.at[0])
    copy_leg = pltpu.make_async_copy(leg_ref, leg_vmem, sems.at[1])
    copy_coeff = pltpu.make_async_copy(coeff_ref, coeff_vmem, sems.at[2])
    copy_blocks = [
        pltpu.make_async_copy(
            block_ref.at[pl.ds(p * depth, depth), :], block_vmem.at[p], sems.at[3 + p]
        )
        for p in range(pieces)
    ]
    for copy in [copy_m, copy_leg, copy_coeff] + copy_blocks:
        copy.start()

    copy_m.wait()
    write_table(table_ref, m_smem, me, at)

    rows = leg_ref.shape[0]
    n = m_ref.shape[0]
    half = rows // 2
    own_bit = (me >> at) & 1
    row, col = iota((half, rows), 0), iota((half, rows), 1)
    same_cycle = row // (n // 2) == col // n
    slot = lax.rem(row, n // 2)
    copy_leg.wait()
    for ref, bit in ((keep_ref, own_bit), (send_ref, 1 - own_bit)):
        pick = same_cycle & (insert_bit(slot, bit, at) == lax.rem(col, n))
        ref[...] = jnp.dot(
            pick.astype(BF16), leg_vmem[...], preferred_element_type=F32
        ).astype(BF16)

    order = LL - m_smem[me]
    copy_coeff.wait()
    coeff = coeff_vmem[...]
    coeff = jnp.where(iota(coeff.shape, 1) < order, coeff, jnp.zeros_like(coeff))
    total = jnp.zeros((columns, order_max), F32)
    for p in range(pieces):
        copy_blocks[p].wait()
        total += jnp.dot(
            coeff[:, p * depth : (p + 1) * depth], block_vmem[p], preferred_element_type=F32
        )
    filtered_ref[...] = jnp.where(iota(total.shape, 1) < order, total, 0.0).astype(BF16)


def prepare(m_list, coeff, block, legendre, at):
    columns, order_max = coeff.shape
    rows = legendre.shape[0]
    n = m_list.shape[0]
    pieces = 6
    operands = (m_list, coeff, block, legendre)
    return pl.pallas_call(
        functools.partial(prepare_kernel, at),
        out_shape=[
            jax.ShapeDtypeStruct((columns, order_max), BF16),
            jax.ShapeDtypeStruct((rows // 2, order_max), BF16),
            jax.ShapeDtypeStruct((rows // 2, order_max), BF16),
            jax.ShapeDtypeStruct((2 * n, NPHI), BF16),
        ],
        in_specs=[HBM] * 4,
        out_specs=[VMEM] * 4,
        scratch_shapes=[
            pltpu.SMEM((n,), jnp.int32),
            pltpu.VMEM((columns, order_max), BF16),
            pltpu.VMEM((pieces, order_max // pieces, order_max), BF16),
            pltpu.VMEM((rows, order_max), BF16),
            pltpu.SemaphoreType.DMA((3 + pieces,)),
        ],
        compiler_params=pltpu.CompilerParams(vmem_limit_bytes=32 << 20),
        cost_estimate=pl.CostEstimate(
            flops=2 * (columns * order_max * order_max + rows * rows * order_max),
            bytes_accessed=2 * (block.size + legendre.size),
            transcendentals=0,
        ),
        name="prepare",
    )(*[pltpu.with_memory_space_constraint(x, pltpu.HBM) for x in operands])


def cross_kernel(at, n, shards, chunk, *refs):
    keep_ref, got_ref = refs[:2]
    shard_refs = refs[2 : 2 + shards]
    own_ref, back_ref = refs[2 + shards :]
    rest = remove_bit(lax.axis_index("mset"), at)
    half = keep_ref.shape[0]
    columns = shard_refs[0].shape[0]
    cycles = own_ref.shape[0]
    wide = chunk * columns
    slot = lax.rem(iota((half, wide), 0), shards)
    local = iota((half, wide), 1) // columns
    fold = (iota((cycles, half), 0) == iota((cycles, half), 1) // shards).astype(BF16)
    for q in range(shards // chunk):
        piece = jnp.concatenate(
            [shard_refs[q * chunk + k][...] for k in range(chunk)], axis=0
        )
        own = slot == (rest ^ (local + q * chunk))
        for source, target in ((keep_ref, own_ref), (got_ref, back_ref)):
            cross = lax.dot_general(
                source[...], piece, (((1,), (1,)), ((), ())), preferred_element_type=F32
            )
            chosen = jnp.where(own, cross, 0.0).astype(BF16)
            target[:, q * wide : (q + 1) * wide] = jnp.dot(
                fold, chosen, preferred_element_type=F32
            ).astype(BF16)


def cross(keep, got, shards, n, at):
    half, order_max = keep.shape
    columns = shards[0].shape[0]
    count = len(shards)
    cycles = half // count
    shape = jax.ShapeDtypeStruct((cycles, count * columns), BF16)
    return pl.pallas_call(
        functools.partial(cross_kernel, at, n, count, min(8, count)),
        out_shape=[shape, shape],
        in_specs=[VMEM] * (2 + count),
        out_specs=[VMEM] * 2,
        compiler_params=pltpu.CompilerParams(vmem_limit_bytes=32 << 20),
        cost_estimate=pl.CostEstimate(
            flops=4 * half * order_max * count * columns,
            bytes_accessed=2 * (2 * keep.size + count * shards[0].size),
            transcendentals=0,
        ),
        name="cross",
    )(keep, got, *shards)


def synthesis_kernel(tiles, columns, own_ref, got_ref, table_ref, out_ref, held, sems):
    cycles, half = own_ref.shape
    wide = 2 * half
    n = wide // columns
    out_rows = cycles * REAL
    joined = jnp.concatenate([own_ref[...], got_ref[...]], axis=1)
    repeat = (iota((out_rows, cycles), 0) // REAL == iota((out_rows, cycles), 1)).astype(BF16)
    spread = jnp.dot(repeat, joined, preferred_element_type=F32)
    same_real = lax.rem(iota((out_rows, wide), 0), REAL) == lax.rem(
        iota((out_rows, wide), 1), REAL
    )
    chosen = jnp.where(same_real, spread, 0.0).astype(BF16)
    row, col = iota((wide, 2 * n), 0), iota((wide, 2 * n), 1)
    pick = (lax.rem(row, columns) // REAL * n + row // columns == col).astype(BF16)
    flat = jnp.dot(chosen, pick, preferred_element_type=F32).astype(BF16)

    width = NPHI // tiles
    copies = []
    for t in range(tiles):
        span = pl.ds(t * width, width)
        summed = jnp.dot(flat, table_ref[:, span], preferred_element_type=F32)
        held[:, span] = (summed * (1.0 / math.sqrt(n))).astype(BF16)
        copy = pltpu.make_async_copy(held.at[:, span], out_ref.at[:, span], sems.at[t])
        copy.start()
        copies.append(copy)
    for copy in copies:
        copy.wait()


def synthesize(own, got, table, columns):
    cycles = own.shape[0]
    tiles = 8
    out_rows = cycles * REAL
    return pl.pallas_call(
        functools.partial(synthesis_kernel, tiles, columns),
        out_shape=jax.ShapeDtypeStruct((out_rows, NPHI), BF16),
        in_specs=[VMEM] * 3,
        out_specs=HBM,
        scratch_shapes=[pltpu.VMEM((out_rows, NPHI), BF16), pltpu.SemaphoreType.DMA((tiles,))],
        compiler_params=pltpu.CompilerParams(vmem_limit_bytes=32 << 20),
        cost_estimate=pl.CostEstimate(
            flops=2 * out_rows * table.size,
            bytes_accessed=2 * (out_rows * NPHI + table.size),
            transcendentals=0,
        ),
        name="synthesis",
    )(own, got, table)


def exchange(value, size, mask):
    return lax.ppermute(value, "mset", [(d, d ^ mask) for d in range(size)])


def gather_xor(value, size, at):
    shards = {0: value}
    bits = [b for b in range(size.bit_length() - 1) if b != at]
    for b in reversed(bits):
        shards.update({k | 1 << b: exchange(v, size, 1 << b) for k, v in shards.items()})
    return [shards[k] for k in sorted(shards)]


def body(m_list, coeff, blocks, legendre):
    size = lax.axis_size("mset")
    per_device, columns, order_max = coeff.shape
    if per_device != 1 or size & (size - 1):
        raise ValueError("unsupported mesh")
    cycles, n, _ = legendre.shape
    at = min(2, size.bit_length() - 2)
    filtered, keep, send, table = prepare(
        m_list, coeff[0], blocks[0], legendre.reshape(cycles * n, order_max), at
    )
    got = exchange(send, size, 1 << at)
    shards = gather_xor(filtered, size, at)
    own, back = cross(keep, got, shards, n, at)
    other = exchange(back, size, 1 << at)
    sky_map = synthesize(own, other, table, columns)
    return sky_map.reshape(cycles, REAL, NPHI)


def solution(mesh):
    in_specs = (
        P(),
        P(("groups", "mset"), None, None),
        P(("groups", "mset"), None, None),
        P(("groups", "mset"), None, None),
    )
    out_specs = P(("groups", "mset"), None, None)
    return jax.shard_map(body, mesh=mesh, in_specs=in_specs, out_specs=out_specs, check_vma=False)
```

time: 67.7 us -> 31.5 us (0.47)
  waiting for transfers between devices: 38.3 us -> 11.9 us
  between operations: 14.1 us -> 0.03 us
  starting transfers between devices: 0.01 us -> 12.7 us
  matrix products: 9.27 us -> 0 us
  Pallas kernels: 0 us -> 6.75 us
  other arithmetic: 4.26 us -> 0 us
  local copies, waits for them, and re-layouts: 1.61 us -> 0 us
    all_gather x1 -> x0, waiting for transfers between devices: 38.3 us -> none  [body(): gathered = lax.all_gather(filtered, 'mset', axis=0, tiled=True)]
    ppermute x0 -> x9, starting transfers between devices: none -> 12.7 us  [exchange(): return lax.ppermute(value, 'mset', [(d, d ^ mask) for d in range(size)])]
    ppermute x0 -> x9, waiting for transfers between devices: none -> 11.9 us  [exchange(): return lax.ppermute(value, 'mset', [(d, d ^ mask) for d in range(size)])]
    dot_general x3 -> x0, matrix products: 9.27 us -> none  [the longest x1 3.95 us: body(): jnp.einsum('mcj,mjk->mck', masked, blocks, preferred_element_type=jnp.flo...]
    pallas_call x0 -> x3, Pallas kernels: none -> 6.75 us  [the longest x1 2.91 us: prepare(): pl.pallas_call(functools.partial(prepare_kernel, at), out_shape=[jax.Shap...]
    neg x1 -> x0, other arithmetic: 2.14 us -> none  [fourier_table(): return jnp.concatenate([cos_part, -sin_part], axis=0)]
    convert_element_type x1 -> x0, other arithmetic: 2.11 us -> none  [fourier_table(): cos_part = jnp.cos(angles).astype(jnp.bfloat16)]
    dynamic_slice x1 -> x0, local copies, waits for them, and re-layouts: 1.32 us -> none  [body(): own_m = lax.dynamic_slice_in_dim(m_list, first_slot, per_device)]
  transfers between devices with their start and end apart: 1 -> 9, of which waited for: 1 -> 4; matrix products, arithmetic and copies ran while one was open for 6% -> 0% of each run, Pallas kernels for 0% -> 0%
where the time goes in v3:
time: 31.5 us; the launch traced here: 31.4 us
  starting transfers between devices  12.7 us (40%)
  waiting for transfers between devices  11.9 us (38%)
  Pallas kernels  6.75 us (21%)
    ppermute x9, starting transfers between devices, exchange(): return lax.ppermute(value, 'mset', [(d, d ^ mask) for d in range(size)])  12.7 us
    ppermute x9, waiting for transfers between devices, exchange(): return lax.ppermute(value, 'mset', [(d, d ^ mask) for d in range(size)])  11.9 us
    pallas_call x1, Pallas kernels, prepare(): pl.pallas_call(functools.partial(prepare_kernel, at), out_shape=[jax.Shap...  2.91 us
    pallas_call x1, Pallas kernels, synthesize(): pl.pallas_call(functools.partial(synthesis_kernel, tiles, columns), out_s...  2.6 us
    pallas_call x1, Pallas kernels, cross(): pl.pallas_call(functools.partial(cross_kernel, at, n, count, min(8, count...  1.24 us
  transfers between devices with their start and end apart: 9, of which 4 were waited for; matrix products, arithmetic and copies ran while one was open for 0% of the time, Pallas kernels for 0%

profile of v3, /device:TPU:0, one launch (start us, length us, event | category | flops | bytes accessed | tf_op | source)
XLA Modules:
  0.0 31.4 jit_solution(8996695052507439732)
XLA Ops:
  0.0 2.9 %prepare.1 = (bf16[32,1536]{1,0:T(8,128)(2,1)S(1)}, bf16[128,1536]{1,0:T(8,128)(2,1)S(1)}, bf16[128,1536]{1,0:T(8,128)(2,1)S(1)}, bf16[32,8192]{1,0:T(8,128)(2,1)S(1)}) custom-call(s32[16]{0:T(128)} %m_ref.1, bf16[32,1536]{1,0:T(8,128)(2,1)} %bitcast.6, bf16[1536,1536]{1,0:T(8,128)(2,1)} %bitcast.4, bf16[256,1536]{1,0:T(8,128)(2,1)} %bitcast.5), custom_call_target="tpu_custom_call" | custom-call | flops 352321536 | bytes 5505024 | tf_op jit(solution)/shard_map/prepare/pallas_call | solution.py:116
  2.9 3.1 %collective-permute-start = (bf16[128,1536]{1,0:T(8,128)(2,1)S(1)}, bf16[128,1536]{1,0:T(8,128)(2,1)S(1)}, u32[]{:S(2)}, u32[]{:S(2)}) collective-permute-start(bf16[128,1536]{1,0:T(8,128)(2,1)S(1)} %get-tuple-element.12), channel_id=1, source_target_pairs={{0,4},{1,5},{2,6},{3,7},{4,0},{5,1},{6,2},{7,3},{8,12},{9,13},{10,... | collective-permute-start | bytes 1179656 | tf_op jit(solution)/shard_map/ppermute | solution.py:241
  6.0 2.6 %collective-permute-start.4 = (bf16[32,1536]{1,0:T(8,128)(2,1)S(1)}, bf16[32,1536]{1,0:T(8,128)(2,1)S(1)}, u32[]{:S(2)}, u32[]{:S(2)}) collective-permute-start(bf16[32,1536]{1,0:T(8,128)(2,1)S(1)} %get-tuple-element.13.refs_2_), channel_id=1, source_target_pairs={{0,8},{1,9},{2,10},{3,11},{4,12},{5,13},{6,14},{7,15},{8,0},{9,1},... | collective-permute-start | bytes 294920 | tf_op jit(solution)/shard_map/ppermute | solution.py:241
  8.6 1.5 %collective-permute-start.2 = (bf16[32,1536]{1,0:T(8,128)(2,1)S(1)}, bf16[32,1536]{1,0:T(8,128)(2,1)S(1)}, u32[]{:S(2)}, u32[]{:S(2)}) collective-permute-start(bf16[32,1536]{1,0:T(8,128)(2,1)S(1)} %get-tuple-element.13.refs_2_), channel_id=1, source_target_pairs={{0,2},{1,3},{2,0},{3,1},{4,6},{5,7},{6,4},{7,5},{8,10},{9,11},{10,... | collective-permute-start | bytes 294920 | tf_op jit(solution)/shard_map/ppermute | solution.py:241
  10.1 6.4 %collective-permute-done.4.refs_6_ = bf16[32,1536]{1,0:T(8,128)(2,1)S(1)} collective-permute-done((bf16[32,1536]{1,0:T(8,128)(2,1)S(1)}, bf16[32,1536]{1,0:T(8,128)(2,1)S(1)}, u32[]{:S(2)}, u32[]{:S(2)}) %collective-permute-start.4) | collective-permute-done | bytes 98336 | tf_op jit(solution)/shard_map/ppermute | solution.py:241
  16.5 1.5 %collective-permute-start.6 = (bf16[32,1536]{1,0:T(8,128)(2,1)S(1)}, bf16[32,1536]{1,0:T(8,128)(2,1)S(1)}, u32[]{:S(2)}, u32[]{:S(2)}) collective-permute-start(bf16[32,1536]{1,0:T(8,128)(2,1)S(1)} %collective-permute-done.4.refs_6_), channel_id=1, source_target_pairs={{0,2},{1,3},{2,0},{3,1},{4,6},{5,7},{6,4},{7,5},{8,10},{9,11},{10,... | collective-permute-start | bytes 294920 | tf_op jit(solution)/shard_map/ppermute | solution.py:241
  18.0 0.0 collective-permute-start.1
  18.0 0.5 %collective-permute-start.5 = (bf16[32,1536]{1,0:T(8,128)(2,1)S(1)}, bf16[32,1536]{1,0:T(8,128)(2,1)S(1)}, u32[]{:S(2)}, u32[]{:S(2)}) collective-permute-start(bf16[32,1536]{1,0:T(8,128)(2,1)S(1)} %collective-permute-done.4.refs_6_), channel_id=1, source_target_pairs={{0,1},{1,0},{2,3},{3,2},{4,5},{5,4},{6,7},{7,6},{8,9},{9,8},{10,11... | collective-permute-start | bytes 294920 | tf_op jit(solution)/shard_map/ppermute | solution.py:241
  18.5 0.0 collective-permute-done.2.refs_4_
  18.5 0.0 collective-permute-start.3
  18.5 2.6 %collective-permute-done.6.refs_8_ = bf16[32,1536]{1,0:T(8,128)(2,1)S(1)} collective-permute-done((bf16[32,1536]{1,0:T(8,128)(2,1)S(1)}, bf16[32,1536]{1,0:T(8,128)(2,1)S(1)}, u32[]{:S(2)}, u32[]{:S(2)}) %collective-permute-start.6) | collective-permute-done | bytes 98336 | tf_op jit(solution)/shard_map/ppermute | solution.py:241
  21.1 0.0 collective-permute-start.7
  21.1 0.0 collective-permute-done.1.refs_3_
  21.1 0.0 collective-permute-done.5.refs_7_
  21.1 0.0 collective-permute-done.3.refs_5_
  21.1 1.3 %collective-permute-done.7.refs_9_ = bf16[32,1536]{1,0:T(8,128)(2,1)S(1)} collective-permute-done((bf16[32,1536]{1,0:T(8,128)(2,1)S(1)}, bf16[32,1536]{1,0:T(8,128)(2,1)S(1)}, u32[]{:S(2)}, u32[]{:S(2)}) %collective-permute-start.7) | collective-permute-done | bytes 98336 | tf_op jit(solution)/shard_map/ppermute | solution.py:241
  22.4 0.0 collective-permute-done.refs_1_
  22.4 1.2 %cross.1 = (bf16[16,256]{1,0:T(8,128)(2,1)S(1)}, bf16[16,256]{1,0:T(8,128)(2,1)S(1)}) custom-call(bf16[128,1536]{1,0:T(8,128)(2,1)S(1)} %get-tuple-element.11.refs_0_, bf16[128,1536]{1,0:T(8,128)(2,1)S(1)} %collective-permute-done.refs_1_, bf16[32,1536]{1,0:T(8,128)(2,1)S(1)} %get-tuple-element.13.refs_2_, ...), custom_call_target="tpu_custom_call" | custom-call | flops 201326592 | bytes 1572864 | tf_op jit(solution)/shard_map/cross/pallas_call | solution.py:176
  23.7 3.5 %collective-permute-start.8 = (bf16[16,256]{1,0:T(8,128)(2,1)S(1)}, bf16[16,256]{1,0:T(8,128)(2,1)S(1)}, u32[]{:S(2)}, u32[]{:S(2)}) collective-permute-start(bf16[16,256]{1,0:T(8,128)(2,1)S(1)} %get-tuple-element.15), channel_id=1, source_target_pairs={{0,4},{1,5},{2,6},{3,7},{4,0},{5,1},{6,2},{7,3},{8,12},{9,13},{10,... | collective-permute-start | bytes 24584 | tf_op jit(solution)/shard_map/ppermute | solution.py:241
  27.2 1.6 %collective-permute-done.8.got_ref = bf16[16,256]{1,0:T(8,128)(2,1)S(1)} collective-permute-done((bf16[16,256]{1,0:T(8,128)(2,1)S(1)}, bf16[16,256]{1,0:T(8,128)(2,1)S(1)}, u32[]{:S(2)}, u32[]{:S(2)}) %collective-permute-start.8) | collective-permute-done | bytes 8224 | tf_op jit(solution)/shard_map/ppermute | solution.py:241
  28.8 2.6 %synthesis.1 = bf16[256,8192]{1,0:T(8,128)(2,1)} custom-call(bf16[16,256]{1,0:T(8,128)(2,1)S(1)} %get-tuple-element.14.own_ref, bf16[16,256]{1,0:T(8,128)(2,1)S(1)} %collective-permute-done.8.got_ref, bf16[32,8192]{1,0:T(8,128)(2,1)S(1)} %get-tuple-element.16.table_ref), custom_call_target="tpu_custom_call" | custom-call | flops 134217728 | bytes 4718592 | tf_op jit(solution)/shard_map/synthesis/pallas_call | solution.py:224
Async XLA Ops:
  2.9 19.5 %collective-permute-start = (bf16[128,1536]{1,0:T(8,128)(2,1)S(1)}, bf16[128,1536]{1,0:T(8,128)(2,1)S(1)}, u32[]{:S(2)}, u32[]{:S(2)}) collective-permute-start(bf16[128,1536]{1,0:T(8,128)(2,1)S(1)} %get-tuple-element.12), channel_id=1, source_target_pairs={{0,4},{1,5},{2,6},{3,7},{4,0},{5,1},{6,2},{7,3},{8,12},{9,13},{10,... | collective-permute-start | bytes 1179656 | tf_op jit(solution)/shard_map/ppermute | solution.py:241
  6.0 10.5 %collective-permute-start.4 = (bf16[32,1536]{1,0:T(8,128)(2,1)S(1)}, bf16[32,1536]{1,0:T(8,128)(2,1)S(1)}, u32[]{:S(2)}, u32[]{:S(2)}) collective-permute-start(bf16[32,1536]{1,0:T(8,128)(2,1)S(1)} %get-tuple-element.13.refs_2_), channel_id=1, source_target_pairs={{0,8},{1,9},{2,10},{3,11},{4,12},{5,13},{6,14},{7,15},{8,0},{9,1},... | collective-permute-start | bytes 294920 | tf_op jit(solution)/shard_map/ppermute | solution.py:241
  8.6 9.9 %collective-permute-start.2 = (bf16[32,1536]{1,0:T(8,128)(2,1)S(1)}, bf16[32,1536]{1,0:T(8,128)(2,1)S(1)}, u32[]{:S(2)}, u32[]{:S(2)}) collective-permute-start(bf16[32,1536]{1,0:T(8,128)(2,1)S(1)} %get-tuple-element.13.refs_2_), channel_id=1, source_target_pairs={{0,2},{1,3},{2,0},{3,1},{4,6},{5,7},{6,4},{7,5},{8,10},{9,11},{10,... | collective-permute-start | bytes 294920 | tf_op jit(solution)/shard_map/ppermute | solution.py:241
  16.5 4.6 %collective-permute-start.6 = (bf16[32,1536]{1,0:T(8,128)(2,1)S(1)}, bf16[32,1536]{1,0:T(8,128)(2,1)S(1)}, u32[]{:S(2)}, u32[]{:S(2)}) collective-permute-start(bf16[32,1536]{1,0:T(8,128)(2,1)S(1)} %collective-permute-done.4.refs_6_), channel_id=1, source_target_pairs={{0,2},{1,3},{2,0},{3,1},{4,6},{5,7},{6,4},{7,5},{8,10},{9,11},{10,... | collective-permute-start | bytes 294920 | tf_op jit(solution)/shard_map/ppermute | solution.py:241
  18.0 3.1 %collective-permute-start.1 = (bf16[32,1536]{1,0:T(8,128)(2,1)S(1)}, bf16[32,1536]{1,0:T(8,128)(2,1)S(1)}, u32[]{:S(2)}, u32[]{:S(2)}) collective-permute-start(bf16[32,1536]{1,0:T(8,128)(2,1)S(1)} %get-tuple-element.13.refs_2_), channel_id=1, source_target_pairs={{0,1},{1,0},{2,3},{3,2},{4,5},{5,4},{6,7},{7,6},{8,9},{9,8},{10,11... | collective-permute-start | bytes 294920 | tf_op jit(solution)/shard_map/ppermute | solution.py:241
  18.0 3.1 %collective-permute-start.5 = (bf16[32,1536]{1,0:T(8,128)(2,1)S(1)}, bf16[32,1536]{1,0:T(8,128)(2,1)S(1)}, u32[]{:S(2)}, u32[]{:S(2)}) collective-permute-start(bf16[32,1536]{1,0:T(8,128)(2,1)S(1)} %collective-permute-done.4.refs_6_), channel_id=1, source_target_pairs={{0,1},{1,0},{2,3},{3,2},{4,5},{5,4},{6,7},{7,6},{8,9},{9,8},{10,11... | collective-permute-start | bytes 294920 | tf_op jit(solution)/shard_map/ppermute | solution.py:241
  18.5 2.6 %collective-permute-start.3 = (bf16[32,1536]{1,0:T(8,128)(2,1)S(1)}, bf16[32,1536]{1,0:T(8,128)(2,1)S(1)}, u32[]{:S(2)}, u32[]{:S(2)}) collective-permute-start(bf16[32,1536]{1,0:T(8,128)(2,1)S(1)} %collective-permute-done.2.refs_4_), channel_id=1, source_target_pairs={{0,1},{1,0},{2,3},{3,2},{4,5},{5,4},{6,7},{7,6},{8,9},{9,8},{10,11... | collective-permute-start | bytes 294920 | tf_op jit(solution)/shard_map/ppermute | solution.py:241
  21.1 1.3 %collective-permute-start.7 = (bf16[32,1536]{1,0:T(8,128)(2,1)S(1)}, bf16[32,1536]{1,0:T(8,128)(2,1)S(1)}, u32[]{:S(2)}, u32[]{:S(2)}) collective-permute-start(bf16[32,1536]{1,0:T(8,128)(2,1)S(1)} %collective-permute-done.6.refs_8_), channel_id=1, source_target_pairs={{0,1},{1,0},{2,3},{3,2},{4,5},{5,4},{6,7},{7,6},{8,9},{9,8},{10,11... | collective-permute-start | bytes 294920 | tf_op jit(solution)/shard_map/ppermute | solution.py:241
  23.7 5.1 %collective-permute-start.8 = (bf16[16,256]{1,0:T(8,128)(2,1)S(1)}, bf16[16,256]{1,0:T(8,128)(2,1)S(1)}, u32[]{:S(2)}, u32[]{:S(2)}) collective-permute-start(bf16[16,256]{1,0:T(8,128)(2,1)S(1)} %get-tuple-element.15), channel_id=1, source_target_pairs={{0,4},{1,5},{2,6},{3,7},{4,0},{5,1},{6,2},{7,3},{8,12},{9,13},{10,... | collective-permute-start | bytes 24584 | tf_op jit(solution)/shard_map/ppermute | solution.py:241

commit v4 on v3

v4 whole, which is shorter than its diff:
```python
import functools
import math

import jax
import jax.numpy as jnp
from jax import lax
from jax.experimental import pallas as pl
from jax.experimental.pallas import tpu as pltpu
from jax.sharding import PartitionSpec as P

LL = 3072
REAL = 16
NPHI = 8192
LANES = 128
BF16 = jnp.bfloat16
F32 = jnp.float32
VMEM = pl.BlockSpec(memory_space=pltpu.VMEM)
HBM = pl.BlockSpec(memory_space=pltpu.HBM)


def iota(shape, dim):
    return lax.broadcasted_iota(jnp.int32, shape, dim)


def angle(phase):
    phase = phase & (NPHI - 1)
    phase = jnp.where(phase >= NPHI // 2, phase - NPHI, phase)
    return phase.astype(F32) * (2.0 * math.pi / NPHI)


def write_table(table_ref, m_smem, quad):
    n = table_ref.shape[0] // 2
    line = n // quad
    index = iota((n, LANES), 0)
    lane = iota((n, LANES), 1)
    values = jnp.zeros((n, LANES), jnp.int32)
    for j in range(n):
        values = jnp.where(index == j, m_smem[j % line * quad + j // line], values)
    fine = angle(values * lane)
    coarse = angle(values * lane * LANES)
    cos_f, sin_f = jnp.cos(fine), jnp.sin(fine)
    cos_c, sin_c = jnp.cos(coarse), jnp.sin(coarse)
    for a in range(NPHI // LANES):
        ca, sa = cos_c[:, a : a + 1], sin_c[:, a : a + 1]
        span = slice(a * LANES, (a + 1) * LANES)
        table_ref[:n, span] = (ca * cos_f - sa * sin_f).astype(BF16)
        table_ref[n:, span] = (-(sa * cos_f + ca * sin_f)).astype(BF16)


def prepare_kernel(
    quad, m_ref, coeff_ref, block_ref, leg_ref, filtered_ref, send_ref, table_ref,
    m_smem, coeff_vmem, block_vmem, leg_vmem, sems,
):
    me = lax.axis_index("mset")
    columns, order_max = coeff_ref.shape
    pieces = block_vmem.shape[0]
    depth = order_max // pieces
    copy_m = pltpu.make_async_copy(m_ref, m_smem, sems.at[0])
    copy_leg = pltpu.make_async_copy(leg_ref, leg_vmem, sems.at[1])
    copy_coeff = pltpu.make_async_copy(coeff_ref, coeff_vmem, sems.at[2])
    copy_blocks = [
        pltpu.make_async_copy(
            block_ref.at[pl.ds(p * depth, depth), :], block_vmem.at[p], sems.at[3 + p]
        )
        for p in range(pieces)
    ]
    for copy in [copy_m, copy_leg, copy_coeff] + copy_blocks:
        copy.start()

    copy_m.wait()
    write_table(table_ref, m_smem, quad)

    rows = leg_ref.shape[0]
    n = m_ref.shape[0]
    line = n // quad
    share = rows // quad
    row, col = iota((share, rows), 0), iota((share, rows), 1)
    wanted = row // line * n + lax.rem(row, line) * quad
    copy_leg.wait()
    for low in range(quad):
        pick = (wanted + low == col).astype(BF16)
        send_ref[low] = jnp.dot(pick, leg_vmem[...], preferred_element_type=F32).astype(BF16)

    order = LL - m_smem[me]
    copy_coeff.wait()
    coeff = coeff_vmem[...]
    coeff = jnp.where(iota(coeff.shape, 1) < order, coeff, jnp.zeros_like(coeff))
    total = jnp.zeros((columns, order_max), F32)
    for p in range(pieces):
        copy_blocks[p].wait()
        total += jnp.dot(
            coeff[:, p * depth : (p + 1) * depth], block_vmem[p], preferred_element_type=F32
        )
    filtered = jnp.where(iota(total.shape, 1) < order, total, 0.0).astype(BF16)
    for z in range(line):
        filtered_ref[z] = filtered


def prepare(m_list, coeff, block, legendre, quad):
    columns, order_max = coeff.shape
    rows = legendre.shape[0]
    n = m_list.shape[0]
    pieces = 6
    operands = (m_list, coeff, block, legendre)
    return pl.pallas_call(
        functools.partial(prepare_kernel, quad),
        out_shape=[
            jax.ShapeDtypeStruct((n // quad, columns, order_max), BF16),
            jax.ShapeDtypeStruct((quad, rows // quad, order_max), BF16),
            jax.ShapeDtypeStruct((2 * n, NPHI), BF16),
        ],
        in_specs=[HBM] * 4,
        out_specs=[VMEM] * 3,
        scratch_shapes=[
            pltpu.SMEM((n,), jnp.int32),
            pltpu.VMEM((columns, order_max), BF16),
            pltpu.VMEM((pieces, order_max // pieces, order_max), BF16),
            pltpu.VMEM((rows, order_max), BF16),
            pltpu.SemaphoreType.DMA((3 + pieces,)),
        ],
        compiler_params=pltpu.CompilerParams(vmem_limit_bytes=32 << 20),
        cost_estimate=pl.CostEstimate(
            flops=2 * (columns * order_max * order_max + rows * rows * order_max),
            bytes_accessed=2 * (block.size + legendre.size),
            transcendentals=0,
        ),
        name="prepare",
    )(*[pltpu.with_memory_space_constraint(x, pltpu.HBM) for x in operands])


def cross_kernel(chunk, leg_ref, filtered_ref, out_ref):
    quad, share, order_max = leg_ref.shape
    line, columns, _ = filtered_ref.shape
    cycles = share // line
    rows = quad * share
    wide = chunk * columns
    legendre = leg_ref[...].reshape(rows, order_max)
    slot = lax.rem(iota((rows, wide), 0), line)
    local = iota((rows, wide), 1) // columns
    fold = (iota((quad * cycles, rows), 0) == iota((quad * cycles, rows), 1) // line).astype(BF16)
    for q in range(line // chunk):
        piece = filtered_ref[q * chunk : (q + 1) * chunk].reshape(wide, order_max)
        product = lax.dot_general(
            legendre, piece, (((1,), (1,)), ((), ())), preferred_element_type=F32
        )
        chosen = jnp.where(slot == local + q * chunk, product, 0.0).astype(BF16)
        folded = jnp.dot(fold, chosen, preferred_element_type=F32).astype(BF16)
        out_ref[:, :, q * wide : (q + 1) * wide] = folded.reshape(quad, cycles, wide)


def cross(legendre, filtered):
    quad, share, order_max = legendre.shape
    line, columns, _ = filtered.shape
    return pl.pallas_call(
        functools.partial(cross_kernel, min(8, line)),
        out_shape=jax.ShapeDtypeStruct((quad, share // line, line * columns), BF16),
        in_specs=[VMEM] * 2,
        out_specs=VMEM,
        compiler_params=pltpu.CompilerParams(vmem_limit_bytes=32 << 20),
        cost_estimate=pl.CostEstimate(
            flops=2 * legendre.size * line * columns,
            bytes_accessed=2 * (legendre.size + filtered.size),
            transcendentals=0,
        ),
        name="cross",
    )(legendre, filtered)


def synthesis_kernel(tiles, columns, parts_ref, table_ref, out_ref, held, sems):
    quad, cycles, part = parts_ref.shape
    wide = quad * part
    n = wide // columns
    out_rows = cycles * REAL
    joined = jnp.concatenate([parts_ref[low] for low in range(quad)], axis=1)
    repeat = (iota((out_rows, cycles), 0) // REAL == iota((out_rows, cycles), 1)).astype(BF16)
    spread = jnp.dot(repeat, joined, preferred_element_type=F32)
    same_real = lax.rem(iota((out_rows, wide), 0), REAL) == lax.rem(
        iota((out_rows, wide), 1), REAL
    )
    chosen = jnp.where(same_real, spread, 0.0).astype(BF16)
    row, col = iota((wide, 2 * n), 0), iota((wide, 2 * n), 1)
    pick = (lax.rem(row, columns) // REAL * n + row // columns == col).astype(BF16)
    flat = jnp.dot(chosen, pick, preferred_element_type=F32).astype(BF16)

    width = NPHI // tiles
    copies = []
    for t in range(tiles):
        span = pl.ds(t * width, width)
        summed = jnp.dot(flat, table_ref[:, span], preferred_element_type=F32)
        held[:, span] = (summed * (1.0 / math.sqrt(n))).astype(BF16)
        copy = pltpu.make_async_copy(held.at[:, span], out_ref.at[:, span], sems.at[t])
        copy.start()
        copies.append(copy)
    for copy in copies:
        copy.wait()


def synthesize(parts, table, columns):
    cycles = parts.shape[1]
    tiles = 8
    out_rows = cycles * REAL
    return pl.pallas_call(
        functools.partial(synthesis_kernel, tiles, columns),
        out_shape=jax.ShapeDtypeStruct((out_rows, NPHI), BF16),
        in_specs=[VMEM] * 2,
        out_specs=HBM,
        scratch_shapes=[pltpu.VMEM((out_rows, NPHI), BF16), pltpu.SemaphoreType.DMA((tiles,))],
        compiler_params=pltpu.CompilerParams(vmem_limit_bytes=32 << 20),
        cost_estimate=pl.CostEstimate(
            flops=2 * out_rows * table.size,
            bytes_accessed=2 * (out_rows * NPHI + table.size),
            transcendentals=0,
        ),
        name="synthesis",
    )(parts, table)


def swap(value, groups):
    return lax.all_to_all(
        value, "mset", split_axis=0, concat_axis=0, axis_index_groups=groups, tiled=True
    )


def body(m_list, coeff, blocks, legendre):
    size = lax.axis_size("mset")
    per_device, columns, order_max = coeff.shape
    quad = min(4, size)
    if per_device != 1 or size % quad:
        raise ValueError("unsupported mesh")
    cycles, n, _ = legendre.shape
    quads = [list(range(d, d + quad)) for d in range(0, size, quad)]
    lines = [list(range(low, size, quad)) for low in range(quad)]
    filtered, send, table = prepare(
        m_list, coeff[0], blocks[0], legendre.reshape(cycles * n, order_max), quad
    )
    shared = swap(send, quads)
    shards = swap(filtered, lines)
    parts = swap(cross(shared, shards), quads)
    sky_map = synthesize(parts, table, columns)
    return sky_map.reshape(cycles, REAL, NPHI)


def solution(mesh):
    in_specs = (
        P(),
        P(("groups", "mset"), None, None),
        P(("groups", "mset"), None, None),
        P(("groups", "mset"), None, None),
    )
    out_specs = P(("groups", "mset"), None, None)
    return jax.shard_map(body, mesh=mesh, in_specs=in_specs, out_specs=out_specs, check_vma=False)
```

time: 31.5 us -> 44.2 us (1.40)
  blocking collectives: 0 us -> 37.9 us
  starting transfers between devices: 12.7 us -> 0 us
  waiting for transfers between devices: 11.9 us -> 0 us
  Pallas kernels: 6.75 us -> 6.05 us
    all_to_all x0 -> x3, blocking collectives: none -> 37.9 us  [swap(): lax.all_to_all(value, 'mset', split_axis=0, concat_axis=0, axis_index_gro...]
    ppermute x9 -> x0, starting transfers between devices: 12.7 us -> none  [exchange(): return lax.ppermute(value, 'mset', [(d, d ^ mask) for d in range(size)])]
    ppermute x9 -> x0, waiting for transfers between devices: 11.9 us -> none  [exchange(): return lax.ppermute(value, 'mset', [(d, d ^ mask) for d in range(size)])]
    pallas_call x2, Pallas kernels: 4.15 us -> 3.45 us  [the longest x1 2.94 us: prepare(): pl.pallas_call(functools.partial(prepare_kernel, quad), out_shape=[jax.Sh...]
  transfers between devices with their start and end apart: 9 -> 0, of which waited for: 4 -> 0; matrix products, arithmetic and copies ran while one was open for 0% -> 0% of each run, Pallas kernels for 0% -> 0%
where the time goes in v4:
time: 44.2 us; the launch traced here: 43.9 us
  blocking collectives  37.9 us (86%)
  Pallas kernels  6.05 us (14%)
    all_to_all x3, blocking collectives, swap(): lax.all_to_all(value, 'mset', split_axis=0, concat_axis=0, axis_index_gro...  37.9 us
    pallas_call x1, Pallas kernels, prepare(): pl.pallas_call(functools.partial(prepare_kernel, quad), out_shape=[jax.Sh...  2.94 us
    pallas_call x1, Pallas kernels, synthesize(): pl.pallas_call(functools.partial(synthesis_kernel, tiles, columns), out_s...  2.6 us

profile of v4, /device:TPU:0, one launch (start us, length us, event | category | flops | bytes accessed | tf_op | source)
XLA Modules:
  0.0 43.9 jit_solution(13769191933483145621)
XLA Ops:
  0.0 2.9 %prepare.1 = (bf16[4,32,1536]{2,1,0:T(8,128)(2,1)S(1)}, bf16[4,64,1536]{2,1,0:T(8,128)(2,1)S(1)}, bf16[32,8192]{1,0:T(8,128)(2,1)S(1)}) custom-call(s32[16]{0:T(128)} %m_ref.1, bf16[32,1536]{1,0:T(8,128)(2,1)} %bitcast.6, bf16[1536,1536]{1,0:T(8,128)(2,1)} %bitcast.4, bf16[256,1536]{1,0:T(8,128)(2,1)} %bitcast.5), custom_call_target="tpu_custom_call" | custom-call | flops 352321536 | bytes 5505024 | tf_op jit(solution)/shard_map/prepare/pallas_call | solution.py:105
  2.9 15.7 %all_to_all.15.leg_ref = bf16[4,64,1536]{2,1,0:T(8,128)(2,1)S(1)} all-to-all(bf16[4,64,1536]{2,1,0:T(8,128)(2,1)S(1)} %get-tuple-element.8), channel_id=1, replica_groups={{0,1,2,3},{4,5,6,7},{8,9,10,11},{12,13,14,15},{16,17,18,19},{20,21,22,2..., dimensions={0} | all-to-all | bytes 1572864 | tf_op jit(solution)/shard_map/all_to_all | solution.py:219
  18.6 16.0 %all_to_all.16.filtered_ref = bf16[4,32,1536]{2,1,0:T(8,128)(2,1)S(1)} all-to-all(bf16[4,32,1536]{2,1,0:T(8,128)(2,1)S(1)} %get-tuple-element.9), channel_id=1, replica_groups={{0,4,8,12},{1,5,9,13},{2,6,10,14},{3,7,11,15},{16,20,24,28},{17,21,25,2..., dimensions={0} | all-to-all | bytes 786432 | tf_op jit(solution)/shard_map/all_to_all | solution.py:219
  34.6 0.5 %cross.1 = bf16[4,16,128]{2,1,0:T(8,128)(2,1)S(1)} custom-call(bf16[4,64,1536]{2,1,0:T(8,128)(2,1)S(1)} %all_to_all.15.leg_ref, bf16[4,32,1536]{2,1,0:T(8,128)(2,1)S(1)} %all_to_all.16.filtered_ref), custom_call_target="tpu_custom_call" | custom-call | flops 100663296 | bytes 1179648 | tf_op jit(solution)/shard_map/cross/pallas_call | solution.py:154
  35.1 6.2 %all_to_all.17.parts_ref = bf16[4,16,128]{2,1,0:T(8,128)(2,1)S(1)} all-to-all(bf16[4,16,128]{2,1,0:T(8,128)(2,1)S(1)} %cross.1), channel_id=1, replica_groups={{0,1,2,3},{4,5,6,7},{8,9,10,11},{12,13,14,15},{16,17,18,19},{20,21,22,2..., dimensions={0} | all-to-all | bytes 32768 | tf_op jit(solution)/shard_map/all_to_all | solution.py:219
  41.3 2.6 %synthesis.1 = bf16[256,8192]{1,0:T(8,128)(2,1)} custom-call(bf16[4,16,128]{2,1,0:T(8,128)(2,1)S(1)} %all_to_all.17.parts_ref, bf16[32,8192]{1,0:T(8,128)(2,1)S(1)} %get-tuple-element.10.table_ref), custom_call_target="tpu_custom_call" | custom-call | flops 134217728 | bytes 4718592 | tf_op jit(solution)/shard_map/synthesis/pallas_call | solution.py:202

commit v5 on v3

--- a/solution.py
+++ b/solution.py
@@ -243,9 +243,12 @@
 
 def gather_xor(value, size, at):
     shards = {0: value}
-    bits = [b for b in range(size.bit_length() - 1) if b != at]
-    for b in reversed(bits):
-        shards.update({k | 1 << b: exchange(v, size, 1 << b) for k, v in shards.items()})
+    top = size.bit_length() - 1
+    stages = [[b, b + 1] if b + 1 < top else [b] for b in range(2, top, 2)]
+    stages = [[b] for b in range(min(2, top)) if b != at] + stages
+    for bits in reversed(stages):
+        masks = [sum(1 << b for e, b in enumerate(bits) if m >> e & 1) for m in range(1, 1 << len(bits))]
+        shards.update({k | m: exchange(v, size, m) for m in masks for k, v in list(shards.items())})
     return [shards[k] for k in sorted(shards)]
 
 
@@ -255,12 +258,12 @@
     if per_device != 1 or size & (size - 1):
         raise ValueError("unsupported mesh")
     cycles, n, _ = legendre.shape
-    at = min(2, size.bit_length() - 2)
+    at = min(1, size.bit_length() - 2)
     filtered, keep, send, table = prepare(
         m_list, coeff[0], blocks[0], legendre.reshape(cycles * n, order_max), at
     )
+    shards = gather_xor(filtered, size, at)
     got = exchange(send, size, 1 << at)
-    shards = gather_xor(filtered, size, at)
     own, back = cross(keep, got, shards, n, at)
     other = exchange(back, size, 1 << at)
     sky_map = synthesize(own, other, table, columns)

time: 31.5 us -> 26.7 us (0.85)
  starting transfers between devices: 12.7 us -> 8.47 us
  waiting for transfers between devices: 11.9 us -> 11.3 us
    ppermute x9, starting transfers between devices: 12.7 us -> 8.47 us  [exchange(): return lax.ppermute(value, 'mset', [(d, d ^ mask) for d in range(size)])]
    ppermute x9, waiting for transfers between devices: 11.9 us -> 11.3 us  [exchange(): return lax.ppermute(value, 'mset', [(d, d ^ mask) for d in range(size)])]
  transfers between devices with their start and end apart: 9 -> 9, of which waited for: 4 -> 5; matrix products, arithmetic and copies ran while one was open for 0% -> 0% of each run, Pallas kernels for 0% -> 0%
where the time goes in v5:
time: 26.7 us; the launch traced here: 26.5 us
  waiting for transfers between devices  11.3 us (42%)
  starting transfers between devices  8.47 us (32%)
  Pallas kernels  6.75 us (25%)
    ppermute x9, waiting for transfers between devices, exchange(): return lax.ppermute(value, 'mset', [(d, d ^ mask) for d in range(size)])  11.3 us
    ppermute x9, starting transfers between devices, exchange(): return lax.ppermute(value, 'mset', [(d, d ^ mask) for d in range(size)])  8.47 us
    pallas_call x1, Pallas kernels, prepare(): pl.pallas_call(functools.partial(prepare_kernel, at), out_shape=[jax.Shap...  2.91 us
    pallas_call x1, Pallas kernels, synthesize(): pl.pallas_call(functools.partial(synthesis_kernel, tiles, columns), out_s...  2.6 us
    pallas_call x1, Pallas kernels, cross(): pl.pallas_call(functools.partial(cross_kernel, at, n, count, min(8, count...  1.24 us
  transfers between devices with their start and end apart: 9, of which 5 were waited for; matrix products, arithmetic and copies ran while one was open for 0% of the time, Pallas kernels for 0%

profile of v5, /device:TPU:0, one launch (start us, length us, event | category | flops | bytes accessed | tf_op | source)
XLA Modules:
  0.0 26.5 jit_solution(11843919469806492302)
XLA Ops:
  0.0 2.9 %prepare.1 = (bf16[32,1536]{1,0:T(8,128)(2,1)S(1)}, bf16[128,1536]{1,0:T(8,128)(2,1)S(1)}, bf16[128,1536]{1,0:T(8,128)(2,1)S(1)}, bf16[32,8192]{1,0:T(8,128)(2,1)S(1)}) custom-call(s32[16]{0:T(128)} %m_ref.1, bf16[32,1536]{1,0:T(8,128)(2,1)} %bitcast.6, bf16[1536,1536]{1,0:T(8,128)(2,1)} %bitcast.4, bf16[256,1536]{1,0:T(8,128)(2,1)} %bitcast.5), custom_call_target="tpu_custom_call" | custom-call | flops 352321536 | bytes 5505024 | tf_op jit(solution)/shard_map/prepare/pallas_call | solution.py:116
  2.9 3.0 %collective-permute-start = (bf16[128,1536]{1,0:T(8,128)(2,1)S(1)}, bf16[128,1536]{1,0:T(8,128)(2,1)S(1)}, u32[]{:S(2)}, u32[]{:S(2)}) collective-permute-start(bf16[128,1536]{1,0:T(8,128)(2,1)S(1)} %get-tuple-element.12), channel_id=1, source_target_pairs={{0,2},{1,3},{2,0},{3,1},{4,6},{5,7},{6,4},{7,5},{8,10},{9,11},{10,... | collective-permute-start | bytes 1179656 | tf_op jit(solution)/shard_map/ppermute | solution.py:241
  5.9 3.6 %collective-permute-start.6 = (bf16[32,1536]{1,0:T(8,128)(2,1)S(1)}, bf16[32,1536]{1,0:T(8,128)(2,1)S(1)}, u32[]{:S(2)}, u32[]{:S(2)}) collective-permute-start(bf16[32,1536]{1,0:T(8,128)(2,1)S(1)} %get-tuple-element.13.refs_2_), channel_id=1, source_target_pairs={{0,12},{1,13},{2,14},{3,15},{4,8},{5,9},{6,10},{7,11},{8,4},{9,5},... | collective-permute-start | bytes 294920 | tf_op jit(solution)/shard_map/ppermute | solution.py:241
  9.5 0.0 collective-permute-start.4
  9.6 0.8 %collective-permute-start.2 = (bf16[32,1536]{1,0:T(8,128)(2,1)S(1)}, bf16[32,1536]{1,0:T(8,128)(2,1)S(1)}, u32[]{:S(2)}, u32[]{:S(2)}) collective-permute-start(bf16[32,1536]{1,0:T(8,128)(2,1)S(1)} %get-tuple-element.13.refs_2_), channel_id=1, source_target_pairs={{0,4},{1,5},{2,6},{3,7},{4,0},{5,1},{6,2},{7,3},{8,12},{9,13},{10,... | collective-permute-start | bytes 294920 | tf_op jit(solution)/shard_map/ppermute | solution.py:241
  10.3 0.0 collective-permute-start.1
  10.3 3.1 %collective-permute-done.6.refs_8_ = bf16[32,1536]{1,0:T(8,128)(2,1)S(1)} collective-permute-done((bf16[32,1536]{1,0:T(8,128)(2,1)S(1)}, bf16[32,1536]{1,0:T(8,128)(2,1)S(1)}, u32[]{:S(2)}, u32[]{:S(2)}) %collective-permute-start.6) | collective-permute-done | bytes 98336 | tf_op jit(solution)/shard_map/ppermute | solution.py:241
  13.5 0.0 collective-permute-start.7
  13.5 4.1 %collective-permute-done.4.refs_6_ = bf16[32,1536]{1,0:T(8,128)(2,1)S(1)} collective-permute-done((bf16[32,1536]{1,0:T(8,128)(2,1)S(1)}, bf16[32,1536]{1,0:T(8,128)(2,1)S(1)}, u32[]{:S(2)}, u32[]{:S(2)}) %collective-permute-start.4) | collective-permute-done | bytes 98336 | tf_op jit(solution)/shard_map/ppermute | solution.py:241
  17.5 0.0 collective-permute-start.5
  17.5 0.0 collective-permute-done.2.refs_4_
  17.5 0.5 %collective-permute-start.3 = (bf16[32,1536]{1,0:T(8,128)(2,1)S(1)}, bf16[32,1536]{1,0:T(8,128)(2,1)S(1)}, u32[]{:S(2)}, u32[]{:S(2)}) collective-permute-start(bf16[32,1536]{1,0:T(8,128)(2,1)S(1)} %collective-permute-done.2.refs_4_), channel_id=1, source_target_pairs={{0,1},{1,0},{2,3},{3,2},{4,5},{5,4},{6,7},{7,6},{8,9},{9,8},{10,11... | collective-permute-start | bytes 294920 | tf_op jit(solution)/shard_map/ppermute | solution.py:241
  18.1 0.0 collective-permute-done.1.refs_3_
  18.1 0.0 collective-permute-done.7.refs_9_
  18.1 0.8 %collective-permute-done.5.refs_7_ = bf16[32,1536]{1,0:T(8,128)(2,1)S(1)} collective-permute-done((bf16[32,1536]{1,0:T(8,128)(2,1)S(1)}, bf16[32,1536]{1,0:T(8,128)(2,1)S(1)}, u32[]{:S(2)}, u32[]{:S(2)}) %collective-permute-start.5) | collective-permute-done | bytes 98336 | tf_op jit(solution)/shard_map/ppermute | solution.py:241
  18.8 0.2 collective-permute-done.3.refs_5_
  19.0 0.0 collective-permute-done.refs_1_
  19.0 1.2 %cross.1 = (bf16[16,256]{1,0:T(8,128)(2,1)S(1)}, bf16[16,256]{1,0:T(8,128)(2,1)S(1)}) custom-call(bf16[128,1536]{1,0:T(8,128)(2,1)S(1)} %get-tuple-element.11.refs_0_, bf16[128,1536]{1,0:T(8,128)(2,1)S(1)} %collective-permute-done.refs_1_, bf16[32,1536]{1,0:T(8,128)(2,1)S(1)} %get-tuple-element.13.refs_2_, ...), custom_call_target="tpu_custom_call" | custom-call | flops 201326592 | bytes 1572864 | tf_op jit(solution)/shard_map/cross/pallas_call | solution.py:176
  20.2 0.5 %collective-permute-start.8 = (bf16[16,256]{1,0:T(8,128)(2,1)S(1)}, bf16[16,256]{1,0:T(8,128)(2,1)S(1)}, u32[]{:S(2)}, u32[]{:S(2)}) collective-permute-start(bf16[16,256]{1,0:T(8,128)(2,1)S(1)} %get-tuple-element.15), channel_id=1, source_target_pairs={{0,2},{1,3},{2,0},{3,1},{4,6},{5,7},{6,4},{7,5},{8,10},{9,11},{10,... | collective-permute-start | bytes 24584 | tf_op jit(solution)/shard_map/ppermute | solution.py:241
  20.8 3.1 %collective-permute-done.8.got_ref = bf16[16,256]{1,0:T(8,128)(2,1)S(1)} collective-permute-done((bf16[16,256]{1,0:T(8,128)(2,1)S(1)}, bf16[16,256]{1,0:T(8,128)(2,1)S(1)}, u32[]{:S(2)}, u32[]{:S(2)}) %collective-permute-start.8) | collective-permute-done | bytes 8224 | tf_op jit(solution)/shard_map/ppermute | solution.py:241
  23.9 2.6 %synthesis.1 = bf16[256,8192]{1,0:T(8,128)(2,1)} custom-call(bf16[16,256]{1,0:T(8,128)(2,1)S(1)} %get-tuple-element.14.own_ref, bf16[16,256]{1,0:T(8,128)(2,1)S(1)} %collective-permute-done.8.got_ref, bf16[32,8192]{1,0:T(8,128)(2,1)S(1)} %get-tuple-element.16.table_ref), custom_call_target="tpu_custom_call" | custom-call | flops 134217728 | bytes 4718592 | tf_op jit(solution)/shard_map/synthesis/pallas_call | solution.py:224
Async XLA Ops:
  2.9 16.1 %collective-permute-start = (bf16[128,1536]{1,0:T(8,128)(2,1)S(1)}, bf16[128,1536]{1,0:T(8,128)(2,1)S(1)}, u32[]{:S(2)}, u32[]{:S(2)}) collective-permute-start(bf16[128,1536]{1,0:T(8,128)(2,1)S(1)} %get-tuple-element.12), channel_id=1, source_target_pairs={{0,2},{1,3},{2,0},{3,1},{4,6},{5,7},{6,4},{7,5},{8,10},{9,11},{10,... | collective-permute-start | bytes 1179656 | tf_op jit(solution)/shard_map/ppermute | solution.py:241
  5.9 7.5 %collective-permute-start.6 = (bf16[32,1536]{1,0:T(8,128)(2,1)S(1)}, bf16[32,1536]{1,0:T(8,128)(2,1)S(1)}, u32[]{:S(2)}, u32[]{:S(2)}) collective-permute-start(bf16[32,1536]{1,0:T(8,128)(2,1)S(1)} %get-tuple-element.13.refs_2_), channel_id=1, source_target_pairs={{0,12},{1,13},{2,14},{3,15},{4,8},{5,9},{6,10},{7,11},{8,4},{9,5},... | collective-permute-start | bytes 294920 | tf_op jit(solution)/shard_map/ppermute | solution.py:241
  9.5 8.0 %collective-permute-start.4 = (bf16[32,1536]{1,0:T(8,128)(2,1)S(1)}, bf16[32,1536]{1,0:T(8,128)(2,1)S(1)}, u32[]{:S(2)}, u32[]{:S(2)}) collective-permute-start(bf16[32,1536]{1,0:T(8,128)(2,1)S(1)} %get-tuple-element.13.refs_2_), channel_id=1, source_target_pairs={{0,8},{1,9},{2,10},{3,11},{4,12},{5,13},{6,14},{7,15},{8,0},{9,1},... | collective-permute-start | bytes 294920 | tf_op jit(solution)/shard_map/ppermute | solution.py:241
  9.6 8.0 %collective-permute-start.2 = (bf16[32,1536]{1,0:T(8,128)(2,1)S(1)}, bf16[32,1536]{1,0:T(8,128)(2,1)S(1)}, u32[]{:S(2)}, u32[]{:S(2)}) collective-permute-start(bf16[32,1536]{1,0:T(8,128)(2,1)S(1)} %get-tuple-element.13.refs_2_), channel_id=1, source_target_pairs={{0,4},{1,5},{2,6},{3,7},{4,0},{5,1},{6,2},{7,3},{8,12},{9,13},{10,... | collective-permute-start | bytes 294920 | tf_op jit(solution)/shard_map/ppermute | solution.py:241
  10.3 7.7 %collective-permute-start.1 = (bf16[32,1536]{1,0:T(8,128)(2,1)S(1)}, bf16[32,1536]{1,0:T(8,128)(2,1)S(1)}, u32[]{:S(2)}, u32[]{:S(2)}) collective-permute-start(bf16[32,1536]{1,0:T(8,128)(2,1)S(1)} %get-tuple-element.13.refs_2_), channel_id=1, source_target_pairs={{0,1},{1,0},{2,3},{3,2},{4,5},{5,4},{6,7},{7,6},{8,9},{9,8},{10,11... | collective-permute-start | bytes 294920 | tf_op jit(solution)/shard_map/ppermute | solution.py:241
  13.5 4.6 %collective-permute-start.7 = (bf16[32,1536]{1,0:T(8,128)(2,1)S(1)}, bf16[32,1536]{1,0:T(8,128)(2,1)S(1)}, u32[]{:S(2)}, u32[]{:S(2)}) collective-permute-start(bf16[32,1536]{1,0:T(8,128)(2,1)S(1)} %collective-permute-done.6.refs_8_), channel_id=1, source_target_pairs={{0,1},{1,0},{2,3},{3,2},{4,5},{5,4},{6,7},{7,6},{8,9},{9,8},{10,11... | collective-permute-start | bytes 294920 | tf_op jit(solution)/shard_map/ppermute | solution.py:241
  17.5 1.3 %collective-permute-start.5 = (bf16[32,1536]{1,0:T(8,128)(2,1)S(1)}, bf16[32,1536]{1,0:T(8,128)(2,1)S(1)}, u32[]{:S(2)}, u32[]{:S(2)}) collective-permute-start(bf16[32,1536]{1,0:T(8,128)(2,1)S(1)} %collective-permute-done.4.refs_6_), channel_id=1, source_target_pairs={{0,1},{1,0},{2,3},{3,2},{4,5},{5,4},{6,7},{7,6},{8,9},{9,8},{10,11... | collective-permute-start | bytes 294920 | tf_op jit(solution)/shard_map/ppermute | solution.py:241
  17.5 1.5 %collective-permute-start.3 = (bf16[32,1536]{1,0:T(8,128)(2,1)S(1)}, bf16[32,1536]{1,0:T(8,128)(2,1)S(1)}, u32[]{:S(2)}, u32[]{:S(2)}) collective-permute-start(bf16[32,1536]{1,0:T(8,128)(2,1)S(1)} %collective-permute-done.2.refs_4_), channel_id=1, source_target_pairs={{0,1},{1,0},{2,3},{3,2},{4,5},{5,4},{6,7},{7,6},{8,9},{9,8},{10,11... | collective-permute-start | bytes 294920 | tf_op jit(solution)/shard_map/ppermute | solution.py:241
  20.2 3.7 %collective-permute-start.8 = (bf16[16,256]{1,0:T(8,128)(2,1)S(1)}, bf16[16,256]{1,0:T(8,128)(2,1)S(1)}, u32[]{:S(2)}, u32[]{:S(2)}) collective-permute-start(bf16[16,256]{1,0:T(8,128)(2,1)S(1)} %get-tuple-element.15), channel_id=1, source_target_pairs={{0,2},{1,3},{2,0},{3,1},{4,6},{5,7},{6,4},{7,5},{8,10},{9,11},{10,... | collective-permute-start | bytes 24584 | tf_op jit(solution)/shard_map/ppermute | solution.py:241

commit v6 on v3

--- a/solution.py
+++ b/solution.py
@@ -58,7 +58,7 @@
 
 
 def prepare_kernel(
-    at, m_ref, coeff_ref, block_ref, leg_ref, filtered_ref, keep_ref, send_ref, table_ref,
+    at, m_ref, coeff_ref, block_ref, leg_ref, filtered_ref, keep_ref, send_ref,
     m_smem, coeff_vmem, block_vmem, leg_vmem, sems,
 ):
     me = lax.axis_index("mset")
@@ -76,9 +76,6 @@
     ]
     for copy in [copy_m, copy_leg, copy_coeff] + copy_blocks:
         copy.start()
-
-    copy_m.wait()
-    write_table(table_ref, m_smem, me, at)
 
     rows = leg_ref.shape[0]
     n = m_ref.shape[0]
@@ -94,6 +91,7 @@
             pick.astype(BF16), leg_vmem[...], preferred_element_type=F32
         ).astype(BF16)
 
+    copy_m.wait()
     order = LL - m_smem[me]
     copy_coeff.wait()
     coeff = coeff_vmem[...]
@@ -119,10 +117,9 @@
             jax.ShapeDtypeStruct((columns, order_max), BF16),
             jax.ShapeDtypeStruct((rows // 2, order_max), BF16),
             jax.ShapeDtypeStruct((rows // 2, order_max), BF16),
-            jax.ShapeDtypeStruct((2 * n, NPHI), BF16),
         ],
         in_specs=[HBM] * 4,
-        out_specs=[VMEM] * 4,
+        out_specs=[VMEM] * 3,
         scratch_shapes=[
             pltpu.SMEM((n,), jnp.int32),
             pltpu.VMEM((columns, order_max), BF16),
@@ -140,7 +137,26 @@
     )(*[pltpu.with_memory_space_constraint(x, pltpu.HBM) for x in operands])
 
 
-def cross_kernel(at, n, shards, chunk, *refs):
+def trig_kernel(at, m_ref, after_ref, table_ref):
+    write_table(table_ref, m_ref, lax.axis_index("mset"), at)
+
+
+def trig_table(m_list, after, at):
+    rows = 2 * m_list.shape[0]
+    return pl.pallas_call(
+        functools.partial(trig_kernel, at),
+        out_shape=jax.ShapeDtypeStruct((rows, NPHI), BF16),
+        in_specs=[pl.BlockSpec(memory_space=pltpu.SMEM), pl.BlockSpec(memory_space=pl.ANY)],
+        out_specs=VMEM,
+        compiler_params=pltpu.CompilerParams(vmem_limit_bytes=16 << 20),
+        cost_estimate=pl.CostEstimate(
+            flops=8 * rows * NPHI, bytes_accessed=2 * rows * NPHI, transcendentals=0
+        ),
+        name="trig_table",
+    )(m_list, after)
+
+
+def cross_kernel(at, shards, chunk, *refs):
     keep_ref, got_ref = refs[:2]
     shard_refs = refs[2 : 2 + shards]
     own_ref, back_ref = refs[2 + shards :]
@@ -149,32 +165,33 @@
     columns = shard_refs[0].shape[0]
     cycles = own_ref.shape[0]
     wide = chunk * columns
-    slot = lax.rem(iota((half, wide), 0), shards)
-    local = iota((half, wide), 1) // columns
-    fold = (iota((cycles, half), 0) == iota((cycles, half), 1) // shards).astype(BF16)
+    legendre = jnp.concatenate([keep_ref[...], got_ref[...]], axis=0)
+    slot = lax.rem(iota((2 * half, wide), 0), shards)
+    local = iota((2 * half, wide), 1) // columns
+    fold = iota((2 * cycles, 2 * half), 0) == iota((2 * cycles, 2 * half), 1) // shards
+    fold = fold.astype(BF16)
     for q in range(shards // chunk):
         piece = jnp.concatenate(
             [shard_refs[q * chunk + k][...] for k in range(chunk)], axis=0
         )
+        product = lax.dot_general(
+            legendre, piece, (((1,), (1,)), ((), ())), preferred_element_type=F32
+        )
         own = slot == (rest ^ (local + q * chunk))
-        for source, target in ((keep_ref, own_ref), (got_ref, back_ref)):
-            cross = lax.dot_general(
-                source[...], piece, (((1,), (1,)), ((), ())), preferred_element_type=F32
-            )
-            chosen = jnp.where(own, cross, 0.0).astype(BF16)
-            target[:, q * wide : (q + 1) * wide] = jnp.dot(
-                fold, chosen, preferred_element_type=F32
-            ).astype(BF16)
-
-
-def cross(keep, got, shards, n, at):
+        chosen = jnp.where(own, product, 0.0).astype(BF16)
+        folded = jnp.dot(fold, chosen, preferred_element_type=F32).astype(BF16)
+        own_ref[:, q * wide : (q + 1) * wide] = folded[:cycles]
+        back_ref[:, q * wide : (q + 1) * wide] = folded[cycles:]
+
+
+def cross(keep, got, shards, at):
     half, order_max = keep.shape
     columns = shards[0].shape[0]
     count = len(shards)
     cycles = half // count
     shape = jax.ShapeDtypeStruct((cycles, count * columns), BF16)
     return pl.pallas_call(
-        functools.partial(cross_kernel, at, n, count, min(8, count)),
+        functools.partial(cross_kernel, at, count, min(8, count)),
         out_shape=[shape, shape],
         in_specs=[VMEM] * (2 + count),
         out_specs=[VMEM] * 2,
@@ -242,8 +259,8 @@
 
 
 def gather_xor(value, size, at):
+    bits = [b for b in range(size.bit_length() - 1) if b != at]
     shards = {0: value}
-    bits = [b for b in range(size.bit_length() - 1) if b != at]
     for b in reversed(bits):
         shards.update({k | 1 << b: exchange(v, size, 1 << b) for k, v in shards.items()})
     return [shards[k] for k in sorted(shards)]
@@ -255,14 +272,15 @@
     if per_device != 1 or size & (size - 1):
         raise ValueError("unsupported mesh")
     cycles, n, _ = legendre.shape
-    at = min(2, size.bit_length() - 2)
-    filtered, keep, send, table = prepare(
+    at = min(1, size.bit_length() - 2)
+    filtered, keep, send = prepare(
         m_list, coeff[0], blocks[0], legendre.reshape(cycles * n, order_max), at
     )
+    shards = gather_xor(filtered, size, at)
     got = exchange(send, size, 1 << at)
-    shards = gather_xor(filtered, size, at)
-    own, back = cross(keep, got, shards, n, at)
+    own, back = cross(keep, got, shards, at)
     other = exchange(back, size, 1 << at)
+    table = trig_table(m_list, own, at)
     sky_map = synthesize(own, other, table, columns)
     return sky_map.reshape(cycles, REAL, NPHI)
 

time: 31.5 us -> 26.1 us (0.83)
  starting transfers between devices: 12.7 us -> 8.45 us
  waiting for transfers between devices: 11.9 us -> 10.4 us
  Pallas kernels: 6.75 us -> 7.12 us
    ppermute x9, starting transfers between devices: 12.7 us -> 8.45 us  [exchange(): return lax.ppermute(value, 'mset', [(d, d ^ mask) for d in range(size)])]
    ppermute x9, waiting for transfers between devices: 11.9 us -> 10.4 us  [exchange(): return lax.ppermute(value, 'mset', [(d, d ^ mask) for d in range(size)])]
    pallas_call x1 -> x2, Pallas kernels: 1.24 us -> 1.6 us  [the longest x1 1.05 us: trig_table(): pl.pallas_call(functools.partial(trig_kernel, at), out_shape=jax.ShapeDty...]
  transfers between devices with their start and end apart: 9 -> 9, of which waited for: 4 -> 4; matrix products, arithmetic and copies ran while one was open for 0% -> 0% of each run, Pallas kernels for 0% -> 4%
where the time goes in v6:
time: 26.1 us; the launch traced here: 26 us
  waiting for transfers between devices  10.4 us (40%)
  starting transfers between devices  8.45 us (32%)
  Pallas kernels  7.12 us (27%)
    ppermute x9, waiting for transfers between devices, exchange(): return lax.ppermute(value, 'mset', [(d, d ^ mask) for d in range(size)])  10.4 us
    ppermute x9, starting transfers between devices, exchange(): return lax.ppermute(value, 'mset', [(d, d ^ mask) for d in range(size)])  8.45 us
    pallas_call x1, Pallas kernels, prepare(): pl.pallas_call(functools.partial(prepare_kernel, at), out_shape=[jax.Shap...  2.92 us
    pallas_call x1, Pallas kernels, synthesize(): pl.pallas_call(functools.partial(synthesis_kernel, tiles, columns), out_s...  2.6 us
    pallas_call x1, Pallas kernels, trig_table(): pl.pallas_call(functools.partial(trig_kernel, at), out_shape=jax.ShapeDty...  1.05 us
    pallas_call x1, Pallas kernels, cross(): pl.pallas_call(functools.partial(cross_kernel, at, count, min(8, count)),...  0.55 us
  transfers between devices with their start and end apart: 9, of which 4 were waited for; matrix products, arithmetic and copies ran while one was open for 0% of the time, Pallas kernels for 4%

profile of v6, /device:TPU:0, one launch (start us, length us, event | category | flops | bytes accessed | tf_op | source)
XLA Modules:
  0.0 26.0 jit_solution(8104630411209213442)
XLA Ops:
  0.0 0.0 copy-start
  0.0 2.9 %prepare.1 = (bf16[32,1536]{1,0:T(8,128)(2,1)S(1)}, bf16[128,1536]{1,0:T(8,128)(2,1)S(1)}, bf16[128,1536]{1,0:T(8,128)(2,1)S(1)}) custom-call(s32[16]{0:T(128)} %m_ref.3, bf16[32,1536]{1,0:T(8,128)(2,1)} %bitcast.6, bf16[1536,1536]{1,0:T(8,128)(2,1)} %bitcast.4, bf16[256,1536]{1,0:T(8,128)(2,1)} %bitcast.5), custom_call_target="tpu_custom_call" | custom-call | flops 352321536 | bytes 5505024 | tf_op jit(solution)/shard_map/prepare/pallas_call | solution.py:114
  2.9 3.0 %collective-permute-start = (bf16[128,1536]{1,0:T(8,128)(2,1)S(1)}, bf16[128,1536]{1,0:T(8,128)(2,1)S(1)}, u32[]{:S(2)}, u32[]{:S(2)}) collective-permute-start(bf16[128,1536]{1,0:T(8,128)(2,1)S(1)} %get-tuple-element.11), channel_id=1, source_target_pairs={{0,2},{1,3},{2,0},{3,1},{4,6},{5,7},{6,4},{7,5},{8,10},{9,11},{10,... | collective-permute-start | bytes 1179656 | tf_op jit(solution)/shard_map/ppermute | solution.py:258
  6.0 2.6 %collective-permute-start.4 = (bf16[32,1536]{1,0:T(8,128)(2,1)S(1)}, bf16[32,1536]{1,0:T(8,128)(2,1)S(1)}, u32[]{:S(2)}, u32[]{:S(2)}) collective-permute-start(bf16[32,1536]{1,0:T(8,128)(2,1)S(1)} %get-tuple-element.12.refs_2_), channel_id=1, source_target_pairs={{0,8},{1,9},{2,10},{3,11},{4,12},{5,13},{6,14},{7,15},{8,0},{9,1},... | collective-permute-start | bytes 294920 | tf_op jit(solution)/shard_map/ppermute | solution.py:258
  8.6 1.6 %collective-permute-start.2 = (bf16[32,1536]{1,0:T(8,128)(2,1)S(1)}, bf16[32,1536]{1,0:T(8,128)(2,1)S(1)}, u32[]{:S(2)}, u32[]{:S(2)}) collective-permute-start(bf16[32,1536]{1,0:T(8,128)(2,1)S(1)} %get-tuple-element.12.refs_2_), channel_id=1, source_target_pairs={{0,4},{1,5},{2,6},{3,7},{4,0},{5,1},{6,2},{7,3},{8,12},{9,13},{10,... | collective-permute-start | bytes 294920 | tf_op jit(solution)/shard_map/ppermute | solution.py:258
  10.1 3.1 %collective-permute-done.4.refs_6_ = bf16[32,1536]{1,0:T(8,128)(2,1)S(1)} collective-permute-done((bf16[32,1536]{1,0:T(8,128)(2,1)S(1)}, bf16[32,1536]{1,0:T(8,128)(2,1)S(1)}, u32[]{:S(2)}, u32[]{:S(2)}) %collective-permute-start.4) | collective-permute-done | bytes 98336 | tf_op jit(solution)/shard_map/ppermute | solution.py:258
  13.2 0.7 %collective-permute-start.6 = (bf16[32,1536]{1,0:T(8,128)(2,1)S(1)}, bf16[32,1536]{1,0:T(8,128)(2,1)S(1)}, u32[]{:S(2)}, u32[]{:S(2)}) collective-permute-start(bf16[32,1536]{1,0:T(8,128)(2,1)S(1)} %collective-permute-done.4.refs_6_), channel_id=1, source_target_pairs={{0,4},{1,5},{2,6},{3,7},{4,0},{5,1},{6,2},{7,3},{8,12},{9,13},{10,... | collective-permute-start | bytes 294920 | tf_op jit(solution)/shard_map/ppermute | solution.py:258
  13.9 0.0 collective-permute-start.1
  13.9 0.5 %collective-permute-start.5 = (bf16[32,1536]{1,0:T(8,128)(2,1)S(1)}, bf16[32,1536]{1,0:T(8,128)(2,1)S(1)}, u32[]{:S(2)}, u32[]{:S(2)}) collective-permute-start(bf16[32,1536]{1,0:T(8,128)(2,1)S(1)} %collective-permute-done.4.refs_6_), channel_id=1, source_target_pairs={{0,1},{1,0},{2,3},{3,2},{4,5},{5,4},{6,7},{7,6},{8,9},{9,8},{10,11... | collective-permute-start | bytes 294920 | tf_op jit(solution)/shard_map/ppermute | solution.py:258
  14.4 0.0 collective-permute-done.2.refs_4_
  14.4 0.0 collective-permute-start.3
  14.4 3.4 %collective-permute-done.6.refs_8_ = bf16[32,1536]{1,0:T(8,128)(2,1)S(1)} collective-permute-done((bf16[32,1536]{1,0:T(8,128)(2,1)S(1)}, bf16[32,1536]{1,0:T(8,128)(2,1)S(1)}, u32[]{:S(2)}, u32[]{:S(2)}) %collective-permute-start.6) | collective-permute-done | bytes 98336 | tf_op jit(solution)/shard_map/ppermute | solution.py:258
  17.8 0.0 collective-permute-start.7
  17.8 0.0 collective-permute-done.1.refs_3_
  17.8 0.0 collective-permute-done.5.refs_7_
  17.9 0.0 collective-permute-done.3.refs_5_
  17.9 1.3 %collective-permute-done.7.refs_9_ = bf16[32,1536]{1,0:T(8,128)(2,1)S(1)} collective-permute-done((bf16[32,1536]{1,0:T(8,128)(2,1)S(1)}, bf16[32,1536]{1,0:T(8,128)(2,1)S(1)}, u32[]{:S(2)}, u32[]{:S(2)}) %collective-permute-start.7) | collective-permute-done | bytes 98336 | tf_op jit(solution)/shard_map/ppermute | solution.py:258
  19.1 0.0 collective-permute-done.refs_1_
  19.1 0.6 %cross.1 = (bf16[16,256]{1,0:T(8,128)(2,1)S(1)}, bf16[16,256]{1,0:T(8,128)(2,1)S(1)}) custom-call(bf16[128,1536]{1,0:T(8,128)(2,1)S(1)} %get-tuple-element.10.refs_0_, bf16[128,1536]{1,0:T(8,128)(2,1)S(1)} %collective-permute-done.refs_1_, bf16[32,1536]{1,0:T(8,128)(2,1)S(1)} %get-tuple-element.12.refs_2_, ...), custom_call_target="tpu_custom_call" | custom-call | flops 201326592 | bytes 1572864 | tf_op jit(solution)/shard_map/cross/pallas_call | solution.py:193
  19.7 0.1 collective-permute-start.8
  19.8 0.0 copy-done
  19.8 1.1 %trig_table.1.table_ref = bf16[32,8192]{1,0:T(8,128)(2,1)S(1)} custom-call(s32[16]{0:T(128)S(1)} %copy-done, bf16[16,256]{1,0:T(8,128)(2,1)S(1)} %get-tuple-element.13.after_ref.own_ref), custom_call_target="tpu_custom_call" | custom-call | flops 2097152 | bytes 524288 | tf_op jit(solution)/shard_map/trig_table/pallas_call | solution.py:146
  20.8 2.5 %collective-permute-done.8.got_ref = bf16[16,256]{1,0:T(8,128)(2,1)S(1)} collective-permute-done((bf16[16,256]{1,0:T(8,128)(2,1)S(1)}, bf16[16,256]{1,0:T(8,128)(2,1)S(1)}, u32[]{:S(2)}, u32[]{:S(2)}) %collective-permute-start.8) | collective-permute-done | bytes 8224 | tf_op jit(solution)/shard_map/ppermute | solution.py:258
  23.4 2.6 %synthesis.1 = bf16[256,8192]{1,0:T(8,128)(2,1)} custom-call(bf16[16,256]{1,0:T(8,128)(2,1)S(1)} %get-tuple-element.13.after_ref.own_ref, bf16[16,256]{1,0:T(8,128)(2,1)S(1)} %collective-permute-done.8.got_ref, bf16[32,8192]{1,0:T(8,128)(2,1)S(1)} %trig_table.1.table_ref), custom_call_target="tpu_custom_call" | custom-call | flops 134217728 | bytes 4718592 | tf_op jit(solution)/shard_map/synthesis/pallas_call | solution.py:241
Async XLA Ops:
  0.0 19.8 %copy-start = (s32[16]{0:T(128)S(1)}, s32[16]{0:T(128)}, u32[]{:S(2)}) copy-start(s32[16]{0:T(128)} %m_ref.3) | copy-start | bytes 196
  2.9 16.2 %collective-permute-start = (bf16[128,1536]{1,0:T(8,128)(2,1)S(1)}, bf16[128,1536]{1,0:T(8,128)(2,1)S(1)}, u32[]{:S(2)}, u32[]{:S(2)}) collective-permute-start(bf16[128,1536]{1,0:T(8,128)(2,1)S(1)} %get-tuple-element.11), channel_id=1, source_target_pairs={{0,2},{1,3},{2,0},{3,1},{4,6},{5,7},{6,4},{7,5},{8,10},{9,11},{10,... | collective-permute-start | bytes 1179656 | tf_op jit(solution)/shard_map/ppermute | solution.py:258
  6.0 7.3 %collective-permute-start.4 = (bf16[32,1536]{1,0:T(8,128)(2,1)S(1)}, bf16[32,1536]{1,0:T(8,128)(2,1)S(1)}, u32[]{:S(2)}, u32[]{:S(2)}) collective-permute-start(bf16[32,1536]{1,0:T(8,128)(2,1)S(1)} %get-tuple-element.12.refs_2_), channel_id=1, source_target_pairs={{0,8},{1,9},{2,10},{3,11},{4,12},{5,13},{6,14},{7,15},{8,0},{9,1},... | collective-permute-start | bytes 294920 | tf_op jit(solution)/shard_map/ppermute | solution.py:258
  8.6 5.9 %collective-permute-start.2 = (bf16[32,1536]{1,0:T(8,128)(2,1)S(1)}, bf16[32,1536]{1,0:T(8,128)(2,1)S(1)}, u32[]{:S(2)}, u32[]{:S(2)}) collective-permute-start(bf16[32,1536]{1,0:T(8,128)(2,1)S(1)} %get-tuple-element.12.refs_2_), channel_id=1, source_target_pairs={{0,4},{1,5},{2,6},{3,7},{4,0},{5,1},{6,2},{7,3},{8,12},{9,13},{10,... | collective-permute-start | bytes 294920 | tf_op jit(solution)/shard_map/ppermute | solution.py:258
  13.2 4.6 %collective-permute-start.6 = (bf16[32,1536]{1,0:T(8,128)(2,1)S(1)}, bf16[32,1536]{1,0:T(8,128)(2,1)S(1)}, u32[]{:S(2)}, u32[]{:S(2)}) collective-permute-start(bf16[32,1536]{1,0:T(8,128)(2,1)S(1)} %collective-permute-done.4.refs_6_), channel_id=1, source_target_pairs={{0,4},{1,5},{2,6},{3,7},{4,0},{5,1},{6,2},{7,3},{8,12},{9,13},{10,... | collective-permute-start | bytes 294920 | tf_op jit(solution)/shard_map/ppermute | solution.py:258
  13.9 4.0 %collective-permute-start.1 = (bf16[32,1536]{1,0:T(8,128)(2,1)S(1)}, bf16[32,1536]{1,0:T(8,128)(2,1)S(1)}, u32[]{:S(2)}, u32[]{:S(2)}) collective-permute-start(bf16[32,1536]{1,0:T(8,128)(2,1)S(1)} %get-tuple-element.12.refs_2_), channel_id=1, source_target_pairs={{0,1},{1,0},{2,3},{3,2},{4,5},{5,4},{6,7},{7,6},{8,9},{9,8},{10,11... | collective-permute-start | bytes 294920 | tf_op jit(solution)/shard_map/ppermute | solution.py:258
  13.9 4.0 %collective-permute-start.5 = (bf16[32,1536]{1,0:T(8,128)(2,1)S(1)}, bf16[32,1536]{1,0:T(8,128)(2,1)S(1)}, u32[]{:S(2)}, u32[]{:S(2)}) collective-permute-start(bf16[32,1536]{1,0:T(8,128)(2,1)S(1)} %collective-permute-done.4.refs_6_), channel_id=1, source_target_pairs={{0,1},{1,0},{2,3},{3,2},{4,5},{5,4},{6,7},{7,6},{8,9},{9,8},{10,11... | collective-permute-start | bytes 294920 | tf_op jit(solution)/shard_map/ppermute | solution.py:258
  14.4 3.4 %collective-permute-start.3 = (bf16[32,1536]{1,0:T(8,128)(2,1)S(1)}, bf16[32,1536]{1,0:T(8,128)(2,1)S(1)}, u32[]{:S(2)}, u32[]{:S(2)}) collective-permute-start(bf16[32,1536]{1,0:T(8,128)(2,1)S(1)} %collective-permute-done.2.refs_4_), channel_id=1, source_target_pairs={{0,1},{1,0},{2,3},{3,2},{4,5},{5,4},{6,7},{7,6},{8,9},{9,8},{10,11... | collective-permute-start | bytes 294920 | tf_op jit(solution)/shard_map/ppermute | solution.py:258
  17.8 1.3 %collective-permute-start.7 = (bf16[32,1536]{1,0:T(8,128)(2,1)S(1)}, bf16[32,1536]{1,0:T(8,128)(2,1)S(1)}, u32[]{:S(2)}, u32[]{:S(2)}) collective-permute-start(bf16[32,1536]{1,0:T(8,128)(2,1)S(1)} %collective-permute-done.6.refs_8_), channel_id=1, source_target_pairs={{0,1},{1,0},{2,3},{3,2},{4,5},{5,4},{6,7},{7,6},{8,9},{9,8},{10,11... | collective-permute-start | bytes 294920 | tf_op jit(solution)/shard_map/ppermute | solution.py:258
  19.7 3.7 %collective-permute-start.8 = (bf16[16,256]{1,0:T(8,128)(2,1)S(1)}, bf16[16,256]{1,0:T(8,128)(2,1)S(1)}, u32[]{:S(2)}, u32[]{:S(2)}) collective-permute-start(bf16[16,256]{1,0:T(8,128)(2,1)S(1)} %get-tuple-element.14), channel_id=1, source_target_pairs={{0,2},{1,3},{2,0},{3,1},{4,6},{5,7},{6,4},{7,5},{8,10},{9,11},{10,... | collective-permute-start | bytes 24584 | tf_op jit(solution)/shard_map/ppermute | solution.py:258

commit v7 on v6

--- a/solution.py
+++ b/solution.py
@@ -38,14 +38,16 @@
     return phase.astype(F32) * (2.0 * math.pi / NPHI)
 
 
-def write_table(table_ref, m_smem, me, at):
+def write_table(table_ref, m_ref, me, at):
     n = table_ref.shape[0] // 2
+    half = n // 2
     index = iota((n, LANES), 0)
     lane = iota((n, LANES), 1)
     values = jnp.zeros((n, LANES), jnp.int32)
     for j in range(n):
-        source = me ^ insert_bit(j % (n // 2), j // (n // 2), at)
-        values = jnp.where(index == j, m_smem[source], values)
+        source = me ^ insert_bit(j % half, j // half, at)
+        values = jnp.where(index == j, m_ref[source], values)
+    scale = 1.0 / math.sqrt(n)
     fine = angle(values * lane)
     coarse = angle(values * lane * LANES)
     cos_f, sin_f = jnp.cos(fine), jnp.sin(fine)
@@ -53,8 +55,12 @@
     for a in range(NPHI // LANES):
         ca, sa = cos_c[:, a : a + 1], sin_c[:, a : a + 1]
         span = slice(a * LANES, (a + 1) * LANES)
-        table_ref[:n, span] = (ca * cos_f - sa * sin_f).astype(BF16)
-        table_ref[n:, span] = (-(sa * cos_f + ca * sin_f)).astype(BF16)
+        cos_part = ((ca * cos_f - sa * sin_f).astype(BF16) * scale).astype(BF16)
+        sin_part = ((-(sa * cos_f + ca * sin_f)).astype(BF16) * scale).astype(BF16)
+        for h in range(2):
+            rows = slice(h * half, (h + 1) * half)
+            table_ref[2 * h * half : (2 * h + 1) * half, span] = cos_part[rows]
+            table_ref[(2 * h + 1) * half : (2 * h + 2) * half, span] = sin_part[rows]
 
 
 def prepare_kernel(
@@ -81,15 +87,17 @@
     n = m_ref.shape[0]
     half = rows // 2
     own_bit = (me >> at) & 1
-    row, col = iota((half, rows), 0), iota((half, rows), 1)
-    same_cycle = row // (n // 2) == col // n
+    row, col = iota((rows, rows), 0), iota((rows, rows), 1)
+    bit = own_bit ^ (row // half)
     slot = lax.rem(row, n // 2)
+    pick = (lax.rem(row, half) // (n // 2) == col // n) & (
+        insert_bit(slot, bit, at) == lax.rem(col, n)
+    )
+    pick = pick.astype(BF16)
     copy_leg.wait()
-    for ref, bit in ((keep_ref, own_bit), (send_ref, 1 - own_bit)):
-        pick = same_cycle & (insert_bit(slot, bit, at) == lax.rem(col, n))
-        ref[...] = jnp.dot(
-            pick.astype(BF16), leg_vmem[...], preferred_element_type=F32
-        ).astype(BF16)
+    ordered = jnp.dot(pick, leg_vmem[...], preferred_element_type=F32).astype(BF16)
+    keep_ref[...] = ordered[:half]
+    send_ref[...] = ordered[half:]
 
     copy_m.wait()
     order = LL - m_smem[me]
@@ -163,13 +171,18 @@
     rest = remove_bit(lax.axis_index("mset"), at)
     half = keep_ref.shape[0]
     columns = shard_refs[0].shape[0]
-    cycles = own_ref.shape[0]
+    out_rows = own_ref.shape[1]
     wide = chunk * columns
     legendre = jnp.concatenate([keep_ref[...], got_ref[...]], axis=0)
     slot = lax.rem(iota((2 * half, wide), 0), shards)
     local = iota((2 * half, wide), 1) // columns
-    fold = iota((2 * cycles, 2 * half), 0) == iota((2 * cycles, 2 * half), 1) // shards
-    fold = fold.astype(BF16)
+    spread = iota((out_rows, half), 0) // REAL == iota((out_rows, half), 1) // shards
+    spread = spread.astype(BF16)
+    same_real = lax.rem(iota((out_rows, wide), 0), REAL) == lax.rem(
+        iota((out_rows, wide), 1), REAL
+    )
+    row, col = iota((2 * shards, wide), 0), iota((2 * shards, wide), 1)
+    totals = [jnp.zeros(own_ref.shape, F32) for _ in range(2)]
     for q in range(shards // chunk):
         piece = jnp.concatenate(
             [shard_refs[q * chunk + k][...] for k in range(chunk)], axis=0
@@ -179,17 +192,25 @@
         )
         own = slot == (rest ^ (local + q * chunk))
         chosen = jnp.where(own, product, 0.0).astype(BF16)
-        folded = jnp.dot(fold, chosen, preferred_element_type=F32).astype(BF16)
-        own_ref[:, q * wide : (q + 1) * wide] = folded[:cycles]
-        back_ref[:, q * wide : (q + 1) * wide] = folded[cycles:]
+        pick = lax.rem(col, columns) // REAL * shards + q * chunk + col // columns == row
+        pick = pick.astype(BF16)
+        for h in range(2):
+            wider = jnp.dot(
+                spread, chosen[h * half : (h + 1) * half], preferred_element_type=F32
+            )
+            wider = jnp.where(same_real, wider, 0.0).astype(BF16)
+            totals[h] += lax.dot_general(
+                pick, wider, (((1,), (1,)), ((), ())), preferred_element_type=F32
+            )
+    own_ref[...] = totals[0].astype(BF16)
+    back_ref[...] = totals[1].astype(BF16)
 
 
 def cross(keep, got, shards, at):
     half, order_max = keep.shape
     columns = shards[0].shape[0]
     count = len(shards)
-    cycles = half // count
-    shape = jax.ShapeDtypeStruct((cycles, count * columns), BF16)
+    shape = jax.ShapeDtypeStruct((2 * count, half // count * REAL), BF16)
     return pl.pallas_call(
         functools.partial(cross_kernel, at, count, min(8, count)),
         out_shape=[shape, shape],
@@ -205,28 +226,16 @@
     )(keep, got, *shards)
 
 
-def synthesis_kernel(tiles, columns, own_ref, got_ref, table_ref, out_ref, held, sems):
-    cycles, half = own_ref.shape
-    wide = 2 * half
-    n = wide // columns
-    out_rows = cycles * REAL
-    joined = jnp.concatenate([own_ref[...], got_ref[...]], axis=1)
-    repeat = (iota((out_rows, cycles), 0) // REAL == iota((out_rows, cycles), 1)).astype(BF16)
-    spread = jnp.dot(repeat, joined, preferred_element_type=F32)
-    same_real = lax.rem(iota((out_rows, wide), 0), REAL) == lax.rem(
-        iota((out_rows, wide), 1), REAL
-    )
-    chosen = jnp.where(same_real, spread, 0.0).astype(BF16)
-    row, col = iota((wide, 2 * n), 0), iota((wide, 2 * n), 1)
-    pick = (lax.rem(row, columns) // REAL * n + row // columns == col).astype(BF16)
-    flat = jnp.dot(chosen, pick, preferred_element_type=F32).astype(BF16)
-
+def synthesis_kernel(tiles, own_ref, got_ref, table_ref, out_ref, held, sems):
+    flat = jnp.concatenate([own_ref[...], got_ref[...]], axis=0)
     width = NPHI // tiles
     copies = []
     for t in range(tiles):
         span = pl.ds(t * width, width)
-        summed = jnp.dot(flat, table_ref[:, span], preferred_element_type=F32)
-        held[:, span] = (summed * (1.0 / math.sqrt(n))).astype(BF16)
+        summed = lax.dot_general(
+            flat, table_ref[:, span], (((0,), (0,)), ((), ())), preferred_element_type=F32
+        )
+        held[:, span] = summed.astype(BF16)
         copy = pltpu.make_async_copy(held.at[:, span], out_ref.at[:, span], sems.at[t])
         copy.start()
         copies.append(copy)
@@ -234,12 +243,11 @@
         copy.wait()
 
 
-def synthesize(own, got, table, columns):
-    cycles = own.shape[0]
-    tiles = 8
-    out_rows = cycles * REAL
+def synthesize(own, got, table):
+    tiles = 16
+    out_rows = own.shape[1]
     return pl.pallas_call(
-        functools.partial(synthesis_kernel, tiles, columns),
+        functools.partial(synthesis_kernel, tiles),
         out_shape=jax.ShapeDtypeStruct((out_rows, NPHI), BF16),
         in_specs=[VMEM] * 3,
         out_specs=HBM,
@@ -259,10 +267,13 @@
 
 
 def gather_xor(value, size, at):
-    bits = [b for b in range(size.bit_length() - 1) if b != at]
     shards = {0: value}
-    for b in reversed(bits):
-        shards.update({k | 1 << b: exchange(v, size, 1 << b) for k, v in shards.items()})
+    top = size.bit_length() - 1
+    stages = [[b, b + 1] if b + 1 < top else [b] for b in range(2, top, 2)]
+    stages = [[b] for b in range(min(2, top)) if b != at] + stages
+    for bits in reversed(stages):
+        masks = [sum(1 << b for e, b in enumerate(bits) if m >> e & 1) for m in range(1, 1 << len(bits))]
+        shards.update({k | m: exchange(v, size, m) for m in masks for k, v in list(shards.items())})
     return [shards[k] for k in sorted(shards)]
 
 
@@ -281,7 +292,7 @@
     own, back = cross(keep, got, shards, at)
     other = exchange(back, size, 1 << at)
     table = trig_table(m_list, own, at)
-    sky_map = synthesize(own, other, table, columns)
+    sky_map = synthesize(own, other, table)
     return sky_map.reshape(cycles, REAL, NPHI)
 
 

time: 26.1 us -> 26.2 us (level)
    pallas_call x1, Pallas kernels: 0.55 us -> 0.97 us  [cross(): pl.pallas_call(functools.partial(cross_kernel, at, count, min(8, count)),...]
  transfers between devices with their start and end apart: 9 -> 9, of which waited for: 4 -> 5; matrix products, arithmetic and copies ran while one was open for 0% -> 0% of each run, Pallas kernels for 4% -> 4%
where the time goes in v7:
time: 26.2 us; the launch traced here: 26 us
  waiting for transfers between devices  10.2 us (39%)
  starting transfers between devices  8.47 us (32%)
  Pallas kernels  7.33 us (28%)
    ppermute x9, waiting for transfers between devices, exchange(): return lax.ppermute(value, 'mset', [(d, d ^ mask) for d in range(size)])  10.2 us
    ppermute x9, starting transfers between devices, exchange(): return lax.ppermute(value, 'mset', [(d, d ^ mask) for d in range(size)])  8.47 us
    pallas_call x1, Pallas kernels, prepare(): pl.pallas_call(functools.partial(prepare_kernel, at), out_shape=[jax.Shap...  2.92 us
    pallas_call x1, Pallas kernels, synthesize(): pl.pallas_call(functools.partial(synthesis_kernel, tiles), out_shape=jax....  2.38 us
    pallas_call x1, Pallas kernels, trig_table(): pl.pallas_call(functools.partial(trig_kernel, at), out_shape=jax.ShapeDty...  1.05 us
    pallas_call x1, Pallas kernels, cross(): pl.pallas_call(functools.partial(cross_kernel, at, count, min(8, count)),...  0.97 us
  transfers between devices with their start and end apart: 9, of which 5 were waited for; matrix products, arithmetic and copies ran while one was open for 0% of the time, Pallas kernels for 4%

profile of v7, /device:TPU:0, one launch (start us, length us, event | category | flops | bytes accessed | tf_op | source)
XLA Modules:
  0.0 26.0 jit_solution(6273839852607514972)
XLA Ops:
  0.0 0.0 copy-start
  0.0 2.9 %prepare.1 = (bf16[32,1536]{1,0:T(8,128)(2,1)S(1)}, bf16[128,1536]{1,0:T(8,128)(2,1)S(1)}, bf16[128,1536]{1,0:T(8,128)(2,1)S(1)}) custom-call(s32[16]{0:T(128)} %m_ref.3, bf16[32,1536]{1,0:T(8,128)(2,1)} %bitcast.6, bf16[1536,1536]{1,0:T(8,128)(2,1)} %bitcast.4, bf16[256,1536]{1,0:T(8,128)(2,1)} %bitcast.5), custom_call_target="tpu_custom_call" | custom-call | flops 352321536 | bytes 5505024 | tf_op jit(solution)/shard_map/prepare/pallas_call | solution.py:122
  2.9 3.0 %collective-permute-start = (bf16[128,1536]{1,0:T(8,128)(2,1)S(1)}, bf16[128,1536]{1,0:T(8,128)(2,1)S(1)}, u32[]{:S(2)}, u32[]{:S(2)}) collective-permute-start(bf16[128,1536]{1,0:T(8,128)(2,1)S(1)} %get-tuple-element.11), channel_id=1, source_target_pairs={{0,2},{1,3},{2,0},{3,1},{4,6},{5,7},{6,4},{7,5},{8,10},{9,11},{10,... | collective-permute-start | bytes 1179656 | tf_op jit(solution)/shard_map/ppermute | solution.py:266
  6.0 3.6 %collective-permute-start.6 = (bf16[32,1536]{1,0:T(8,128)(2,1)S(1)}, bf16[32,1536]{1,0:T(8,128)(2,1)S(1)}, u32[]{:S(2)}, u32[]{:S(2)}) collective-permute-start(bf16[32,1536]{1,0:T(8,128)(2,1)S(1)} %get-tuple-element.12.refs_2_), channel_id=1, source_target_pairs={{0,12},{1,13},{2,14},{3,15},{4,8},{5,9},{6,10},{7,11},{8,4},{9,5},... | collective-permute-start | bytes 294920 | tf_op jit(solution)/shard_map/ppermute | solution.py:266
  9.6 0.0 collective-permute-start.4
  9.6 0.8 %collective-permute-start.2 = (bf16[32,1536]{1,0:T(8,128)(2,1)S(1)}, bf16[32,1536]{1,0:T(8,128)(2,1)S(1)}, u32[]{:S(2)}, u32[]{:S(2)}) collective-permute-start(bf16[32,1536]{1,0:T(8,128)(2,1)S(1)} %get-tuple-element.12.refs_2_), channel_id=1, source_target_pairs={{0,4},{1,5},{2,6},{3,7},{4,0},{5,1},{6,2},{7,3},{8,12},{9,13},{10,... | collective-permute-start | bytes 294920 | tf_op jit(solution)/shard_map/ppermute | solution.py:266
  10.4 0.0 collective-permute-start.1
  10.4 3.1 %collective-permute-done.6.refs_8_ = bf16[32,1536]{1,0:T(8,128)(2,1)S(1)} collective-permute-done((bf16[32,1536]{1,0:T(8,128)(2,1)S(1)}, bf16[32,1536]{1,0:T(8,128)(2,1)S(1)}, u32[]{:S(2)}, u32[]{:S(2)}) %collective-permute-start.6) | collective-permute-done | bytes 98336 | tf_op jit(solution)/shard_map/ppermute | solution.py:266
  13.5 0.0 collective-permute-start.7
  13.5 4.1 %collective-permute-done.4.refs_6_ = bf16[32,1536]{1,0:T(8,128)(2,1)S(1)} collective-permute-done((bf16[32,1536]{1,0:T(8,128)(2,1)S(1)}, bf16[32,1536]{1,0:T(8,128)(2,1)S(1)}, u32[]{:S(2)}, u32[]{:S(2)}) %collective-permute-start.4) | collective-permute-done | bytes 98336 | tf_op jit(solution)/shard_map/ppermute | solution.py:266
  17.6 0.0 collective-permute-start.5
  17.6 0.0 collective-permute-done.2.refs_4_
  17.6 0.5 %collective-permute-start.3 = (bf16[32,1536]{1,0:T(8,128)(2,1)S(1)}, bf16[32,1536]{1,0:T(8,128)(2,1)S(1)}, u32[]{:S(2)}, u32[]{:S(2)}) collective-permute-start(bf16[32,1536]{1,0:T(8,128)(2,1)S(1)} %collective-permute-done.2.refs_4_), channel_id=1, source_target_pairs={{0,1},{1,0},{2,3},{3,2},{4,5},{5,4},{6,7},{7,6},{8,9},{9,8},{10,11... | collective-permute-start | bytes 294920 | tf_op jit(solution)/shard_map/ppermute | solution.py:266
  18.1 0.0 collective-permute-done.1.refs_3_
  18.1 0.0 collective-permute-done.7.refs_9_
  18.1 0.8 %collective-permute-done.5.refs_7_ = bf16[32,1536]{1,0:T(8,128)(2,1)S(1)} collective-permute-done((bf16[32,1536]{1,0:T(8,128)(2,1)S(1)}, bf16[32,1536]{1,0:T(8,128)(2,1)S(1)}, u32[]{:S(2)}, u32[]{:S(2)}) %collective-permute-start.5) | collective-permute-done | bytes 98336 | tf_op jit(solution)/shard_map/ppermute | solution.py:266
  18.9 0.2 collective-permute-done.3.refs_5_
  19.0 0.0 collective-permute-done.refs_1_
  19.0 1.0 %cross.1 = (bf16[16,256]{1,0:T(8,128)(2,1)S(1)}, bf16[16,256]{1,0:T(8,128)(2,1)S(1)}) custom-call(bf16[128,1536]{1,0:T(8,128)(2,1)S(1)} %get-tuple-element.10.refs_0_, bf16[128,1536]{1,0:T(8,128)(2,1)S(1)} %collective-permute-done.refs_1_, bf16[32,1536]{1,0:T(8,128)(2,1)S(1)} %get-tuple-element.12.refs_2_, ...), custom_call_target="tpu_custom_call" | custom-call | flops 201326592 | bytes 1572864 | tf_op jit(solution)/shard_map/cross/pallas_call | solution.py:214
  20.0 0.5 %collective-permute-start.8 = (bf16[16,256]{1,0:T(8,128)(2,1)S(1)}, bf16[16,256]{1,0:T(8,128)(2,1)S(1)}, u32[]{:S(2)}, u32[]{:S(2)}) collective-permute-start(bf16[16,256]{1,0:T(8,128)(2,1)S(1)} %get-tuple-element.14), channel_id=1, source_target_pairs={{0,2},{1,3},{2,0},{3,1},{4,6},{5,7},{6,4},{7,5},{8,10},{9,11},{10,... | collective-permute-start | bytes 24584 | tf_op jit(solution)/shard_map/ppermute | solution.py:266
  20.5 0.0 copy-done
  20.5 1.1 %trig_table.1.table_ref = bf16[32,8192]{1,0:T(8,128)(2,1)S(1)} custom-call(s32[16]{0:T(128)S(1)} %copy-done, bf16[16,256]{1,0:T(8,128)(2,1)S(1)} %get-tuple-element.13.after_ref.own_ref), custom_call_target="tpu_custom_call" | custom-call | flops 2097152 | bytes 524288 | tf_op jit(solution)/shard_map/trig_table/pallas_call | solution.py:154
  21.6 2.1 %collective-permute-done.8.got_ref = bf16[16,256]{1,0:T(8,128)(2,1)S(1)} collective-permute-done((bf16[16,256]{1,0:T(8,128)(2,1)S(1)}, bf16[16,256]{1,0:T(8,128)(2,1)S(1)}, u32[]{:S(2)}, u32[]{:S(2)}) %collective-permute-start.8) | collective-permute-done | bytes 8224 | tf_op jit(solution)/shard_map/ppermute | solution.py:266
  23.7 2.4 %synthesis.1 = bf16[256,8192]{1,0:T(8,128)(2,1)} custom-call(bf16[16,256]{1,0:T(8,128)(2,1)S(1)} %get-tuple-element.13.after_ref.own_ref, bf16[16,256]{1,0:T(8,128)(2,1)S(1)} %collective-permute-done.8.got_ref, bf16[32,8192]{1,0:T(8,128)(2,1)S(1)} %trig_table.1.table_ref), custom_call_target="tpu_custom_call" | custom-call | flops 134217728 | bytes 4718592 | tf_op jit(solution)/shard_map/synthesis/pallas_call | solution.py:249
Async XLA Ops:
  0.0 20.5 %copy-start = (s32[16]{0:T(128)S(1)}, s32[16]{0:T(128)}, u32[]{:S(2)}) copy-start(s32[16]{0:T(128)} %m_ref.3) | copy-start | bytes 196
  2.9 16.1 %collective-permute-start = (bf16[128,1536]{1,0:T(8,128)(2,1)S(1)}, bf16[128,1536]{1,0:T(8,128)(2,1)S(1)}, u32[]{:S(2)}, u32[]{:S(2)}) collective-permute-start(bf16[128,1536]{1,0:T(8,128)(2,1)S(1)} %get-tuple-element.11), channel_id=1, source_target_pairs={{0,2},{1,3},{2,0},{3,1},{4,6},{5,7},{6,4},{7,5},{8,10},{9,11},{10,... | collective-permute-start | bytes 1179656 | tf_op jit(solution)/shard_map/ppermute | solution.py:266
  6.0 7.5 %collective-permute-start.6 = (bf16[32,1536]{1,0:T(8,128)(2,1)S(1)}, bf16[32,1536]{1,0:T(8,128)(2,1)S(1)}, u32[]{:S(2)}, u32[]{:S(2)}) collective-permute-start(bf16[32,1536]{1,0:T(8,128)(2,1)S(1)} %get-tuple-element.12.refs_2_), channel_id=1, source_target_pairs={{0,12},{1,13},{2,14},{3,15},{4,8},{5,9},{6,10},{7,11},{8,4},{9,5},... | collective-permute-start | bytes 294920 | tf_op jit(solution)/shard_map/ppermute | solution.py:266
  9.6 8.0 %collective-permute-start.4 = (bf16[32,1536]{1,0:T(8,128)(2,1)S(1)}, bf16[32,1536]{1,0:T(8,128)(2,1)S(1)}, u32[]{:S(2)}, u32[]{:S(2)}) collective-permute-start(bf16[32,1536]{1,0:T(8,128)(2,1)S(1)} %get-tuple-element.12.refs_2_), channel_id=1, source_target_pairs={{0,8},{1,9},{2,10},{3,11},{4,12},{5,13},{6,14},{7,15},{8,0},{9,1},... | collective-permute-start | bytes 294920 | tf_op jit(solution)/shard_map/ppermute | solution.py:266
  9.6 8.0 %collective-permute-start.2 = (bf16[32,1536]{1,0:T(8,128)(2,1)S(1)}, bf16[32,1536]{1,0:T(8,128)(2,1)S(1)}, u32[]{:S(2)}, u32[]{:S(2)}) collective-permute-start(bf16[32,1536]{1,0:T(8,128)(2,1)S(1)} %get-tuple-element.12.refs_2_), channel_id=1, source_target_pairs={{0,4},{1,5},{2,6},{3,7},{4,0},{5,1},{6,2},{7,3},{8,12},{9,13},{10,... | collective-permute-start | bytes 294920 | tf_op jit(solution)/shard_map/ppermute | solution.py:266
  10.4 7.7 %collective-permute-start.1 = (bf16[32,1536]{1,0:T(8,128)(2,1)S(1)}, bf16[32,1536]{1,0:T(8,128)(2,1)S(1)}, u32[]{:S(2)}, u32[]{:S(2)}) collective-permute-start(bf16[32,1536]{1,0:T(8,128)(2,1)S(1)} %get-tuple-element.12.refs_2_), channel_id=1, source_target_pairs={{0,1},{1,0},{2,3},{3,2},{4,5},{5,4},{6,7},{7,6},{8,9},{9,8},{10,11... | collective-permute-start | bytes 294920 | tf_op jit(solution)/shard_map/ppermute | solution.py:266
  13.5 4.6 %collective-permute-start.7 = (bf16[32,1536]{1,0:T(8,128)(2,1)S(1)}, bf16[32,1536]{1,0:T(8,128)(2,1)S(1)}, u32[]{:S(2)}, u32[]{:S(2)}) collective-permute-start(bf16[32,1536]{1,0:T(8,128)(2,1)S(1)} %collective-permute-done.6.refs_8_), channel_id=1, source_target_pairs={{0,1},{1,0},{2,3},{3,2},{4,5},{5,4},{6,7},{7,6},{8,9},{9,8},{10,11... | collective-permute-start | bytes 294920 | tf_op jit(solution)/shard_map/ppermute | solution.py:266
  17.6 1.3 %collective-permute-start.5 = (bf16[32,1536]{1,0:T(8,128)(2,1)S(1)}, bf16[32,1536]{1,0:T(8,128)(2,1)S(1)}, u32[]{:S(2)}, u32[]{:S(2)}) collective-permute-start(bf16[32,1536]{1,0:T(8,128)(2,1)S(1)} %collective-permute-done.4.refs_6_), channel_id=1, source_target_pairs={{0,1},{1,0},{2,3},{3,2},{4,5},{5,4},{6,7},{7,6},{8,9},{9,8},{10,11... | collective-permute-start | bytes 294920 | tf_op jit(solution)/shard_map/ppermute | solution.py:266
  17.6 1.5 %collective-permute-start.3 = (bf16[32,1536]{1,0:T(8,128)(2,1)S(1)}, bf16[32,1536]{1,0:T(8,128)(2,1)S(1)}, u32[]{:S(2)}, u32[]{:S(2)}) collective-permute-start(bf16[32,1536]{1,0:T(8,128)(2,1)S(1)} %collective-permute-done.2.refs_4_), channel_id=1, source_target_pairs={{0,1},{1,0},{2,3},{3,2},{4,5},{5,4},{6,7},{7,6},{8,9},{9,8},{10,11... | collective-permute-start | bytes 294920 | tf_op jit(solution)/shard_map/ppermute | solution.py:266
  20.0 3.7 %collective-permute-start.8 = (bf16[16,256]{1,0:T(8,128)(2,1)S(1)}, bf16[16,256]{1,0:T(8,128)(2,1)S(1)}, u32[]{:S(2)}, u32[]{:S(2)}) collective-permute-start(bf16[16,256]{1,0:T(8,128)(2,1)S(1)} %get-tuple-element.14), channel_id=1, source_target_pairs={{0,2},{1,3},{2,0},{3,1},{4,6},{5,7},{6,4},{7,5},{8,10},{9,11},{10,... | collective-permute-start | bytes 24584 | tf_op jit(solution)/shard_map/ppermute | solution.py:266

commit v8 on v7

--- a/solution.py
+++ b/solution.py
@@ -27,9 +27,10 @@
     return (value & low) | (bit << at) | ((value >> at) << (at + 1))
 
 
-def remove_bit(value, at):
-    low = (1 << at) - 1
-    return (value & low) | ((value >> (at + 1)) << at)
+def shard_source(position, me, at, line):
+    z, other = me >> (at + 1), me & ((1 << at) - 1)
+    turn, flip = position >> at, position & ((1 << at) - 1)
+    return (((z - turn) & (line - 1)) << at) | (other ^ flip)
 
 
 def angle(phase):
@@ -38,14 +39,15 @@
     return phase.astype(F32) * (2.0 * math.pi / NPHI)
 
 
-def write_table(table_ref, m_ref, me, at):
+def write_table(table_ref, m_ref, me, at, line):
     n = table_ref.shape[0] // 2
     half = n // 2
     index = iota((n, LANES), 0)
     lane = iota((n, LANES), 1)
+    own_bit = (me >> at) & 1
     values = jnp.zeros((n, LANES), jnp.int32)
     for j in range(n):
-        source = me ^ insert_bit(j % half, j // half, at)
+        source = insert_bit(shard_source(j % half, me, at, line), own_bit ^ (j // half), at)
         values = jnp.where(index == j, m_ref[source], values)
     scale = 1.0 / math.sqrt(n)
     fine = angle(values * lane)
@@ -55,12 +57,20 @@
     for a in range(NPHI // LANES):
         ca, sa = cos_c[:, a : a + 1], sin_c[:, a : a + 1]
         span = slice(a * LANES, (a + 1) * LANES)
-        cos_part = ((ca * cos_f - sa * sin_f).astype(BF16) * scale).astype(BF16)
-        sin_part = ((-(sa * cos_f + ca * sin_f)).astype(BF16) * scale).astype(BF16)
-        for h in range(2):
-            rows = slice(h * half, (h + 1) * half)
-            table_ref[2 * h * half : (2 * h + 1) * half, span] = cos_part[rows]
-            table_ref[(2 * h + 1) * half : (2 * h + 2) * half, span] = sin_part[rows]
+        table_ref[:n, span] = ((ca * cos_f - sa * sin_f).astype(BF16) * scale).astype(BF16)
+        table_ref[n:, span] = ((-(sa * cos_f + ca * sin_f)).astype(BF16) * scale).astype(BF16)
+
+
+def map_rows(half_ref, first, total):
+    cycles, wide = half_ref.shape
+    rows = cycles * REAL
+    repeat = (iota((rows, cycles), 0) // REAL == iota((rows, cycles), 1)).astype(BF16)
+    spread = jnp.dot(repeat, half_ref[...], preferred_element_type=F32)
+    same_real = lax.rem(iota((rows, wide), 0), REAL) == lax.rem(iota((rows, wide), 1), REAL)
+    chosen = jnp.where(same_real, spread, 0.0).astype(BF16)
+    row, col = iota((wide, 2 * total), 0), iota((wide, 2 * total), 1)
+    pick = lax.rem(row, 2 * REAL) // REAL * total + first + row // (2 * REAL) == col
+    return jnp.dot(chosen, pick.astype(BF16), preferred_element_type=F32)
 
 
 def prepare_kernel(
@@ -145,44 +155,44 @@
     )(*[pltpu.with_memory_space_constraint(x, pltpu.HBM) for x in operands])
 
 
-def trig_kernel(at, m_ref, after_ref, table_ref):
-    write_table(table_ref, m_ref, lax.axis_index("mset"), at)
-
-
-def trig_table(m_list, after, at):
-    rows = 2 * m_list.shape[0]
+def table_kernel(at, line, m_ref, own_ref, table_ref, rows_ref):
+    write_table(table_ref, m_ref, lax.axis_index("mset"), at, line)
+    rows_ref[...] = map_rows(own_ref, 0, m_ref.shape[0]).astype(BF16)
+
+
+def table_and_own(m_list, own, at, line):
+    n = m_list.shape[0]
+    out_rows = own.shape[0] * REAL
     return pl.pallas_call(
-        functools.partial(trig_kernel, at),
-        out_shape=jax.ShapeDtypeStruct((rows, NPHI), BF16),
-        in_specs=[pl.BlockSpec(memory_space=pltpu.SMEM), pl.BlockSpec(memory_space=pl.ANY)],
-        out_specs=VMEM,
+        functools.partial(table_kernel, at, line),
+        out_shape=[
+            jax.ShapeDtypeStruct((2 * n, NPHI), BF16),
+            jax.ShapeDtypeStruct((out_rows, 2 * n), BF16),
+        ],
+        in_specs=[pl.BlockSpec(memory_space=pltpu.SMEM), VMEM],
+        out_specs=[VMEM] * 2,
         compiler_params=pltpu.CompilerParams(vmem_limit_bytes=16 << 20),
         cost_estimate=pl.CostEstimate(
-            flops=8 * rows * NPHI, bytes_accessed=2 * rows * NPHI, transcendentals=0
+            flops=16 * n * NPHI, bytes_accessed=4 * n * NPHI, transcendentals=0
         ),
-        name="trig_table",
-    )(m_list, after)
-
-
-def cross_kernel(at, shards, chunk, *refs):
-    keep_ref, got_ref = refs[:2]
-    shard_refs = refs[2 : 2 + shards]
-    own_ref, back_ref = refs[2 + shards :]
-    rest = remove_bit(lax.axis_index("mset"), at)
+        name="table_and_own",
+    )(m_list, own)
+
+
+def cross_kernel(at, line, order, chunk, *refs):
+    shards = len(order)
+    shard_refs = dict(zip(order, refs[:shards]))
+    keep_ref, got_ref, own_ref, back_ref = refs[shards:]
     half = keep_ref.shape[0]
     columns = shard_refs[0].shape[0]
-    out_rows = own_ref.shape[1]
+    cycles = own_ref.shape[0]
     wide = chunk * columns
     legendre = jnp.concatenate([keep_ref[...], got_ref[...]], axis=0)
     slot = lax.rem(iota((2 * half, wide), 0), shards)
     local = iota((2 * half, wide), 1) // columns
-    spread = iota((out_rows, half), 0) // REAL == iota((out_rows, half), 1) // shards
-    spread = spread.astype(BF16)
-    same_real = lax.rem(iota((out_rows, wide), 0), REAL) == lax.rem(
-        iota((out_rows, wide), 1), REAL
-    )
-    row, col = iota((2 * shards, wide), 0), iota((2 * shards, wide), 1)
-    totals = [jnp.zeros(own_ref.shape, F32) for _ in range(2)]
+    fold = iota((2 * cycles, 2 * half), 0) == iota((2 * cycles, 2 * half), 1) // shards
+    fold = fold.astype(BF16)
+    me = lax.axis_index("mset")
     for q in range(shards // chunk):
         piece = jnp.concatenate(
             [shard_refs[q * chunk + k][...] for k in range(chunk)], axis=0
@@ -190,29 +200,21 @@
         product = lax.dot_general(
             legendre, piece, (((1,), (1,)), ((), ())), preferred_element_type=F32
         )
-        own = slot == (rest ^ (local + q * chunk))
+        own = slot == shard_source(local + q * chunk, me, at, line)
         chosen = jnp.where(own, product, 0.0).astype(BF16)
-        pick = lax.rem(col, columns) // REAL * shards + q * chunk + col // columns == row
-        pick = pick.astype(BF16)
-        for h in range(2):
-            wider = jnp.dot(
-                spread, chosen[h * half : (h + 1) * half], preferred_element_type=F32
-            )
-            wider = jnp.where(same_real, wider, 0.0).astype(BF16)
-            totals[h] += lax.dot_general(
-                pick, wider, (((1,), (1,)), ((), ())), preferred_element_type=F32
-            )
-    own_ref[...] = totals[0].astype(BF16)
-    back_ref[...] = totals[1].astype(BF16)
-
-
-def cross(keep, got, shards, at):
+        folded = jnp.dot(fold, chosen, preferred_element_type=F32).astype(BF16)
+        own_ref[:, q * wide : (q + 1) * wide] = folded[:cycles]
+        back_ref[:, q * wide : (q + 1) * wide] = folded[cycles:]
+
+
+def cross(keep, got, shards, at, line):
     half, order_max = keep.shape
     columns = shards[0].shape[0]
     count = len(shards)
-    shape = jax.ShapeDtypeStruct((2 * count, half // count * REAL), BF16)
+    order = sorted(shards, key=lambda k: -(k >> at) % line)
+    shape = jax.ShapeDtypeStruct((half // count, count * columns), BF16)
     return pl.pallas_call(
-        functools.partial(cross_kernel, at, count, min(8, count)),
+        functools.partial(cross_kernel, at, line, order, min(8, count)),
         out_shape=[shape, shape],
         in_specs=[VMEM] * (2 + count),
         out_specs=[VMEM] * 2,
@@ -223,18 +225,17 @@
             transcendentals=0,
         ),
         name="cross",
-    )(keep, got, *shards)
+    )(*[shards[k] for k in order], keep, got)
 
 
 def synthesis_kernel(tiles, own_ref, got_ref, table_ref, out_ref, held, sems):
-    flat = jnp.concatenate([own_ref[...], got_ref[...]], axis=0)
+    n = table_ref.shape[0] // 2
+    flat = (map_rows(got_ref, n // 2, n) + own_ref[...].astype(F32)).astype(BF16)
     width = NPHI // tiles
     copies = []
     for t in range(tiles):
         span = pl.ds(t * width, width)
-        summed = lax.dot_general(
-            flat, table_ref[:, span], (((0,), (0,)), ((), ())), preferred_element_type=F32
-        )
+        summed = jnp.dot(flat, table_ref[:, span], preferred_element_type=F32)
         held[:, span] = summed.astype(BF16)
         copy = pltpu.make_async_copy(held.at[:, span], out_ref.at[:, span], sems.at[t])
         copy.start()
@@ -245,7 +246,7 @@
 
 def synthesize(own, got, table):
     tiles = 16
-    out_rows = own.shape[1]
+    out_rows = own.shape[0]
     return pl.pallas_call(
         functools.partial(synthesis_kernel, tiles),
         out_shape=jax.ShapeDtypeStruct((out_rows, NPHI), BF16),
@@ -266,15 +267,15 @@
     return lax.ppermute(value, "mset", [(d, d ^ mask) for d in range(size)])
 
 
-def gather_xor(value, size, at):
+def gather_shards(value, size, at, line):
+    step = size // line
     shards = {0: value}
-    top = size.bit_length() - 1
-    stages = [[b, b + 1] if b + 1 < top else [b] for b in range(2, top, 2)]
-    stages = [[b] for b in range(min(2, top)) if b != at] + stages
-    for bits in reversed(stages):
-        masks = [sum(1 << b for e, b in enumerate(bits) if m >> e & 1) for m in range(1, 1 << len(bits))]
-        shards.update({k | m: exchange(v, size, m) for m in masks for k, v in list(shards.items())})
-    return [shards[k] for k in sorted(shards)]
+    for turn in range(1, line):
+        pairs = [(d, (d + turn * step) % size) for d in range(size)]
+        shards[turn << at] = lax.ppermute(value, "mset", pairs)
+    for b in range(at):
+        shards.update({k | 1 << b: exchange(v, size, 1 << b) for k, v in shards.items()})
+    return shards
 
 
 def body(m_list, coeff, blocks, legendre):
@@ -284,15 +285,16 @@
         raise ValueError("unsupported mesh")
     cycles, n, _ = legendre.shape
     at = min(1, size.bit_length() - 2)
+    line = size >> (at + 1)
     filtered, keep, send = prepare(
         m_list, coeff[0], blocks[0], legendre.reshape(cycles * n, order_max), at
     )
-    shards = gather_xor(filtered, size, at)
+    shards = gather_shards(filtered, size, at, line)
     got = exchange(send, size, 1 << at)
-    own, back = cross(keep, got, shards, at)
+    own, back = cross(keep, got, shards, at, line)
     other = exchange(back, size, 1 << at)
-    table = trig_table(m_list, own, at)
-    sky_map = synthesize(own, other, table)
+    table, own_rows = table_and_own(m_list, own, at, line)
+    sky_map = synthesize(own_rows, other, table)
     return sky_map.reshape(cycles, REAL, NPHI)
 
 

time: 26.2 us -> 25 us (0.954)
  waiting for transfers between devices: 10.2 us -> 8.24 us
  starting transfers between devices: 8.47 us -> 9.42 us
    ppermute x9 -> x6, waiting for transfers between devices: 10.2 us -> 3.14 us  [exchange(): return lax.ppermute(value, 'mset', [(d, d ^ mask) for d in range(size)])]
    ppermute x0 -> x3, starting transfers between devices: none -> 5.51 us  [gather_shards(): shards[turn << at] = lax.ppermute(value, 'mset', pairs)]
    ppermute x0 -> x3, waiting for transfers between devices: none -> 5.1 us  [gather_shards(): shards[turn << at] = lax.ppermute(value, 'mset', pairs)]
    ppermute x9 -> x6, starting transfers between devices: 8.47 us -> 3.91 us  [exchange(): return lax.ppermute(value, 'mset', [(d, d ^ mask) for d in range(size)])]
    pallas_call x2, Pallas kernels: 2.03 us -> 1.65 us  [the longest x1 1.1 us: table_and_own(): pl.pallas_call(functools.partial(table_kernel, at, line), out_shape=[jax....]
where the time goes in v8:
time: 25 us; the launch traced here: 24.8 us
  starting transfers between devices  9.42 us (38%)
  waiting for transfers between devices  8.24 us (33%)
  Pallas kernels  7.15 us (29%)
    ppermute x3, starting transfers between devices, gather_shards(): shards[turn << at] = lax.ppermute(value, 'mset', pairs)  5.51 us
    ppermute x3, waiting for transfers between devices, gather_shards(): shards[turn << at] = lax.ppermute(value, 'mset', pairs)  5.1 us
    ppermute x6, starting transfers between devices, exchange(): return lax.ppermute(value, 'mset', [(d, d ^ mask) for d in range(size)])  3.91 us
    ppermute x6, waiting for transfers between devices, exchange(): return lax.ppermute(value, 'mset', [(d, d ^ mask) for d in range(size)])  3.14 us
    pallas_call x1, Pallas kernels, prepare(): pl.pallas_call(functools.partial(prepare_kernel, at), out_shape=[jax.Shap...  2.92 us
    pallas_call x1, Pallas kernels, synthesize(): pl.pallas_call(functools.partial(synthesis_kernel, tiles), out_shape=jax....  2.58 us
    pallas_call x1, Pallas kernels, table_and_own(): pl.pallas_call(functools.partial(table_kernel, at, line), out_shape=[jax....  1.1 us
    pallas_call x1, Pallas kernels, cross(): pl.pallas_call(functools.partial(cross_kernel, at, line, order, min(8, co...  0.55 us
  transfers between devices with their start and end apart: 9, of which 5 were waited for; matrix products, arithmetic and copies ran while one was open for 0% of the time, Pallas kernels for 4%

profile of v8, /device:TPU:0, one launch (start us, length us, event | category | flops | bytes accessed | tf_op | source)
XLA Modules:
  0.0 24.8 jit_solution(5265128082615940529)
XLA Ops:
  0.0 0.0 copy-start
  0.0 2.9 %prepare.1 = (bf16[32,1536]{1,0:T(8,128)(2,1)S(1)}, bf16[128,1536]{1,0:T(8,128)(2,1)S(1)}, bf16[128,1536]{1,0:T(8,128)(2,1)S(1)}) custom-call(s32[16]{0:T(128)} %m_ref.3, bf16[32,1536]{1,0:T(8,128)(2,1)} %bitcast.6, bf16[1536,1536]{1,0:T(8,128)(2,1)} %bitcast.4, bf16[256,1536]{1,0:T(8,128)(2,1)} %bitcast.5), custom_call_target="tpu_custom_call" | custom-call | flops 352321536 | bytes 5505024 | tf_op jit(solution)/shard_map/prepare/pallas_call | solution.py:132
  2.9 3.0 %collective-permute-start.7 = (bf16[128,1536]{1,0:T(8,128)(2,1)S(1)}, bf16[128,1536]{1,0:T(8,128)(2,1)S(1)}, u32[]{:S(2)}, u32[]{:S(2)}) collective-permute-start(bf16[128,1536]{1,0:T(8,128)(2,1)S(1)} %get-tuple-element.14), channel_id=1, source_target_pairs={{0,2},{1,3},{2,0},{3,1},{4,6},{5,7},{6,4},{7,5},{8,10},{9,11},{10,... | collective-permute-start | bytes 1179656 | tf_op jit(solution)/shard_map/ppermute | solution.py:267
  6.0 1.6 %collective-permute-start.5 = (bf16[32,1536]{1,0:T(8,128)(2,1)S(1)}, bf16[32,1536]{1,0:T(8,128)(2,1)S(1)}, u32[]{:S(2)}, u32[]{:S(2)}) collective-permute-start(bf16[32,1536]{1,0:T(8,128)(2,1)S(1)} %get-tuple-element.12.refs_0_), channel_id=1, source_target_pairs={{0,4},{1,5},{2,6},{3,7},{4,8},{5,9},{6,10},{7,11},{8,12},{9,13},{1... | collective-permute-start | bytes 294920 | tf_op jit(solution)/shard_map/ppermute | solution.py:275
  7.5 2.6 %collective-permute-start.3 = (bf16[32,1536]{1,0:T(8,128)(2,1)S(1)}, bf16[32,1536]{1,0:T(8,128)(2,1)S(1)}, u32[]{:S(2)}, u32[]{:S(2)}) collective-permute-start(bf16[32,1536]{1,0:T(8,128)(2,1)S(1)} %get-tuple-element.12.refs_0_), channel_id=1, source_target_pairs={{0,8},{1,9},{2,10},{3,11},{4,12},{5,13},{6,14},{7,15},{8,0},{9,1},... | collective-permute-start | bytes 294920 | tf_op jit(solution)/shard_map/ppermute | solution.py:275
  10.1 1.3 %collective-permute-start.1 = (bf16[32,1536]{1,0:T(8,128)(2,1)S(1)}, bf16[32,1536]{1,0:T(8,128)(2,1)S(1)}, u32[]{:S(2)}, u32[]{:S(2)}) collective-permute-start(bf16[32,1536]{1,0:T(8,128)(2,1)S(1)} %get-tuple-element.12.refs_0_), channel_id=1, source_target_pairs={{0,12},{1,13},{2,14},{3,15},{4,0},{5,1},{6,2},{7,3},{8,4},{9,5},{1... | collective-permute-start | bytes 294920 | tf_op jit(solution)/shard_map/ppermute | solution.py:275
  11.5 0.0 collective-permute-start
  11.5 2.0 %collective-permute-done.5.refs_6_ = bf16[32,1536]{1,0:T(8,128)(2,1)S(1)} collective-permute-done((bf16[32,1536]{1,0:T(8,128)(2,1)S(1)}, bf16[32,1536]{1,0:T(8,128)(2,1)S(1)}, u32[]{:S(2)}, u32[]{:S(2)}) %collective-permute-start.5) | collective-permute-done | bytes 98336 | tf_op jit(solution)/shard_map/ppermute | solution.py:275
  13.4 0.0 collective-permute-start.6
  13.4 3.2 %collective-permute-done.3.refs_4_ = bf16[32,1536]{1,0:T(8,128)(2,1)S(1)} collective-permute-done((bf16[32,1536]{1,0:T(8,128)(2,1)S(1)}, bf16[32,1536]{1,0:T(8,128)(2,1)S(1)}, u32[]{:S(2)}, u32[]{:S(2)}) %collective-permute-start.3) | collective-permute-done | bytes 98336 | tf_op jit(solution)/shard_map/ppermute | solution.py:275
  16.6 0.0 collective-permute-start.4
  16.6 0.0 collective-permute-done.1.refs_2_
  16.6 0.5 %collective-permute-start.2 = (bf16[32,1536]{1,0:T(8,128)(2,1)S(1)}, bf16[32,1536]{1,0:T(8,128)(2,1)S(1)}, u32[]{:S(2)}, u32[]{:S(2)}) collective-permute-start(bf16[32,1536]{1,0:T(8,128)(2,1)S(1)} %collective-permute-done.1.refs_2_), channel_id=1, source_target_pairs={{0,1},{1,0},{2,3},{3,2},{4,5},{5,4},{6,7},{7,6},{8,9},{9,8},{10,11... | collective-permute-start | bytes 294920 | tf_op jit(solution)/shard_map/ppermute | solution.py:267
  17.1 0.0 collective-permute-done.refs_1_
  17.1 0.0 collective-permute-done.6.refs_7_
  17.1 0.8 %collective-permute-done.4.refs_5_ = bf16[32,1536]{1,0:T(8,128)(2,1)S(1)} collective-permute-done((bf16[32,1536]{1,0:T(8,128)(2,1)S(1)}, bf16[32,1536]{1,0:T(8,128)(2,1)S(1)}, u32[]{:S(2)}, u32[]{:S(2)}) %collective-permute-start.4) | collective-permute-done | bytes 98336 | tf_op jit(solution)/shard_map/ppermute | solution.py:267
  17.9 0.2 collective-permute-done.2.refs_3_
  18.0 0.0 collective-permute-done.7.refs_9_
  18.0 0.6 %cross.1 = (bf16[16,256]{1,0:T(8,128)(2,1)S(1)}, bf16[16,256]{1,0:T(8,128)(2,1)S(1)}) custom-call(bf16[32,1536]{1,0:T(8,128)(2,1)S(1)} %get-tuple-element.12.refs_0_, bf16[32,1536]{1,0:T(8,128)(2,1)S(1)} %collective-permute-done.refs_1_, bf16[32,1536]{1,0:T(8,128)(2,1)S(1)} %collective-permute-done.1.refs_2_, ...), custom_call_target="tpu_custom_call" | custom-call | flops 201326592 | bytes 1572864 | tf_op jit(solution)/shard_map/cross/pallas_call | solution.py:216
  18.6 0.4 %collective-permute-start.8 = (bf16[16,256]{1,0:T(8,128)(2,1)S(1)}, bf16[16,256]{1,0:T(8,128)(2,1)S(1)}, u32[]{:S(2)}, u32[]{:S(2)}) collective-permute-start(bf16[16,256]{1,0:T(8,128)(2,1)S(1)} %get-tuple-element.17), channel_id=1, source_target_pairs={{0,2},{1,3},{2,0},{3,1},{4,6},{5,7},{6,4},{7,5},{8,10},{9,11},{10,... | collective-permute-start | bytes 24584 | tf_op jit(solution)/shard_map/ppermute | solution.py:267
  19.0 0.0 copy-done
  19.0 1.1 %table_and_own.1 = (bf16[32,8192]{1,0:T(8,128)(2,1)S(1)}, bf16[256,32]{1,0:T(8,128)(2,1)S(1)}) custom-call(s32[16]{0:T(128)S(1)} %copy-done, bf16[16,256]{1,0:T(8,128)(2,1)S(1)} %get-tuple-element.15.own_ref), custom_call_target="tpu_custom_call" | custom-call | flops 2097152 | bytes 524288 | tf_op jit(solution)/shard_map/table_and_own/pallas_call | solution.py:166
  20.1 2.2 %collective-permute-done.8.got_ref = bf16[16,256]{1,0:T(8,128)(2,1)S(1)} collective-permute-done((bf16[16,256]{1,0:T(8,128)(2,1)S(1)}, bf16[16,256]{1,0:T(8,128)(2,1)S(1)}, u32[]{:S(2)}, u32[]{:S(2)}) %collective-permute-start.8) | collective-permute-done | bytes 8224 | tf_op jit(solution)/shard_map/ppermute | solution.py:267
  22.3 2.6 %synthesis.1 = bf16[256,8192]{1,0:T(8,128)(2,1)} custom-call(bf16[256,32]{1,0:T(8,128)(2,1)S(1)} %get-tuple-element.16.own_ref, bf16[16,256]{1,0:T(8,128)(2,1)S(1)} %collective-permute-done.8.got_ref, bf16[32,8192]{1,0:T(8,128)(2,1)S(1)} %get-tuple-element.18.table_ref), custom_call_target="tpu_custom_call" | custom-call | flops 134217728 | bytes 4718592 | tf_op jit(solution)/shard_map/synthesis/pallas_call | solution.py:250
Async XLA Ops:
  0.0 19.0 %copy-start = (s32[16]{0:T(128)S(1)}, s32[16]{0:T(128)}, u32[]{:S(2)}) copy-start(s32[16]{0:T(128)} %m_ref.3) | copy-start | bytes 196
  2.9 15.1 %collective-permute-start.7 = (bf16[128,1536]{1,0:T(8,128)(2,1)S(1)}, bf16[128,1536]{1,0:T(8,128)(2,1)S(1)}, u32[]{:S(2)}, u32[]{:S(2)}) collective-permute-start(bf16[128,1536]{1,0:T(8,128)(2,1)S(1)} %get-tuple-element.14), channel_id=1, source_target_pairs={{0,2},{1,3},{2,0},{3,1},{4,6},{5,7},{6,4},{7,5},{8,10},{9,11},{10,... | collective-permute-start | bytes 1179656 | tf_op jit(solution)/shard_map/ppermute | solution.py:267
  6.0 7.5 %collective-permute-start.5 = (bf16[32,1536]{1,0:T(8,128)(2,1)S(1)}, bf16[32,1536]{1,0:T(8,128)(2,1)S(1)}, u32[]{:S(2)}, u32[]{:S(2)}) collective-permute-start(bf16[32,1536]{1,0:T(8,128)(2,1)S(1)} %get-tuple-element.12.refs_0_), channel_id=1, source_target_pairs={{0,4},{1,5},{2,6},{3,7},{4,8},{5,9},{6,10},{7,11},{8,12},{9,13},{1... | collective-permute-start | bytes 294920 | tf_op jit(solution)/shard_map/ppermute | solution.py:275
  7.5 9.0 %collective-permute-start.3 = (bf16[32,1536]{1,0:T(8,128)(2,1)S(1)}, bf16[32,1536]{1,0:T(8,128)(2,1)S(1)}, u32[]{:S(2)}, u32[]{:S(2)}) collective-permute-start(bf16[32,1536]{1,0:T(8,128)(2,1)S(1)} %get-tuple-element.12.refs_0_), channel_id=1, source_target_pairs={{0,8},{1,9},{2,10},{3,11},{4,12},{5,13},{6,14},{7,15},{8,0},{9,1},... | collective-permute-start | bytes 294920 | tf_op jit(solution)/shard_map/ppermute | solution.py:275
  10.1 6.5 %collective-permute-start.1 = (bf16[32,1536]{1,0:T(8,128)(2,1)S(1)}, bf16[32,1536]{1,0:T(8,128)(2,1)S(1)}, u32[]{:S(2)}, u32[]{:S(2)}) collective-permute-start(bf16[32,1536]{1,0:T(8,128)(2,1)S(1)} %get-tuple-element.12.refs_0_), channel_id=1, source_target_pairs={{0,12},{1,13},{2,14},{3,15},{4,0},{5,1},{6,2},{7,3},{8,4},{9,5},{1... | collective-permute-start | bytes 294920 | tf_op jit(solution)/shard_map/ppermute | solution.py:275
  11.5 5.6 %collective-permute-start = (bf16[32,1536]{1,0:T(8,128)(2,1)S(1)}, bf16[32,1536]{1,0:T(8,128)(2,1)S(1)}, u32[]{:S(2)}, u32[]{:S(2)}) collective-permute-start(bf16[32,1536]{1,0:T(8,128)(2,1)S(1)} %get-tuple-element.12.refs_0_), channel_id=1, source_target_pairs={{0,1},{1,0},{2,3},{3,2},{4,5},{5,4},{6,7},{7,6},{8,9},{9,8},{10,11... | collective-permute-start | bytes 294920 | tf_op jit(solution)/shard_map/ppermute | solution.py:267
  13.4 3.7 %collective-permute-start.6 = (bf16[32,1536]{1,0:T(8,128)(2,1)S(1)}, bf16[32,1536]{1,0:T(8,128)(2,1)S(1)}, u32[]{:S(2)}, u32[]{:S(2)}) collective-permute-start(bf16[32,1536]{1,0:T(8,128)(2,1)S(1)} %collective-permute-done.5.refs_6_), channel_id=1, source_target_pairs={{0,1},{1,0},{2,3},{3,2},{4,5},{5,4},{6,7},{7,6},{8,9},{9,8},{10,11... | collective-permute-start | bytes 294920 | tf_op jit(solution)/shard_map/ppermute | solution.py:267
  16.6 1.3 %collective-permute-start.4 = (bf16[32,1536]{1,0:T(8,128)(2,1)S(1)}, bf16[32,1536]{1,0:T(8,128)(2,1)S(1)}, u32[]{:S(2)}, u32[]{:S(2)}) collective-permute-start(bf16[32,1536]{1,0:T(8,128)(2,1)S(1)} %collective-permute-done.3.refs_4_), channel_id=1, source_target_pairs={{0,1},{1,0},{2,3},{3,2},{4,5},{5,4},{6,7},{7,6},{8,9},{9,8},{10,11... | collective-permute-start | bytes 294920 | tf_op jit(solution)/shard_map/ppermute | solution.py:267
  16.6 1.5 %collective-permute-start.2 = (bf16[32,1536]{1,0:T(8,128)(2,1)S(1)}, bf16[32,1536]{1,0:T(8,128)(2,1)S(1)}, u32[]{:S(2)}, u32[]{:S(2)}) collective-permute-start(bf16[32,1536]{1,0:T(8,128)(2,1)S(1)} %collective-permute-done.1.refs_2_), channel_id=1, source_target_pairs={{0,1},{1,0},{2,3},{3,2},{4,5},{5,4},{6,7},{7,6},{8,9},{9,8},{10,11... | collective-permute-start | bytes 294920 | tf_op jit(solution)/shard_map/ppermute | solution.py:267
  18.6 3.7 %collective-permute-start.8 = (bf16[16,256]{1,0:T(8,128)(2,1)S(1)}, bf16[16,256]{1,0:T(8,128)(2,1)S(1)}, u32[]{:S(2)}, u32[]{:S(2)}) collective-permute-start(bf16[16,256]{1,0:T(8,128)(2,1)S(1)} %get-tuple-element.17), channel_id=1, source_target_pairs={{0,2},{1,3},{2,0},{3,1},{4,6},{5,7},{6,4},{7,5},{8,10},{9,11},{10,... | collective-permute-start | bytes 24584 | tf_op jit(solution)/shard_map/ppermute | solution.py:267

commit v9 on v8

--- a/solution.py
+++ b/solution.py
@@ -27,10 +27,36 @@
     return (value & low) | (bit << at) | ((value >> at) << (at + 1))
 
 
-def shard_source(position, me, at, line):
+def sends(line):
+    if line == 4:
+        return [[3, 0, 1, 2], [2, 1, 3, 0], [1, 3, 0, 2], [0, 2, 3, 1]]
+    return [[(z - turn) % line for z in range(line)] for turn in range(1, line)]
+
+
+def slots(line):
+    found = []
+    for z in range(line):
+        seen, own = {z}, []
+        for number, sources in enumerate(sends(line)):
+            if sources[z] not in seen:
+                seen.add(sources[z])
+                own.append((number, sources[z]))
+        found.append(own)
+    return list(zip(*found))
+
+
+def by_place(values, z):
+    result = values[0]
+    for place, value in enumerate(values):
+        if value != values[0]:
+            result = jnp.where(z == place, value, result)
+    return result
+
+
+def shard_ranks(me, at, line):
     z, other = me >> (at + 1), me & ((1 << at) - 1)
-    turn, flip = position >> at, position & ((1 << at) - 1)
-    return (((z - turn) & (line - 1)) << at) | (other ^ flip)
+    places = [z] + [by_place([source for _, source in slot], z) for slot in slots(line)]
+    return [(place << at) | (other ^ flip) for place in places for flip in range(1 << at)]
 
 
 def angle(phase):
@@ -46,8 +72,9 @@
     lane = iota((n, LANES), 1)
     own_bit = (me >> at) & 1
     values = jnp.zeros((n, LANES), jnp.int32)
+    ranks = shard_ranks(me, at, line)
     for j in range(n):
-        source = insert_bit(shard_source(j % half, me, at, line), own_bit ^ (j // half), at)
+        source = insert_bit(ranks[j % half], own_bit ^ (j // half), at)
         values = jnp.where(index == j, m_ref[source], values)
     scale = 1.0 / math.sqrt(n)
     fine = angle(values * lane)
@@ -180,9 +207,9 @@
 
 
 def cross_kernel(at, line, order, chunk, *refs):
-    shards = len(order)
-    shard_refs = dict(zip(order, refs[:shards]))
-    keep_ref, got_ref, own_ref, back_ref = refs[shards:]
+    shard_refs = dict(zip(order, refs[: len(order)]))
+    keep_ref, got_ref, own_ref, back_ref = refs[len(order) :]
+    shards = line << at
     half = keep_ref.shape[0]
     columns = shard_refs[0].shape[0]
     cycles = own_ref.shape[0]
@@ -193,15 +220,29 @@
     fold = iota((2 * cycles, 2 * half), 0) == iota((2 * cycles, 2 * half), 1) // shards
     fold = fold.astype(BF16)
     me = lax.axis_index("mset")
+    z = me >> (at + 1)
+    ranks = shard_ranks(me, at, line)
+
+    def shard(position):
+        turn, flip = position >> at, position & ((1 << at) - 1)
+        if turn == 0:
+            return shard_refs[flip][...]
+        numbers = [number for number, _ in slots(line)[turn - 1]]
+        value = shard_refs[(numbers[0] + 1) << at | flip][...]
+        for number in sorted(set(numbers) - {numbers[0]}):
+            here = by_place([int(k == number) for k in numbers], z)
+            value = jnp.where(here == 1, shard_refs[(number + 1) << at | flip][...], value)
+        return value
+
     for q in range(shards // chunk):
-        piece = jnp.concatenate(
-            [shard_refs[q * chunk + k][...] for k in range(chunk)], axis=0
-        )
+        piece = jnp.concatenate([shard(q * chunk + k) for k in range(chunk)], axis=0)
+        rank = jnp.zeros_like(local)
+        for k in range(chunk):
+            rank = jnp.where(local == k, ranks[q * chunk + k], rank)
         product = lax.dot_general(
             legendre, piece, (((1,), (1,)), ((), ())), preferred_element_type=F32
         )
-        own = slot == shard_source(local + q * chunk, me, at, line)
-        chosen = jnp.where(own, product, 0.0).astype(BF16)
+        chosen = jnp.where(slot == rank, product, 0.0).astype(BF16)
         folded = jnp.dot(fold, chosen, preferred_element_type=F32).astype(BF16)
         own_ref[:, q * wide : (q + 1) * wide] = folded[:cycles]
         back_ref[:, q * wide : (q + 1) * wide] = folded[cycles:]
@@ -210,13 +251,13 @@
 def cross(keep, got, shards, at, line):
     half, order_max = keep.shape
     columns = shards[0].shape[0]
-    count = len(shards)
-    order = sorted(shards, key=lambda k: -(k >> at) % line)
+    count = line << at
+    order = sorted(shards, key=lambda k: (k >> at != 0, -k))
     shape = jax.ShapeDtypeStruct((half // count, count * columns), BF16)
     return pl.pallas_call(
         functools.partial(cross_kernel, at, line, order, min(8, count)),
         out_shape=[shape, shape],
-        in_specs=[VMEM] * (2 + count),
+        in_specs=[VMEM] * (2 + len(order)),
         out_specs=[VMEM] * 2,
         compiler_params=pltpu.CompilerParams(vmem_limit_bytes=32 << 20),
         cost_estimate=pl.CostEstimate(
@@ -270,9 +311,9 @@
 def gather_shards(value, size, at, line):
     step = size // line
     shards = {0: value}
-    for turn in range(1, line):
-        pairs = [(d, (d + turn * step) % size) for d in range(size)]
-        shards[turn << at] = lax.ppermute(value, "mset", pairs)
+    for number, sources in enumerate(sends(line)):
+        pairs = [(s * step + k, z * step + k) for z, s in enumerate(sources) for k in range(step)]
+        shards[(number + 1) << at] = lax.ppermute(value, "mset", pairs)
     for b in range(at):
         shards.update({k | 1 << b: exchange(v, size, 1 << b) for k, v in shards.items()})
     return shards

time: 25 us -> 25.7 us (1.028)
  starting transfers between devices: 9.42 us -> 11.1 us
  waiting for transfers between devices: 8.24 us -> 7.11 us
    ppermute x3 -> x4, starting transfers between devices: 5.51 us -> 7.11 us  [gather_shards(): shards[number + 1 << at] = lax.ppermute(value, 'mset', pairs)]
    ppermute x3 -> x4, waiting for transfers between devices: 5.1 us -> 3.64 us  [gather_shards(): shards[number + 1 << at] = lax.ppermute(value, 'mset', pairs)]
    ppermute x6 -> x7, waiting for transfers between devices: 3.14 us -> 3.47 us  [exchange(): return lax.ppermute(value, 'mset', [(d, d ^ mask) for d in range(size)])]
    ppermute x6 -> x7, starting transfers between devices: 3.91 us -> 4 us  [exchange(): return lax.ppermute(value, 'mset', [(d, d ^ mask) for d in range(size)])]
  transfers between devices with their start and end apart: 9 -> 11, of which waited for: 5 -> 6; matrix products, arithmetic and copies ran while one was open for 0% -> 0% of each run, Pallas kernels for 4% -> 4%
where the time goes in v9:
time: 25.7 us; the launch traced here: 25.4 us
  starting transfers between devices  11.1 us (43%)
  Pallas kernels  7.15 us (28%)
  waiting for transfers between devices  7.11 us (28%)
    ppermute x4, starting transfers between devices, gather_shards(): shards[number + 1 << at] = lax.ppermute(value, 'mset', pairs)  7.11 us
    ppermute x7, starting transfers between devices, exchange(): return lax.ppermute(value, 'mset', [(d, d ^ mask) for d in range(size)])  4 us
    ppermute x4, waiting for transfers between devices, gather_shards(): shards[number + 1 << at] = lax.ppermute(value, 'mset', pairs)  3.64 us
    ppermute x7, waiting for transfers between devices, exchange(): return lax.ppermute(value, 'mset', [(d, d ^ mask) for d in range(size)])  3.47 us
    pallas_call x1, Pallas kernels, prepare(): pl.pallas_call(functools.partial(prepare_kernel, at), out_shape=[jax.Shap...  2.92 us
    pallas_call x1, Pallas kernels, synthesize(): pl.pallas_call(functools.partial(synthesis_kernel, tiles), out_shape=jax....  2.58 us
    pallas_call x1, Pallas kernels, table_and_own(): pl.pallas_call(functools.partial(table_kernel, at, line), out_shape=[jax....  1.1 us
    pallas_call x1, Pallas kernels, cross(): pl.pallas_call(functools.partial(cross_kernel, at, line, order, min(8, co...  0.55 us
  transfers between devices with their start and end apart: 11, of which 6 were waited for; matrix products, arithmetic and copies ran while one was open for 0% of the time, Pallas kernels for 4%

profile of v9, /device:TPU:0, one launch (start us, length us, event | category | flops | bytes accessed | tf_op | source)
XLA Modules:
  0.0 25.4 jit_solution(3797037327143098352)
XLA Ops:
  0.0 0.0 copy-start
  0.0 2.9 %prepare.1 = (bf16[32,1536]{1,0:T(8,128)(2,1)S(1)}, bf16[128,1536]{1,0:T(8,128)(2,1)S(1)}, bf16[128,1536]{1,0:T(8,128)(2,1)S(1)}) custom-call(s32[16]{0:T(128)} %m_ref.3, bf16[32,1536]{1,0:T(8,128)(2,1)} %bitcast.6, bf16[1536,1536]{1,0:T(8,128)(2,1)} %bitcast.4, bf16[256,1536]{1,0:T(8,128)(2,1)} %bitcast.5), custom_call_target="tpu_custom_call" | custom-call | flops 352321536 | bytes 5505024 | tf_op jit(solution)/shard_map/prepare/pallas_call | solution.py:159
  2.9 3.0 %collective-permute-start.9 = (bf16[128,1536]{1,0:T(8,128)(2,1)S(1)}, bf16[128,1536]{1,0:T(8,128)(2,1)S(1)}, u32[]{:S(2)}, u32[]{:S(2)}) collective-permute-start(bf16[128,1536]{1,0:T(8,128)(2,1)S(1)} %get-tuple-element.14), channel_id=1, source_target_pairs={{0,2},{1,3},{2,0},{3,1},{4,6},{5,7},{6,4},{7,5},{8,10},{9,11},{10,... | collective-permute-start | bytes 1179656 | tf_op jit(solution)/shard_map/ppermute | solution.py:308
  6.0 1.6 %collective-permute-start.7 = (bf16[32,1536]{1,0:T(8,128)(2,1)S(1)}, bf16[32,1536]{1,0:T(8,128)(2,1)S(1)}, u32[]{:S(2)}, u32[]{:S(2)}) collective-permute-start(bf16[32,1536]{1,0:T(8,128)(2,1)S(1)} %get-tuple-element.12.refs_1_), channel_id=1, source_target_pairs={{12,0},{13,1},{14,2},{15,3},{0,4},{1,5},{2,6},{3,7},{4,8},{5,9},{6... | collective-permute-start | bytes 294920 | tf_op jit(solution)/shard_map/ppermute | solution.py:316
  7.5 4.1 %collective-permute-start.5 = (bf16[32,1536]{1,0:T(8,128)(2,1)S(1)}, bf16[32,1536]{1,0:T(8,128)(2,1)S(1)}, u32[]{:S(2)}, u32[]{:S(2)}) collective-permute-start(bf16[32,1536]{1,0:T(8,128)(2,1)S(1)} %get-tuple-element.12.refs_1_), channel_id=1, source_target_pairs={{8,0},{9,1},{10,2},{11,3},{4,4},{5,5},{6,6},{7,7},{12,8},{13,9},{1... | collective-permute-start | bytes 294920 | tf_op jit(solution)/shard_map/ppermute | solution.py:316
  11.7 0.7 %collective-permute-start.3 = (bf16[32,1536]{1,0:T(8,128)(2,1)S(1)}, bf16[32,1536]{1,0:T(8,128)(2,1)S(1)}, u32[]{:S(2)}, u32[]{:S(2)}) collective-permute-start(bf16[32,1536]{1,0:T(8,128)(2,1)S(1)} %get-tuple-element.12.refs_1_), channel_id=1, source_target_pairs={{4,0},{5,1},{6,2},{7,3},{12,4},{13,5},{14,6},{15,7},{0,8},{1,9},{2... | collective-permute-start | bytes 294920 | tf_op jit(solution)/shard_map/ppermute | solution.py:316
  12.4 0.7 %collective-permute-start.1 = (bf16[32,1536]{1,0:T(8,128)(2,1)S(1)}, bf16[32,1536]{1,0:T(8,128)(2,1)S(1)}, u32[]{:S(2)}, u32[]{:S(2)}) collective-permute-start(bf16[32,1536]{1,0:T(8,128)(2,1)S(1)} %get-tuple-element.12.refs_1_), channel_id=1, source_target_pairs={{0,0},{1,1},{2,2},{3,3},{8,4},{9,5},{10,6},{11,7},{12,8},{13,9},{1... | collective-permute-start | bytes 294920 | tf_op jit(solution)/shard_map/ppermute | solution.py:316
  13.1 0.0 collective-permute-done.7.refs_9_
  13.1 0.1 collective-permute-start
  13.2 2.9 %collective-permute-done.5.refs_7_ = bf16[32,1536]{1,0:T(8,128)(2,1)S(1)} collective-permute-done((bf16[32,1536]{1,0:T(8,128)(2,1)S(1)}, bf16[32,1536]{1,0:T(8,128)(2,1)S(1)}, u32[]{:S(2)}, u32[]{:S(2)}) %collective-permute-start.5) | collective-permute-done | bytes 98336 | tf_op jit(solution)/shard_map/ppermute | solution.py:316
  16.1 0.0 collective-permute-start.8
  16.1 0.7 %collective-permute-done.3.refs_5_ = bf16[32,1536]{1,0:T(8,128)(2,1)S(1)} collective-permute-done((bf16[32,1536]{1,0:T(8,128)(2,1)S(1)}, bf16[32,1536]{1,0:T(8,128)(2,1)S(1)}, u32[]{:S(2)}, u32[]{:S(2)}) %collective-permute-start.3) | collective-permute-done | bytes 98336 | tf_op jit(solution)/shard_map/ppermute | solution.py:316
  16.8 0.0 collective-permute-start.6
  16.8 0.0 collective-permute-done.1.refs_3_
  16.8 0.5 %collective-permute-start.4 = (bf16[32,1536]{1,0:T(8,128)(2,1)S(1)}, bf16[32,1536]{1,0:T(8,128)(2,1)S(1)}, u32[]{:S(2)}, u32[]{:S(2)}) collective-permute-start(bf16[32,1536]{1,0:T(8,128)(2,1)S(1)} %collective-permute-done.3.refs_5_), channel_id=1, source_target_pairs={{0,1},{1,0},{2,3},{3,2},{4,5},{5,4},{6,7},{7,6},{8,9},{9,8},{10,11... | collective-permute-start | bytes 294920 | tf_op jit(solution)/shard_map/ppermute | solution.py:308
  17.3 0.0 collective-permute-done.refs_0_
  17.3 0.1 collective-permute-start.2
  17.4 0.0 collective-permute-done.8.refs_8_
  17.4 0.7 %collective-permute-done.6.refs_6_ = bf16[32,1536]{1,0:T(8,128)(2,1)S(1)} collective-permute-done((bf16[32,1536]{1,0:T(8,128)(2,1)S(1)}, bf16[32,1536]{1,0:T(8,128)(2,1)S(1)}, u32[]{:S(2)}, u32[]{:S(2)}) %collective-permute-start.6) | collective-permute-done | bytes 98336 | tf_op jit(solution)/shard_map/ppermute | solution.py:308
  18.1 0.2 collective-permute-done.4.refs_4_
  18.3 0.4 %collective-permute-done.2.refs_2_ = bf16[32,1536]{1,0:T(8,128)(2,1)S(1)} collective-permute-done((bf16[32,1536]{1,0:T(8,128)(2,1)S(1)}, bf16[32,1536]{1,0:T(8,128)(2,1)S(1)}, u32[]{:S(2)}, u32[]{:S(2)}) %collective-permute-start.2) | collective-permute-done | bytes 98336 | tf_op jit(solution)/shard_map/ppermute | solution.py:308
  18.6 0.0 collective-permute-done.9.refs_11_
  18.6 0.6 %cross.1 = (bf16[16,256]{1,0:T(8,128)(2,1)S(1)}, bf16[16,256]{1,0:T(8,128)(2,1)S(1)}) custom-call(bf16[32,1536]{1,0:T(8,128)(2,1)S(1)} %collective-permute-done.refs_0_, bf16[32,1536]{1,0:T(8,128)(2,1)S(1)} %get-tuple-element.12.refs_1_, bf16[32,1536]{1,0:T(8,128)(2,1)S(1)} %collective-permute-done.2.refs_2_, ...), custom_call_target="tpu_custom_call" | custom-call | flops 201326592 | bytes 1572864 | tf_op jit(solution)/shard_map/cross/pallas_call | solution.py:257
  19.2 0.3 %collective-permute-start.10 = (bf16[16,256]{1,0:T(8,128)(2,1)S(1)}, bf16[16,256]{1,0:T(8,128)(2,1)S(1)}, u32[]{:S(2)}, u32[]{:S(2)}) collective-permute-start(bf16[16,256]{1,0:T(8,128)(2,1)S(1)} %get-tuple-element.17), channel_id=1, source_target_pairs={{0,2},{1,3},{2,0},{3,1},{4,6},{5,7},{6,4},{7,5},{8,10},{9,11},{10,... | collective-permute-start | bytes 24584 | tf_op jit(solution)/shard_map/ppermute | solution.py:308
  19.5 0.0 copy-done
  19.5 1.1 %table_and_own.1 = (bf16[32,8192]{1,0:T(8,128)(2,1)S(1)}, bf16[256,32]{1,0:T(8,128)(2,1)S(1)}) custom-call(s32[16]{0:T(128)S(1)} %copy-done, bf16[16,256]{1,0:T(8,128)(2,1)S(1)} %get-tuple-element.15.own_ref), custom_call_target="tpu_custom_call" | custom-call | flops 2097152 | bytes 524288 | tf_op jit(solution)/shard_map/table_and_own/pallas_call | solution.py:193
  20.6 2.2 %collective-permute-done.10.got_ref = bf16[16,256]{1,0:T(8,128)(2,1)S(1)} collective-permute-done((bf16[16,256]{1,0:T(8,128)(2,1)S(1)}, bf16[16,256]{1,0:T(8,128)(2,1)S(1)}, u32[]{:S(2)}, u32[]{:S(2)}) %collective-permute-start.10) | collective-permute-done | bytes 8224 | tf_op jit(solution)/shard_map/ppermute | solution.py:308
  22.8 2.6 %synthesis.1 = bf16[256,8192]{1,0:T(8,128)(2,1)} custom-call(bf16[256,32]{1,0:T(8,128)(2,1)S(1)} %get-tuple-element.16.own_ref, bf16[16,256]{1,0:T(8,128)(2,1)S(1)} %collective-permute-done.10.got_ref, bf16[32,8192]{1,0:T(8,128)(2,1)S(1)} %get-tuple-element.18.table_ref), custom_call_target="tpu_custom_call" | custom-call | flops 134217728 | bytes 4718592 | tf_op jit(solution)/shard_map/synthesis/pallas_call | solution.py:291
Async XLA Ops:
  0.0 19.5 %copy-start = (s32[16]{0:T(128)S(1)}, s32[16]{0:T(128)}, u32[]{:S(2)}) copy-start(s32[16]{0:T(128)} %m_ref.3) | copy-start | bytes 196
  2.9 15.7 %collective-permute-start.9 = (bf16[128,1536]{1,0:T(8,128)(2,1)S(1)}, bf16[128,1536]{1,0:T(8,128)(2,1)S(1)}, u32[]{:S(2)}, u32[]{:S(2)}) collective-permute-start(bf16[128,1536]{1,0:T(8,128)(2,1)S(1)} %get-tuple-element.14), channel_id=1, source_target_pairs={{0,2},{1,3},{2,0},{3,1},{4,6},{5,7},{6,4},{7,5},{8,10},{9,11},{10,... | collective-permute-start | bytes 1179656 | tf_op jit(solution)/shard_map/ppermute | solution.py:308
  6.0 7.1 %collective-permute-start.7 = (bf16[32,1536]{1,0:T(8,128)(2,1)S(1)}, bf16[32,1536]{1,0:T(8,128)(2,1)S(1)}, u32[]{:S(2)}, u32[]{:S(2)}) collective-permute-start(bf16[32,1536]{1,0:T(8,128)(2,1)S(1)} %get-tuple-element.12.refs_1_), channel_id=1, source_target_pairs={{12,0},{13,1},{14,2},{15,3},{0,4},{1,5},{2,6},{3,7},{4,8},{5,9},{6... | collective-permute-start | bytes 294920 | tf_op jit(solution)/shard_map/ppermute | solution.py:316
  7.5 8.6 %collective-permute-start.5 = (bf16[32,1536]{1,0:T(8,128)(2,1)S(1)}, bf16[32,1536]{1,0:T(8,128)(2,1)S(1)}, u32[]{:S(2)}, u32[]{:S(2)}) collective-permute-start(bf16[32,1536]{1,0:T(8,128)(2,1)S(1)} %get-tuple-element.12.refs_1_), channel_id=1, source_target_pairs={{8,0},{9,1},{10,2},{11,3},{4,4},{5,5},{6,6},{7,7},{12,8},{13,9},{1... | collective-permute-start | bytes 294920 | tf_op jit(solution)/shard_map/ppermute | solution.py:316
  11.7 5.1 %collective-permute-start.3 = (bf16[32,1536]{1,0:T(8,128)(2,1)S(1)}, bf16[32,1536]{1,0:T(8,128)(2,1)S(1)}, u32[]{:S(2)}, u32[]{:S(2)}) collective-permute-start(bf16[32,1536]{1,0:T(8,128)(2,1)S(1)} %get-tuple-element.12.refs_1_), channel_id=1, source_target_pairs={{4,0},{5,1},{6,2},{7,3},{12,4},{13,5},{14,6},{15,7},{0,8},{1,9},{2... | collective-permute-start | bytes 294920 | tf_op jit(solution)/shard_map/ppermute | solution.py:316
  12.4 4.4 %collective-permute-start.1 = (bf16[32,1536]{1,0:T(8,128)(2,1)S(1)}, bf16[32,1536]{1,0:T(8,128)(2,1)S(1)}, u32[]{:S(2)}, u32[]{:S(2)}) collective-permute-start(bf16[32,1536]{1,0:T(8,128)(2,1)S(1)} %get-tuple-element.12.refs_1_), channel_id=1, source_target_pairs={{0,0},{1,1},{2,2},{3,3},{8,4},{9,5},{10,6},{11,7},{12,8},{13,9},{1... | collective-permute-start | bytes 294920 | tf_op jit(solution)/shard_map/ppermute | solution.py:316
  13.1 4.2 %collective-permute-start = (bf16[32,1536]{1,0:T(8,128)(2,1)S(1)}, bf16[32,1536]{1,0:T(8,128)(2,1)S(1)}, u32[]{:S(2)}, u32[]{:S(2)}) collective-permute-start(bf16[32,1536]{1,0:T(8,128)(2,1)S(1)} %get-tuple-element.12.refs_1_), channel_id=1, source_target_pairs={{0,1},{1,0},{2,3},{3,2},{4,5},{5,4},{6,7},{7,6},{8,9},{9,8},{10,11... | collective-permute-start | bytes 294920 | tf_op jit(solution)/shard_map/ppermute | solution.py:308
  16.1 1.3 %collective-permute-start.8 = (bf16[32,1536]{1,0:T(8,128)(2,1)S(1)}, bf16[32,1536]{1,0:T(8,128)(2,1)S(1)}, u32[]{:S(2)}, u32[]{:S(2)}) collective-permute-start(bf16[32,1536]{1,0:T(8,128)(2,1)S(1)} %collective-permute-done.7.refs_9_), channel_id=1, source_target_pairs={{0,1},{1,0},{2,3},{3,2},{4,5},{5,4},{6,7},{7,6},{8,9},{9,8},{10,11... | collective-permute-start | bytes 294920 | tf_op jit(solution)/shard_map/ppermute | solution.py:308
  16.8 1.3 %collective-permute-start.6 = (bf16[32,1536]{1,0:T(8,128)(2,1)S(1)}, bf16[32,1536]{1,0:T(8,128)(2,1)S(1)}, u32[]{:S(2)}, u32[]{:S(2)}) collective-permute-start(bf16[32,1536]{1,0:T(8,128)(2,1)S(1)} %collective-permute-done.5.refs_7_), channel_id=1, source_target_pairs={{0,1},{1,0},{2,3},{3,2},{4,5},{5,4},{6,7},{7,6},{8,9},{9,8},{10,11... | collective-permute-start | bytes 294920 | tf_op jit(solution)/shard_map/ppermute | solution.py:308
  16.8 1.5 %collective-permute-start.4 = (bf16[32,1536]{1,0:T(8,128)(2,1)S(1)}, bf16[32,1536]{1,0:T(8,128)(2,1)S(1)}, u32[]{:S(2)}, u32[]{:S(2)}) collective-permute-start(bf16[32,1536]{1,0:T(8,128)(2,1)S(1)} %collective-permute-done.3.refs_5_), channel_id=1, source_target_pairs={{0,1},{1,0},{2,3},{3,2},{4,5},{5,4},{6,7},{7,6},{8,9},{9,8},{10,11... | collective-permute-start | bytes 294920 | tf_op jit(solution)/shard_map/ppermute | solution.py:308
  17.3 1.3 %collective-permute-start.2 = (bf16[32,1536]{1,0:T(8,128)(2,1)S(1)}, bf16[32,1536]{1,0:T(8,128)(2,1)S(1)}, u32[]{:S(2)}, u32[]{:S(2)}) collective-permute-start(bf16[32,1536]{1,0:T(8,128)(2,1)S(1)} %collective-permute-done.1.refs_3_), channel_id=1, source_target_pairs={{0,1},{1,0},{2,3},{3,2},{4,5},{5,4},{6,7},{7,6},{8,9},{9,8},{10,11... | collective-permute-start | bytes 294920 | tf_op jit(solution)/shard_map/ppermute | solution.py:308
  19.2 3.7 %collective-permute-start.10 = (bf16[16,256]{1,0:T(8,128)(2,1)S(1)}, bf16[16,256]{1,0:T(8,128)(2,1)S(1)}, u32[]{:S(2)}, u32[]{:S(2)}) collective-permute-start(bf16[16,256]{1,0:T(8,128)(2,1)S(1)} %get-tuple-element.17), channel_id=1, source_target_pairs={{0,2},{1,3},{2,0},{3,1},{4,6},{5,7},{6,4},{7,5},{8,10},{9,11},{10,... | collective-permute-start | bytes 24584 | tf_op jit(solution)/shard_map/ppermute | solution.py:308

commit v10 on v8

--- a/solution.py
+++ b/solution.py
@@ -11,6 +11,7 @@
 LL = 3072
 REAL = 16
 NPHI = 8192
+RELAY_FLOPS = 2_750_000_000
 LANES = 128
 BF16 = jnp.bfloat16
 F32 = jnp.float32
@@ -177,6 +178,23 @@
         ),
         name="table_and_own",
     )(m_list, own)
+
+
+def relay_kernel(shard_ref, out_ref):
+    out_ref[...] = shard_ref[...]
+
+
+def relay(shard):
+    return pl.pallas_call(
+        relay_kernel,
+        out_shape=jax.ShapeDtypeStruct(shard.shape, BF16),
+        in_specs=[VMEM],
+        out_specs=VMEM,
+        cost_estimate=pl.CostEstimate(
+            flops=RELAY_FLOPS, bytes_accessed=4 * shard.size, transcendentals=0
+        ),
+        name="relay",
+    )(shard)
 
 
 def cross_kernel(at, line, order, chunk, *refs):
@@ -273,6 +291,7 @@
     for turn in range(1, line):
         pairs = [(d, (d + turn * step) % size) for d in range(size)]
         shards[turn << at] = lax.ppermute(value, "mset", pairs)
+    shards[1 << at] = relay(shards[1 << at])
     for b in range(at):
         shards.update({k | 1 << b: exchange(v, size, 1 << b) for k, v in shards.items()})
     return shards

time: 25 us -> 24.9 us (level)
  waiting for transfers between devices: 8.24 us -> 3.82 us
  local copies, waits for them, and re-layouts: 0.01 us -> 1.54 us
  Pallas kernels: 7.15 us -> 8.67 us
  starting transfers between devices: 9.42 us -> 10.7 us
    ppermute x3, waiting for transfers between devices: 5.1 us -> 1.44 us  [gather_shards(): shards[turn << at] = lax.ppermute(value, 'mset', pairs)]
    unnamed x2 -> x6, local copies, waits for them, and re-layouts: 0.01 us -> 1.54 us
    pallas_call x0 -> x1, Pallas kernels: none -> 1.53 us  [relay(): pl.pallas_call(relay_kernel, out_shape=jax.ShapeDtypeStruct(shard.shape,...]
    ppermute x3, starting transfers between devices: 5.51 us -> 7.01 us  [gather_shards(): shards[turn << at] = lax.ppermute(value, 'mset', pairs)]
    ppermute x6, waiting for transfers between devices: 3.14 us -> 2.38 us  [exchange(): return lax.ppermute(value, 'mset', [(d, d ^ mask) for d in range(size)])]
  transfers between devices with their start and end apart: 9 -> 9, of which waited for: 5 -> 4; matrix products, arithmetic and copies ran while one was open for 0% -> 0% of each run, Pallas kernels for 4% -> 11%
where the time goes in v10:
time: 24.9 us; the launch traced here: 24.7 us
  starting transfers between devices  10.7 us (43%)
  Pallas kernels  8.67 us (35%)
  waiting for transfers between devices  3.82 us (15%)
  local copies, waits for them, and re-layouts  1.54 us (6%)
    ppermute x3, starting transfers between devices, gather_shards(): shards[turn << at] = lax.ppermute(value, 'mset', pairs)  7.01 us
    ppermute x6, starting transfers between devices, exchange(): return lax.ppermute(value, 'mset', [(d, d ^ mask) for d in range(size)])  3.67 us
    pallas_call x1, Pallas kernels, prepare(): pl.pallas_call(functools.partial(prepare_kernel, at), out_shape=[jax.Shap...  2.91 us
    pallas_call x1, Pallas kernels, synthesize(): pl.pallas_call(functools.partial(synthesis_kernel, tiles), out_shape=jax....  2.58 us
    ppermute x6, waiting for transfers between devices, exchange(): return lax.ppermute(value, 'mset', [(d, d ^ mask) for d in range(size)])  2.38 us
    unnamed x6, local copies, waits for them, and re-layouts  1.54 us
    pallas_call x1, Pallas kernels, relay(): pl.pallas_call(relay_kernel, out_shape=jax.ShapeDtypeStruct(shard.shape,...  1.53 us
    ppermute x3, waiting for transfers between devices, gather_shards(): shards[turn << at] = lax.ppermute(value, 'mset', pairs)  1.44 us
  transfers between devices with their start and end apart: 9, of which 4 were waited for; matrix products, arithmetic and copies ran while one was open for 0% of the time, Pallas kernels for 11%

profile of v10, /device:TPU:0, one launch (start us, length us, event | category | flops | bytes accessed | tf_op | source)
XLA Modules:
  0.0 24.7 jit_solution(11805761489446533709)
XLA Ops:
  0.0 2.9 %prepare.1 = (bf16[32,1536]{1,0:T(8,128)(2,1)S(1)}, bf16[128,1536]{1,0:T(8,128)(2,1)S(1)}, bf16[128,1536]{1,0:T(8,128)(2,1)S(1)}) custom-call(s32[16]{0:T(128)} %m_ref.3, bf16[32,1536]{1,0:T(8,128)(2,1)} %bitcast.6, bf16[1536,1536]{1,0:T(8,128)(2,1)} %bitcast.4, bf16[256,1536]{1,0:T(8,128)(2,1)} %bitcast.5), custom_call_target="tpu_custom_call" | custom-call | flops 352321536 | bytes 5505024 | tf_op jit(solution)/shard_map/prepare/pallas_call | solution.py:133
  2.9 3.1 %collective-permute-start.5 = (bf16[32,1536]{1,0:T(8,128)(2,1)S(1)}, bf16[32,1536]{1,0:T(8,128)(2,1)S(1)}, u32[]{:S(2)}, u32[]{:S(2)}) collective-permute-start(bf16[32,1536]{1,0:T(8,128)(2,1)S(1)} %get-tuple-element.12.refs_0_), channel_id=1, source_target_pairs={{0,4},{1,5},{2,6},{3,7},{4,8},{5,9},{6,10},{7,11},{8,12},{9,13},{1... | collective-permute-start | bytes 294920 | tf_op jit(solution)/shard_map/ppermute | solution.py:293
  6.0 0.0 copy-start.1
  6.0 1.5 %collective-permute-start.7 = (bf16[128,1536]{1,0:T(8,128)(2,1)S(1)}, bf16[128,1536]{1,0:T(8,128)(2,1)S(1)}, u32[]{:S(2)}, u32[]{:S(2)}) collective-permute-start(bf16[128,1536]{1,0:T(8,128)(2,1)S(1)} %get-tuple-element.14), channel_id=1, source_target_pairs={{0,2},{1,3},{2,0},{3,1},{4,6},{5,7},{6,4},{7,5},{8,10},{9,11},{10,... | collective-permute-start | bytes 1179656 | tf_op jit(solution)/shard_map/ppermute | solution.py:285
  7.5 2.6 %collective-permute-start.3 = (bf16[32,1536]{1,0:T(8,128)(2,1)S(1)}, bf16[32,1536]{1,0:T(8,128)(2,1)S(1)}, u32[]{:S(2)}, u32[]{:S(2)}) collective-permute-start(bf16[32,1536]{1,0:T(8,128)(2,1)S(1)} %get-tuple-element.12.refs_0_), channel_id=1, source_target_pairs={{0,8},{1,9},{2,10},{3,11},{4,12},{5,13},{6,14},{7,15},{8,0},{9,1},... | collective-permute-start | bytes 294920 | tf_op jit(solution)/shard_map/ppermute | solution.py:293
  10.1 1.3 %collective-permute-start.1 = (bf16[32,1536]{1,0:T(8,128)(2,1)S(1)}, bf16[32,1536]{1,0:T(8,128)(2,1)S(1)}, u32[]{:S(2)}, u32[]{:S(2)}) collective-permute-start(bf16[32,1536]{1,0:T(8,128)(2,1)S(1)} %get-tuple-element.12.refs_0_), channel_id=1, source_target_pairs={{0,12},{1,13},{2,14},{3,15},{4,0},{5,1},{6,2},{7,3},{8,4},{9,5},{1... | collective-permute-start | bytes 294920 | tf_op jit(solution)/shard_map/ppermute | solution.py:293
  11.5 0.0 collective-permute-start
  11.5 0.0 collective-permute-done.5.shard_ref
  11.5 0.0 copy-start.2
  11.5 0.6 %copy-done.2 = bf16[32,1536]{1,0:T(8,128)(2,1)} copy-done((bf16[32,1536]{1,0:T(8,128)(2,1)}, bf16[32,1536]{1,0:T(8,128)(2,1)S(1)}, u32[]{:S(2)}) %copy-start.2) | copy-done | bytes 98328
  12.1 1.5 %relay.1.refs_6_ = bf16[32,1536]{1,0:T(8,128)(2,1)} custom-call(bf16[32,1536]{1,0:T(8,128)(2,1)} %copy-done.2), custom_call_target="tpu_custom_call" | custom-call | flops 2750000128 | bytes 196608 | tf_op jit(solution)/shard_map/relay/pallas_call | solution.py:188
  13.6 0.5 %collective-permute-start.6 = (bf16[32,1536]{1,0:T(8,128)(2,1)}, bf16[32,1536]{1,0:T(8,128)(2,1)S(1)}, u32[]{:S(2)}, u32[]{:S(2)}) collective-permute-start(bf16[32,1536]{1,0:T(8,128)(2,1)} %relay.1.refs_6_), channel_id=1, source_target_pairs={{0,1},{1,0},{2,3},{3,2},{4,5},{5,4},{6,7},{7,6},{8,9},{9,8},{10,11... | collective-permute-start | bytes 294920 | tf_op jit(solution)/shard_map/ppermute | solution.py:285
  14.1 1.4 %collective-permute-done.3.refs_4_ = bf16[32,1536]{1,0:T(8,128)(2,1)S(1)} collective-permute-done((bf16[32,1536]{1,0:T(8,128)(2,1)S(1)}, bf16[32,1536]{1,0:T(8,128)(2,1)S(1)}, u32[]{:S(2)}, u32[]{:S(2)}) %collective-permute-start.3) | collective-permute-done | bytes 98336 | tf_op jit(solution)/shard_map/ppermute | solution.py:293
  15.6 0.0 collective-permute-start.4
  15.6 0.0 collective-permute-done.1.refs_2_
  15.6 0.5 %collective-permute-start.2 = (bf16[32,1536]{1,0:T(8,128)(2,1)S(1)}, bf16[32,1536]{1,0:T(8,128)(2,1)S(1)}, u32[]{:S(2)}, u32[]{:S(2)}) collective-permute-start(bf16[32,1536]{1,0:T(8,128)(2,1)S(1)} %collective-permute-done.1.refs_2_), channel_id=1, source_target_pairs={{0,1},{1,0},{2,3},{3,2},{4,5},{5,4},{6,7},{7,6},{8,9},{9,8},{10,11... | collective-permute-start | bytes 294920 | tf_op jit(solution)/shard_map/ppermute | solution.py:285
  16.1 0.0 collective-permute-done.refs_1_
  16.1 0.0 collective-permute-done.6.refs_7_
  16.1 0.8 %collective-permute-done.4.refs_5_ = bf16[32,1536]{1,0:T(8,128)(2,1)S(1)} collective-permute-done((bf16[32,1536]{1,0:T(8,128)(2,1)S(1)}, bf16[32,1536]{1,0:T(8,128)(2,1)S(1)}, u32[]{:S(2)}, u32[]{:S(2)}) %collective-permute-start.4) | collective-permute-done | bytes 98336 | tf_op jit(solution)/shard_map/ppermute | solution.py:285
  16.9 0.2 collective-permute-done.2.refs_3_
  17.0 0.0 collective-permute-done.7.refs_9_
  17.0 0.0 copy-start
  17.0 0.9 %copy-done = bf16[32,1536]{1,0:T(8,128)(2,1)S(1)} copy-done((bf16[32,1536]{1,0:T(8,128)(2,1)S(1)}, bf16[32,1536]{1,0:T(8,128)(2,1)}, u32[]{:S(2)}) %copy-start) | copy-done | bytes 98328
  17.9 0.6 %cross.1 = (bf16[16,256]{1,0:T(8,128)(2,1)S(1)}, bf16[16,256]{1,0:T(8,128)(2,1)S(1)}) custom-call(bf16[32,1536]{1,0:T(8,128)(2,1)S(1)} %get-tuple-element.12.refs_0_, bf16[32,1536]{1,0:T(8,128)(2,1)S(1)} %collective-permute-done.refs_1_, bf16[32,1536]{1,0:T(8,128)(2,1)S(1)} %collective-permute-done.1.refs_2_, ...), custom_call_target="tpu_custom_call" | custom-call | flops 201326592 | bytes 1572864 | tf_op jit(solution)/shard_map/cross/pallas_call | solution.py:234
  18.5 1.1 %collective-permute-start.8 = (bf16[16,256]{1,0:T(8,128)(2,1)S(1)}, bf16[16,256]{1,0:T(8,128)(2,1)S(1)}, u32[]{:S(2)}, u32[]{:S(2)}) collective-permute-start(bf16[16,256]{1,0:T(8,128)(2,1)S(1)} %get-tuple-element.17), channel_id=1, source_target_pairs={{0,2},{1,3},{2,0},{3,1},{4,6},{5,7},{6,4},{7,5},{8,10},{9,11},{10,... | collective-permute-start | bytes 24584 | tf_op jit(solution)/shard_map/ppermute | solution.py:285
  19.6 0.0 copy-done.1
  19.6 1.1 %table_and_own.1 = (bf16[32,8192]{1,0:T(8,128)(2,1)S(1)}, bf16[256,32]{1,0:T(8,128)(2,1)S(1)}) custom-call(s32[16]{0:T(128)S(1)} %copy-done.1, bf16[16,256]{1,0:T(8,128)(2,1)S(1)} %get-tuple-element.15.own_ref), custom_call_target="tpu_custom_call" | custom-call | flops 2097152 | bytes 524288 | tf_op jit(solution)/shard_map/table_and_own/pallas_call | solution.py:167
  20.7 1.4 %collective-permute-done.8.got_ref = bf16[16,256]{1,0:T(8,128)(2,1)S(1)} collective-permute-done((bf16[16,256]{1,0:T(8,128)(2,1)S(1)}, bf16[16,256]{1,0:T(8,128)(2,1)S(1)}, u32[]{:S(2)}, u32[]{:S(2)}) %collective-permute-start.8) | collective-permute-done | bytes 8224 | tf_op jit(solution)/shard_map/ppermute | solution.py:285
  22.2 2.6 %synthesis.1 = bf16[256,8192]{1,0:T(8,128)(2,1)} custom-call(bf16[256,32]{1,0:T(8,128)(2,1)S(1)} %get-tuple-element.16.own_ref, bf16[16,256]{1,0:T(8,128)(2,1)S(1)} %collective-permute-done.8.got_ref, bf16[32,8192]{1,0:T(8,128)(2,1)S(1)} %get-tuple-element.18.table_ref), custom_call_target="tpu_custom_call" | custom-call | flops 134217728 | bytes 4718592 | tf_op jit(solution)/shard_map/synthesis/pallas_call | solution.py:268
Async XLA Ops:
  2.9 8.5 %collective-permute-start.5 = (bf16[32,1536]{1,0:T(8,128)(2,1)S(1)}, bf16[32,1536]{1,0:T(8,128)(2,1)S(1)}, u32[]{:S(2)}, u32[]{:S(2)}) collective-permute-start(bf16[32,1536]{1,0:T(8,128)(2,1)S(1)} %get-tuple-element.12.refs_0_), channel_id=1, source_target_pairs={{0,4},{1,5},{2,6},{3,7},{4,8},{5,9},{6,10},{7,11},{8,12},{9,13},{1... | collective-permute-start | bytes 294920 | tf_op jit(solution)/shard_map/ppermute | solution.py:293
  6.0 13.6 %copy-start.1 = (s32[16]{0:T(128)S(1)}, s32[16]{0:T(128)}, u32[]{:S(2)}) copy-start(s32[16]{0:T(128)} %m_ref.3) | copy-start | bytes 196
  6.0 11.0 %collective-permute-start.7 = (bf16[128,1536]{1,0:T(8,128)(2,1)S(1)}, bf16[128,1536]{1,0:T(8,128)(2,1)S(1)}, u32[]{:S(2)}, u32[]{:S(2)}) collective-permute-start(bf16[128,1536]{1,0:T(8,128)(2,1)S(1)} %get-tuple-element.14), channel_id=1, source_target_pairs={{0,2},{1,3},{2,0},{3,1},{4,6},{5,7},{6,4},{7,5},{8,10},{9,11},{10,... | collective-permute-start | bytes 1179656 | tf_op jit(solution)/shard_map/ppermute | solution.py:285
  7.5 8.1 %collective-permute-start.3 = (bf16[32,1536]{1,0:T(8,128)(2,1)S(1)}, bf16[32,1536]{1,0:T(8,128)(2,1)S(1)}, u32[]{:S(2)}, u32[]{:S(2)}) collective-permute-start(bf16[32,1536]{1,0:T(8,128)(2,1)S(1)} %get-tuple-element.12.refs_0_), channel_id=1, source_target_pairs={{0,8},{1,9},{2,10},{3,11},{4,12},{5,13},{6,14},{7,15},{8,0},{9,1},... | collective-permute-start | bytes 294920 | tf_op jit(solution)/shard_map/ppermute | solution.py:293
  10.1 5.5 %collective-permute-start.1 = (bf16[32,1536]{1,0:T(8,128)(2,1)S(1)}, bf16[32,1536]{1,0:T(8,128)(2,1)S(1)}, u32[]{:S(2)}, u32[]{:S(2)}) collective-permute-start(bf16[32,1536]{1,0:T(8,128)(2,1)S(1)} %get-tuple-element.12.refs_0_), channel_id=1, source_target_pairs={{0,12},{1,13},{2,14},{3,15},{4,0},{5,1},{6,2},{7,3},{8,4},{9,5},{1... | collective-permute-start | bytes 294920 | tf_op jit(solution)/shard_map/ppermute | solution.py:293
  11.5 4.6 %collective-permute-start = (bf16[32,1536]{1,0:T(8,128)(2,1)S(1)}, bf16[32,1536]{1,0:T(8,128)(2,1)S(1)}, u32[]{:S(2)}, u32[]{:S(2)}) collective-permute-start(bf16[32,1536]{1,0:T(8,128)(2,1)S(1)} %get-tuple-element.12.refs_0_), channel_id=1, source_target_pairs={{0,1},{1,0},{2,3},{3,2},{4,5},{5,4},{6,7},{7,6},{8,9},{9,8},{10,11... | collective-permute-start | bytes 294920 | tf_op jit(solution)/shard_map/ppermute | solution.py:285
  11.5 0.6 %copy-start.2 = (bf16[32,1536]{1,0:T(8,128)(2,1)}, bf16[32,1536]{1,0:T(8,128)(2,1)S(1)}, u32[]{:S(2)}) copy-start(bf16[32,1536]{1,0:T(8,128)(2,1)S(1)} %collective-permute-done.5.shard_ref) | copy-start | bytes 294916
  13.6 2.5 %collective-permute-start.6 = (bf16[32,1536]{1,0:T(8,128)(2,1)}, bf16[32,1536]{1,0:T(8,128)(2,1)S(1)}, u32[]{:S(2)}, u32[]{:S(2)}) collective-permute-start(bf16[32,1536]{1,0:T(8,128)(2,1)} %relay.1.refs_6_), channel_id=1, source_target_pairs={{0,1},{1,0},{2,3},{3,2},{4,5},{5,4},{6,7},{7,6},{8,9},{9,8},{10,11... | collective-permute-start | bytes 294920 | tf_op jit(solution)/shard_map/ppermute | solution.py:285
  15.6 1.3 %collective-permute-start.4 = (bf16[32,1536]{1,0:T(8,128)(2,1)S(1)}, bf16[32,1536]{1,0:T(8,128)(2,1)S(1)}, u32[]{:S(2)}, u32[]{:S(2)}) collective-permute-start(bf16[32,1536]{1,0:T(8,128)(2,1)S(1)} %collective-permute-done.3.refs_4_), channel_id=1, source_target_pairs={{0,1},{1,0},{2,3},{3,2},{4,5},{5,4},{6,7},{7,6},{8,9},{9,8},{10,11... | collective-permute-start | bytes 294920 | tf_op jit(solution)/shard_map/ppermute | solution.py:285
  15.6 1.5 %collective-permute-start.2 = (bf16[32,1536]{1,0:T(8,128)(2,1)S(1)}, bf16[32,1536]{1,0:T(8,128)(2,1)S(1)}, u32[]{:S(2)}, u32[]{:S(2)}) collective-permute-start(bf16[32,1536]{1,0:T(8,128)(2,1)S(1)} %collective-permute-done.1.refs_2_), channel_id=1, source_target_pairs={{0,1},{1,0},{2,3},{3,2},{4,5},{5,4},{6,7},{7,6},{8,9},{9,8},{10,11... | collective-permute-start | bytes 294920 | tf_op jit(solution)/shard_map/ppermute | solution.py:285
  17.0 0.9 %copy-start = (bf16[32,1536]{1,0:T(8,128)(2,1)S(1)}, bf16[32,1536]{1,0:T(8,128)(2,1)}, u32[]{:S(2)}) copy-start(bf16[32,1536]{1,0:T(8,128)(2,1)} %relay.1.refs_6_) | copy-start | bytes 294916
  18.5 3.7 %collective-permute-start.8 = (bf16[16,256]{1,0:T(8,128)(2,1)S(1)}, bf16[16,256]{1,0:T(8,128)(2,1)S(1)}, u32[]{:S(2)}, u32[]{:S(2)}) collective-permute-start(bf16[16,256]{1,0:T(8,128)(2,1)S(1)} %get-tuple-element.17), channel_id=1, source_target_pairs={{0,2},{1,3},{2,0},{3,1},{4,6},{5,7},{6,4},{7,5},{8,10},{9,11},{10,... | collective-permute-start | bytes 24584 | tf_op jit(solution)/shard_map/ppermute | solution.py:285

commit v11 on v10

--- a/solution.py
+++ b/solution.py
@@ -190,6 +190,7 @@
         out_shape=jax.ShapeDtypeStruct(shard.shape, BF16),
         in_specs=[VMEM],
         out_specs=VMEM,
+        compiler_params=pltpu.CompilerParams(vmem_limit_bytes=8 << 20),
         cost_estimate=pl.CostEstimate(
             flops=RELAY_FLOPS, bytes_accessed=4 * shard.size, transcendentals=0
         ),

time: 24.9 us -> 24 us (0.964)
  waiting for transfers between devices: 3.82 us -> 5.91 us
  local copies, waits for them, and re-layouts: 1.54 us -> 0.01 us
  Pallas kernels: 8.67 us -> 7.15 us
    ppermute x3, waiting for transfers between devices: 1.44 us -> 3.53 us  [gather_shards(): shards[turn << at] = lax.ppermute(value, 'mset', pairs)]
    unnamed x6 -> x2, local copies, waits for them, and re-layouts: 1.54 us -> 0.01 us
    pallas_call x1, Pallas kernels: 1.53 us -> 0.01 us  [relay(): pl.pallas_call(relay_kernel, out_shape=jax.ShapeDtypeStruct(shard.shape,...]
  transfers between devices with their start and end apart: 9 -> 9, of which waited for: 4 -> 4; matrix products, arithmetic and copies ran while one was open for 0% -> 0% of each run, Pallas kernels for 11% -> 5%
where the time goes in v11:
time: 24 us; the launch traced here: 23.8 us
  starting transfers between devices  10.8 us (45%)
  Pallas kernels  7.15 us (30%)
  waiting for transfers between devices  5.91 us (25%)
    ppermute x3, starting transfers between devices, gather_shards(): shards[turn << at] = lax.ppermute(value, 'mset', pairs)  7.01 us
    ppermute x6, starting transfers between devices, exchange(): return lax.ppermute(value, 'mset', [(d, d ^ mask) for d in range(size)])  3.74 us
    ppermute x3, waiting for transfers between devices, gather_shards(): shards[turn << at] = lax.ppermute(value, 'mset', pairs)  3.53 us
    pallas_call x1, Pallas kernels, prepare(): pl.pallas_call(functools.partial(prepare_kernel, at), out_shape=[jax.Shap...  2.91 us
    pallas_call x1, Pallas kernels, synthesize(): pl.pallas_call(functools.partial(synthesis_kernel, tiles), out_shape=jax....  2.58 us
    ppermute x6, waiting for transfers between devices, exchange(): return lax.ppermute(value, 'mset', [(d, d ^ mask) for d in range(size)])  2.38 us
    pallas_call x1, Pallas kernels, table_and_own(): pl.pallas_call(functools.partial(table_kernel, at, line), out_shape=[jax....  1.1 us
    pallas_call x1, Pallas kernels, cross(): pl.pallas_call(functools.partial(cross_kernel, at, line, order, min(8, co...  0.55 us
  transfers between devices with their start and end apart: 9, of which 4 were waited for; matrix products, arithmetic and copies ran while one was open for 0% of the time, Pallas kernels for 5%

profile of v11, /device:TPU:0, one launch (start us, length us, event | category | flops | bytes accessed | tf_op | source)
XLA Modules:
  0.0 23.8 jit_solution(13616317571554337497)
XLA Ops:
  0.0 2.9 %prepare.1 = (bf16[32,1536]{1,0:T(8,128)(2,1)S(1)}, bf16[128,1536]{1,0:T(8,128)(2,1)S(1)}, bf16[128,1536]{1,0:T(8,128)(2,1)S(1)}) custom-call(s32[16]{0:T(128)} %m_ref.3, bf16[32,1536]{1,0:T(8,128)(2,1)} %bitcast.6, bf16[1536,1536]{1,0:T(8,128)(2,1)} %bitcast.4, bf16[256,1536]{1,0:T(8,128)(2,1)} %bitcast.5), custom_call_target="tpu_custom_call" | custom-call | flops 352321536 | bytes 5505024 | tf_op jit(solution)/shard_map/prepare/pallas_call | solution.py:133
  2.9 3.1 %collective-permute-start.5 = (bf16[32,1536]{1,0:T(8,128)(2,1)S(1)}, bf16[32,1536]{1,0:T(8,128)(2,1)S(1)}, u32[]{:S(2)}, u32[]{:S(2)}) collective-permute-start(bf16[32,1536]{1,0:T(8,128)(2,1)S(1)} %get-tuple-element.12.refs_0_), channel_id=1, source_target_pairs={{0,4},{1,5},{2,6},{3,7},{4,8},{5,9},{6,10},{7,11},{8,12},{9,13},{1... | collective-permute-start | bytes 294920 | tf_op jit(solution)/shard_map/ppermute | solution.py:294
  6.0 0.0 copy-start
  6.0 1.5 %collective-permute-start.7 = (bf16[128,1536]{1,0:T(8,128)(2,1)S(1)}, bf16[128,1536]{1,0:T(8,128)(2,1)S(1)}, u32[]{:S(2)}, u32[]{:S(2)}) collective-permute-start(bf16[128,1536]{1,0:T(8,128)(2,1)S(1)} %get-tuple-element.14), channel_id=1, source_target_pairs={{0,2},{1,3},{2,0},{3,1},{4,6},{5,7},{6,4},{7,5},{8,10},{9,11},{10,... | collective-permute-start | bytes 1179656 | tf_op jit(solution)/shard_map/ppermute | solution.py:286
  7.5 2.6 %collective-permute-start.3 = (bf16[32,1536]{1,0:T(8,128)(2,1)S(1)}, bf16[32,1536]{1,0:T(8,128)(2,1)S(1)}, u32[]{:S(2)}, u32[]{:S(2)}) collective-permute-start(bf16[32,1536]{1,0:T(8,128)(2,1)S(1)} %get-tuple-element.12.refs_0_), channel_id=1, source_target_pairs={{0,8},{1,9},{2,10},{3,11},{4,12},{5,13},{6,14},{7,15},{8,0},{9,1},... | collective-permute-start | bytes 294920 | tf_op jit(solution)/shard_map/ppermute | solution.py:294
  10.1 1.3 %collective-permute-start.1 = (bf16[32,1536]{1,0:T(8,128)(2,1)S(1)}, bf16[32,1536]{1,0:T(8,128)(2,1)S(1)}, u32[]{:S(2)}, u32[]{:S(2)}) collective-permute-start(bf16[32,1536]{1,0:T(8,128)(2,1)S(1)} %get-tuple-element.12.refs_0_), channel_id=1, source_target_pairs={{0,12},{1,13},{2,14},{3,15},{4,0},{5,1},{6,2},{7,3},{8,4},{9,5},{1... | collective-permute-start | bytes 294920 | tf_op jit(solution)/shard_map/ppermute | solution.py:294
  11.5 0.0 collective-permute-start
  11.5 0.0 collective-permute-done.5.shard_ref
  11.5 0.6 %collective-permute-start.6 = (bf16[32,1536]{1,0:T(8,128)(2,1)S(1)}, bf16[32,1536]{1,0:T(8,128)(2,1)S(1)}, u32[]{:S(2)}, u32[]{:S(2)}) collective-permute-start(bf16[32,1536]{1,0:T(8,128)(2,1)S(1)} %relay.1.refs_6_), channel_id=1, source_target_pairs={{0,1},{1,0},{2,3},{3,2},{4,5},{5,4},{6,7},{7,6},{8,9},{9,8},{10,11... | collective-permute-start | bytes 294920 | tf_op jit(solution)/shard_map/ppermute | solution.py:286
  12.0 3.5 %collective-permute-done.3.refs_4_ = bf16[32,1536]{1,0:T(8,128)(2,1)S(1)} collective-permute-done((bf16[32,1536]{1,0:T(8,128)(2,1)S(1)}, bf16[32,1536]{1,0:T(8,128)(2,1)S(1)}, u32[]{:S(2)}, u32[]{:S(2)}) %collective-permute-start.3) | collective-permute-done | bytes 98336 | tf_op jit(solution)/shard_map/ppermute | solution.py:294
  15.6 0.0 collective-permute-start.4
  15.6 0.0 collective-permute-done.1.refs_2_
  15.6 0.5 %collective-permute-start.2 = (bf16[32,1536]{1,0:T(8,128)(2,1)S(1)}, bf16[32,1536]{1,0:T(8,128)(2,1)S(1)}, u32[]{:S(2)}, u32[]{:S(2)}) collective-permute-start(bf16[32,1536]{1,0:T(8,128)(2,1)S(1)} %collective-permute-done.1.refs_2_), channel_id=1, source_target_pairs={{0,1},{1,0},{2,3},{3,2},{4,5},{5,4},{6,7},{7,6},{8,9},{9,8},{10,11... | collective-permute-start | bytes 294920 | tf_op jit(solution)/shard_map/ppermute | solution.py:286
  16.1 0.0 collective-permute-done.refs_1_
  16.1 0.0 collective-permute-done.6.refs_7_
  16.1 0.8 %collective-permute-done.4.refs_5_ = bf16[32,1536]{1,0:T(8,128)(2,1)S(1)} collective-permute-done((bf16[32,1536]{1,0:T(8,128)(2,1)S(1)}, bf16[32,1536]{1,0:T(8,128)(2,1)S(1)}, u32[]{:S(2)}, u32[]{:S(2)}) %collective-permute-start.4) | collective-permute-done | bytes 98336 | tf_op jit(solution)/shard_map/ppermute | solution.py:286
  16.9 0.2 collective-permute-done.2.refs_3_
  17.0 0.0 collective-permute-done.7.refs_9_
  17.0 0.6 %cross.1 = (bf16[16,256]{1,0:T(8,128)(2,1)S(1)}, bf16[16,256]{1,0:T(8,128)(2,1)S(1)}) custom-call(bf16[32,1536]{1,0:T(8,128)(2,1)S(1)} %get-tuple-element.12.refs_0_, bf16[32,1536]{1,0:T(8,128)(2,1)S(1)} %collective-permute-done.refs_1_, bf16[32,1536]{1,0:T(8,128)(2,1)S(1)} %collective-permute-done.1.refs_2_, ...), custom_call_target="tpu_custom_call" | custom-call | flops 201326592 | bytes 1572864 | tf_op jit(solution)/shard_map/cross/pallas_call | solution.py:235
  17.6 1.1 %collective-permute-start.8 = (bf16[16,256]{1,0:T(8,128)(2,1)S(1)}, bf16[16,256]{1,0:T(8,128)(2,1)S(1)}, u32[]{:S(2)}, u32[]{:S(2)}) collective-permute-start(bf16[16,256]{1,0:T(8,128)(2,1)S(1)} %get-tuple-element.17), channel_id=1, source_target_pairs={{0,2},{1,3},{2,0},{3,1},{4,6},{5,7},{6,4},{7,5},{8,10},{9,11},{10,... | collective-permute-start | bytes 24584 | tf_op jit(solution)/shard_map/ppermute | solution.py:286
  18.7 0.0 copy-done
  18.7 1.1 %table_and_own.1 = (bf16[32,8192]{1,0:T(8,128)(2,1)S(1)}, bf16[256,32]{1,0:T(8,128)(2,1)S(1)}) custom-call(s32[16]{0:T(128)S(1)} %copy-done, bf16[16,256]{1,0:T(8,128)(2,1)S(1)} %get-tuple-element.15.own_ref), custom_call_target="tpu_custom_call" | custom-call | flops 2097152 | bytes 524288 | tf_op jit(solution)/shard_map/table_and_own/pallas_call | solution.py:167
  19.8 1.4 %collective-permute-done.8.got_ref = bf16[16,256]{1,0:T(8,128)(2,1)S(1)} collective-permute-done((bf16[16,256]{1,0:T(8,128)(2,1)S(1)}, bf16[16,256]{1,0:T(8,128)(2,1)S(1)}, u32[]{:S(2)}, u32[]{:S(2)}) %collective-permute-start.8) | collective-permute-done | bytes 8224 | tf_op jit(solution)/shard_map/ppermute | solution.py:286
  21.3 2.6 %synthesis.1 = bf16[256,8192]{1,0:T(8,128)(2,1)} custom-call(bf16[256,32]{1,0:T(8,128)(2,1)S(1)} %get-tuple-element.16.own_ref, bf16[16,256]{1,0:T(8,128)(2,1)S(1)} %collective-permute-done.8.got_ref, bf16[32,8192]{1,0:T(8,128)(2,1)S(1)} %get-tuple-element.18.table_ref), custom_call_target="tpu_custom_call" | custom-call | flops 134217728 | bytes 4718592 | tf_op jit(solution)/shard_map/synthesis/pallas_call | solution.py:269
  (1 shorter events, 0.0 us)
Async XLA Ops:
  2.9 8.5 %collective-permute-start.5 = (bf16[32,1536]{1,0:T(8,128)(2,1)S(1)}, bf16[32,1536]{1,0:T(8,128)(2,1)S(1)}, u32[]{:S(2)}, u32[]{:S(2)}) collective-permute-start(bf16[32,1536]{1,0:T(8,128)(2,1)S(1)} %get-tuple-element.12.refs_0_), channel_id=1, source_target_pairs={{0,4},{1,5},{2,6},{3,7},{4,8},{5,9},{6,10},{7,11},{8,12},{9,13},{1... | collective-permute-start | bytes 294920 | tf_op jit(solution)/shard_map/ppermute | solution.py:294
  6.0 12.7 %copy-start = (s32[16]{0:T(128)S(1)}, s32[16]{0:T(128)}, u32[]{:S(2)}) copy-start(s32[16]{0:T(128)} %m_ref.3) | copy-start | bytes 196
  6.0 11.0 %collective-permute-start.7 = (bf16[128,1536]{1,0:T(8,128)(2,1)S(1)}, bf16[128,1536]{1,0:T(8,128)(2,1)S(1)}, u32[]{:S(2)}, u32[]{:S(2)}) collective-permute-start(bf16[128,1536]{1,0:T(8,128)(2,1)S(1)} %get-tuple-element.14), channel_id=1, source_target_pairs={{0,2},{1,3},{2,0},{3,1},{4,6},{5,7},{6,4},{7,5},{8,10},{9,11},{10,... | collective-permute-start | bytes 1179656 | tf_op jit(solution)/shard_map/ppermute | solution.py:286
  7.5 8.1 %collective-permute-start.3 = (bf16[32,1536]{1,0:T(8,128)(2,1)S(1)}, bf16[32,1536]{1,0:T(8,128)(2,1)S(1)}, u32[]{:S(2)}, u32[]{:S(2)}) collective-permute-start(bf16[32,1536]{1,0:T(8,128)(2,1)S(1)} %get-tuple-element.12.refs_0_), channel_id=1, source_target_pairs={{0,8},{1,9},{2,10},{3,11},{4,12},{5,13},{6,14},{7,15},{8,0},{9,1},... | collective-permute-start | bytes 294920 | tf_op jit(solution)/shard_map/ppermute | solution.py:294
  10.1 5.5 %collective-permute-start.1 = (bf16[32,1536]{1,0:T(8,128)(2,1)S(1)}, bf16[32,1536]{1,0:T(8,128)(2,1)S(1)}, u32[]{:S(2)}, u32[]{:S(2)}) collective-permute-start(bf16[32,1536]{1,0:T(8,128)(2,1)S(1)} %get-tuple-element.12.refs_0_), channel_id=1, source_target_pairs={{0,12},{1,13},{2,14},{3,15},{4,0},{5,1},{6,2},{7,3},{8,4},{9,5},{1... | collective-permute-start | bytes 294920 | tf_op jit(solution)/shard_map/ppermute | solution.py:294
  11.5 4.6 %collective-permute-start = (bf16[32,1536]{1,0:T(8,128)(2,1)S(1)}, bf16[32,1536]{1,0:T(8,128)(2,1)S(1)}, u32[]{:S(2)}, u32[]{:S(2)}) collective-permute-start(bf16[32,1536]{1,0:T(8,128)(2,1)S(1)} %get-tuple-element.12.refs_0_), channel_id=1, source_target_pairs={{0,1},{1,0},{2,3},{3,2},{4,5},{5,4},{6,7},{7,6},{8,9},{9,8},{10,11... | collective-permute-start | bytes 294920 | tf_op jit(solution)/shard_map/ppermute | solution.py:286
  11.5 4.6 %collective-permute-start.6 = (bf16[32,1536]{1,0:T(8,128)(2,1)S(1)}, bf16[32,1536]{1,0:T(8,128)(2,1)S(1)}, u32[]{:S(2)}, u32[]{:S(2)}) collective-permute-start(bf16[32,1536]{1,0:T(8,128)(2,1)S(1)} %relay.1.refs_6_), channel_id=1, source_target_pairs={{0,1},{1,0},{2,3},{3,2},{4,5},{5,4},{6,7},{7,6},{8,9},{9,8},{10,11... | collective-permute-start | bytes 294920 | tf_op jit(solution)/shard_map/ppermute | solution.py:286
  15.6 1.3 %collective-permute-start.4 = (bf16[32,1536]{1,0:T(8,128)(2,1)S(1)}, bf16[32,1536]{1,0:T(8,128)(2,1)S(1)}, u32[]{:S(2)}, u32[]{:S(2)}) collective-permute-start(bf16[32,1536]{1,0:T(8,128)(2,1)S(1)} %collective-permute-done.3.refs_4_), channel_id=1, source_target_pairs={{0,1},{1,0},{2,3},{3,2},{4,5},{5,4},{6,7},{7,6},{8,9},{9,8},{10,11... | collective-permute-start | bytes 294920 | tf_op jit(solution)/shard_map/ppermute | solution.py:286
  15.6 1.5 %collective-permute-start.2 = (bf16[32,1536]{1,0:T(8,128)(2,1)S(1)}, bf16[32,1536]{1,0:T(8,128)(2,1)S(1)}, u32[]{:S(2)}, u32[]{:S(2)}) collective-permute-start(bf16[32,1536]{1,0:T(8,128)(2,1)S(1)} %collective-permute-done.1.refs_2_), channel_id=1, source_target_pairs={{0,1},{1,0},{2,3},{3,2},{4,5},{5,4},{6,7},{7,6},{8,9},{9,8},{10,11... | collective-permute-start | bytes 294920 | tf_op jit(solution)/shard_map/ppermute | solution.py:286
  17.6 3.7 %collective-permute-start.8 = (bf16[16,256]{1,0:T(8,128)(2,1)S(1)}, bf16[16,256]{1,0:T(8,128)(2,1)S(1)}, u32[]{:S(2)}, u32[]{:S(2)}) collective-permute-start(bf16[16,256]{1,0:T(8,128)(2,1)S(1)} %get-tuple-element.17), channel_id=1, source_target_pairs={{0,2},{1,3},{2,0},{3,1},{4,6},{5,7},{6,4},{7,5},{8,10},{9,11},{10,... | collective-permute-start | bytes 24584 | tf_op jit(solution)/shard_map/ppermute | solution.py:286

commit v12 on v11

--- a/solution.py
+++ b/solution.py
@@ -156,28 +156,33 @@
     )(*[pltpu.with_memory_space_constraint(x, pltpu.HBM) for x in operands])
 
 
-def table_kernel(at, line, m_ref, own_ref, table_ref, rows_ref):
+def table_kernel(at, line, order, *refs):
+    shard_refs = dict(zip(order, refs))
+    m_ref, leg_ref, _, table_ref, rows_ref, half_ref = refs[len(order) :]
+    half_ref[...] = half_harmonics(leg_ref[...], shard_refs, at, line)
     write_table(table_ref, m_ref, lax.axis_index("mset"), at, line)
-    rows_ref[...] = map_rows(own_ref, 0, m_ref.shape[0]).astype(BF16)
-
-
-def table_and_own(m_list, own, at, line):
+    rows_ref[...] = map_rows(half_ref, 0, m_ref.shape[0]).astype(BF16)
+
+
+def table_and_own(m_list, legendre, shards, after, at, line):
     n = m_list.shape[0]
-    out_rows = own.shape[0] * REAL
-    return pl.pallas_call(
-        functools.partial(table_kernel, at, line),
+    order = sorted(shards, key=lambda k: -(k >> at) % line)
+    return pl.pallas_call(
+        functools.partial(table_kernel, at, line, order),
         out_shape=[
             jax.ShapeDtypeStruct((2 * n, NPHI), BF16),
-            jax.ShapeDtypeStruct((out_rows, 2 * n), BF16),
+            jax.ShapeDtypeStruct((after.shape[0] * REAL, 2 * n), BF16),
         ],
-        in_specs=[pl.BlockSpec(memory_space=pltpu.SMEM), VMEM],
+        in_specs=[VMEM] * len(order)
+        + [pl.BlockSpec(memory_space=pltpu.SMEM), VMEM, pl.BlockSpec(memory_space=pl.ANY)],
         out_specs=[VMEM] * 2,
-        compiler_params=pltpu.CompilerParams(vmem_limit_bytes=16 << 20),
+        scratch_shapes=[pltpu.VMEM(after.shape, BF16)],
+        compiler_params=pltpu.CompilerParams(vmem_limit_bytes=32 << 20),
         cost_estimate=pl.CostEstimate(
             flops=16 * n * NPHI, bytes_accessed=4 * n * NPHI, transcendentals=0
         ),
         name="table_and_own",
-    )(m_list, own)
+    )(*[shards[k] for k in order], m_list, legendre, after)
 
 
 def relay_kernel(shard_ref, out_ref):
@@ -198,20 +203,18 @@
     )(shard)
 
 
-def cross_kernel(at, line, order, chunk, *refs):
-    shards = len(order)
-    shard_refs = dict(zip(order, refs[:shards]))
-    keep_ref, got_ref, own_ref, back_ref = refs[shards:]
-    half = keep_ref.shape[0]
+def half_harmonics(legendre, shard_refs, at, line):
+    rows = legendre.shape[0]
+    shards = len(shard_refs)
     columns = shard_refs[0].shape[0]
-    cycles = own_ref.shape[0]
+    cycles = rows // shards
+    chunk = min(8, shards)
     wide = chunk * columns
-    legendre = jnp.concatenate([keep_ref[...], got_ref[...]], axis=0)
-    slot = lax.rem(iota((2 * half, wide), 0), shards)
-    local = iota((2 * half, wide), 1) // columns
-    fold = iota((2 * cycles, 2 * half), 0) == iota((2 * cycles, 2 * half), 1) // shards
-    fold = fold.astype(BF16)
+    slot = lax.rem(iota((rows, wide), 0), shards)
+    local = iota((rows, wide), 1) // columns
+    fold = (iota((cycles, rows), 0) == iota((cycles, rows), 1) // shards).astype(BF16)
     me = lax.axis_index("mset")
+    pieces = []
     for q in range(shards // chunk):
         piece = jnp.concatenate(
             [shard_refs[q * chunk + k][...] for k in range(chunk)], axis=0
@@ -221,30 +224,34 @@
         )
         own = slot == shard_source(local + q * chunk, me, at, line)
         chosen = jnp.where(own, product, 0.0).astype(BF16)
-        folded = jnp.dot(fold, chosen, preferred_element_type=F32).astype(BF16)
-        own_ref[:, q * wide : (q + 1) * wide] = folded[:cycles]
-        back_ref[:, q * wide : (q + 1) * wide] = folded[cycles:]
-
-
-def cross(keep, got, shards, at, line):
-    half, order_max = keep.shape
+        pieces.append(jnp.dot(fold, chosen, preferred_element_type=F32).astype(BF16))
+    return jnp.concatenate(pieces, axis=1)
+
+
+def cross_kernel(at, line, order, *refs):
+    shard_refs = dict(zip(order, refs))
+    leg_ref, out_ref = refs[len(order) :]
+    out_ref[...] = half_harmonics(leg_ref[...], shard_refs, at, line)
+
+
+def cross(legendre, shards, at, line):
+    rows, order_max = legendre.shape
     columns = shards[0].shape[0]
     count = len(shards)
     order = sorted(shards, key=lambda k: -(k >> at) % line)
-    shape = jax.ShapeDtypeStruct((half // count, count * columns), BF16)
-    return pl.pallas_call(
-        functools.partial(cross_kernel, at, line, order, min(8, count)),
-        out_shape=[shape, shape],
-        in_specs=[VMEM] * (2 + count),
-        out_specs=[VMEM] * 2,
+    return pl.pallas_call(
+        functools.partial(cross_kernel, at, line, order),
+        out_shape=jax.ShapeDtypeStruct((rows // count, count * columns), BF16),
+        in_specs=[VMEM] * (1 + count),
+        out_specs=VMEM,
         compiler_params=pltpu.CompilerParams(vmem_limit_bytes=32 << 20),
         cost_estimate=pl.CostEstimate(
-            flops=4 * half * order_max * count * columns,
-            bytes_accessed=2 * (2 * keep.size + count * shards[0].size),
+            flops=2 * rows * order_max * count * columns,
+            bytes_accessed=2 * (legendre.size + count * shards[0].size),
             transcendentals=0,
         ),
         name="cross",
-    )(*[shards[k] for k in order], keep, got)
+    )(*[shards[k] for k in order], legendre)
 
 
 def synthesis_kernel(tiles, own_ref, got_ref, table_ref, out_ref, held, sems):
@@ -254,8 +261,13 @@
     copies = []
     for t in range(tiles):
         span = pl.ds(t * width, width)
-        summed = jnp.dot(flat, table_ref[:, span], preferred_element_type=F32)
-        held[:, span] = summed.astype(BF16)
+        for first in range(0, width, 256):
+            columns = pl.ds(t * width + first, min(256, width))
+            piece = table_ref[:, columns]
+            for row in range(0, flat.shape[0], 128):
+                rows = slice(row, row + 128)
+                summed = jnp.dot(flat[rows], piece, preferred_element_type=F32)
+                held[rows, columns] = summed.astype(BF16)
         copy = pltpu.make_async_copy(held.at[:, span], out_ref.at[:, span], sems.at[t])
         copy.start()
         copies.append(copy)
@@ -311,9 +323,9 @@
     )
     shards = gather_shards(filtered, size, at, line)
     got = exchange(send, size, 1 << at)
-    own, back = cross(keep, got, shards, at, line)
+    back = cross(got, shards, at, line)
     other = exchange(back, size, 1 << at)
-    table, own_rows = table_and_own(m_list, own, at, line)
+    table, own_rows = table_and_own(m_list, keep, shards, back, at, line)
     sky_map = synthesize(own_rows, other, table)
     return sky_map.reshape(cycles, REAL, NPHI)
 

time: 24 us -> 24 us (level)
  waiting for transfers between devices: 5.91 us -> 5.59 us
  Pallas kernels: 7.15 us -> 7.45 us
    ppermute x6, waiting for transfers between devices: 2.38 us -> 2.05 us  [exchange(): return lax.ppermute(value, 'mset', [(d, d ^ mask) for d in range(size)])]
    pallas_call x2, Pallas kernels: 1.65 us -> 1.92 us  [the longest x1 1.42 us: table_and_own(): pl.pallas_call(functools.partial(table_kernel, at, line, order), out_shap...]
  transfers between devices with their start and end apart: 9 -> 9, of which waited for: 4 -> 4; matrix products, arithmetic and copies ran while one was open for 0% -> 0% of each run, Pallas kernels for 5% -> 6%
where the time goes in v12:
time: 24 us; the launch traced here: 23.8 us
  starting transfers between devices  10.7 us (45%)
  Pallas kernels  7.45 us (31%)
  waiting for transfers between devices  5.59 us (23%)
    ppermute x3, starting transfers between devices, gather_shards(): shards[turn << at] = lax.ppermute(value, 'mset', pairs)  7.01 us
    ppermute x6, starting transfers between devices, exchange(): return lax.ppermute(value, 'mset', [(d, d ^ mask) for d in range(size)])  3.73 us
    ppermute x3, waiting for transfers between devices, gather_shards(): shards[turn << at] = lax.ppermute(value, 'mset', pairs)  3.53 us
    pallas_call x1, Pallas kernels, prepare(): pl.pallas_call(functools.partial(prepare_kernel, at), out_shape=[jax.Shap...  2.91 us
    pallas_call x1, Pallas kernels, synthesize(): pl.pallas_call(functools.partial(synthesis_kernel, tiles), out_shape=jax....  2.61 us
    ppermute x6, waiting for transfers between devices, exchange(): return lax.ppermute(value, 'mset', [(d, d ^ mask) for d in range(size)])  2.05 us
    pallas_call x1, Pallas kernels, table_and_own(): pl.pallas_call(functools.partial(table_kernel, at, line, order), out_shap...  1.42 us
    pallas_call x1, Pallas kernels, cross(): pl.pallas_call(functools.partial(cross_kernel, at, line, order), out_shap...  0.5 us
  transfers between devices with their start and end apart: 9, of which 4 were waited for; matrix products, arithmetic and copies ran while one was open for 0% of the time, Pallas kernels for 6%

profile of v12, /device:TPU:0, one launch (start us, length us, event | category | flops | bytes accessed | tf_op | source)
XLA Modules:
  0.0 23.8 jit_solution(12954659465054295679)
XLA Ops:
  0.0 2.9 %prepare.1 = (bf16[32,1536]{1,0:T(8,128)(2,1)S(1)}, bf16[128,1536]{1,0:T(8,128)(2,1)S(1)}, bf16[128,1536]{1,0:T(8,128)(2,1)S(1)}) custom-call(s32[16]{0:T(128)} %refs_8_.1, bf16[32,1536]{1,0:T(8,128)(2,1)} %bitcast.6, bf16[1536,1536]{1,0:T(8,128)(2,1)} %bitcast.4, bf16[256,1536]{1,0:T(8,128)(2,1)} %bitcast.5), custom_call_target="tpu_custom_call" | custom-call | flops 352321536 | bytes 5505024 | tf_op jit(solution)/shard_map/prepare/pallas_call | solution.py:133
  2.9 3.1 %collective-permute-start.5 = (bf16[32,1536]{1,0:T(8,128)(2,1)S(1)}, bf16[32,1536]{1,0:T(8,128)(2,1)S(1)}, u32[]{:S(2)}, u32[]{:S(2)}) collective-permute-start(bf16[32,1536]{1,0:T(8,128)(2,1)S(1)} %get-tuple-element.10.refs_0_), channel_id=1, source_target_pairs={{0,4},{1,5},{2,6},{3,7},{4,8},{5,9},{6,10},{7,11},{8,12},{9,13},{1... | collective-permute-start | bytes 294920 | tf_op jit(solution)/shard_map/ppermute | solution.py:306
  6.0 0.0 copy-start
  6.0 1.5 %collective-permute-start.7 = (bf16[128,1536]{1,0:T(8,128)(2,1)S(1)}, bf16[128,1536]{1,0:T(8,128)(2,1)S(1)}, u32[]{:S(2)}, u32[]{:S(2)}) collective-permute-start(bf16[128,1536]{1,0:T(8,128)(2,1)S(1)} %get-tuple-element.12), channel_id=1, source_target_pairs={{0,2},{1,3},{2,0},{3,1},{4,6},{5,7},{6,4},{7,5},{8,10},{9,11},{10,... | collective-permute-start | bytes 1179656 | tf_op jit(solution)/shard_map/ppermute | solution.py:298
  7.5 2.6 %collective-permute-start.3 = (bf16[32,1536]{1,0:T(8,128)(2,1)S(1)}, bf16[32,1536]{1,0:T(8,128)(2,1)S(1)}, u32[]{:S(2)}, u32[]{:S(2)}) collective-permute-start(bf16[32,1536]{1,0:T(8,128)(2,1)S(1)} %get-tuple-element.10.refs_0_), channel_id=1, source_target_pairs={{0,8},{1,9},{2,10},{3,11},{4,12},{5,13},{6,14},{7,15},{8,0},{9,1},... | collective-permute-start | bytes 294920 | tf_op jit(solution)/shard_map/ppermute | solution.py:306
  10.1 1.3 %collective-permute-start.1 = (bf16[32,1536]{1,0:T(8,128)(2,1)S(1)}, bf16[32,1536]{1,0:T(8,128)(2,1)S(1)}, u32[]{:S(2)}, u32[]{:S(2)}) collective-permute-start(bf16[32,1536]{1,0:T(8,128)(2,1)S(1)} %get-tuple-element.10.refs_0_), channel_id=1, source_target_pairs={{0,12},{1,13},{2,14},{3,15},{4,0},{5,1},{6,2},{7,3},{8,4},{9,5},{1... | collective-permute-start | bytes 294920 | tf_op jit(solution)/shard_map/ppermute | solution.py:306
  11.5 0.0 collective-permute-start
  11.5 0.0 collective-permute-done.5.shard_ref
  11.5 0.6 %collective-permute-start.6 = (bf16[32,1536]{1,0:T(8,128)(2,1)S(1)}, bf16[32,1536]{1,0:T(8,128)(2,1)S(1)}, u32[]{:S(2)}, u32[]{:S(2)}) collective-permute-start(bf16[32,1536]{1,0:T(8,128)(2,1)S(1)} %relay.1.refs_6_), channel_id=1, source_target_pairs={{0,1},{1,0},{2,3},{3,2},{4,5},{5,4},{6,7},{7,6},{8,9},{9,8},{10,11... | collective-permute-start | bytes 294920 | tf_op jit(solution)/shard_map/ppermute | solution.py:298
  12.0 3.5 %collective-permute-done.3.refs_4_ = bf16[32,1536]{1,0:T(8,128)(2,1)S(1)} collective-permute-done((bf16[32,1536]{1,0:T(8,128)(2,1)S(1)}, bf16[32,1536]{1,0:T(8,128)(2,1)S(1)}, u32[]{:S(2)}, u32[]{:S(2)}) %collective-permute-start.3) | collective-permute-done | bytes 98336 | tf_op jit(solution)/shard_map/ppermute | solution.py:306
  15.6 0.0 collective-permute-start.4
  15.6 0.0 collective-permute-done.1.refs_2_
  15.6 0.5 %collective-permute-start.2 = (bf16[32,1536]{1,0:T(8,128)(2,1)S(1)}, bf16[32,1536]{1,0:T(8,128)(2,1)S(1)}, u32[]{:S(2)}, u32[]{:S(2)}) collective-permute-start(bf16[32,1536]{1,0:T(8,128)(2,1)S(1)} %collective-permute-done.1.refs_2_), channel_id=1, source_target_pairs={{0,1},{1,0},{2,3},{3,2},{4,5},{5,4},{6,7},{7,6},{8,9},{9,8},{10,11... | collective-permute-start | bytes 294920 | tf_op jit(solution)/shard_map/ppermute | solution.py:298
  16.1 0.0 collective-permute-done.refs_1_
  16.1 0.0 collective-permute-done.6.refs_7_
  16.1 0.8 %collective-permute-done.4.refs_5_ = bf16[32,1536]{1,0:T(8,128)(2,1)S(1)} collective-permute-done((bf16[32,1536]{1,0:T(8,128)(2,1)S(1)}, bf16[32,1536]{1,0:T(8,128)(2,1)S(1)}, u32[]{:S(2)}, u32[]{:S(2)}) %collective-permute-start.4) | collective-permute-done | bytes 98336 | tf_op jit(solution)/shard_map/ppermute | solution.py:298
  16.9 0.2 collective-permute-done.2.refs_3_
  17.0 0.0 collective-permute-done.7.refs_8_
  17.0 0.5 %cross.1.refs_10_ = bf16[16,256]{1,0:T(8,128)(2,1)S(1)} custom-call(bf16[32,1536]{1,0:T(8,128)(2,1)S(1)} %get-tuple-element.10.refs_0_, bf16[32,1536]{1,0:T(8,128)(2,1)S(1)} %collective-permute-done.refs_1_, bf16[32,1536]{1,0:T(8,128)(2,1)S(1)} %collective-permute-done.1.refs_2_, bf16[32,1536]{1,0:T(8,128)(2,1)S(1)} %collective-permute-done.2.refs_3_, ...), custom_call_target="tpu_custom_call" | custom-call | flops 100663296 | bytes 1179648 | tf_op jit(solution)/shard_map/cross/pallas_call | solution.py:242
  17.5 1.1 %collective-permute-start.8 = (bf16[16,256]{1,0:T(8,128)(2,1)S(1)}, bf16[16,256]{1,0:T(8,128)(2,1)S(1)}, u32[]{:S(2)}, u32[]{:S(2)}) collective-permute-start(bf16[16,256]{1,0:T(8,128)(2,1)S(1)} %cross.1.refs_10_), channel_id=1, source_target_pairs={{0,2},{1,3},{2,0},{3,1},{4,6},{5,7},{6,4},{7,5},{8,10},{9,11},{10,... | collective-permute-start | bytes 24584 | tf_op jit(solution)/shard_map/ppermute | solution.py:298
  18.7 0.0 copy-done
  18.7 1.4 %table_and_own.1 = (bf16[32,8192]{1,0:T(8,128)(2,1)S(1)}, bf16[256,32]{1,0:T(8,128)(2,1)S(1)}) custom-call(bf16[32,1536]{1,0:T(8,128)(2,1)S(1)} %get-tuple-element.10.refs_0_, bf16[32,1536]{1,0:T(8,128)(2,1)S(1)} %collective-permute-done.refs_1_, bf16[32,1536]{1,0:T(8,128)(2,1)S(1)} %collective-permute-done.1.refs_2_, ...), custom_call_target="tpu_custom_call" | custom-call | flops 2097152 | bytes 524288 | tf_op jit(solution)/shard_map/table_and_own/pallas_call | solution.py:170
  20.1 1.1 %collective-permute-done.8.got_ref = bf16[16,256]{1,0:T(8,128)(2,1)S(1)} collective-permute-done((bf16[16,256]{1,0:T(8,128)(2,1)S(1)}, bf16[16,256]{1,0:T(8,128)(2,1)S(1)}, u32[]{:S(2)}, u32[]{:S(2)}) %collective-permute-start.8) | collective-permute-done | bytes 8224 | tf_op jit(solution)/shard_map/ppermute | solution.py:298
  21.2 2.6 %synthesis.1 = bf16[256,8192]{1,0:T(8,128)(2,1)} custom-call(bf16[256,32]{1,0:T(8,128)(2,1)S(1)} %get-tuple-element.13.own_ref, bf16[16,256]{1,0:T(8,128)(2,1)S(1)} %collective-permute-done.8.got_ref, bf16[32,8192]{1,0:T(8,128)(2,1)S(1)} %get-tuple-element.14.table_ref), custom_call_target="tpu_custom_call" | custom-call | flops 134217728 | bytes 4718592 | tf_op jit(solution)/shard_map/synthesis/pallas_call | solution.py:281
  (1 shorter events, 0.0 us)
Async XLA Ops:
  2.9 8.5 %collective-permute-start.5 = (bf16[32,1536]{1,0:T(8,128)(2,1)S(1)}, bf16[32,1536]{1,0:T(8,128)(2,1)S(1)}, u32[]{:S(2)}, u32[]{:S(2)}) collective-permute-start(bf16[32,1536]{1,0:T(8,128)(2,1)S(1)} %get-tuple-element.10.refs_0_), channel_id=1, source_target_pairs={{0,4},{1,5},{2,6},{3,7},{4,8},{5,9},{6,10},{7,11},{8,12},{9,13},{1... | collective-permute-start | bytes 294920 | tf_op jit(solution)/shard_map/ppermute | solution.py:306
  6.0 12.7 %copy-start = (s32[16]{0:T(128)S(1)}, s32[16]{0:T(128)}, u32[]{:S(2)}) copy-start(s32[16]{0:T(128)} %refs_8_.1) | copy-start | bytes 196
  6.0 11.0 %collective-permute-start.7 = (bf16[128,1536]{1,0:T(8,128)(2,1)S(1)}, bf16[128,1536]{1,0:T(8,128)(2,1)S(1)}, u32[]{:S(2)}, u32[]{:S(2)}) collective-permute-start(bf16[128,1536]{1,0:T(8,128)(2,1)S(1)} %get-tuple-element.12), channel_id=1, source_target_pairs={{0,2},{1,3},{2,0},{3,1},{4,6},{5,7},{6,4},{7,5},{8,10},{9,11},{10,... | collective-permute-start | bytes 1179656 | tf_op jit(solution)/shard_map/ppermute | solution.py:298
  7.5 8.1 %collective-permute-start.3 = (bf16[32,1536]{1,0:T(8,128)(2,1)S(1)}, bf16[32,1536]{1,0:T(8,128)(2,1)S(1)}, u32[]{:S(2)}, u32[]{:S(2)}) collective-permute-start(bf16[32,1536]{1,0:T(8,128)(2,1)S(1)} %get-tuple-element.10.refs_0_), channel_id=1, source_target_pairs={{0,8},{1,9},{2,10},{3,11},{4,12},{5,13},{6,14},{7,15},{8,0},{9,1},... | collective-permute-start | bytes 294920 | tf_op jit(solution)/shard_map/ppermute | solution.py:306
  10.1 5.5 %collective-permute-start.1 = (bf16[32,1536]{1,0:T(8,128)(2,1)S(1)}, bf16[32,1536]{1,0:T(8,128)(2,1)S(1)}, u32[]{:S(2)}, u32[]{:S(2)}) collective-permute-start(bf16[32,1536]{1,0:T(8,128)(2,1)S(1)} %get-tuple-element.10.refs_0_), channel_id=1, source_target_pairs={{0,12},{1,13},{2,14},{3,15},{4,0},{5,1},{6,2},{7,3},{8,4},{9,5},{1... | collective-permute-start | bytes 294920 | tf_op jit(solution)/shard_map/ppermute | solution.py:306
  11.5 4.6 %collective-permute-start = (bf16[32,1536]{1,0:T(8,128)(2,1)S(1)}, bf16[32,1536]{1,0:T(8,128)(2,1)S(1)}, u32[]{:S(2)}, u32[]{:S(2)}) collective-permute-start(bf16[32,1536]{1,0:T(8,128)(2,1)S(1)} %get-tuple-element.10.refs_0_), channel_id=1, source_target_pairs={{0,1},{1,0},{2,3},{3,2},{4,5},{5,4},{6,7},{7,6},{8,9},{9,8},{10,11... | collective-permute-start | bytes 294920 | tf_op jit(solution)/shard_map/ppermute | solution.py:298
  11.5 4.6 %collective-permute-start.6 = (bf16[32,1536]{1,0:T(8,128)(2,1)S(1)}, bf16[32,1536]{1,0:T(8,128)(2,1)S(1)}, u32[]{:S(2)}, u32[]{:S(2)}) collective-permute-start(bf16[32,1536]{1,0:T(8,128)(2,1)S(1)} %relay.1.refs_6_), channel_id=1, source_target_pairs={{0,1},{1,0},{2,3},{3,2},{4,5},{5,4},{6,7},{7,6},{8,9},{9,8},{10,11... | collective-permute-start | bytes 294920 | tf_op jit(solution)/shard_map/ppermute | solution.py:298
  15.6 1.3 %collective-permute-start.4 = (bf16[32,1536]{1,0:T(8,128)(2,1)S(1)}, bf16[32,1536]{1,0:T(8,128)(2,1)S(1)}, u32[]{:S(2)}, u32[]{:S(2)}) collective-permute-start(bf16[32,1536]{1,0:T(8,128)(2,1)S(1)} %collective-permute-done.3.refs_4_), channel_id=1, source_target_pairs={{0,1},{1,0},{2,3},{3,2},{4,5},{5,4},{6,7},{7,6},{8,9},{9,8},{10,11... | collective-permute-start | bytes 294920 | tf_op jit(solution)/shard_map/ppermute | solution.py:298
  15.6 1.5 %collective-permute-start.2 = (bf16[32,1536]{1,0:T(8,128)(2,1)S(1)}, bf16[32,1536]{1,0:T(8,128)(2,1)S(1)}, u32[]{:S(2)}, u32[]{:S(2)}) collective-permute-start(bf16[32,1536]{1,0:T(8,128)(2,1)S(1)} %collective-permute-done.1.refs_2_), channel_id=1, source_target_pairs={{0,1},{1,0},{2,3},{3,2},{4,5},{5,4},{6,7},{7,6},{8,9},{9,8},{10,11... | collective-permute-start | bytes 294920 | tf_op jit(solution)/shard_map/ppermute | solution.py:298
  17.5 3.7 %collective-permute-start.8 = (bf16[16,256]{1,0:T(8,128)(2,1)S(1)}, bf16[16,256]{1,0:T(8,128)(2,1)S(1)}, u32[]{:S(2)}, u32[]{:S(2)}) collective-permute-start(bf16[16,256]{1,0:T(8,128)(2,1)S(1)} %cross.1.refs_10_), channel_id=1, source_target_pairs={{0,2},{1,3},{2,0},{3,1},{4,6},{5,7},{6,4},{7,5},{8,10},{9,11},{10,... | collective-permute-start | bytes 24584 | tf_op jit(solution)/shard_map/ppermute | solution.py:298

commit v13 on v12

--- a/solution.py
+++ b/solution.py
@@ -74,86 +74,104 @@
     return jnp.dot(chosen, pick.astype(BF16), preferred_element_type=F32)
 
 
-def prepare_kernel(
-    at, m_ref, coeff_ref, block_ref, leg_ref, filtered_ref, keep_ref, send_ref,
-    m_smem, coeff_vmem, block_vmem, leg_vmem, sems,
-):
-    me = lax.axis_index("mset")
-    columns, order_max = coeff_ref.shape
+def filter_kernel(m_ref, coeff_ref, block_ref, out_ref, m_smem, coeff_vmem, block_vmem, total, sems):
+    order_max = coeff_ref.shape[1]
     pieces = block_vmem.shape[0]
     depth = order_max // pieces
+    first = min(2, pieces)
     copy_m = pltpu.make_async_copy(m_ref, m_smem, sems.at[0])
-    copy_leg = pltpu.make_async_copy(leg_ref, leg_vmem, sems.at[1])
-    copy_coeff = pltpu.make_async_copy(coeff_ref, coeff_vmem, sems.at[2])
+    copy_coeff = pltpu.make_async_copy(coeff_ref, coeff_vmem, sems.at[1])
     copy_blocks = [
         pltpu.make_async_copy(
-            block_ref.at[pl.ds(p * depth, depth), :], block_vmem.at[p], sems.at[3 + p]
+            block_ref.at[pl.ds(p * depth, depth), :], block_vmem.at[p], sems.at[2 + p]
         )
         for p in range(pieces)
     ]
-    for copy in [copy_m, copy_leg, copy_coeff] + copy_blocks:
+    for copy in [copy_m, copy_coeff] + copy_blocks[:first]:
         copy.start()
-
+    copy_m.wait()
+    order = LL - m_smem[lax.axis_index("mset")]
+    for p in range(first, pieces):
+        pl.when(p * depth < order)(copy_blocks[p].start)
+
+    def masked(p):
+        span = slice(p * depth, (p + 1) * depth)
+        coeff = coeff_vmem[:, span]
+        place = iota(coeff.shape, 1) + p * depth
+        return jnp.where(place < order, coeff, jnp.zeros_like(coeff))
+
+    copy_coeff.wait()
+    value = None
+    for p in range(first):
+        copy_blocks[p].wait()
+        term = jnp.dot(masked(p), block_vmem[p], preferred_element_type=F32)
+        value = term if value is None else value + term
+    total[...] = value
+
+    def add(p):
+        copy_blocks[p].wait()
+        total[...] += jnp.dot(masked(p), block_vmem[p], preferred_element_type=F32)
+
+    for p in range(first, pieces):
+        pl.when(p * depth < order)(functools.partial(add, p))
+    out_ref[...] = jnp.where(iota(total.shape, 1) < order, total[...], 0.0).astype(BF16)
+
+
+def filter_block(m_list, coeff, block):
+    columns, order_max = coeff.shape
+    pieces = 6
+    operands = (m_list, coeff, block)
+    return pl.pallas_call(
+        filter_kernel,
+        out_shape=jax.ShapeDtypeStruct((columns, order_max), BF16),
+        in_specs=[HBM] * 3,
+        out_specs=VMEM,
+        scratch_shapes=[
+            pltpu.SMEM(m_list.shape, jnp.int32),
+            pltpu.VMEM((columns, order_max), BF16),
+            pltpu.VMEM((pieces, order_max // pieces, order_max), BF16),
+            pltpu.VMEM((columns, order_max), F32),
+            pltpu.SemaphoreType.DMA((2 + pieces,)),
+        ],
+        compiler_params=pltpu.CompilerParams(vmem_limit_bytes=16 << 20),
+        cost_estimate=pl.CostEstimate(
+            flops=2 * coeff.size * order_max, bytes_accessed=2 * block.size, transcendentals=0
+        ),
+        name="filter_block",
+    )(*[pltpu.with_memory_space_constraint(x, pltpu.HBM) for x in operands])
+
+
+def sort_kernel(at, n, leg_ref, _, keep_ref, send_ref):
     rows = leg_ref.shape[0]
-    n = m_ref.shape[0]
     half = rows // 2
-    own_bit = (me >> at) & 1
+    own_bit = (lax.axis_index("mset") >> at) & 1
     row, col = iota((rows, rows), 0), iota((rows, rows), 1)
     bit = own_bit ^ (row // half)
     slot = lax.rem(row, n // 2)
     pick = (lax.rem(row, half) // (n // 2) == col // n) & (
         insert_bit(slot, bit, at) == lax.rem(col, n)
     )
-    pick = pick.astype(BF16)
-    copy_leg.wait()
-    ordered = jnp.dot(pick, leg_vmem[...], preferred_element_type=F32).astype(BF16)
+    ordered = jnp.dot(pick.astype(BF16), leg_ref[...], preferred_element_type=F32).astype(BF16)
     keep_ref[...] = ordered[:half]
     send_ref[...] = ordered[half:]
 
-    copy_m.wait()
-    order = LL - m_smem[me]
-    copy_coeff.wait()
-    coeff = coeff_vmem[...]
-    coeff = jnp.where(iota(coeff.shape, 1) < order, coeff, jnp.zeros_like(coeff))
-    total = jnp.zeros((columns, order_max), F32)
-    for p in range(pieces):
-        copy_blocks[p].wait()
-        total += jnp.dot(
-            coeff[:, p * depth : (p + 1) * depth], block_vmem[p], preferred_element_type=F32
-        )
-    filtered_ref[...] = jnp.where(iota(total.shape, 1) < order, total, 0.0).astype(BF16)
-
-
-def prepare(m_list, coeff, block, legendre, at):
-    columns, order_max = coeff.shape
-    rows = legendre.shape[0]
-    n = m_list.shape[0]
-    pieces = 6
-    operands = (m_list, coeff, block, legendre)
-    return pl.pallas_call(
-        functools.partial(prepare_kernel, at),
-        out_shape=[
-            jax.ShapeDtypeStruct((columns, order_max), BF16),
-            jax.ShapeDtypeStruct((rows // 2, order_max), BF16),
-            jax.ShapeDtypeStruct((rows // 2, order_max), BF16),
-        ],
-        in_specs=[HBM] * 4,
-        out_specs=[VMEM] * 3,
-        scratch_shapes=[
-            pltpu.SMEM((n,), jnp.int32),
-            pltpu.VMEM((columns, order_max), BF16),
-            pltpu.VMEM((pieces, order_max // pieces, order_max), BF16),
-            pltpu.VMEM((rows, order_max), BF16),
-            pltpu.SemaphoreType.DMA((3 + pieces,)),
-        ],
+
+def sort_legendre(legendre, after, n, at):
+    rows, order_max = legendre.shape
+    half = jax.ShapeDtypeStruct((rows // 2, order_max), BF16)
+    return pl.pallas_call(
+        functools.partial(sort_kernel, at, n),
+        out_shape=[half, half],
+        in_specs=[VMEM, pl.BlockSpec(memory_space=pl.ANY)],
+        out_specs=[VMEM] * 2,
         compiler_params=pltpu.CompilerParams(vmem_limit_bytes=32 << 20),
         cost_estimate=pl.CostEstimate(
-            flops=2 * (columns * order_max * order_max + rows * rows * order_max),
-            bytes_accessed=2 * (block.size + legendre.size),
+            flops=2 * rows * rows * order_max,
+            bytes_accessed=4 * legendre.size,
             transcendentals=0,
         ),
-        name="prepare",
-    )(*[pltpu.with_memory_space_constraint(x, pltpu.HBM) for x in operands])
+        name="sort_legendre",
+    )(legendre, after)
 
 
 def table_kernel(at, line, order, *refs):
@@ -318,9 +336,8 @@
     cycles, n, _ = legendre.shape
     at = min(1, size.bit_length() - 2)
     line = size >> (at + 1)
-    filtered, keep, send = prepare(
-        m_list, coeff[0], blocks[0], legendre.reshape(cycles * n, order_max), at
-    )
+    filtered = filter_block(m_list, coeff[0], blocks[0])
+    keep, send = sort_legendre(legendre.reshape(cycles * n, order_max), filtered, n, at)
     shards = gather_shards(filtered, size, at, line)
     got = exchange(send, size, 1 << at)
     back = cross(got, shards, at, line)

time: 24 us -> 24.5 us (1.021)
  starting transfers between devices: 10.7 us -> 11.3 us
  Pallas kernels: 7.45 us -> 6.86 us
  waiting for transfers between devices: 5.59 us -> 6.08 us
    pallas_call x1 -> x2, Pallas kernels: 2.91 us -> 2.33 us  [the longest x1 1.95 us: filter_block(): pl.pallas_call(filter_kernel, out_shape=jax.ShapeDtypeStruct((columns, or...]
    ppermute x6, starting transfers between devices: 3.73 us -> 4.3 us  [exchange(): return lax.ppermute(value, 'mset', [(d, d ^ mask) for d in range(size)])]
    ppermute x6, waiting for transfers between devices: 2.05 us -> 2.49 us  [exchange(): return lax.ppermute(value, 'mset', [(d, d ^ mask) for d in range(size)])]
  transfers between devices with their start and end apart: 9 -> 9, of which waited for: 4 -> 4; matrix products, arithmetic and copies ran while one was open for 0% -> 0% of each run, Pallas kernels for 6% -> 7%
where the time goes in v13:
time: 24.5 us; the launch traced here: 24.3 us
  starting transfers between devices  11.3 us (46%)
  Pallas kernels  6.86 us (28%)
  waiting for transfers between devices  6.08 us (25%)
    ppermute x3, starting transfers between devices, gather_shards(): shards[turn << at] = lax.ppermute(value, 'mset', pairs)  7.01 us
    ppermute x6, starting transfers between devices, exchange(): return lax.ppermute(value, 'mset', [(d, d ^ mask) for d in range(size)])  4.3 us
    ppermute x3, waiting for transfers between devices, gather_shards(): shards[turn << at] = lax.ppermute(value, 'mset', pairs)  3.59 us
    pallas_call x1, Pallas kernels, synthesize(): pl.pallas_call(functools.partial(synthesis_kernel, tiles), out_shape=jax....  2.61 us
    ppermute x6, waiting for transfers between devices, exchange(): return lax.ppermute(value, 'mset', [(d, d ^ mask) for d in range(size)])  2.49 us
    pallas_call x1, Pallas kernels, filter_block(): pl.pallas_call(filter_kernel, out_shape=jax.ShapeDtypeStruct((columns, or...  1.95 us
    pallas_call x1, Pallas kernels, table_and_own(): pl.pallas_call(functools.partial(table_kernel, at, line, order), out_shap...  1.42 us
    pallas_call x1, Pallas kernels, cross(): pl.pallas_call(functools.partial(cross_kernel, at, line, order), out_shap...  0.5 us
  transfers between devices with their start and end apart: 9, of which 4 were waited for; matrix products, arithmetic and copies ran while one was open for 0% of the time, Pallas kernels for 7%

profile of v13, /device:TPU:0, one launch (start us, length us, event | category | flops | bytes accessed | tf_op | source)
XLA Modules:
  0.0 24.3 jit_solution(10045100400417552642)
XLA Ops:
  0.0 0.0 copy-start
  0.0 1.9 %filter_block.1._.refs_0_ = bf16[32,1536]{1,0:T(8,128)(2,1)S(1)} custom-call(s32[16]{0:T(128)} %refs_8_.1, bf16[32,1536]{1,0:T(8,128)(2,1)} %bitcast.6, bf16[1536,1536]{1,0:T(8,128)(2,1)} %bitcast.5), custom_call_target="tpu_custom_call" | custom-call | flops 150994944 | bytes 4718592 | tf_op jit(solution)/shard_map/filter_block/pallas_call | solution.py:124
  2.0 3.1 %collective-permute-start.5 = (bf16[32,1536]{1,0:T(8,128)(2,1)S(1)}, bf16[32,1536]{1,0:T(8,128)(2,1)S(1)}, u32[]{:S(2)}, u32[]{:S(2)}) collective-permute-start(bf16[32,1536]{1,0:T(8,128)(2,1)S(1)} %filter_block.1._.refs_0_), channel_id=1, source_target_pairs={{0,4},{1,5},{2,6},{3,7},{4,8},{5,9},{6,10},{7,11},{8,12},{9,13},{1... | collective-permute-start | bytes 294920 | tf_op jit(solution)/shard_map/ppermute | solution.py:324
  5.0 0.0 copy-done
  5.0 0.4 %sort_legendre.1 = (bf16[128,1536]{1,0:T(8,128)(2,1)S(1)}, bf16[128,1536]{1,0:T(8,128)(2,1)S(1)}) custom-call(bf16[256,1536]{1,0:T(8,128)(2,1)S(1)} %bitcast.4, bf16[32,1536]{1,0:T(8,128)(2,1)S(1)} %filter_block.1._.refs_0_), custom_call_target="tpu_custom_call" | custom-call | flops 201326592 | bytes 1572864 | tf_op jit(solution)/shard_map/sort_legendre/pallas_call | solution.py:162
  5.4 0.0 copy-start.1
  5.4 2.5 %collective-permute-start.7 = (bf16[128,1536]{1,0:T(8,128)(2,1)S(1)}, bf16[128,1536]{1,0:T(8,128)(2,1)S(1)}, u32[]{:S(2)}, u32[]{:S(2)}) collective-permute-start(bf16[128,1536]{1,0:T(8,128)(2,1)S(1)} %get-tuple-element.10), channel_id=1, source_target_pairs={{0,2},{1,3},{2,0},{3,1},{4,6},{5,7},{6,4},{7,5},{8,10},{9,11},{10,... | collective-permute-start | bytes 1179656 | tf_op jit(solution)/shard_map/ppermute | solution.py:316
  8.0 2.8 %collective-permute-start.3 = (bf16[32,1536]{1,0:T(8,128)(2,1)S(1)}, bf16[32,1536]{1,0:T(8,128)(2,1)S(1)}, u32[]{:S(2)}, u32[]{:S(2)}) collective-permute-start(bf16[32,1536]{1,0:T(8,128)(2,1)S(1)} %filter_block.1._.refs_0_), channel_id=1, source_target_pairs={{0,8},{1,9},{2,10},{3,11},{4,12},{5,13},{6,14},{7,15},{8,0},{9,1},... | collective-permute-start | bytes 294920 | tf_op jit(solution)/shard_map/ppermute | solution.py:324
  10.8 1.1 %collective-permute-start.1 = (bf16[32,1536]{1,0:T(8,128)(2,1)S(1)}, bf16[32,1536]{1,0:T(8,128)(2,1)S(1)}, u32[]{:S(2)}, u32[]{:S(2)}) collective-permute-start(bf16[32,1536]{1,0:T(8,128)(2,1)S(1)} %filter_block.1._.refs_0_), channel_id=1, source_target_pairs={{0,12},{1,13},{2,14},{3,15},{4,0},{5,1},{6,2},{7,3},{8,4},{9,5},{1... | collective-permute-start | bytes 294920 | tf_op jit(solution)/shard_map/ppermute | solution.py:324
  11.9 0.0 collective-permute-start
  11.9 0.0 collective-permute-done.5.shard_ref
  11.9 0.6 %collective-permute-start.6 = (bf16[32,1536]{1,0:T(8,128)(2,1)S(1)}, bf16[32,1536]{1,0:T(8,128)(2,1)S(1)}, u32[]{:S(2)}, u32[]{:S(2)}) collective-permute-start(bf16[32,1536]{1,0:T(8,128)(2,1)S(1)} %relay.1.refs_6_), channel_id=1, source_target_pairs={{0,1},{1,0},{2,3},{3,2},{4,5},{5,4},{6,7},{7,6},{8,9},{9,8},{10,11... | collective-permute-start | bytes 294920 | tf_op jit(solution)/shard_map/ppermute | solution.py:316
  12.5 3.6 %collective-permute-done.3.refs_4_ = bf16[32,1536]{1,0:T(8,128)(2,1)S(1)} collective-permute-done((bf16[32,1536]{1,0:T(8,128)(2,1)S(1)}, bf16[32,1536]{1,0:T(8,128)(2,1)S(1)}, u32[]{:S(2)}, u32[]{:S(2)}) %collective-permute-start.3) | collective-permute-done | bytes 98336 | tf_op jit(solution)/shard_map/ppermute | solution.py:324
  16.1 0.0 collective-permute-start.4
  16.1 0.0 collective-permute-done.1.refs_2_
  16.1 0.5 %collective-permute-start.2 = (bf16[32,1536]{1,0:T(8,128)(2,1)S(1)}, bf16[32,1536]{1,0:T(8,128)(2,1)S(1)}, u32[]{:S(2)}, u32[]{:S(2)}) collective-permute-start(bf16[32,1536]{1,0:T(8,128)(2,1)S(1)} %collective-permute-done.1.refs_2_), channel_id=1, source_target_pairs={{0,1},{1,0},{2,3},{3,2},{4,5},{5,4},{6,7},{7,6},{8,9},{9,8},{10,11... | collective-permute-start | bytes 294920 | tf_op jit(solution)/shard_map/ppermute | solution.py:316
  16.6 0.0 collective-permute-done.refs_1_
  16.6 0.0 collective-permute-done.6.refs_7_
  16.6 0.8 %collective-permute-done.4.refs_5_ = bf16[32,1536]{1,0:T(8,128)(2,1)S(1)} collective-permute-done((bf16[32,1536]{1,0:T(8,128)(2,1)S(1)}, bf16[32,1536]{1,0:T(8,128)(2,1)S(1)}, u32[]{:S(2)}, u32[]{:S(2)}) %collective-permute-start.4) | collective-permute-done | bytes 98336 | tf_op jit(solution)/shard_map/ppermute | solution.py:316
  17.4 0.2 collective-permute-done.2.refs_3_
  17.5 0.0 collective-permute-done.7.refs_8_
  17.5 0.5 %cross.1.refs_10_ = bf16[16,256]{1,0:T(8,128)(2,1)S(1)} custom-call(bf16[32,1536]{1,0:T(8,128)(2,1)S(1)} %filter_block.1._.refs_0_, bf16[32,1536]{1,0:T(8,128)(2,1)S(1)} %collective-permute-done.refs_1_, bf16[32,1536]{1,0:T(8,128)(2,1)S(1)} %collective-permute-done.1.refs_2_, bf16[32,1536]{1,0:T(8,128)(2,1)S(1)} %collective-permute-done.2.refs_3_, ...), custom_call_target="tpu_custom_call" | custom-call | flops 100663296 | bytes 1179648 | tf_op jit(solution)/shard_map/cross/pallas_call | solution.py:260
  18.0 0.7 %collective-permute-start.8 = (bf16[16,256]{1,0:T(8,128)(2,1)S(1)}, bf16[16,256]{1,0:T(8,128)(2,1)S(1)}, u32[]{:S(2)}, u32[]{:S(2)}) collective-permute-start(bf16[16,256]{1,0:T(8,128)(2,1)S(1)} %cross.1.refs_10_), channel_id=1, source_target_pairs={{0,2},{1,3},{2,0},{3,1},{4,6},{5,7},{6,4},{7,5},{8,10},{9,11},{10,... | collective-permute-start | bytes 24584 | tf_op jit(solution)/shard_map/ppermute | solution.py:316
  18.7 0.0 copy-done.1
  18.7 1.4 %table_and_own.1 = (bf16[32,8192]{1,0:T(8,128)(2,1)S(1)}, bf16[256,32]{1,0:T(8,128)(2,1)S(1)}) custom-call(bf16[32,1536]{1,0:T(8,128)(2,1)S(1)} %filter_block.1._.refs_0_, bf16[32,1536]{1,0:T(8,128)(2,1)S(1)} %collective-permute-done.refs_1_, bf16[32,1536]{1,0:T(8,128)(2,1)S(1)} %collective-permute-done.1.refs_2_, ...), custom_call_target="tpu_custom_call" | custom-call | flops 2097152 | bytes 524288 | tf_op jit(solution)/shard_map/table_and_own/pallas_call | solution.py:188
  20.2 1.5 %collective-permute-done.8.got_ref = bf16[16,256]{1,0:T(8,128)(2,1)S(1)} collective-permute-done((bf16[16,256]{1,0:T(8,128)(2,1)S(1)}, bf16[16,256]{1,0:T(8,128)(2,1)S(1)}, u32[]{:S(2)}, u32[]{:S(2)}) %collective-permute-start.8) | collective-permute-done | bytes 8224 | tf_op jit(solution)/shard_map/ppermute | solution.py:316
  21.7 2.6 %synthesis.1 = bf16[256,8192]{1,0:T(8,128)(2,1)} custom-call(bf16[256,32]{1,0:T(8,128)(2,1)S(1)} %get-tuple-element.11.own_ref, bf16[16,256]{1,0:T(8,128)(2,1)S(1)} %collective-permute-done.8.got_ref, bf16[32,8192]{1,0:T(8,128)(2,1)S(1)} %get-tuple-element.12.table_ref), custom_call_target="tpu_custom_call" | custom-call | flops 134217728 | bytes 4718592 | tf_op jit(solution)/shard_map/synthesis/pallas_call | solution.py:299
  (1 shorter events, 0.0 us)
Async XLA Ops:
  0.0 5.0 %copy-start = (bf16[16,16,1536]{2,1,0:T(8,128)(2,1)S(1)}, bf16[16,16,1536]{2,1,0:T(8,128)(2,1)}, u32[]{:S(2)}) copy-start(bf16[16,16,1536]{2,1,0:T(8,128)(2,1)} %param.7) | copy-start | bytes 2359300
  2.0 9.9 %collective-permute-start.5 = (bf16[32,1536]{1,0:T(8,128)(2,1)S(1)}, bf16[32,1536]{1,0:T(8,128)(2,1)S(1)}, u32[]{:S(2)}, u32[]{:S(2)}) collective-permute-start(bf16[32,1536]{1,0:T(8,128)(2,1)S(1)} %filter_block.1._.refs_0_), channel_id=1, source_target_pairs={{0,4},{1,5},{2,6},{3,7},{4,8},{5,9},{6,10},{7,11},{8,12},{9,13},{1... | collective-permute-start | bytes 294920 | tf_op jit(solution)/shard_map/ppermute | solution.py:324
  5.4 13.3 %copy-start.1 = (s32[16]{0:T(128)S(1)}, s32[16]{0:T(128)}, u32[]{:S(2)}) copy-start(s32[16]{0:T(128)} %refs_8_.1) | copy-start | bytes 196
  5.4 12.1 %collective-permute-start.7 = (bf16[128,1536]{1,0:T(8,128)(2,1)S(1)}, bf16[128,1536]{1,0:T(8,128)(2,1)S(1)}, u32[]{:S(2)}, u32[]{:S(2)}) collective-permute-start(bf16[128,1536]{1,0:T(8,128)(2,1)S(1)} %get-tuple-element.10), channel_id=1, source_target_pairs={{0,2},{1,3},{2,0},{3,1},{4,6},{5,7},{6,4},{7,5},{8,10},{9,11},{10,... | collective-permute-start | bytes 1179656 | tf_op jit(solution)/shard_map/ppermute | solution.py:316
  8.0 8.1 %collective-permute-start.3 = (bf16[32,1536]{1,0:T(8,128)(2,1)S(1)}, bf16[32,1536]{1,0:T(8,128)(2,1)S(1)}, u32[]{:S(2)}, u32[]{:S(2)}) collective-permute-start(bf16[32,1536]{1,0:T(8,128)(2,1)S(1)} %filter_block.1._.refs_0_), channel_id=1, source_target_pairs={{0,8},{1,9},{2,10},{3,11},{4,12},{5,13},{6,14},{7,15},{8,0},{9,1},... | collective-permute-start | bytes 294920 | tf_op jit(solution)/shard_map/ppermute | solution.py:324
  10.8 5.3 %collective-permute-start.1 = (bf16[32,1536]{1,0:T(8,128)(2,1)S(1)}, bf16[32,1536]{1,0:T(8,128)(2,1)S(1)}, u32[]{:S(2)}, u32[]{:S(2)}) collective-permute-start(bf16[32,1536]{1,0:T(8,128)(2,1)S(1)} %filter_block.1._.refs_0_), channel_id=1, source_target_pairs={{0,12},{1,13},{2,14},{3,15},{4,0},{5,1},{6,2},{7,3},{8,4},{9,5},{1... | collective-permute-start | bytes 294920 | tf_op jit(solution)/shard_map/ppermute | solution.py:324
  11.9 4.7 %collective-permute-start = (bf16[32,1536]{1,0:T(8,128)(2,1)S(1)}, bf16[32,1536]{1,0:T(8,128)(2,1)S(1)}, u32[]{:S(2)}, u32[]{:S(2)}) collective-permute-start(bf16[32,1536]{1,0:T(8,128)(2,1)S(1)} %filter_block.1._.refs_0_), channel_id=1, source_target_pairs={{0,1},{1,0},{2,3},{3,2},{4,5},{5,4},{6,7},{7,6},{8,9},{9,8},{10,11... | collective-permute-start | bytes 294920 | tf_op jit(solution)/shard_map/ppermute | solution.py:316
  11.9 4.7 %collective-permute-start.6 = (bf16[32,1536]{1,0:T(8,128)(2,1)S(1)}, bf16[32,1536]{1,0:T(8,128)(2,1)S(1)}, u32[]{:S(2)}, u32[]{:S(2)}) collective-permute-start(bf16[32,1536]{1,0:T(8,128)(2,1)S(1)} %relay.1.refs_6_), channel_id=1, source_target_pairs={{0,1},{1,0},{2,3},{3,2},{4,5},{5,4},{6,7},{7,6},{8,9},{9,8},{10,11... | collective-permute-start | bytes 294920 | tf_op jit(solution)/shard_map/ppermute | solution.py:316
  16.1 1.3 %collective-permute-start.4 = (bf16[32,1536]{1,0:T(8,128)(2,1)S(1)}, bf16[32,1536]{1,0:T(8,128)(2,1)S(1)}, u32[]{:S(2)}, u32[]{:S(2)}) collective-permute-start(bf16[32,1536]{1,0:T(8,128)(2,1)S(1)} %collective-permute-done.3.refs_4_), channel_id=1, source_target_pairs={{0,1},{1,0},{2,3},{3,2},{4,5},{5,4},{6,7},{7,6},{8,9},{9,8},{10,11... | collective-permute-start | bytes 294920 | tf_op jit(solution)/shard_map/ppermute | solution.py:316
  16.1 1.5 %collective-permute-start.2 = (bf16[32,1536]{1,0:T(8,128)(2,1)S(1)}, bf16[32,1536]{1,0:T(8,128)(2,1)S(1)}, u32[]{:S(2)}, u32[]{:S(2)}) collective-permute-start(bf16[32,1536]{1,0:T(8,128)(2,1)S(1)} %collective-permute-done.1.refs_2_), channel_id=1, source_target_pairs={{0,1},{1,0},{2,3},{3,2},{4,5},{5,4},{6,7},{7,6},{8,9},{9,8},{10,11... | collective-permute-start | bytes 294920 | tf_op jit(solution)/shard_map/ppermute | solution.py:316
  18.0 3.7 %collective-permute-start.8 = (bf16[16,256]{1,0:T(8,128)(2,1)S(1)}, bf16[16,256]{1,0:T(8,128)(2,1)S(1)}, u32[]{:S(2)}, u32[]{:S(2)}) collective-permute-start(bf16[16,256]{1,0:T(8,128)(2,1)S(1)} %cross.1.refs_10_), channel_id=1, source_target_pairs={{0,2},{1,3},{2,0},{3,1},{4,6},{5,7},{6,4},{7,5},{8,10},{9,11},{10,... | collective-permute-start | bytes 24584 | tf_op jit(solution)/shard_map/ppermute | solution.py:316

commit v14 on v13

--- a/solution.py
+++ b/solution.py
@@ -184,7 +184,7 @@
 
 def table_and_own(m_list, legendre, shards, after, at, line):
     n = m_list.shape[0]
-    order = sorted(shards, key=lambda k: -(k >> at) % line)
+    order = visiting(shards, at, line)
     return pl.pallas_call(
         functools.partial(table_kernel, at, line, order),
         out_shape=[
@@ -256,7 +256,7 @@
     rows, order_max = legendre.shape
     columns = shards[0].shape[0]
     count = len(shards)
-    order = sorted(shards, key=lambda k: -(k >> at) % line)
+    order = visiting(shards, at, line)
     return pl.pallas_call(
         functools.partial(cross_kernel, at, line, order),
         out_shape=jax.ShapeDtypeStruct((rows // count, count * columns), BF16),
@@ -316,13 +316,19 @@
     return lax.ppermute(value, "mset", [(d, d ^ mask) for d in range(size)])
 
 
+def visiting(shards, at, line):
+    issue = [0, line // 2] + [turn for turn in range(1, line) if turn != line // 2]
+    return sorted(shards, key=lambda k: (k >> at != 0, -issue.index(k >> at)))
+
+
 def gather_shards(value, size, at, line):
     step = size // line
     shards = {0: value}
     for turn in range(1, line):
         pairs = [(d, (d + turn * step) % size) for d in range(size)]
         shards[turn << at] = lax.ppermute(value, "mset", pairs)
-    shards[1 << at] = relay(shards[1 << at])
+    first = line // 2 << at
+    shards[first] = relay(shards[first])
     for b in range(at):
         shards.update({k | 1 << b: exchange(v, size, 1 << b) for k, v in shards.items()})
     return shards

time: 24.5 us -> 25.1 us (1.024)
  Pallas kernels: 6.86 us -> 7.79 us
  starting transfers between devices: 11.3 us -> 10.6 us
  waiting for transfers between devices: 6.08 us -> 6.4 us
    ppermute x6, starting transfers between devices: 4.3 us -> 2.41 us  [exchange(): return lax.ppermute(value, 'mset', [(d, d ^ mask) for d in range(size)])]
    ppermute x3, starting transfers between devices: 7.01 us -> 8.17 us  [gather_shards(): shards[turn << at] = lax.ppermute(value, 'mset', pairs)]
    pallas_call x1, Pallas kernels: 1.95 us -> 2.88 us  [filter_block(): pl.pallas_call(filter_kernel, out_shape=jax.ShapeDtypeStruct((columns, or...]
    ppermute x3, waiting for transfers between devices: 3.59 us -> 4.12 us  [gather_shards(): shards[turn << at] = lax.ppermute(value, 'mset', pairs)]
  transfers between devices with their start and end apart: 9 -> 9, of which waited for: 4 -> 7; matrix products, arithmetic and copies ran while one was open for 0% -> 0% of each run, Pallas kernels for 7% -> 7%
where the time goes in v14:
time: 25.1 us; the launch traced here: 24.8 us
  starting transfers between devices  10.6 us (42%)
  Pallas kernels  7.79 us (31%)
  waiting for transfers between devices  6.4 us (25%)
    ppermute x3, starting transfers between devices, gather_shards(): shards[turn << at] = lax.ppermute(value, 'mset', pairs)  8.17 us
    ppermute x3, waiting for transfers between devices, gather_shards(): shards[turn << at] = lax.ppermute(value, 'mset', pairs)  4.12 us
    pallas_call x1, Pallas kernels, filter_block(): pl.pallas_call(filter_kernel, out_shape=jax.ShapeDtypeStruct((columns, or...  2.88 us
    pallas_call x1, Pallas kernels, synthesize(): pl.pallas_call(functools.partial(synthesis_kernel, tiles), out_shape=jax....  2.61 us
    ppermute x6, starting transfers between devices, exchange(): return lax.ppermute(value, 'mset', [(d, d ^ mask) for d in range(size)])  2.41 us
    ppermute x6, waiting for transfers between devices, exchange(): return lax.ppermute(value, 'mset', [(d, d ^ mask) for d in range(size)])  2.28 us
    pallas_call x1, Pallas kernels, table_and_own(): pl.pallas_call(functools.partial(table_kernel, at, line, order), out_shap...  1.41 us
  transfers between devices with their start and end apart: 9, of which 7 were waited for; matrix products, arithmetic and copies ran while one was open for 0% of the time, Pallas kernels for 7%

profile of v14, /device:TPU:0, one launch (start us, length us, event | category | flops | bytes accessed | tf_op | source)
XLA Modules:
  0.0 24.8 jit_solution(12761936325975136339)
XLA Ops:
  0.0 0.0 copy-start
  0.0 2.9 %filter_block.1._.refs_0_ = bf16[32,1536]{1,0:T(8,128)(2,1)S(1)} custom-call(s32[16]{0:T(128)} %refs_8_.1, bf16[32,1536]{1,0:T(8,128)(2,1)} %bitcast.6, bf16[1536,1536]{1,0:T(8,128)(2,1)} %bitcast.5), custom_call_target="tpu_custom_call" | custom-call | flops 150994944 | bytes 4718592 | tf_op jit(solution)/shard_map/filter_block/pallas_call | solution.py:124
  2.9 4.3 %collective-permute-start.5 = (bf16[32,1536]{1,0:T(8,128)(2,1)S(1)}, bf16[32,1536]{1,0:T(8,128)(2,1)S(1)}, u32[]{:S(2)}, u32[]{:S(2)}) collective-permute-start(bf16[32,1536]{1,0:T(8,128)(2,1)S(1)} %filter_block.1._.refs_0_), channel_id=1, source_target_pairs={{0,8},{1,9},{2,10},{3,11},{4,12},{5,13},{6,14},{7,15},{8,0},{9,1},... | collective-permute-start | bytes 294920 | tf_op jit(solution)/shard_map/ppermute | solution.py:329
  7.2 0.0 copy-done
  7.2 0.4 %sort_legendre.1 = (bf16[128,1536]{1,0:T(8,128)(2,1)S(1)}, bf16[128,1536]{1,0:T(8,128)(2,1)S(1)}) custom-call(bf16[256,1536]{1,0:T(8,128)(2,1)S(1)} %bitcast.4, bf16[32,1536]{1,0:T(8,128)(2,1)S(1)} %filter_block.1._.refs_0_), custom_call_target="tpu_custom_call" | custom-call | flops 201326592 | bytes 1572864 | tf_op jit(solution)/shard_map/sort_legendre/pallas_call | solution.py:162
  7.6 0.0 copy-start.1
  7.6 0.4 %collective-permute-start.7 = (bf16[128,1536]{1,0:T(8,128)(2,1)S(1)}, bf16[128,1536]{1,0:T(8,128)(2,1)S(1)}, u32[]{:S(2)}, u32[]{:S(2)}) collective-permute-start(bf16[128,1536]{1,0:T(8,128)(2,1)S(1)} %get-tuple-element.10), channel_id=1, source_target_pairs={{0,2},{1,3},{2,0},{3,1},{4,6},{5,7},{6,4},{7,5},{8,10},{9,11},{10,... | collective-permute-start | bytes 1179656 | tf_op jit(solution)/shard_map/ppermute | solution.py:316
  8.0 2.3 %collective-permute-start.3 = (bf16[32,1536]{1,0:T(8,128)(2,1)S(1)}, bf16[32,1536]{1,0:T(8,128)(2,1)S(1)}, u32[]{:S(2)}, u32[]{:S(2)}) collective-permute-start(bf16[32,1536]{1,0:T(8,128)(2,1)S(1)} %filter_block.1._.refs_0_), channel_id=1, source_target_pairs={{0,4},{1,5},{2,6},{3,7},{4,8},{5,9},{6,10},{7,11},{8,12},{9,13},{1... | collective-permute-start | bytes 294920 | tf_op jit(solution)/shard_map/ppermute | solution.py:329
  10.3 1.6 %collective-permute-start.1 = (bf16[32,1536]{1,0:T(8,128)(2,1)S(1)}, bf16[32,1536]{1,0:T(8,128)(2,1)S(1)}, u32[]{:S(2)}, u32[]{:S(2)}) collective-permute-start(bf16[32,1536]{1,0:T(8,128)(2,1)S(1)} %filter_block.1._.refs_0_), channel_id=1, source_target_pairs={{0,12},{1,13},{2,14},{3,15},{4,0},{5,1},{6,2},{7,3},{8,4},{9,5},{1... | collective-permute-start | bytes 294920 | tf_op jit(solution)/shard_map/ppermute | solution.py:329
  11.9 0.0 collective-permute-start
  11.9 0.3 %collective-permute-done.5.shard_ref = bf16[32,1536]{1,0:T(8,128)(2,1)S(1)} collective-permute-done((bf16[32,1536]{1,0:T(8,128)(2,1)S(1)}, bf16[32,1536]{1,0:T(8,128)(2,1)S(1)}, u32[]{:S(2)}, u32[]{:S(2)}) %collective-permute-start.5) | collective-permute-done | bytes 98336 | tf_op jit(solution)/shard_map/ppermute | solution.py:329
  12.2 0.3 %collective-permute-start.6 = (bf16[32,1536]{1,0:T(8,128)(2,1)S(1)}, bf16[32,1536]{1,0:T(8,128)(2,1)S(1)}, u32[]{:S(2)}, u32[]{:S(2)}) collective-permute-start(bf16[32,1536]{1,0:T(8,128)(2,1)S(1)} %relay.1.refs_6_), channel_id=1, source_target_pairs={{0,1},{1,0},{2,3},{3,2},{4,5},{5,4},{6,7},{7,6},{8,9},{9,8},{10,11... | collective-permute-start | bytes 294920 | tf_op jit(solution)/shard_map/ppermute | solution.py:316
  12.5 3.0 %collective-permute-done.3.refs_4_ = bf16[32,1536]{1,0:T(8,128)(2,1)S(1)} collective-permute-done((bf16[32,1536]{1,0:T(8,128)(2,1)S(1)}, bf16[32,1536]{1,0:T(8,128)(2,1)S(1)}, u32[]{:S(2)}, u32[]{:S(2)}) %collective-permute-start.3) | collective-permute-done | bytes 98336 | tf_op jit(solution)/shard_map/ppermute | solution.py:329
  15.5 0.0 collective-permute-start.4
  15.5 0.8 %collective-permute-done.1.refs_2_ = bf16[32,1536]{1,0:T(8,128)(2,1)S(1)} collective-permute-done((bf16[32,1536]{1,0:T(8,128)(2,1)S(1)}, bf16[32,1536]{1,0:T(8,128)(2,1)S(1)}, u32[]{:S(2)}, u32[]{:S(2)}) %collective-permute-start.1) | collective-permute-done | bytes 98336 | tf_op jit(solution)/shard_map/ppermute | solution.py:329
  16.3 0.0 collective-permute-start.2
  16.3 0.0 collective-permute-done.refs_1_
  16.3 0.0 collective-permute-done.6.refs_7_
  16.3 0.5 %collective-permute-done.4.refs_5_ = bf16[32,1536]{1,0:T(8,128)(2,1)S(1)} collective-permute-done((bf16[32,1536]{1,0:T(8,128)(2,1)S(1)}, bf16[32,1536]{1,0:T(8,128)(2,1)S(1)}, u32[]{:S(2)}, u32[]{:S(2)}) %collective-permute-start.4) | collective-permute-done | bytes 98336 | tf_op jit(solution)/shard_map/ppermute | solution.py:316
  16.8 0.8 %collective-permute-done.2.refs_3_ = bf16[32,1536]{1,0:T(8,128)(2,1)S(1)} collective-permute-done((bf16[32,1536]{1,0:T(8,128)(2,1)S(1)}, bf16[32,1536]{1,0:T(8,128)(2,1)S(1)}, u32[]{:S(2)}, u32[]{:S(2)}) %collective-permute-start.2) | collective-permute-done | bytes 98336 | tf_op jit(solution)/shard_map/ppermute | solution.py:316
  17.6 0.5 %collective-permute-done.7.refs_8_ = bf16[128,1536]{1,0:T(8,128)(2,1)S(1)} collective-permute-done((bf16[128,1536]{1,0:T(8,128)(2,1)S(1)}, bf16[128,1536]{1,0:T(8,128)(2,1)S(1)}, u32[]{:S(2)}, u32[]{:S(2)}) %collective-permute-start.7) | collective-permute-done | bytes 393248 | tf_op jit(solution)/shard_map/ppermute | solution.py:316
  18.1 0.5 %cross.1.refs_10_ = bf16[16,256]{1,0:T(8,128)(2,1)S(1)} custom-call(bf16[32,1536]{1,0:T(8,128)(2,1)S(1)} %filter_block.1._.refs_0_, bf16[32,1536]{1,0:T(8,128)(2,1)S(1)} %collective-permute-done.refs_1_, bf16[32,1536]{1,0:T(8,128)(2,1)S(1)} %collective-permute-done.1.refs_2_, bf16[32,1536]{1,0:T(8,128)(2,1)S(1)} %collective-permute-done.2.refs_3_, ...), custom_call_target="tpu_custom_call" | custom-call | flops 100663296 | bytes 1179648 | tf_op jit(solution)/shard_map/cross/pallas_call | solution.py:260
  18.6 1.7 %collective-permute-start.8 = (bf16[16,256]{1,0:T(8,128)(2,1)S(1)}, bf16[16,256]{1,0:T(8,128)(2,1)S(1)}, u32[]{:S(2)}, u32[]{:S(2)}) collective-permute-start(bf16[16,256]{1,0:T(8,128)(2,1)S(1)} %cross.1.refs_10_), channel_id=1, source_target_pairs={{0,2},{1,3},{2,0},{3,1},{4,6},{5,7},{6,4},{7,5},{8,10},{9,11},{10,... | collective-permute-start | bytes 24584 | tf_op jit(solution)/shard_map/ppermute | solution.py:316
  20.3 0.0 copy-done.1
  20.3 1.4 %table_and_own.1 = (bf16[32,8192]{1,0:T(8,128)(2,1)S(1)}, bf16[256,32]{1,0:T(8,128)(2,1)S(1)}) custom-call(bf16[32,1536]{1,0:T(8,128)(2,1)S(1)} %filter_block.1._.refs_0_, bf16[32,1536]{1,0:T(8,128)(2,1)S(1)} %collective-permute-done.refs_1_, bf16[32,1536]{1,0:T(8,128)(2,1)S(1)} %collective-permute-done.1.refs_2_, ...), custom_call_target="tpu_custom_call" | custom-call | flops 2097152 | bytes 524288 | tf_op jit(solution)/shard_map/table_and_own/pallas_call | solution.py:188
  21.7 0.5 %collective-permute-done.8.got_ref = bf16[16,256]{1,0:T(8,128)(2,1)S(1)} collective-permute-done((bf16[16,256]{1,0:T(8,128)(2,1)S(1)}, bf16[16,256]{1,0:T(8,128)(2,1)S(1)}, u32[]{:S(2)}, u32[]{:S(2)}) %collective-permute-start.8) | collective-permute-done | bytes 8224 | tf_op jit(solution)/shard_map/ppermute | solution.py:316
  22.2 2.6 %synthesis.1 = bf16[256,8192]{1,0:T(8,128)(2,1)} custom-call(bf16[256,32]{1,0:T(8,128)(2,1)S(1)} %get-tuple-element.11.own_ref, bf16[16,256]{1,0:T(8,128)(2,1)S(1)} %collective-permute-done.8.got_ref, bf16[32,8192]{1,0:T(8,128)(2,1)S(1)} %get-tuple-element.12.table_ref), custom_call_target="tpu_custom_call" | custom-call | flops 134217728 | bytes 4718592 | tf_op jit(solution)/shard_map/synthesis/pallas_call | solution.py:299
  (1 shorter events, 0.0 us)
Async XLA Ops:
  0.0 7.2 %copy-start = (bf16[16,16,1536]{2,1,0:T(8,128)(2,1)S(1)}, bf16[16,16,1536]{2,1,0:T(8,128)(2,1)}, u32[]{:S(2)}) copy-start(bf16[16,16,1536]{2,1,0:T(8,128)(2,1)} %param.7) | copy-start | bytes 2359300
  2.9 9.3 %collective-permute-start.5 = (bf16[32,1536]{1,0:T(8,128)(2,1)S(1)}, bf16[32,1536]{1,0:T(8,128)(2,1)S(1)}, u32[]{:S(2)}, u32[]{:S(2)}) collective-permute-start(bf16[32,1536]{1,0:T(8,128)(2,1)S(1)} %filter_block.1._.refs_0_), channel_id=1, source_target_pairs={{0,8},{1,9},{2,10},{3,11},{4,12},{5,13},{6,14},{7,15},{8,0},{9,1},... | collective-permute-start | bytes 294920 | tf_op jit(solution)/shard_map/ppermute | solution.py:329
  7.6 12.7 %copy-start.1 = (s32[16]{0:T(128)S(1)}, s32[16]{0:T(128)}, u32[]{:S(2)}) copy-start(s32[16]{0:T(128)} %refs_8_.1) | copy-start | bytes 196
  7.6 10.4 %collective-permute-start.7 = (bf16[128,1536]{1,0:T(8,128)(2,1)S(1)}, bf16[128,1536]{1,0:T(8,128)(2,1)S(1)}, u32[]{:S(2)}, u32[]{:S(2)}) collective-permute-start(bf16[128,1536]{1,0:T(8,128)(2,1)S(1)} %get-tuple-element.10), channel_id=1, source_target_pairs={{0,2},{1,3},{2,0},{3,1},{4,6},{5,7},{6,4},{7,5},{8,10},{9,11},{10,... | collective-permute-start | bytes 1179656 | tf_op jit(solution)/shard_map/ppermute | solution.py:316
  8.0 7.4 %collective-permute-start.3 = (bf16[32,1536]{1,0:T(8,128)(2,1)S(1)}, bf16[32,1536]{1,0:T(8,128)(2,1)S(1)}, u32[]{:S(2)}, u32[]{:S(2)}) collective-permute-start(bf16[32,1536]{1,0:T(8,128)(2,1)S(1)} %filter_block.1._.refs_0_), channel_id=1, source_target_pairs={{0,4},{1,5},{2,6},{3,7},{4,8},{5,9},{6,10},{7,11},{8,12},{9,13},{1... | collective-permute-start | bytes 294920 | tf_op jit(solution)/shard_map/ppermute | solution.py:329
  10.3 5.9 %collective-permute-start.1 = (bf16[32,1536]{1,0:T(8,128)(2,1)S(1)}, bf16[32,1536]{1,0:T(8,128)(2,1)S(1)}, u32[]{:S(2)}, u32[]{:S(2)}) collective-permute-start(bf16[32,1536]{1,0:T(8,128)(2,1)S(1)} %filter_block.1._.refs_0_), channel_id=1, source_target_pairs={{0,12},{1,13},{2,14},{3,15},{4,0},{5,1},{6,2},{7,3},{8,4},{9,5},{1... | collective-permute-start | bytes 294920 | tf_op jit(solution)/shard_map/ppermute | solution.py:329
  11.9 4.4 %collective-permute-start = (bf16[32,1536]{1,0:T(8,128)(2,1)S(1)}, bf16[32,1536]{1,0:T(8,128)(2,1)S(1)}, u32[]{:S(2)}, u32[]{:S(2)}) collective-permute-start(bf16[32,1536]{1,0:T(8,128)(2,1)S(1)} %filter_block.1._.refs_0_), channel_id=1, source_target_pairs={{0,1},{1,0},{2,3},{3,2},{4,5},{5,4},{6,7},{7,6},{8,9},{9,8},{10,11... | collective-permute-start | bytes 294920 | tf_op jit(solution)/shard_map/ppermute | solution.py:316
  12.2 4.1 %collective-permute-start.6 = (bf16[32,1536]{1,0:T(8,128)(2,1)S(1)}, bf16[32,1536]{1,0:T(8,128)(2,1)S(1)}, u32[]{:S(2)}, u32[]{:S(2)}) collective-permute-start(bf16[32,1536]{1,0:T(8,128)(2,1)S(1)} %relay.1.refs_6_), channel_id=1, source_target_pairs={{0,1},{1,0},{2,3},{3,2},{4,5},{5,4},{6,7},{7,6},{8,9},{9,8},{10,11... | collective-permute-start | bytes 294920 | tf_op jit(solution)/shard_map/ppermute | solution.py:316
  15.5 1.3 %collective-permute-start.4 = (bf16[32,1536]{1,0:T(8,128)(2,1)S(1)}, bf16[32,1536]{1,0:T(8,128)(2,1)S(1)}, u32[]{:S(2)}, u32[]{:S(2)}) collective-permute-start(bf16[32,1536]{1,0:T(8,128)(2,1)S(1)} %collective-permute-done.3.refs_4_), channel_id=1, source_target_pairs={{0,1},{1,0},{2,3},{3,2},{4,5},{5,4},{6,7},{7,6},{8,9},{9,8},{10,11... | collective-permute-start | bytes 294920 | tf_op jit(solution)/shard_map/ppermute | solution.py:316
  16.3 1.3 %collective-permute-start.2 = (bf16[32,1536]{1,0:T(8,128)(2,1)S(1)}, bf16[32,1536]{1,0:T(8,128)(2,1)S(1)}, u32[]{:S(2)}, u32[]{:S(2)}) collective-permute-start(bf16[32,1536]{1,0:T(8,128)(2,1)S(1)} %collective-permute-done.1.refs_2_), channel_id=1, source_target_pairs={{0,1},{1,0},{2,3},{3,2},{4,5},{5,4},{6,7},{7,6},{8,9},{9,8},{10,11... | collective-permute-start | bytes 294920 | tf_op jit(solution)/shard_map/ppermute | solution.py:316
  18.6 3.7 %collective-permute-start.8 = (bf16[16,256]{1,0:T(8,128)(2,1)S(1)}, bf16[16,256]{1,0:T(8,128)(2,1)S(1)}, u32[]{:S(2)}, u32[]{:S(2)}) collective-permute-start(bf16[16,256]{1,0:T(8,128)(2,1)S(1)} %cross.1.refs_10_), channel_id=1, source_target_pairs={{0,2},{1,3},{2,0},{3,1},{4,6},{5,7},{6,4},{7,5},{8,10},{9,11},{10,... | collective-permute-start | bytes 24584 | tf_op jit(solution)/shard_map/ppermute | solution.py:316

commit v15 on v12

--- a/solution.py
+++ b/solution.py
@@ -91,8 +91,8 @@
         )
         for p in range(pieces)
     ]
-    for copy in [copy_m, copy_leg, copy_coeff] + copy_blocks:
-        copy.start()
+    for turn, copy in enumerate([copy_m, copy_leg, copy_coeff] + copy_blocks):
+        copy.start(priority=turn % 2)
 
     rows = leg_ref.shape[0]
     n = m_ref.shape[0]
@@ -269,7 +269,7 @@
                 summed = jnp.dot(flat[rows], piece, preferred_element_type=F32)
                 held[rows, columns] = summed.astype(BF16)
         copy = pltpu.make_async_copy(held.at[:, span], out_ref.at[:, span], sems.at[t])
-        copy.start()
+        copy.start(priority=t % 2)
         copies.append(copy)
     for copy in copies:
         copy.wait()

time: 24 us -> 24.4 us (1.017)
  Pallas kernels: 7.45 us -> 7.89 us
    pallas_call x1, Pallas kernels: 2.91 us -> 3.36 us  [prepare(): pl.pallas_call(functools.partial(prepare_kernel, at), out_shape=[jax.Shap...]
where the time goes in v15:
time: 24.4 us; the launch traced here: 24.3 us
  starting transfers between devices  10.7 us (44%)
  Pallas kernels  7.89 us (32%)
  waiting for transfers between devices  5.59 us (23%)
    ppermute x3, starting transfers between devices, gather_shards(): shards[turn << at] = lax.ppermute(value, 'mset', pairs)  7.02 us
    ppermute x6, starting transfers between devices, exchange(): return lax.ppermute(value, 'mset', [(d, d ^ mask) for d in range(size)])  3.73 us
    ppermute x3, waiting for transfers between devices, gather_shards(): shards[turn << at] = lax.ppermute(value, 'mset', pairs)  3.53 us
    pallas_call x1, Pallas kernels, prepare(): pl.pallas_call(functools.partial(prepare_kernel, at), out_shape=[jax.Shap...  3.36 us
    pallas_call x1, Pallas kernels, synthesize(): pl.pallas_call(functools.partial(synthesis_kernel, tiles), out_shape=jax....  2.61 us
    ppermute x6, waiting for transfers between devices, exchange(): return lax.ppermute(value, 'mset', [(d, d ^ mask) for d in range(size)])  2.05 us
    pallas_call x1, Pallas kernels, table_and_own(): pl.pallas_call(functools.partial(table_kernel, at, line, order), out_shap...  1.42 us
    pallas_call x1, Pallas kernels, cross(): pl.pallas_call(functools.partial(cross_kernel, at, line, order), out_shap...  0.5 us
  transfers between devices with their start and end apart: 9, of which 4 were waited for; matrix products, arithmetic and copies ran while one was open for 0% of the time, Pallas kernels for 6%

profile of v15, /device:TPU:0, one launch (start us, length us, event | category | flops | bytes accessed | tf_op | source)
XLA Modules:
  0.0 24.3 jit_solution(10323117805839096035)
XLA Ops:
  0.0 3.4 %prepare.1 = (bf16[32,1536]{1,0:T(8,128)(2,1)S(1)}, bf16[128,1536]{1,0:T(8,128)(2,1)S(1)}, bf16[128,1536]{1,0:T(8,128)(2,1)S(1)}) custom-call(s32[16]{0:T(128)} %refs_8_.1, bf16[32,1536]{1,0:T(8,128)(2,1)} %bitcast.6, bf16[1536,1536]{1,0:T(8,128)(2,1)} %bitcast.4, bf16[256,1536]{1,0:T(8,128)(2,1)} %bitcast.5), custom_call_target="tpu_custom_call" | custom-call | flops 352321536 | bytes 5505024 | tf_op jit(solution)/shard_map/prepare/pallas_call | solution.py:133
  3.4 3.1 %collective-permute-start.5 = (bf16[32,1536]{1,0:T(8,128)(2,1)S(1)}, bf16[32,1536]{1,0:T(8,128)(2,1)S(1)}, u32[]{:S(2)}, u32[]{:S(2)}) collective-permute-start(bf16[32,1536]{1,0:T(8,128)(2,1)S(1)} %get-tuple-element.10.refs_0_), channel_id=1, source_target_pairs={{0,4},{1,5},{2,6},{3,7},{4,8},{5,9},{6,10},{7,11},{8,12},{9,13},{1... | collective-permute-start | bytes 294920 | tf_op jit(solution)/shard_map/ppermute | solution.py:306
  6.4 0.0 copy-start
  6.4 1.5 %collective-permute-start.7 = (bf16[128,1536]{1,0:T(8,128)(2,1)S(1)}, bf16[128,1536]{1,0:T(8,128)(2,1)S(1)}, u32[]{:S(2)}, u32[]{:S(2)}) collective-permute-start(bf16[128,1536]{1,0:T(8,128)(2,1)S(1)} %get-tuple-element.12), channel_id=1, source_target_pairs={{0,2},{1,3},{2,0},{3,1},{4,6},{5,7},{6,4},{7,5},{8,10},{9,11},{10,... | collective-permute-start | bytes 1179656 | tf_op jit(solution)/shard_map/ppermute | solution.py:298
  8.0 2.6 %collective-permute-start.3 = (bf16[32,1536]{1,0:T(8,128)(2,1)S(1)}, bf16[32,1536]{1,0:T(8,128)(2,1)S(1)}, u32[]{:S(2)}, u32[]{:S(2)}) collective-permute-start(bf16[32,1536]{1,0:T(8,128)(2,1)S(1)} %get-tuple-element.10.refs_0_), channel_id=1, source_target_pairs={{0,8},{1,9},{2,10},{3,11},{4,12},{5,13},{6,14},{7,15},{8,0},{9,1},... | collective-permute-start | bytes 294920 | tf_op jit(solution)/shard_map/ppermute | solution.py:306
  10.6 1.3 %collective-permute-start.1 = (bf16[32,1536]{1,0:T(8,128)(2,1)S(1)}, bf16[32,1536]{1,0:T(8,128)(2,1)S(1)}, u32[]{:S(2)}, u32[]{:S(2)}) collective-permute-start(bf16[32,1536]{1,0:T(8,128)(2,1)S(1)} %get-tuple-element.10.refs_0_), channel_id=1, source_target_pairs={{0,12},{1,13},{2,14},{3,15},{4,0},{5,1},{6,2},{7,3},{8,4},{9,5},{1... | collective-permute-start | bytes 294920 | tf_op jit(solution)/shard_map/ppermute | solution.py:306
  11.9 0.0 collective-permute-start
  11.9 0.0 collective-permute-done.5.shard_ref
  11.9 0.6 %collective-permute-start.6 = (bf16[32,1536]{1,0:T(8,128)(2,1)S(1)}, bf16[32,1536]{1,0:T(8,128)(2,1)S(1)}, u32[]{:S(2)}, u32[]{:S(2)}) collective-permute-start(bf16[32,1536]{1,0:T(8,128)(2,1)S(1)} %relay.1.refs_6_), channel_id=1, source_target_pairs={{0,1},{1,0},{2,3},{3,2},{4,5},{5,4},{6,7},{7,6},{8,9},{9,8},{10,11... | collective-permute-start | bytes 294920 | tf_op jit(solution)/shard_map/ppermute | solution.py:298
  12.5 3.5 %collective-permute-done.3.refs_4_ = bf16[32,1536]{1,0:T(8,128)(2,1)S(1)} collective-permute-done((bf16[32,1536]{1,0:T(8,128)(2,1)S(1)}, bf16[32,1536]{1,0:T(8,128)(2,1)S(1)}, u32[]{:S(2)}, u32[]{:S(2)}) %collective-permute-start.3) | collective-permute-done | bytes 98336 | tf_op jit(solution)/shard_map/ppermute | solution.py:306
  16.0 0.0 collective-permute-start.4
  16.0 0.0 collective-permute-done.1.refs_2_
  16.0 0.5 %collective-permute-start.2 = (bf16[32,1536]{1,0:T(8,128)(2,1)S(1)}, bf16[32,1536]{1,0:T(8,128)(2,1)S(1)}, u32[]{:S(2)}, u32[]{:S(2)}) collective-permute-start(bf16[32,1536]{1,0:T(8,128)(2,1)S(1)} %collective-permute-done.1.refs_2_), channel_id=1, source_target_pairs={{0,1},{1,0},{2,3},{3,2},{4,5},{5,4},{6,7},{7,6},{8,9},{9,8},{10,11... | collective-permute-start | bytes 294920 | tf_op jit(solution)/shard_map/ppermute | solution.py:298
  16.5 0.0 collective-permute-done.refs_1_
  16.5 0.0 collective-permute-done.6.refs_7_
  16.5 0.8 %collective-permute-done.4.refs_5_ = bf16[32,1536]{1,0:T(8,128)(2,1)S(1)} collective-permute-done((bf16[32,1536]{1,0:T(8,128)(2,1)S(1)}, bf16[32,1536]{1,0:T(8,128)(2,1)S(1)}, u32[]{:S(2)}, u32[]{:S(2)}) %collective-permute-start.4) | collective-permute-done | bytes 98336 | tf_op jit(solution)/shard_map/ppermute | solution.py:298
  17.3 0.2 collective-permute-done.2.refs_3_
  17.5 0.0 collective-permute-done.7.refs_8_
  17.5 0.5 %cross.1.refs_10_ = bf16[16,256]{1,0:T(8,128)(2,1)S(1)} custom-call(bf16[32,1536]{1,0:T(8,128)(2,1)S(1)} %get-tuple-element.10.refs_0_, bf16[32,1536]{1,0:T(8,128)(2,1)S(1)} %collective-permute-done.refs_1_, bf16[32,1536]{1,0:T(8,128)(2,1)S(1)} %collective-permute-done.1.refs_2_, bf16[32,1536]{1,0:T(8,128)(2,1)S(1)} %collective-permute-done.2.refs_3_, ...), custom_call_target="tpu_custom_call" | custom-call | flops 100663296 | bytes 1179648 | tf_op jit(solution)/shard_map/cross/pallas_call | solution.py:242
  18.0 1.1 %collective-permute-start.8 = (bf16[16,256]{1,0:T(8,128)(2,1)S(1)}, bf16[16,256]{1,0:T(8,128)(2,1)S(1)}, u32[]{:S(2)}, u32[]{:S(2)}) collective-permute-start(bf16[16,256]{1,0:T(8,128)(2,1)S(1)} %cross.1.refs_10_), channel_id=1, source_target_pairs={{0,2},{1,3},{2,0},{3,1},{4,6},{5,7},{6,4},{7,5},{8,10},{9,11},{10,... | collective-permute-start | bytes 24584 | tf_op jit(solution)/shard_map/ppermute | solution.py:298
  19.1 0.0 copy-done
  19.1 1.4 %table_and_own.1 = (bf16[32,8192]{1,0:T(8,128)(2,1)S(1)}, bf16[256,32]{1,0:T(8,128)(2,1)S(1)}) custom-call(bf16[32,1536]{1,0:T(8,128)(2,1)S(1)} %get-tuple-element.10.refs_0_, bf16[32,1536]{1,0:T(8,128)(2,1)S(1)} %collective-permute-done.refs_1_, bf16[32,1536]{1,0:T(8,128)(2,1)S(1)} %collective-permute-done.1.refs_2_, ...), custom_call_target="tpu_custom_call" | custom-call | flops 2097152 | bytes 524288 | tf_op jit(solution)/shard_map/table_and_own/pallas_call | solution.py:170
  20.5 1.1 %collective-permute-done.8.got_ref = bf16[16,256]{1,0:T(8,128)(2,1)S(1)} collective-permute-done((bf16[16,256]{1,0:T(8,128)(2,1)S(1)}, bf16[16,256]{1,0:T(8,128)(2,1)S(1)}, u32[]{:S(2)}, u32[]{:S(2)}) %collective-permute-start.8) | collective-permute-done | bytes 8224 | tf_op jit(solution)/shard_map/ppermute | solution.py:298
  21.6 2.6 %synthesis.1 = bf16[256,8192]{1,0:T(8,128)(2,1)} custom-call(bf16[256,32]{1,0:T(8,128)(2,1)S(1)} %get-tuple-element.13.own_ref, bf16[16,256]{1,0:T(8,128)(2,1)S(1)} %collective-permute-done.8.got_ref, bf16[32,8192]{1,0:T(8,128)(2,1)S(1)} %get-tuple-element.14.table_ref), custom_call_target="tpu_custom_call" | custom-call | flops 134217728 | bytes 4718592 | tf_op jit(solution)/shard_map/synthesis/pallas_call | solution.py:281
  (1 shorter events, 0.0 us)
Async XLA Ops:
  3.4 8.5 %collective-permute-start.5 = (bf16[32,1536]{1,0:T(8,128)(2,1)S(1)}, bf16[32,1536]{1,0:T(8,128)(2,1)S(1)}, u32[]{:S(2)}, u32[]{:S(2)}) collective-permute-start(bf16[32,1536]{1,0:T(8,128)(2,1)S(1)} %get-tuple-element.10.refs_0_), channel_id=1, source_target_pairs={{0,4},{1,5},{2,6},{3,7},{4,8},{5,9},{6,10},{7,11},{8,12},{9,13},{1... | collective-permute-start | bytes 294920 | tf_op jit(solution)/shard_map/ppermute | solution.py:306
  6.4 12.7 %copy-start = (s32[16]{0:T(128)S(1)}, s32[16]{0:T(128)}, u32[]{:S(2)}) copy-start(s32[16]{0:T(128)} %refs_8_.1) | copy-start | bytes 196
  6.4 11.0 %collective-permute-start.7 = (bf16[128,1536]{1,0:T(8,128)(2,1)S(1)}, bf16[128,1536]{1,0:T(8,128)(2,1)S(1)}, u32[]{:S(2)}, u32[]{:S(2)}) collective-permute-start(bf16[128,1536]{1,0:T(8,128)(2,1)S(1)} %get-tuple-element.12), channel_id=1, source_target_pairs={{0,2},{1,3},{2,0},{3,1},{4,6},{5,7},{6,4},{7,5},{8,10},{9,11},{10,... | collective-permute-start | bytes 1179656 | tf_op jit(solution)/shard_map/ppermute | solution.py:298
  8.0 8.1 %collective-permute-start.3 = (bf16[32,1536]{1,0:T(8,128)(2,1)S(1)}, bf16[32,1536]{1,0:T(8,128)(2,1)S(1)}, u32[]{:S(2)}, u32[]{:S(2)}) collective-permute-start(bf16[32,1536]{1,0:T(8,128)(2,1)S(1)} %get-tuple-element.10.refs_0_), channel_id=1, source_target_pairs={{0,8},{1,9},{2,10},{3,11},{4,12},{5,13},{6,14},{7,15},{8,0},{9,1},... | collective-permute-start | bytes 294920 | tf_op jit(solution)/shard_map/ppermute | solution.py:306
  10.6 5.5 %collective-permute-start.1 = (bf16[32,1536]{1,0:T(8,128)(2,1)S(1)}, bf16[32,1536]{1,0:T(8,128)(2,1)S(1)}, u32[]{:S(2)}, u32[]{:S(2)}) collective-permute-start(bf16[32,1536]{1,0:T(8,128)(2,1)S(1)} %get-tuple-element.10.refs_0_), channel_id=1, source_target_pairs={{0,12},{1,13},{2,14},{3,15},{4,0},{5,1},{6,2},{7,3},{8,4},{9,5},{1... | collective-permute-start | bytes 294920 | tf_op jit(solution)/shard_map/ppermute | solution.py:306
  11.9 4.6 %collective-permute-start = (bf16[32,1536]{1,0:T(8,128)(2,1)S(1)}, bf16[32,1536]{1,0:T(8,128)(2,1)S(1)}, u32[]{:S(2)}, u32[]{:S(2)}) collective-permute-start(bf16[32,1536]{1,0:T(8,128)(2,1)S(1)} %get-tuple-element.10.refs_0_), channel_id=1, source_target_pairs={{0,1},{1,0},{2,3},{3,2},{4,5},{5,4},{6,7},{7,6},{8,9},{9,8},{10,11... | collective-permute-start | bytes 294920 | tf_op jit(solution)/shard_map/ppermute | solution.py:298
  11.9 4.6 %collective-permute-start.6 = (bf16[32,1536]{1,0:T(8,128)(2,1)S(1)}, bf16[32,1536]{1,0:T(8,128)(2,1)S(1)}, u32[]{:S(2)}, u32[]{:S(2)}) collective-permute-start(bf16[32,1536]{1,0:T(8,128)(2,1)S(1)} %relay.1.refs_6_), channel_id=1, source_target_pairs={{0,1},{1,0},{2,3},{3,2},{4,5},{5,4},{6,7},{7,6},{8,9},{9,8},{10,11... | collective-permute-start | bytes 294920 | tf_op jit(solution)/shard_map/ppermute | solution.py:298
  16.0 1.3 %collective-permute-start.4 = (bf16[32,1536]{1,0:T(8,128)(2,1)S(1)}, bf16[32,1536]{1,0:T(8,128)(2,1)S(1)}, u32[]{:S(2)}, u32[]{:S(2)}) collective-permute-start(bf16[32,1536]{1,0:T(8,128)(2,1)S(1)} %collective-permute-done.3.refs_4_), channel_id=1, source_target_pairs={{0,1},{1,0},{2,3},{3,2},{4,5},{5,4},{6,7},{7,6},{8,9},{9,8},{10,11... | collective-permute-start | bytes 294920 | tf_op jit(solution)/shard_map/ppermute | solution.py:298
  16.0 1.5 %collective-permute-start.2 = (bf16[32,1536]{1,0:T(8,128)(2,1)S(1)}, bf16[32,1536]{1,0:T(8,128)(2,1)S(1)}, u32[]{:S(2)}, u32[]{:S(2)}) collective-permute-start(bf16[32,1536]{1,0:T(8,128)(2,1)S(1)} %collective-permute-done.1.refs_2_), channel_id=1, source_target_pairs={{0,1},{1,0},{2,3},{3,2},{4,5},{5,4},{6,7},{7,6},{8,9},{9,8},{10,11... | collective-permute-start | bytes 294920 | tf_op jit(solution)/shard_map/ppermute | solution.py:298
  18.0 3.7 %collective-permute-start.8 = (bf16[16,256]{1,0:T(8,128)(2,1)S(1)}, bf16[16,256]{1,0:T(8,128)(2,1)S(1)}, u32[]{:S(2)}, u32[]{:S(2)}) collective-permute-start(bf16[16,256]{1,0:T(8,128)(2,1)S(1)} %cross.1.refs_10_), channel_id=1, source_target_pairs={{0,2},{1,3},{2,0},{3,1},{4,6},{5,7},{6,4},{7,5},{8,10},{9,11},{10,... | collective-permute-start | bytes 24584 | tf_op jit(solution)/shard_map/ppermute | solution.py:298

commit v16 on v12

--- a/solution.py
+++ b/solution.py
@@ -156,19 +156,19 @@
     )(*[pltpu.with_memory_space_constraint(x, pltpu.HBM) for x in operands])
 
 
-def table_kernel(at, line, order, *refs):
+def own_kernel(at, line, order, *refs):
     shard_refs = dict(zip(order, refs))
     m_ref, leg_ref, _, table_ref, rows_ref, half_ref = refs[len(order) :]
     half_ref[...] = half_harmonics(leg_ref[...], shard_refs, at, line)
     write_table(table_ref, m_ref, lax.axis_index("mset"), at, line)
-    rows_ref[...] = map_rows(half_ref, 0, m_ref.shape[0]).astype(BF16)
+    rows_ref[...] = map_rows(half_ref, 0, rows_ref.shape[1] // 2).astype(BF16)
 
 
 def table_and_own(m_list, legendre, shards, after, at, line):
     n = m_list.shape[0]
     order = sorted(shards, key=lambda k: -(k >> at) % line)
     return pl.pallas_call(
-        functools.partial(table_kernel, at, line, order),
+        functools.partial(own_kernel, at, line, order),
         out_shape=[
             jax.ShapeDtypeStruct((2 * n, NPHI), BF16),
             jax.ShapeDtypeStruct((after.shape[0] * REAL, 2 * n), BF16),
@@ -179,7 +179,9 @@
         scratch_shapes=[pltpu.VMEM(after.shape, BF16)],
         compiler_params=pltpu.CompilerParams(vmem_limit_bytes=32 << 20),
         cost_estimate=pl.CostEstimate(
-            flops=16 * n * NPHI, bytes_accessed=4 * n * NPHI, transcendentals=0
+            flops=2 * legendre.size * after.shape[1] + 16 * n * NPHI,
+            bytes_accessed=4 * n * NPHI,
+            transcendentals=0,
         ),
         name="table_and_own",
     )(*[shards[k] for k in order], m_list, legendre, after)
@@ -228,21 +230,24 @@
     return jnp.concatenate(pieces, axis=1)
 
 
-def cross_kernel(at, line, order, *refs):
+def cross_kernel(at, line, order, bit, *refs):
     shard_refs = dict(zip(order, refs))
-    leg_ref, out_ref = refs[len(order) :]
-    out_ref[...] = half_harmonics(leg_ref[...], shard_refs, at, line)
-
-
-def cross(legendre, shards, at, line):
+    leg_ref, out_ref = refs[len(order)], refs[-1]
+
+    @pl.when((lax.axis_index("mset") >> at) & 1 == bit)
+    def _():
+        out_ref[...] = half_harmonics(leg_ref[...], shard_refs, at, line)
+
+
+def cross(legendre, shards, at, line, bit, after=()):
     rows, order_max = legendre.shape
     columns = shards[0].shape[0]
     count = len(shards)
     order = sorted(shards, key=lambda k: -(k >> at) % line)
     return pl.pallas_call(
-        functools.partial(cross_kernel, at, line, order),
+        functools.partial(cross_kernel, at, line, order, bit),
         out_shape=jax.ShapeDtypeStruct((rows // count, count * columns), BF16),
-        in_specs=[VMEM] * (1 + count),
+        in_specs=[VMEM] * (1 + count) + [pl.BlockSpec(memory_space=pl.ANY)] * len(after),
         out_specs=VMEM,
         compiler_params=pltpu.CompilerParams(vmem_limit_bytes=32 << 20),
         cost_estimate=pl.CostEstimate(
@@ -251,11 +256,18 @@
             transcendentals=0,
         ),
         name="cross",
-    )(*[shards[k] for k in order], legendre)
-
-
-def synthesis_kernel(tiles, own_ref, got_ref, table_ref, out_ref, held, sems):
+    )(*[shards[k] for k in order], legendre, *after)
+
+
+def synthesis_kernel(tiles, at, own_ref, low_ref, high_ref, table_ref, out_ref, held, got_ref, sems):
     n = table_ref.shape[0] // 2
+    own_bit = (lax.axis_index("mset") >> at) & 1
+    for bit, ref in enumerate((low_ref, high_ref)):
+
+        @pl.when(own_bit == bit)
+        def _():
+            got_ref[...] = ref[...]
+
     flat = (map_rows(got_ref, n // 2, n) + own_ref[...].astype(F32)).astype(BF16)
     width = NPHI // tiles
     copies = []
@@ -275,15 +287,19 @@
         copy.wait()
 
 
-def synthesize(own, got, table):
+def synthesize(own, low, high, table, at):
     tiles = 16
     out_rows = own.shape[0]
     return pl.pallas_call(
-        functools.partial(synthesis_kernel, tiles),
+        functools.partial(synthesis_kernel, tiles, at),
         out_shape=jax.ShapeDtypeStruct((out_rows, NPHI), BF16),
-        in_specs=[VMEM] * 3,
+        in_specs=[VMEM] * 4,
         out_specs=HBM,
-        scratch_shapes=[pltpu.VMEM((out_rows, NPHI), BF16), pltpu.SemaphoreType.DMA((tiles,))],
+        scratch_shapes=[
+            pltpu.VMEM((out_rows, NPHI), BF16),
+            pltpu.VMEM(low.shape, BF16),
+            pltpu.SemaphoreType.DMA((tiles,)),
+        ],
         compiler_params=pltpu.CompilerParams(vmem_limit_bytes=32 << 20),
         cost_estimate=pl.CostEstimate(
             flops=2 * out_rows * table.size,
@@ -291,7 +307,7 @@
             transcendentals=0,
         ),
         name="synthesis",
-    )(own, got, table)
+    )(own, low, high, table)
 
 
 def exchange(value, size, mask):
@@ -321,12 +337,15 @@
     filtered, keep, send = prepare(
         m_list, coeff[0], blocks[0], legendre.reshape(cycles * n, order_max), at
     )
+    bit = 1 << at
     shards = gather_shards(filtered, size, at, line)
-    got = exchange(send, size, 1 << at)
-    back = cross(got, shards, at, line)
-    other = exchange(back, size, 1 << at)
-    table, own_rows = table_and_own(m_list, keep, shards, back, at, line)
-    sky_map = synthesize(own_rows, other, table)
+    got = exchange(send, size, bit)
+    high = cross(got, shards, at, line, 1)
+    to_low = lax.ppermute(high, "mset", [(d, d ^ bit) for d in range(size) if d & bit])
+    low = cross(got, shards, at, line, 0, after=(high,))
+    to_high = lax.ppermute(low, "mset", [(d, d ^ bit) for d in range(size) if not d & bit])
+    table, own_rows = table_and_own(m_list, keep, shards, low, at, line)
+    sky_map = synthesize(own_rows, to_low, to_high, table, at)
     return sky_map.reshape(cycles, REAL, NPHI)
 
 

time: 24 us -> 27.2 us (1.13)
  starting transfers between devices: 10.7 us -> 15 us
  waiting for transfers between devices: 5.59 us -> 4.49 us
    ppermute x0 -> x2, starting transfers between devices: none -> 5.35 us  [the longest x1 4.07 us: body(): lax.ppermute(low, 'mset', [(d, d ^ bit) for d in range(size) if not d & b...]
    ppermute x6 -> x5, starting transfers between devices: 3.73 us -> 2.6 us  [exchange(): return lax.ppermute(value, 'mset', [(d, d ^ mask) for d in range(size)])]
    ppermute x6 -> x5, waiting for transfers between devices: 2.05 us -> 0.95 us  [exchange(): return lax.ppermute(value, 'mset', [(d, d ^ mask) for d in range(size)])]
    pallas_call x3 -> x4, Pallas kernels: 4.53 us -> 4.56 us  [the longest x1 2.62 us: synthesize(): pl.pallas_call(functools.partial(synthesis_kernel, tiles, at), out_shape=...]
  transfers between devices with their start and end apart: 9 -> 10, of which waited for: 4 -> 3; matrix products, arithmetic and copies ran while one was open for 0% -> 0% of each run, Pallas kernels for 6% -> 7%
where the time goes in v16:
time: 27.2 us; the launch traced here: 27 us
  starting transfers between devices  15 us (55%)
  Pallas kernels  7.47 us (27%)
  waiting for transfers between devices  4.49 us (17%)
    ppermute x3, starting transfers between devices, gather_shards(): shards[turn << at] = lax.ppermute(value, 'mset', pairs)  7.01 us
    ppermute x1, starting transfers between devices, body(): lax.ppermute(low, 'mset', [(d, d ^ bit) for d in range(size) if not d & b...  4.07 us
    ppermute x3, waiting for transfers between devices, gather_shards(): shards[turn << at] = lax.ppermute(value, 'mset', pairs)  3.53 us
    pallas_call x1, Pallas kernels, prepare(): pl.pallas_call(functools.partial(prepare_kernel, at), out_shape=[jax.Shap...  2.91 us
    pallas_call x1, Pallas kernels, synthesize(): pl.pallas_call(functools.partial(synthesis_kernel, tiles, at), out_shape=...  2.62 us
    ppermute x5, starting transfers between devices, exchange(): return lax.ppermute(value, 'mset', [(d, d ^ mask) for d in range(size)])  2.6 us
    pallas_call x1, Pallas kernels, table_and_own(): pl.pallas_call(functools.partial(own_kernel, at, line, order), out_shape=...  1.42 us
    ppermute x1, starting transfers between devices, body(): lax.ppermute(high, 'mset', [(d, d ^ bit) for d in range(size) if d & bit])  1.28 us
  transfers between devices with their start and end apart: 10, of which 3 were waited for; matrix products, arithmetic and copies ran while one was open for 0% of the time, Pallas kernels for 7%

profile of v16, /device:TPU:0, one launch (start us, length us, event | category | flops | bytes accessed | tf_op | source)
XLA Modules:
  0.0 27.0 jit_solution(12060765659926345083)
XLA Ops:
  0.0 2.9 %prepare.1 = (bf16[32,1536]{1,0:T(8,128)(2,1)S(1)}, bf16[128,1536]{1,0:T(8,128)(2,1)S(1)}, bf16[128,1536]{1,0:T(8,128)(2,1)S(1)}) custom-call(s32[16]{0:T(128)} %refs_8_.1, bf16[32,1536]{1,0:T(8,128)(2,1)} %bitcast.6, bf16[1536,1536]{1,0:T(8,128)(2,1)} %bitcast.4, bf16[256,1536]{1,0:T(8,128)(2,1)} %bitcast.5), custom_call_target="tpu_custom_call" | custom-call | flops 352321536 | bytes 5505024 | tf_op jit(solution)/shard_map/prepare/pallas_call | solution.py:133
  2.9 3.1 %collective-permute-start.5 = (bf16[32,1536]{1,0:T(8,128)(2,1)S(1)}, bf16[32,1536]{1,0:T(8,128)(2,1)S(1)}, u32[]{:S(2)}, u32[]{:S(2)}) collective-permute-start(bf16[32,1536]{1,0:T(8,128)(2,1)S(1)} %get-tuple-element.10.refs_0_), channel_id=1, source_target_pairs={{0,4},{1,5},{2,6},{3,7},{4,8},{5,9},{6,10},{7,11},{8,12},{9,13},{1... | collective-permute-start | bytes 294920 | tf_op jit(solution)/shard_map/ppermute | solution.py:322
  6.0 0.0 copy-start
  6.0 1.5 %collective-permute-start.7 = (bf16[128,1536]{1,0:T(8,128)(2,1)S(1)}, bf16[128,1536]{1,0:T(8,128)(2,1)S(1)}, u32[]{:S(2)}, u32[]{:S(2)}) collective-permute-start(bf16[128,1536]{1,0:T(8,128)(2,1)S(1)} %get-tuple-element.12), channel_id=1, source_target_pairs={{0,2},{1,3},{2,0},{3,1},{4,6},{5,7},{6,4},{7,5},{8,10},{9,11},{10,... | collective-permute-start | bytes 1179656 | tf_op jit(solution)/shard_map/ppermute | solution.py:314
  7.5 2.6 %collective-permute-start.3 = (bf16[32,1536]{1,0:T(8,128)(2,1)S(1)}, bf16[32,1536]{1,0:T(8,128)(2,1)S(1)}, u32[]{:S(2)}, u32[]{:S(2)}) collective-permute-start(bf16[32,1536]{1,0:T(8,128)(2,1)S(1)} %get-tuple-element.10.refs_0_), channel_id=1, source_target_pairs={{0,8},{1,9},{2,10},{3,11},{4,12},{5,13},{6,14},{7,15},{8,0},{9,1},... | collective-permute-start | bytes 294920 | tf_op jit(solution)/shard_map/ppermute | solution.py:322
  10.1 1.3 %collective-permute-start.1 = (bf16[32,1536]{1,0:T(8,128)(2,1)S(1)}, bf16[32,1536]{1,0:T(8,128)(2,1)S(1)}, u32[]{:S(2)}, u32[]{:S(2)}) collective-permute-start(bf16[32,1536]{1,0:T(8,128)(2,1)S(1)} %get-tuple-element.10.refs_0_), channel_id=1, source_target_pairs={{0,12},{1,13},{2,14},{3,15},{4,0},{5,1},{6,2},{7,3},{8,4},{9,5},{1... | collective-permute-start | bytes 294920 | tf_op jit(solution)/shard_map/ppermute | solution.py:322
  11.5 0.0 collective-permute-start
  11.5 0.0 collective-permute-done.5.shard_ref
  11.5 0.6 %collective-permute-start.6 = (bf16[32,1536]{1,0:T(8,128)(2,1)S(1)}, bf16[32,1536]{1,0:T(8,128)(2,1)S(1)}, u32[]{:S(2)}, u32[]{:S(2)}) collective-permute-start(bf16[32,1536]{1,0:T(8,128)(2,1)S(1)} %relay.1.refs_6_), channel_id=1, source_target_pairs={{0,1},{1,0},{2,3},{3,2},{4,5},{5,4},{6,7},{7,6},{8,9},{9,8},{10,11... | collective-permute-start | bytes 294920 | tf_op jit(solution)/shard_map/ppermute | solution.py:314
  12.0 3.5 %collective-permute-done.3.refs_4_ = bf16[32,1536]{1,0:T(8,128)(2,1)S(1)} collective-permute-done((bf16[32,1536]{1,0:T(8,128)(2,1)S(1)}, bf16[32,1536]{1,0:T(8,128)(2,1)S(1)}, u32[]{:S(2)}, u32[]{:S(2)}) %collective-permute-start.3) | collective-permute-done | bytes 98336 | tf_op jit(solution)/shard_map/ppermute | solution.py:322
  15.6 0.0 collective-permute-start.4
  15.6 0.0 collective-permute-done.1.refs_2_
  15.6 0.5 %collective-permute-start.2 = (bf16[32,1536]{1,0:T(8,128)(2,1)S(1)}, bf16[32,1536]{1,0:T(8,128)(2,1)S(1)}, u32[]{:S(2)}, u32[]{:S(2)}) collective-permute-start(bf16[32,1536]{1,0:T(8,128)(2,1)S(1)} %collective-permute-done.1.refs_2_), channel_id=1, source_target_pairs={{0,1},{1,0},{2,3},{3,2},{4,5},{5,4},{6,7},{7,6},{8,9},{9,8},{10,11... | collective-permute-start | bytes 294920 | tf_op jit(solution)/shard_map/ppermute | solution.py:314
  16.1 0.0 collective-permute-done.refs_1_
  16.1 0.0 collective-permute-done.6.refs_7_
  16.1 0.8 %collective-permute-done.4.refs_5_ = bf16[32,1536]{1,0:T(8,128)(2,1)S(1)} collective-permute-done((bf16[32,1536]{1,0:T(8,128)(2,1)S(1)}, bf16[32,1536]{1,0:T(8,128)(2,1)S(1)}, u32[]{:S(2)}, u32[]{:S(2)}) %collective-permute-start.4) | collective-permute-done | bytes 98336 | tf_op jit(solution)/shard_map/ppermute | solution.py:314
  16.9 0.2 collective-permute-done.2.refs_3_
  17.0 0.0 collective-permute-done.7.refs_8_
  17.0 1.3 %collective-permute-start.8 = (bf16[16,256]{1,0:T(8,128)(2,1)S(1)}, bf16[16,256]{1,0:T(8,128)(2,1)S(1)}, u32[]{:S(2)}, u32[]{:S(2)}) collective-permute-start(bf16[16,256]{1,0:T(8,128)(2,1)S(1)} %cross.2.refs_9_), channel_id=1, source_target_pairs={{2,0},{3,1},{6,4},{7,5},{10,8},{11,9},{14,12},{15,13},{18,16},{19,... | collective-permute-start | bytes 24584 | tf_op jit(solution)/shard_map/ppermute | solution.py:344
  18.3 0.5 %cross.3.refs_10_ = bf16[16,256]{1,0:T(8,128)(2,1)S(1)} custom-call(bf16[32,1536]{1,0:T(8,128)(2,1)S(1)} %get-tuple-element.10.refs_0_, bf16[32,1536]{1,0:T(8,128)(2,1)S(1)} %collective-permute-done.refs_1_, bf16[32,1536]{1,0:T(8,128)(2,1)S(1)} %collective-permute-done.1.refs_2_, bf16[32,1536]{1,0:T(8,128)(2,1)S(1)} %collective-permute-done.2.refs_3_, ...), custom_call_target="tpu_custom_call" | custom-call | flops 100663296 | bytes 1179648 | tf_op jit(solution)/shard_map/cross/pallas_call | solution.py:247
  18.8 4.1 %collective-permute-start.9 = (bf16[16,256]{1,0:T(8,128)(2,1)S(1)}, bf16[16,256]{1,0:T(8,128)(2,1)S(1)}, u32[]{:S(2)}, u32[]{:S(2)}) collective-permute-start(bf16[16,256]{1,0:T(8,128)(2,1)S(1)} %cross.3.refs_10_), channel_id=1, source_target_pairs={{0,2},{1,3},{4,6},{5,7},{8,10},{9,11},{12,14},{13,15},{16,18},{17,... | collective-permute-start | bytes 24584 | tf_op jit(solution)/shard_map/ppermute | solution.py:346
  22.9 0.0 copy-done
  22.9 1.4 %table_and_own.1 = (bf16[32,8192]{1,0:T(8,128)(2,1)S(1)}, bf16[256,32]{1,0:T(8,128)(2,1)S(1)}) custom-call(bf16[32,1536]{1,0:T(8,128)(2,1)S(1)} %get-tuple-element.10.refs_0_, bf16[32,1536]{1,0:T(8,128)(2,1)S(1)} %collective-permute-done.refs_1_, bf16[32,1536]{1,0:T(8,128)(2,1)S(1)} %collective-permute-done.1.refs_2_, ...), custom_call_target="tpu_custom_call" | custom-call | flops 102760448 | bytes 524288 | tf_op jit(solution)/shard_map/table_and_own/pallas_call | solution.py:170
  24.4 0.0 collective-permute-done.9.high_ref
  24.4 0.0 collective-permute-done.8.low_ref
  24.4 2.6 %synthesis.1 = bf16[256,8192]{1,0:T(8,128)(2,1)} custom-call(bf16[256,32]{1,0:T(8,128)(2,1)S(1)} %get-tuple-element.13.own_ref, bf16[16,256]{1,0:T(8,128)(2,1)S(1)} %collective-permute-done.8.low_ref, bf16[16,256]{1,0:T(8,128)(2,1)S(1)} %collective-permute-done.9.high_ref, bf16[32,8192]{1,0:T(8,128)(2,1)S(1)} %get-tuple-element.14.table_ref), custom_call_target="tpu_custom_call" | custom-call | flops 134217728 | bytes 4718592 | tf_op jit(solution)/shard_map/synthesis/pallas_call | solution.py:293
  (2 shorter events, 0.0 us)
Async XLA Ops:
  2.9 8.5 %collective-permute-start.5 = (bf16[32,1536]{1,0:T(8,128)(2,1)S(1)}, bf16[32,1536]{1,0:T(8,128)(2,1)S(1)}, u32[]{:S(2)}, u32[]{:S(2)}) collective-permute-start(bf16[32,1536]{1,0:T(8,128)(2,1)S(1)} %get-tuple-element.10.refs_0_), channel_id=1, source_target_pairs={{0,4},{1,5},{2,6},{3,7},{4,8},{5,9},{6,10},{7,11},{8,12},{9,13},{1... | collective-permute-start | bytes 294920 | tf_op jit(solution)/shard_map/ppermute | solution.py:322
  6.0 16.9 %copy-start = (s32[16]{0:T(128)S(1)}, s32[16]{0:T(128)}, u32[]{:S(2)}) copy-start(s32[16]{0:T(128)} %refs_8_.1) | copy-start | bytes 196
  6.0 11.0 %collective-permute-start.7 = (bf16[128,1536]{1,0:T(8,128)(2,1)S(1)}, bf16[128,1536]{1,0:T(8,128)(2,1)S(1)}, u32[]{:S(2)}, u32[]{:S(2)}) collective-permute-start(bf16[128,1536]{1,0:T(8,128)(2,1)S(1)} %get-tuple-element.12), channel_id=1, source_target_pairs={{0,2},{1,3},{2,0},{3,1},{4,6},{5,7},{6,4},{7,5},{8,10},{9,11},{10,... | collective-permute-start | bytes 1179656 | tf_op jit(solution)/shard_map/ppermute | solution.py:314
  7.5 8.1 %collective-permute-start.3 = (bf16[32,1536]{1,0:T(8,128)(2,1)S(1)}, bf16[32,1536]{1,0:T(8,128)(2,1)S(1)}, u32[]{:S(2)}, u32[]{:S(2)}) collective-permute-start(bf16[32,1536]{1,0:T(8,128)(2,1)S(1)} %get-tuple-element.10.refs_0_), channel_id=1, source_target_pairs={{0,8},{1,9},{2,10},{3,11},{4,12},{5,13},{6,14},{7,15},{8,0},{9,1},... | collective-permute-start | bytes 294920 | tf_op jit(solution)/shard_map/ppermute | solution.py:322
  10.1 5.5 %collective-permute-start.1 = (bf16[32,1536]{1,0:T(8,128)(2,1)S(1)}, bf16[32,1536]{1,0:T(8,128)(2,1)S(1)}, u32[]{:S(2)}, u32[]{:S(2)}) collective-permute-start(bf16[32,1536]{1,0:T(8,128)(2,1)S(1)} %get-tuple-element.10.refs_0_), channel_id=1, source_target_pairs={{0,12},{1,13},{2,14},{3,15},{4,0},{5,1},{6,2},{7,3},{8,4},{9,5},{1... | collective-permute-start | bytes 294920 | tf_op jit(solution)/shard_map/ppermute | solution.py:322
  11.5 4.6 %collective-permute-start = (bf16[32,1536]{1,0:T(8,128)(2,1)S(1)}, bf16[32,1536]{1,0:T(8,128)(2,1)S(1)}, u32[]{:S(2)}, u32[]{:S(2)}) collective-permute-start(bf16[32,1536]{1,0:T(8,128)(2,1)S(1)} %get-tuple-element.10.refs_0_), channel_id=1, source_target_pairs={{0,1},{1,0},{2,3},{3,2},{4,5},{5,4},{6,7},{7,6},{8,9},{9,8},{10,11... | collective-permute-start | bytes 294920 | tf_op jit(solution)/shard_map/ppermute | solution.py:314
  11.5 4.6 %collective-permute-start.6 = (bf16[32,1536]{1,0:T(8,128)(2,1)S(1)}, bf16[32,1536]{1,0:T(8,128)(2,1)S(1)}, u32[]{:S(2)}, u32[]{:S(2)}) collective-permute-start(bf16[32,1536]{1,0:T(8,128)(2,1)S(1)} %relay.1.refs_6_), channel_id=1, source_target_pairs={{0,1},{1,0},{2,3},{3,2},{4,5},{5,4},{6,7},{7,6},{8,9},{9,8},{10,11... | collective-permute-start | bytes 294920 | tf_op jit(solution)/shard_map/ppermute | solution.py:314
  15.6 1.3 %collective-permute-start.4 = (bf16[32,1536]{1,0:T(8,128)(2,1)S(1)}, bf16[32,1536]{1,0:T(8,128)(2,1)S(1)}, u32[]{:S(2)}, u32[]{:S(2)}) collective-permute-start(bf16[32,1536]{1,0:T(8,128)(2,1)S(1)} %collective-permute-done.3.refs_4_), channel_id=1, source_target_pairs={{0,1},{1,0},{2,3},{3,2},{4,5},{5,4},{6,7},{7,6},{8,9},{9,8},{10,11... | collective-permute-start | bytes 294920 | tf_op jit(solution)/shard_map/ppermute | solution.py:314
  15.6 1.5 %collective-permute-start.2 = (bf16[32,1536]{1,0:T(8,128)(2,1)S(1)}, bf16[32,1536]{1,0:T(8,128)(2,1)S(1)}, u32[]{:S(2)}, u32[]{:S(2)}) collective-permute-start(bf16[32,1536]{1,0:T(8,128)(2,1)S(1)} %collective-permute-done.1.refs_2_), channel_id=1, source_target_pairs={{0,1},{1,0},{2,3},{3,2},{4,5},{5,4},{6,7},{7,6},{8,9},{9,8},{10,11... | collective-permute-start | bytes 294920 | tf_op jit(solution)/shard_map/ppermute | solution.py:314
  17.0 7.3 %collective-permute-start.8 = (bf16[16,256]{1,0:T(8,128)(2,1)S(1)}, bf16[16,256]{1,0:T(8,128)(2,1)S(1)}, u32[]{:S(2)}, u32[]{:S(2)}) collective-permute-start(bf16[16,256]{1,0:T(8,128)(2,1)S(1)} %cross.2.refs_9_), channel_id=1, source_target_pairs={{2,0},{3,1},{6,4},{7,5},{10,8},{11,9},{14,12},{15,13},{18,16},{19,... | collective-permute-start | bytes 24584 | tf_op jit(solution)/shard_map/ppermute | solution.py:344
  18.8 5.5 %collective-permute-start.9 = (bf16[16,256]{1,0:T(8,128)(2,1)S(1)}, bf16[16,256]{1,0:T(8,128)(2,1)S(1)}, u32[]{:S(2)}, u32[]{:S(2)}) collective-permute-start(bf16[16,256]{1,0:T(8,128)(2,1)S(1)} %cross.3.refs_10_), channel_id=1, source_target_pairs={{0,2},{1,3},{4,6},{5,7},{8,10},{9,11},{12,14},{13,15},{16,18},{17,... | collective-permute-start | bytes 24584 | tf_op jit(solution)/shard_map/ppermute | solution.py:346

commit v17 on v12

--- a/solution.py
+++ b/solution.py
@@ -21,6 +21,14 @@
 
 def iota(shape, dim):
     return lax.broadcasted_iota(jnp.int32, shape, dim)
+
+
+def div(value, size):
+    return value >> (size.bit_length() - 1) if size & (size - 1) == 0 else value // size
+
+
+def mod(value, size):
+    return value & (size - 1) if size & (size - 1) == 0 else lax.rem(value, size)
 
 
 def insert_bit(value, bit, at):
@@ -65,12 +73,12 @@
 def map_rows(half_ref, first, total):
     cycles, wide = half_ref.shape
     rows = cycles * REAL
-    repeat = (iota((rows, cycles), 0) // REAL == iota((rows, cycles), 1)).astype(BF16)
+    repeat = (div(iota((rows, cycles), 0), REAL) == iota((rows, cycles), 1)).astype(BF16)
     spread = jnp.dot(repeat, half_ref[...], preferred_element_type=F32)
-    same_real = lax.rem(iota((rows, wide), 0), REAL) == lax.rem(iota((rows, wide), 1), REAL)
+    same_real = mod(iota((rows, wide), 0), REAL) == mod(iota((rows, wide), 1), REAL)
     chosen = jnp.where(same_real, spread, 0.0).astype(BF16)
     row, col = iota((wide, 2 * total), 0), iota((wide, 2 * total), 1)
-    pick = lax.rem(row, 2 * REAL) // REAL * total + first + row // (2 * REAL) == col
+    pick = div(mod(row, 2 * REAL), REAL) * total + first + div(row, 2 * REAL) == col
     return jnp.dot(chosen, pick.astype(BF16), preferred_element_type=F32)
 
 
@@ -99,10 +107,10 @@
     half = rows // 2
     own_bit = (me >> at) & 1
     row, col = iota((rows, rows), 0), iota((rows, rows), 1)
-    bit = own_bit ^ (row // half)
-    slot = lax.rem(row, n // 2)
-    pick = (lax.rem(row, half) // (n // 2) == col // n) & (
-        insert_bit(slot, bit, at) == lax.rem(col, n)
+    bit = own_bit ^ div(row, half)
+    slot = mod(row, n // 2)
+    pick = (div(mod(row, half), n // 2) == div(col, n)) & (
+        insert_bit(slot, bit, at) == mod(col, n)
     )
     pick = pick.astype(BF16)
     copy_leg.wait()
@@ -210,9 +218,9 @@
     cycles = rows // shards
     chunk = min(8, shards)
     wide = chunk * columns
-    slot = lax.rem(iota((rows, wide), 0), shards)
-    local = iota((rows, wide), 1) // columns
-    fold = (iota((cycles, rows), 0) == iota((cycles, rows), 1) // shards).astype(BF16)
+    slot = mod(iota((rows, wide), 0), shards)
+    local = div(iota((rows, wide), 1), columns)
+    fold = (iota((cycles, rows), 0) == div(iota((cycles, rows), 1), shards)).astype(BF16)
     me = lax.axis_index("mset")
     pieces = []
     for q in range(shards // chunk):

time: 24 us -> 24 us (level)
  no operation moved by 1% of the time
where the time goes in v17:
time: 24 us; the launch traced here: 23.8 us
  starting transfers between devices  10.7 us (45%)
  Pallas kernels  7.45 us (31%)
  waiting for transfers between devices  5.59 us (23%)
    ppermute x3, starting transfers between devices, gather_shards(): shards[turn << at] = lax.ppermute(value, 'mset', pairs)  7.01 us
    ppermute x6, starting transfers between devices, exchange(): return lax.ppermute(value, 'mset', [(d, d ^ mask) for d in range(size)])  3.73 us
    ppermute x3, waiting for transfers between devices, gather_shards(): shards[turn << at] = lax.ppermute(value, 'mset', pairs)  3.54 us
    pallas_call x1, Pallas kernels, prepare(): pl.pallas_call(functools.partial(prepare_kernel, at), out_shape=[jax.Shap...  2.91 us
    pallas_call x1, Pallas kernels, synthesize(): pl.pallas_call(functools.partial(synthesis_kernel, tiles), out_shape=jax....  2.61 us
    ppermute x6, waiting for transfers between devices, exchange(): return lax.ppermute(value, 'mset', [(d, d ^ mask) for d in range(size)])  2.05 us
    pallas_call x1, Pallas kernels, table_and_own(): pl.pallas_call(functools.partial(table_kernel, at, line, order), out_shap...  1.42 us
    pallas_call x1, Pallas kernels, cross(): pl.pallas_call(functools.partial(cross_kernel, at, line, order), out_shap...  0.5 us
  transfers between devices with their start and end apart: 9, of which 4 were waited for; matrix products, arithmetic and copies ran while one was open for 0% of the time, Pallas kernels for 6%

profile of v17, /device:TPU:0, one launch (start us, length us, event | category | flops | bytes accessed | tf_op | source)
XLA Modules:
  0.0 23.8 jit_solution(11433916622979542209)
XLA Ops:
  0.0 2.9 %prepare.1 = (bf16[32,1536]{1,0:T(8,128)(2,1)S(1)}, bf16[128,1536]{1,0:T(8,128)(2,1)S(1)}, bf16[128,1536]{1,0:T(8,128)(2,1)S(1)}) custom-call(s32[16]{0:T(128)} %refs_8_.1, bf16[32,1536]{1,0:T(8,128)(2,1)} %bitcast.6, bf16[1536,1536]{1,0:T(8,128)(2,1)} %bitcast.4, bf16[256,1536]{1,0:T(8,128)(2,1)} %bitcast.5), custom_call_target="tpu_custom_call" | custom-call | flops 352321536 | bytes 5505024 | tf_op jit(solution)/shard_map/prepare/pallas_call | solution.py:141
  2.9 3.1 %collective-permute-start.5 = (bf16[32,1536]{1,0:T(8,128)(2,1)S(1)}, bf16[32,1536]{1,0:T(8,128)(2,1)S(1)}, u32[]{:S(2)}, u32[]{:S(2)}) collective-permute-start(bf16[32,1536]{1,0:T(8,128)(2,1)S(1)} %get-tuple-element.10.refs_0_), channel_id=1, source_target_pairs={{0,4},{1,5},{2,6},{3,7},{4,8},{5,9},{6,10},{7,11},{8,12},{9,13},{1... | collective-permute-start | bytes 294920 | tf_op jit(solution)/shard_map/ppermute | solution.py:314
  6.0 0.0 copy-start
  6.0 1.5 %collective-permute-start.7 = (bf16[128,1536]{1,0:T(8,128)(2,1)S(1)}, bf16[128,1536]{1,0:T(8,128)(2,1)S(1)}, u32[]{:S(2)}, u32[]{:S(2)}) collective-permute-start(bf16[128,1536]{1,0:T(8,128)(2,1)S(1)} %get-tuple-element.12), channel_id=1, source_target_pairs={{0,2},{1,3},{2,0},{3,1},{4,6},{5,7},{6,4},{7,5},{8,10},{9,11},{10,... | collective-permute-start | bytes 1179656 | tf_op jit(solution)/shard_map/ppermute | solution.py:306
  7.5 2.6 %collective-permute-start.3 = (bf16[32,1536]{1,0:T(8,128)(2,1)S(1)}, bf16[32,1536]{1,0:T(8,128)(2,1)S(1)}, u32[]{:S(2)}, u32[]{:S(2)}) collective-permute-start(bf16[32,1536]{1,0:T(8,128)(2,1)S(1)} %get-tuple-element.10.refs_0_), channel_id=1, source_target_pairs={{0,8},{1,9},{2,10},{3,11},{4,12},{5,13},{6,14},{7,15},{8,0},{9,1},... | collective-permute-start | bytes 294920 | tf_op jit(solution)/shard_map/ppermute | solution.py:314
  10.1 1.3 %collective-permute-start.1 = (bf16[32,1536]{1,0:T(8,128)(2,1)S(1)}, bf16[32,1536]{1,0:T(8,128)(2,1)S(1)}, u32[]{:S(2)}, u32[]{:S(2)}) collective-permute-start(bf16[32,1536]{1,0:T(8,128)(2,1)S(1)} %get-tuple-element.10.refs_0_), channel_id=1, source_target_pairs={{0,12},{1,13},{2,14},{3,15},{4,0},{5,1},{6,2},{7,3},{8,4},{9,5},{1... | collective-permute-start | bytes 294920 | tf_op jit(solution)/shard_map/ppermute | solution.py:314
  11.5 0.0 collective-permute-start
  11.5 0.0 collective-permute-done.5.shard_ref
  11.5 0.6 %collective-permute-start.6 = (bf16[32,1536]{1,0:T(8,128)(2,1)S(1)}, bf16[32,1536]{1,0:T(8,128)(2,1)S(1)}, u32[]{:S(2)}, u32[]{:S(2)}) collective-permute-start(bf16[32,1536]{1,0:T(8,128)(2,1)S(1)} %relay.1.refs_6_), channel_id=1, source_target_pairs={{0,1},{1,0},{2,3},{3,2},{4,5},{5,4},{6,7},{7,6},{8,9},{9,8},{10,11... | collective-permute-start | bytes 294920 | tf_op jit(solution)/shard_map/ppermute | solution.py:306
  12.0 3.5 %collective-permute-done.3.refs_4_ = bf16[32,1536]{1,0:T(8,128)(2,1)S(1)} collective-permute-done((bf16[32,1536]{1,0:T(8,128)(2,1)S(1)}, bf16[32,1536]{1,0:T(8,128)(2,1)S(1)}, u32[]{:S(2)}, u32[]{:S(2)}) %collective-permute-start.3) | collective-permute-done | bytes 98336 | tf_op jit(solution)/shard_map/ppermute | solution.py:314
  15.6 0.0 collective-permute-start.4
  15.6 0.0 collective-permute-done.1.refs_2_
  15.6 0.5 %collective-permute-start.2 = (bf16[32,1536]{1,0:T(8,128)(2,1)S(1)}, bf16[32,1536]{1,0:T(8,128)(2,1)S(1)}, u32[]{:S(2)}, u32[]{:S(2)}) collective-permute-start(bf16[32,1536]{1,0:T(8,128)(2,1)S(1)} %collective-permute-done.1.refs_2_), channel_id=1, source_target_pairs={{0,1},{1,0},{2,3},{3,2},{4,5},{5,4},{6,7},{7,6},{8,9},{9,8},{10,11... | collective-permute-start | bytes 294920 | tf_op jit(solution)/shard_map/ppermute | solution.py:306
  16.1 0.0 collective-permute-done.refs_1_
  16.1 0.0 collective-permute-done.6.refs_7_
  16.1 0.8 %collective-permute-done.4.refs_5_ = bf16[32,1536]{1,0:T(8,128)(2,1)S(1)} collective-permute-done((bf16[32,1536]{1,0:T(8,128)(2,1)S(1)}, bf16[32,1536]{1,0:T(8,128)(2,1)S(1)}, u32[]{:S(2)}, u32[]{:S(2)}) %collective-permute-start.4) | collective-permute-done | bytes 98336 | tf_op jit(solution)/shard_map/ppermute | solution.py:306
  16.9 0.2 collective-permute-done.2.refs_3_
  17.0 0.0 collective-permute-done.7.refs_8_
  17.0 0.5 %cross.1.refs_10_ = bf16[16,256]{1,0:T(8,128)(2,1)S(1)} custom-call(bf16[32,1536]{1,0:T(8,128)(2,1)S(1)} %get-tuple-element.10.refs_0_, bf16[32,1536]{1,0:T(8,128)(2,1)S(1)} %collective-permute-done.refs_1_, bf16[32,1536]{1,0:T(8,128)(2,1)S(1)} %collective-permute-done.1.refs_2_, bf16[32,1536]{1,0:T(8,128)(2,1)S(1)} %collective-permute-done.2.refs_3_, ...), custom_call_target="tpu_custom_call" | custom-call | flops 100663296 | bytes 1179648 | tf_op jit(solution)/shard_map/cross/pallas_call | solution.py:250
  17.5 1.1 %collective-permute-start.8 = (bf16[16,256]{1,0:T(8,128)(2,1)S(1)}, bf16[16,256]{1,0:T(8,128)(2,1)S(1)}, u32[]{:S(2)}, u32[]{:S(2)}) collective-permute-start(bf16[16,256]{1,0:T(8,128)(2,1)S(1)} %cross.1.refs_10_), channel_id=1, source_target_pairs={{0,2},{1,3},{2,0},{3,1},{4,6},{5,7},{6,4},{7,5},{8,10},{9,11},{10,... | collective-permute-start | bytes 24584 | tf_op jit(solution)/shard_map/ppermute | solution.py:306
  18.7 0.0 copy-done
  18.7 1.4 %table_and_own.1 = (bf16[32,8192]{1,0:T(8,128)(2,1)S(1)}, bf16[256,32]{1,0:T(8,128)(2,1)S(1)}) custom-call(bf16[32,1536]{1,0:T(8,128)(2,1)S(1)} %get-tuple-element.10.refs_0_, bf16[32,1536]{1,0:T(8,128)(2,1)S(1)} %collective-permute-done.refs_1_, bf16[32,1536]{1,0:T(8,128)(2,1)S(1)} %collective-permute-done.1.refs_2_, ...), custom_call_target="tpu_custom_call" | custom-call | flops 2097152 | bytes 524288 | tf_op jit(solution)/shard_map/table_and_own/pallas_call | solution.py:178
  20.1 1.1 %collective-permute-done.8.got_ref = bf16[16,256]{1,0:T(8,128)(2,1)S(1)} collective-permute-done((bf16[16,256]{1,0:T(8,128)(2,1)S(1)}, bf16[16,256]{1,0:T(8,128)(2,1)S(1)}, u32[]{:S(2)}, u32[]{:S(2)}) %collective-permute-start.8) | collective-permute-done | bytes 8224 | tf_op jit(solution)/shard_map/ppermute | solution.py:306
  21.2 2.6 %synthesis.1 = bf16[256,8192]{1,0:T(8,128)(2,1)} custom-call(bf16[256,32]{1,0:T(8,128)(2,1)S(1)} %get-tuple-element.13.own_ref, bf16[16,256]{1,0:T(8,128)(2,1)S(1)} %collective-permute-done.8.got_ref, bf16[32,8192]{1,0:T(8,128)(2,1)S(1)} %get-tuple-element.14.table_ref), custom_call_target="tpu_custom_call" | custom-call | flops 134217728 | bytes 4718592 | tf_op jit(solution)/shard_map/synthesis/pallas_call | solution.py:289
  (1 shorter events, 0.0 us)
Async XLA Ops:
  2.9 8.5 %collective-permute-start.5 = (bf16[32,1536]{1,0:T(8,128)(2,1)S(1)}, bf16[32,1536]{1,0:T(8,128)(2,1)S(1)}, u32[]{:S(2)}, u32[]{:S(2)}) collective-permute-start(bf16[32,1536]{1,0:T(8,128)(2,1)S(1)} %get-tuple-element.10.refs_0_), channel_id=1, source_target_pairs={{0,4},{1,5},{2,6},{3,7},{4,8},{5,9},{6,10},{7,11},{8,12},{9,13},{1... | collective-permute-start | bytes 294920 | tf_op jit(solution)/shard_map/ppermute | solution.py:314
  6.0 12.7 %copy-start = (s32[16]{0:T(128)S(1)}, s32[16]{0:T(128)}, u32[]{:S(2)}) copy-start(s32[16]{0:T(128)} %refs_8_.1) | copy-start | bytes 196
  6.0 11.0 %collective-permute-start.7 = (bf16[128,1536]{1,0:T(8,128)(2,1)S(1)}, bf16[128,1536]{1,0:T(8,128)(2,1)S(1)}, u32[]{:S(2)}, u32[]{:S(2)}) collective-permute-start(bf16[128,1536]{1,0:T(8,128)(2,1)S(1)} %get-tuple-element.12), channel_id=1, source_target_pairs={{0,2},{1,3},{2,0},{3,1},{4,6},{5,7},{6,4},{7,5},{8,10},{9,11},{10,... | collective-permute-start | bytes 1179656 | tf_op jit(solution)/shard_map/ppermute | solution.py:306
  7.5 8.1 %collective-permute-start.3 = (bf16[32,1536]{1,0:T(8,128)(2,1)S(1)}, bf16[32,1536]{1,0:T(8,128)(2,1)S(1)}, u32[]{:S(2)}, u32[]{:S(2)}) collective-permute-start(bf16[32,1536]{1,0:T(8,128)(2,1)S(1)} %get-tuple-element.10.refs_0_), channel_id=1, source_target_pairs={{0,8},{1,9},{2,10},{3,11},{4,12},{5,13},{6,14},{7,15},{8,0},{9,1},... | collective-permute-start | bytes 294920 | tf_op jit(solution)/shard_map/ppermute | solution.py:314
  10.1 5.5 %collective-permute-start.1 = (bf16[32,1536]{1,0:T(8,128)(2,1)S(1)}, bf16[32,1536]{1,0:T(8,128)(2,1)S(1)}, u32[]{:S(2)}, u32[]{:S(2)}) collective-permute-start(bf16[32,1536]{1,0:T(8,128)(2,1)S(1)} %get-tuple-element.10.refs_0_), channel_id=1, source_target_pairs={{0,12},{1,13},{2,14},{3,15},{4,0},{5,1},{6,2},{7,3},{8,4},{9,5},{1... | collective-permute-start | bytes 294920 | tf_op jit(solution)/shard_map/ppermute | solution.py:314
  11.5 4.6 %collective-permute-start = (bf16[32,1536]{1,0:T(8,128)(2,1)S(1)}, bf16[32,1536]{1,0:T(8,128)(2,1)S(1)}, u32[]{:S(2)}, u32[]{:S(2)}) collective-permute-start(bf16[32,1536]{1,0:T(8,128)(2,1)S(1)} %get-tuple-element.10.refs_0_), channel_id=1, source_target_pairs={{0,1},{1,0},{2,3},{3,2},{4,5},{5,4},{6,7},{7,6},{8,9},{9,8},{10,11... | collective-permute-start | bytes 294920 | tf_op jit(solution)/shard_map/ppermute | solution.py:306
  11.5 4.6 %collective-permute-start.6 = (bf16[32,1536]{1,0:T(8,128)(2,1)S(1)}, bf16[32,1536]{1,0:T(8,128)(2,1)S(1)}, u32[]{:S(2)}, u32[]{:S(2)}) collective-permute-start(bf16[32,1536]{1,0:T(8,128)(2,1)S(1)} %relay.1.refs_6_), channel_id=1, source_target_pairs={{0,1},{1,0},{2,3},{3,2},{4,5},{5,4},{6,7},{7,6},{8,9},{9,8},{10,11... | collective-permute-start | bytes 294920 | tf_op jit(solution)/shard_map/ppermute | solution.py:306
  15.6 1.3 %collective-permute-start.4 = (bf16[32,1536]{1,0:T(8,128)(2,1)S(1)}, bf16[32,1536]{1,0:T(8,128)(2,1)S(1)}, u32[]{:S(2)}, u32[]{:S(2)}) collective-permute-start(bf16[32,1536]{1,0:T(8,128)(2,1)S(1)} %collective-permute-done.3.refs_4_), channel_id=1, source_target_pairs={{0,1},{1,0},{2,3},{3,2},{4,5},{5,4},{6,7},{7,6},{8,9},{9,8},{10,11... | collective-permute-start | bytes 294920 | tf_op jit(solution)/shard_map/ppermute | solution.py:306
  15.6 1.5 %collective-permute-start.2 = (bf16[32,1536]{1,0:T(8,128)(2,1)S(1)}, bf16[32,1536]{1,0:T(8,128)(2,1)S(1)}, u32[]{:S(2)}, u32[]{:S(2)}) collective-permute-start(bf16[32,1536]{1,0:T(8,128)(2,1)S(1)} %collective-permute-done.1.refs_2_), channel_id=1, source_target_pairs={{0,1},{1,0},{2,3},{3,2},{4,5},{5,4},{6,7},{7,6},{8,9},{9,8},{10,11... | collective-permute-start | bytes 294920 | tf_op jit(solution)/shard_map/ppermute | solution.py:306
  17.5 3.7 %collective-permute-start.8 = (bf16[16,256]{1,0:T(8,128)(2,1)S(1)}, bf16[16,256]{1,0:T(8,128)(2,1)S(1)}, u32[]{:S(2)}, u32[]{:S(2)}) collective-permute-start(bf16[16,256]{1,0:T(8,128)(2,1)S(1)} %cross.1.refs_10_), channel_id=1, source_target_pairs={{0,2},{1,3},{2,0},{3,1},{4,6},{5,7},{6,4},{7,5},{8,10},{9,11},{10,... | collective-permute-start | bytes 24584 | tf_op jit(solution)/shard_map/ppermute | solution.py:306

commit v18 on v12

--- a/solution.py
+++ b/solution.py
@@ -76,12 +76,13 @@
 
 def prepare_kernel(
     at, m_ref, coeff_ref, block_ref, leg_ref, filtered_ref, keep_ref, send_ref,
-    m_smem, coeff_vmem, block_vmem, leg_vmem, sems,
+    m_smem, coeff_vmem, block_vmem, leg_vmem, total, sems,
 ):
     me = lax.axis_index("mset")
-    columns, order_max = coeff_ref.shape
+    order_max = coeff_ref.shape[1]
     pieces = block_vmem.shape[0]
     depth = order_max // pieces
+    first = min(2, pieces)
     copy_m = pltpu.make_async_copy(m_ref, m_smem, sems.at[0])
     copy_leg = pltpu.make_async_copy(leg_ref, leg_vmem, sems.at[1])
     copy_coeff = pltpu.make_async_copy(coeff_ref, coeff_vmem, sems.at[2])
@@ -91,8 +92,12 @@
         )
         for p in range(pieces)
     ]
-    for copy in [copy_m, copy_leg, copy_coeff] + copy_blocks:
+    for copy in [copy_m, copy_leg, copy_coeff] + copy_blocks[:first]:
         copy.start()
+    copy_m.wait()
+    order = LL - m_smem[me]
+    for p in range(first, pieces):
+        pl.when(p * depth < order)(copy_blocks[p].start)
 
     rows = leg_ref.shape[0]
     n = m_ref.shape[0]
@@ -110,18 +115,20 @@
     keep_ref[...] = ordered[:half]
     send_ref[...] = ordered[half:]
 
-    copy_m.wait()
-    order = LL - m_smem[me]
+    def product(p):
+        copy_blocks[p].wait()
+        coeff = coeff_vmem[:, p * depth : (p + 1) * depth]
+        coeff = jnp.where(iota(coeff.shape, 1) + p * depth < order, coeff, jnp.zeros_like(coeff))
+        return jnp.dot(coeff, block_vmem[p], preferred_element_type=F32)
+
+    def add(p):
+        total[...] += product(p)
+
     copy_coeff.wait()
-    coeff = coeff_vmem[...]
-    coeff = jnp.where(iota(coeff.shape, 1) < order, coeff, jnp.zeros_like(coeff))
-    total = jnp.zeros((columns, order_max), F32)
-    for p in range(pieces):
-        copy_blocks[p].wait()
-        total += jnp.dot(
-            coeff[:, p * depth : (p + 1) * depth], block_vmem[p], preferred_element_type=F32
-        )
-    filtered_ref[...] = jnp.where(iota(total.shape, 1) < order, total, 0.0).astype(BF16)
+    total[...] = sum((product(p) for p in range(1, first)), product(0))
+    for p in range(first, pieces):
+        pl.when(p * depth < order)(functools.partial(add, p))
+    filtered_ref[...] = jnp.where(iota(total.shape, 1) < order, total[...], 0.0).astype(BF16)
 
 
 def prepare(m_list, coeff, block, legendre, at):
@@ -144,6 +151,7 @@
             pltpu.VMEM((columns, order_max), BF16),
             pltpu.VMEM((pieces, order_max // pieces, order_max), BF16),
             pltpu.VMEM((rows, order_max), BF16),
+            pltpu.VMEM((columns, order_max), F32),
             pltpu.SemaphoreType.DMA((3 + pieces,)),
         ],
         compiler_params=pltpu.CompilerParams(vmem_limit_bytes=32 << 20),

time: 24 us -> 23.9 us (level)
  waiting for transfers between devices: 5.59 us -> 6.41 us
  starting transfers between devices: 10.7 us -> 10.2 us
  Pallas kernels: 7.45 us -> 7.15 us
    ppermute x3, waiting for transfers between devices: 3.53 us -> 4.2 us  [gather_shards(): shards[turn << at] = lax.ppermute(value, 'mset', pairs)]
    ppermute x3, starting transfers between devices: 7.01 us -> 6.51 us  [gather_shards(): shards[turn << at] = lax.ppermute(value, 'mset', pairs)]
    pallas_call x1, Pallas kernels: 2.91 us -> 2.62 us  [prepare(): pl.pallas_call(functools.partial(prepare_kernel, at), out_shape=[jax.Shap...]
  transfers between devices with their start and end apart: 9 -> 9, of which waited for: 4 -> 5; matrix products, arithmetic and copies ran while one was open for 0% -> 0% of each run, Pallas kernels for 6% -> 6%
where the time goes in v18:
time: 23.9 us; the launch traced here: 23.8 us
  starting transfers between devices  10.2 us (43%)
  Pallas kernels  7.15 us (30%)
  waiting for transfers between devices  6.41 us (27%)
    ppermute x3, starting transfers between devices, gather_shards(): shards[turn << at] = lax.ppermute(value, 'mset', pairs)  6.51 us
    ppermute x3, waiting for transfers between devices, gather_shards(): shards[turn << at] = lax.ppermute(value, 'mset', pairs)  4.2 us
    ppermute x6, starting transfers between devices, exchange(): return lax.ppermute(value, 'mset', [(d, d ^ mask) for d in range(size)])  3.67 us
    pallas_call x1, Pallas kernels, prepare(): pl.pallas_call(functools.partial(prepare_kernel, at), out_shape=[jax.Shap...  2.62 us
    pallas_call x1, Pallas kernels, synthesize(): pl.pallas_call(functools.partial(synthesis_kernel, tiles), out_shape=jax....  2.61 us
    ppermute x6, waiting for transfers between devices, exchange(): return lax.ppermute(value, 'mset', [(d, d ^ mask) for d in range(size)])  2.21 us
    pallas_call x1, Pallas kernels, table_and_own(): pl.pallas_call(functools.partial(table_kernel, at, line, order), out_shap...  1.42 us
    pallas_call x1, Pallas kernels, cross(): pl.pallas_call(functools.partial(cross_kernel, at, line, order), out_shap...  0.5 us
  transfers between devices with their start and end apart: 9, of which 5 were waited for; matrix products, arithmetic and copies ran while one was open for 0% of the time, Pallas kernels for 6%

profile of v18, /device:TPU:0, one launch (start us, length us, event | category | flops | bytes accessed | tf_op | source)
XLA Modules:
  0.0 23.8 jit_solution(11208043850074579779)
XLA Ops:
  0.0 2.6 %prepare.1 = (bf16[32,1536]{1,0:T(8,128)(2,1)S(1)}, bf16[128,1536]{1,0:T(8,128)(2,1)S(1)}, bf16[128,1536]{1,0:T(8,128)(2,1)S(1)}) custom-call(s32[16]{0:T(128)} %refs_8_.1, bf16[32,1536]{1,0:T(8,128)(2,1)} %bitcast.6, bf16[1536,1536]{1,0:T(8,128)(2,1)} %bitcast.4, bf16[256,1536]{1,0:T(8,128)(2,1)} %bitcast.5), custom_call_target="tpu_custom_call" | custom-call | flops 352321536 | bytes 5505024 | tf_op jit(solution)/shard_map/prepare/pallas_call | solution.py:140
  2.6 2.8 %collective-permute-start.5 = (bf16[32,1536]{1,0:T(8,128)(2,1)S(1)}, bf16[32,1536]{1,0:T(8,128)(2,1)S(1)}, u32[]{:S(2)}, u32[]{:S(2)}) collective-permute-start(bf16[32,1536]{1,0:T(8,128)(2,1)S(1)} %get-tuple-element.10.refs_0_), channel_id=1, source_target_pairs={{0,4},{1,5},{2,6},{3,7},{4,8},{5,9},{6,10},{7,11},{8,12},{9,13},{1... | collective-permute-start | bytes 294920 | tf_op jit(solution)/shard_map/ppermute | solution.py:314
  5.5 0.0 copy-start
  5.5 1.8 %collective-permute-start.7 = (bf16[128,1536]{1,0:T(8,128)(2,1)S(1)}, bf16[128,1536]{1,0:T(8,128)(2,1)S(1)}, u32[]{:S(2)}, u32[]{:S(2)}) collective-permute-start(bf16[128,1536]{1,0:T(8,128)(2,1)S(1)} %get-tuple-element.12), channel_id=1, source_target_pairs={{0,2},{1,3},{2,0},{3,1},{4,6},{5,7},{6,4},{7,5},{8,10},{9,11},{10,... | collective-permute-start | bytes 1179656 | tf_op jit(solution)/shard_map/ppermute | solution.py:306
  7.2 2.3 %collective-permute-start.3 = (bf16[32,1536]{1,0:T(8,128)(2,1)S(1)}, bf16[32,1536]{1,0:T(8,128)(2,1)S(1)}, u32[]{:S(2)}, u32[]{:S(2)}) collective-permute-start(bf16[32,1536]{1,0:T(8,128)(2,1)S(1)} %get-tuple-element.10.refs_0_), channel_id=1, source_target_pairs={{0,8},{1,9},{2,10},{3,11},{4,12},{5,13},{6,14},{7,15},{8,0},{9,1},... | collective-permute-start | bytes 294920 | tf_op jit(solution)/shard_map/ppermute | solution.py:314
  9.6 1.3 %collective-permute-start.1 = (bf16[32,1536]{1,0:T(8,128)(2,1)S(1)}, bf16[32,1536]{1,0:T(8,128)(2,1)S(1)}, u32[]{:S(2)}, u32[]{:S(2)}) collective-permute-start(bf16[32,1536]{1,0:T(8,128)(2,1)S(1)} %get-tuple-element.10.refs_0_), channel_id=1, source_target_pairs={{0,12},{1,13},{2,14},{3,15},{4,0},{5,1},{6,2},{7,3},{8,4},{9,5},{1... | collective-permute-start | bytes 294920 | tf_op jit(solution)/shard_map/ppermute | solution.py:314
  10.9 0.0 collective-permute-start
  10.9 0.0 collective-permute-done.5.shard_ref
  10.9 0.6 %collective-permute-start.6 = (bf16[32,1536]{1,0:T(8,128)(2,1)S(1)}, bf16[32,1536]{1,0:T(8,128)(2,1)S(1)}, u32[]{:S(2)}, u32[]{:S(2)}) collective-permute-start(bf16[32,1536]{1,0:T(8,128)(2,1)S(1)} %relay.1.refs_6_), channel_id=1, source_target_pairs={{0,1},{1,0},{2,3},{3,2},{4,5},{5,4},{6,7},{7,6},{8,9},{9,8},{10,11... | collective-permute-start | bytes 294920 | tf_op jit(solution)/shard_map/ppermute | solution.py:306
  11.5 3.3 %collective-permute-done.3.refs_4_ = bf16[32,1536]{1,0:T(8,128)(2,1)S(1)} collective-permute-done((bf16[32,1536]{1,0:T(8,128)(2,1)S(1)}, bf16[32,1536]{1,0:T(8,128)(2,1)S(1)}, u32[]{:S(2)}, u32[]{:S(2)}) %collective-permute-start.3) | collective-permute-done | bytes 98336 | tf_op jit(solution)/shard_map/ppermute | solution.py:314
  14.8 0.0 collective-permute-start.4
  14.9 0.9 %collective-permute-done.1.refs_2_ = bf16[32,1536]{1,0:T(8,128)(2,1)S(1)} collective-permute-done((bf16[32,1536]{1,0:T(8,128)(2,1)S(1)}, bf16[32,1536]{1,0:T(8,128)(2,1)S(1)}, u32[]{:S(2)}, u32[]{:S(2)}) %collective-permute-start.1) | collective-permute-done | bytes 98336 | tf_op jit(solution)/shard_map/ppermute | solution.py:314
  15.7 0.0 collective-permute-start.2
  15.7 0.0 collective-permute-done.refs_1_
  15.7 0.0 collective-permute-done.6.refs_7_
  15.7 0.4 %collective-permute-done.4.refs_5_ = bf16[32,1536]{1,0:T(8,128)(2,1)S(1)} collective-permute-done((bf16[32,1536]{1,0:T(8,128)(2,1)S(1)}, bf16[32,1536]{1,0:T(8,128)(2,1)S(1)}, u32[]{:S(2)}, u32[]{:S(2)}) %collective-permute-start.4) | collective-permute-done | bytes 98336 | tf_op jit(solution)/shard_map/ppermute | solution.py:306
  16.1 0.9 %collective-permute-done.2.refs_3_ = bf16[32,1536]{1,0:T(8,128)(2,1)S(1)} collective-permute-done((bf16[32,1536]{1,0:T(8,128)(2,1)S(1)}, bf16[32,1536]{1,0:T(8,128)(2,1)S(1)}, u32[]{:S(2)}, u32[]{:S(2)}) %collective-permute-start.2) | collective-permute-done | bytes 98336 | tf_op jit(solution)/shard_map/ppermute | solution.py:306
  17.0 0.0 collective-permute-done.7.refs_8_
  17.0 0.5 %cross.1.refs_10_ = bf16[16,256]{1,0:T(8,128)(2,1)S(1)} custom-call(bf16[32,1536]{1,0:T(8,128)(2,1)S(1)} %get-tuple-element.10.refs_0_, bf16[32,1536]{1,0:T(8,128)(2,1)S(1)} %collective-permute-done.refs_1_, bf16[32,1536]{1,0:T(8,128)(2,1)S(1)} %collective-permute-done.1.refs_2_, bf16[32,1536]{1,0:T(8,128)(2,1)S(1)} %collective-permute-done.2.refs_3_, ...), custom_call_target="tpu_custom_call" | custom-call | flops 100663296 | bytes 1179648 | tf_op jit(solution)/shard_map/cross/pallas_call | solution.py:250
  17.5 1.3 %collective-permute-start.8 = (bf16[16,256]{1,0:T(8,128)(2,1)S(1)}, bf16[16,256]{1,0:T(8,128)(2,1)S(1)}, u32[]{:S(2)}, u32[]{:S(2)}) collective-permute-start(bf16[16,256]{1,0:T(8,128)(2,1)S(1)} %cross.1.refs_10_), channel_id=1, source_target_pairs={{0,2},{1,3},{2,0},{3,1},{4,6},{5,7},{6,4},{7,5},{8,10},{9,11},{10,... | collective-permute-start | bytes 24584 | tf_op jit(solution)/shard_map/ppermute | solution.py:306
  18.8 0.0 copy-done
  18.8 1.4 %table_and_own.1 = (bf16[32,8192]{1,0:T(8,128)(2,1)S(1)}, bf16[256,32]{1,0:T(8,128)(2,1)S(1)}) custom-call(bf16[32,1536]{1,0:T(8,128)(2,1)S(1)} %get-tuple-element.10.refs_0_, bf16[32,1536]{1,0:T(8,128)(2,1)S(1)} %collective-permute-done.refs_1_, bf16[32,1536]{1,0:T(8,128)(2,1)S(1)} %collective-permute-done.1.refs_2_, ...), custom_call_target="tpu_custom_call" | custom-call | flops 2097152 | bytes 524288 | tf_op jit(solution)/shard_map/table_and_own/pallas_call | solution.py:178
  20.3 0.9 %collective-permute-done.8.got_ref = bf16[16,256]{1,0:T(8,128)(2,1)S(1)} collective-permute-done((bf16[16,256]{1,0:T(8,128)(2,1)S(1)}, bf16[16,256]{1,0:T(8,128)(2,1)S(1)}, u32[]{:S(2)}, u32[]{:S(2)}) %collective-permute-start.8) | collective-permute-done | bytes 8224 | tf_op jit(solution)/shard_map/ppermute | solution.py:306
  21.2 2.6 %synthesis.1 = bf16[256,8192]{1,0:T(8,128)(2,1)} custom-call(bf16[256,32]{1,0:T(8,128)(2,1)S(1)} %get-tuple-element.13.own_ref, bf16[16,256]{1,0:T(8,128)(2,1)S(1)} %collective-permute-done.8.got_ref, bf16[32,8192]{1,0:T(8,128)(2,1)S(1)} %get-tuple-element.14.table_ref), custom_call_target="tpu_custom_call" | custom-call | flops 134217728 | bytes 4718592 | tf_op jit(solution)/shard_map/synthesis/pallas_call | solution.py:289
  (1 shorter events, 0.0 us)
Async XLA Ops:
  2.6 8.3 %collective-permute-start.5 = (bf16[32,1536]{1,0:T(8,128)(2,1)S(1)}, bf16[32,1536]{1,0:T(8,128)(2,1)S(1)}, u32[]{:S(2)}, u32[]{:S(2)}) collective-permute-start(bf16[32,1536]{1,0:T(8,128)(2,1)S(1)} %get-tuple-element.10.refs_0_), channel_id=1, source_target_pairs={{0,4},{1,5},{2,6},{3,7},{4,8},{5,9},{6,10},{7,11},{8,12},{9,13},{1... | collective-permute-start | bytes 294920 | tf_op jit(solution)/shard_map/ppermute | solution.py:314
  5.5 13.4 %copy-start = (s32[16]{0:T(128)S(1)}, s32[16]{0:T(128)}, u32[]{:S(2)}) copy-start(s32[16]{0:T(128)} %refs_8_.1) | copy-start | bytes 196
  5.5 11.6 %collective-permute-start.7 = (bf16[128,1536]{1,0:T(8,128)(2,1)S(1)}, bf16[128,1536]{1,0:T(8,128)(2,1)S(1)}, u32[]{:S(2)}, u32[]{:S(2)}) collective-permute-start(bf16[128,1536]{1,0:T(8,128)(2,1)S(1)} %get-tuple-element.12), channel_id=1, source_target_pairs={{0,2},{1,3},{2,0},{3,1},{4,6},{5,7},{6,4},{7,5},{8,10},{9,11},{10,... | collective-permute-start | bytes 1179656 | tf_op jit(solution)/shard_map/ppermute | solution.py:306
  7.2 7.6 %collective-permute-start.3 = (bf16[32,1536]{1,0:T(8,128)(2,1)S(1)}, bf16[32,1536]{1,0:T(8,128)(2,1)S(1)}, u32[]{:S(2)}, u32[]{:S(2)}) collective-permute-start(bf16[32,1536]{1,0:T(8,128)(2,1)S(1)} %get-tuple-element.10.refs_0_), channel_id=1, source_target_pairs={{0,8},{1,9},{2,10},{3,11},{4,12},{5,13},{6,14},{7,15},{8,0},{9,1},... | collective-permute-start | bytes 294920 | tf_op jit(solution)/shard_map/ppermute | solution.py:314
  9.6 6.1 %collective-permute-start.1 = (bf16[32,1536]{1,0:T(8,128)(2,1)S(1)}, bf16[32,1536]{1,0:T(8,128)(2,1)S(1)}, u32[]{:S(2)}, u32[]{:S(2)}) collective-permute-start(bf16[32,1536]{1,0:T(8,128)(2,1)S(1)} %get-tuple-element.10.refs_0_), channel_id=1, source_target_pairs={{0,12},{1,13},{2,14},{3,15},{4,0},{5,1},{6,2},{7,3},{8,4},{9,5},{1... | collective-permute-start | bytes 294920 | tf_op jit(solution)/shard_map/ppermute | solution.py:314
  10.9 4.8 %collective-permute-start = (bf16[32,1536]{1,0:T(8,128)(2,1)S(1)}, bf16[32,1536]{1,0:T(8,128)(2,1)S(1)}, u32[]{:S(2)}, u32[]{:S(2)}) collective-permute-start(bf16[32,1536]{1,0:T(8,128)(2,1)S(1)} %get-tuple-element.10.refs_0_), channel_id=1, source_target_pairs={{0,1},{1,0},{2,3},{3,2},{4,5},{5,4},{6,7},{7,6},{8,9},{9,8},{10,11... | collective-permute-start | bytes 294920 | tf_op jit(solution)/shard_map/ppermute | solution.py:306
  10.9 4.8 %collective-permute-start.6 = (bf16[32,1536]{1,0:T(8,128)(2,1)S(1)}, bf16[32,1536]{1,0:T(8,128)(2,1)S(1)}, u32[]{:S(2)}, u32[]{:S(2)}) collective-permute-start(bf16[32,1536]{1,0:T(8,128)(2,1)S(1)} %relay.1.refs_6_), channel_id=1, source_target_pairs={{0,1},{1,0},{2,3},{3,2},{4,5},{5,4},{6,7},{7,6},{8,9},{9,8},{10,11... | collective-permute-start | bytes 294920 | tf_op jit(solution)/shard_map/ppermute | solution.py:306
  14.8 1.3 %collective-permute-start.4 = (bf16[32,1536]{1,0:T(8,128)(2,1)S(1)}, bf16[32,1536]{1,0:T(8,128)(2,1)S(1)}, u32[]{:S(2)}, u32[]{:S(2)}) collective-permute-start(bf16[32,1536]{1,0:T(8,128)(2,1)S(1)} %collective-permute-done.3.refs_4_), channel_id=1, source_target_pairs={{0,1},{1,0},{2,3},{3,2},{4,5},{5,4},{6,7},{7,6},{8,9},{9,8},{10,11... | collective-permute-start | bytes 294920 | tf_op jit(solution)/shard_map/ppermute | solution.py:306
  15.7 1.3 %collective-permute-start.2 = (bf16[32,1536]{1,0:T(8,128)(2,1)S(1)}, bf16[32,1536]{1,0:T(8,128)(2,1)S(1)}, u32[]{:S(2)}, u32[]{:S(2)}) collective-permute-start(bf16[32,1536]{1,0:T(8,128)(2,1)S(1)} %collective-permute-done.1.refs_2_), channel_id=1, source_target_pairs={{0,1},{1,0},{2,3},{3,2},{4,5},{5,4},{6,7},{7,6},{8,9},{9,8},{10,11... | collective-permute-start | bytes 294920 | tf_op jit(solution)/shard_map/ppermute | solution.py:306
  17.5 3.7 %collective-permute-start.8 = (bf16[16,256]{1,0:T(8,128)(2,1)S(1)}, bf16[16,256]{1,0:T(8,128)(2,1)S(1)}, u32[]{:S(2)}, u32[]{:S(2)}) collective-permute-start(bf16[16,256]{1,0:T(8,128)(2,1)S(1)} %cross.1.refs_10_), channel_id=1, source_target_pairs={{0,2},{1,3},{2,0},{3,1},{4,6},{5,7},{6,4},{7,5},{8,10},{9,11},{10,... | collective-permute-start | bytes 24584 | tf_op jit(solution)/shard_map/ppermute | solution.py:306

commit v19 on v18

--- a/solution.py
+++ b/solution.py
@@ -82,7 +82,7 @@
     order_max = coeff_ref.shape[1]
     pieces = block_vmem.shape[0]
     depth = order_max // pieces
-    first = min(2, pieces)
+    first = min(4, pieces)
     copy_m = pltpu.make_async_copy(m_ref, m_smem, sems.at[0])
     copy_leg = pltpu.make_async_copy(leg_ref, leg_vmem, sems.at[1])
     copy_coeff = pltpu.make_async_copy(coeff_ref, coeff_vmem, sems.at[2])
@@ -135,7 +135,7 @@
     columns, order_max = coeff.shape
     rows = legendre.shape[0]
     n = m_list.shape[0]
-    pieces = 6
+    pieces = 12
     operands = (m_list, coeff, block, legendre)
     return pl.pallas_call(
         functools.partial(prepare_kernel, at),

time: 23.9 us -> 23.9 us (level)
  starting transfers between devices: 10.2 us -> 10.6 us
    ppermute x6, starting transfers between devices: 3.67 us -> 5.44 us  [exchange(): return lax.ppermute(value, 'mset', [(d, d ^ mask) for d in range(size)])]
    ppermute x3, starting transfers between devices: 6.51 us -> 5.13 us  [gather_shards(): shards[turn << at] = lax.ppermute(value, 'mset', pairs)]
    ppermute x6, waiting for transfers between devices: 2.21 us -> 1.93 us  [exchange(): return lax.ppermute(value, 'mset', [(d, d ^ mask) for d in range(size)])]
  transfers between devices with their start and end apart: 9 -> 9, of which waited for: 5 -> 4; matrix products, arithmetic and copies ran while one was open for 0% -> 0% of each run, Pallas kernels for 6% -> 6%
where the time goes in v19:
time: 23.9 us
  starting transfers between devices  10.6 us (44%)
  Pallas kernels  6.97 us (29%)
  waiting for transfers between devices  6.35 us (27%)
    ppermute x6, starting transfers between devices, exchange(): return lax.ppermute(value, 'mset', [(d, d ^ mask) for d in range(size)])  5.44 us
    ppermute x3, starting transfers between devices, gather_shards(): shards[turn << at] = lax.ppermute(value, 'mset', pairs)  5.13 us
    ppermute x3, waiting for transfers between devices, gather_shards(): shards[turn << at] = lax.ppermute(value, 'mset', pairs)  4.42 us
    pallas_call x1, Pallas kernels, synthesize(): pl.pallas_call(functools.partial(synthesis_kernel, tiles), out_shape=jax....  2.61 us
    pallas_call x1, Pallas kernels, prepare(): pl.pallas_call(functools.partial(prepare_kernel, at), out_shape=[jax.Shap...  2.43 us
    ppermute x6, waiting for transfers between devices, exchange(): return lax.ppermute(value, 'mset', [(d, d ^ mask) for d in range(size)])  1.93 us
    pallas_call x1, Pallas kernels, table_and_own(): pl.pallas_call(functools.partial(table_kernel, at, line, order), out_shap...  1.42 us
    pallas_call x1, Pallas kernels, cross(): pl.pallas_call(functools.partial(cross_kernel, at, line, order), out_shap...  0.5 us
  transfers between devices with their start and end apart: 9, of which 4 were waited for; matrix products, arithmetic and copies ran while one was open for 0% of the time, Pallas kernels for 6%

profile of v19, /device:TPU:0, one launch (start us, length us, event | category | flops | bytes accessed | tf_op | source)
XLA Modules:
  0.0 23.9 jit_solution(9714367223289698912)
XLA Ops:
  0.0 2.4 %prepare.1 = (bf16[32,1536]{1,0:T(8,128)(2,1)S(1)}, bf16[128,1536]{1,0:T(8,128)(2,1)S(1)}, bf16[128,1536]{1,0:T(8,128)(2,1)S(1)}) custom-call(s32[16]{0:T(128)} %refs_8_.1, bf16[32,1536]{1,0:T(8,128)(2,1)} %bitcast.6, bf16[1536,1536]{1,0:T(8,128)(2,1)} %bitcast.4, bf16[256,1536]{1,0:T(8,128)(2,1)} %bitcast.5), custom_call_target="tpu_custom_call" | custom-call | flops 352321536 | bytes 5505024 | tf_op jit(solution)/shard_map/prepare/pallas_call | solution.py:140
  2.4 2.7 %collective-permute-start.5 = (bf16[32,1536]{1,0:T(8,128)(2,1)S(1)}, bf16[32,1536]{1,0:T(8,128)(2,1)S(1)}, u32[]{:S(2)}, u32[]{:S(2)}) collective-permute-start(bf16[32,1536]{1,0:T(8,128)(2,1)S(1)} %get-tuple-element.10.refs_0_), channel_id=1, source_target_pairs={{0,4},{1,5},{2,6},{3,7},{4,8},{5,9},{6,10},{7,11},{8,12},{9,13},{1... | collective-permute-start | bytes 294920 | tf_op jit(solution)/shard_map/ppermute | solution.py:314
  5.1 0.0 copy-start
  5.1 3.1 %collective-permute-start.7 = (bf16[128,1536]{1,0:T(8,128)(2,1)S(1)}, bf16[128,1536]{1,0:T(8,128)(2,1)S(1)}, u32[]{:S(2)}, u32[]{:S(2)}) collective-permute-start(bf16[128,1536]{1,0:T(8,128)(2,1)S(1)} %get-tuple-element.12), channel_id=1, source_target_pairs={{0,2},{1,3},{2,0},{3,1},{4,6},{5,7},{6,4},{7,5},{8,10},{9,11},{10,... | collective-permute-start | bytes 1179656 | tf_op jit(solution)/shard_map/ppermute | solution.py:306
  8.2 1.0 %collective-permute-start.3 = (bf16[32,1536]{1,0:T(8,128)(2,1)S(1)}, bf16[32,1536]{1,0:T(8,128)(2,1)S(1)}, u32[]{:S(2)}, u32[]{:S(2)}) collective-permute-start(bf16[32,1536]{1,0:T(8,128)(2,1)S(1)} %get-tuple-element.10.refs_0_), channel_id=1, source_target_pairs={{0,8},{1,9},{2,10},{3,11},{4,12},{5,13},{6,14},{7,15},{8,0},{9,1},... | collective-permute-start | bytes 294920 | tf_op jit(solution)/shard_map/ppermute | solution.py:314
  9.2 1.4 %collective-permute-start.1 = (bf16[32,1536]{1,0:T(8,128)(2,1)S(1)}, bf16[32,1536]{1,0:T(8,128)(2,1)S(1)}, u32[]{:S(2)}, u32[]{:S(2)}) collective-permute-start(bf16[32,1536]{1,0:T(8,128)(2,1)S(1)} %get-tuple-element.10.refs_0_), channel_id=1, source_target_pairs={{0,12},{1,13},{2,14},{3,15},{4,0},{5,1},{6,2},{7,3},{8,4},{9,5},{1... | collective-permute-start | bytes 294920 | tf_op jit(solution)/shard_map/ppermute | solution.py:314
  10.7 0.0 collective-permute-start
  10.7 0.0 collective-permute-done.5.shard_ref
  10.7 0.6 %collective-permute-start.6 = (bf16[32,1536]{1,0:T(8,128)(2,1)S(1)}, bf16[32,1536]{1,0:T(8,128)(2,1)S(1)}, u32[]{:S(2)}, u32[]{:S(2)}) collective-permute-start(bf16[32,1536]{1,0:T(8,128)(2,1)S(1)} %relay.1.refs_6_), channel_id=1, source_target_pairs={{0,1},{1,0},{2,3},{3,2},{4,5},{5,4},{6,7},{7,6},{8,9},{9,8},{10,11... | collective-permute-start | bytes 294920 | tf_op jit(solution)/shard_map/ppermute | solution.py:306
  11.3 4.4 %collective-permute-done.3.refs_4_ = bf16[32,1536]{1,0:T(8,128)(2,1)S(1)} collective-permute-done((bf16[32,1536]{1,0:T(8,128)(2,1)S(1)}, bf16[32,1536]{1,0:T(8,128)(2,1)S(1)}, u32[]{:S(2)}, u32[]{:S(2)}) %collective-permute-start.3) | collective-permute-done | bytes 98336 | tf_op jit(solution)/shard_map/ppermute | solution.py:314
  15.7 0.0 collective-permute-start.4
  15.7 0.0 collective-permute-done.1.refs_2_
  15.7 0.5 %collective-permute-start.2 = (bf16[32,1536]{1,0:T(8,128)(2,1)S(1)}, bf16[32,1536]{1,0:T(8,128)(2,1)S(1)}, u32[]{:S(2)}, u32[]{:S(2)}) collective-permute-start(bf16[32,1536]{1,0:T(8,128)(2,1)S(1)} %collective-permute-done.1.refs_2_), channel_id=1, source_target_pairs={{0,1},{1,0},{2,3},{3,2},{4,5},{5,4},{6,7},{7,6},{8,9},{9,8},{10,11... | collective-permute-start | bytes 294920 | tf_op jit(solution)/shard_map/ppermute | solution.py:306
  16.2 0.0 collective-permute-done.refs_1_
  16.2 0.0 collective-permute-done.6.refs_7_
  16.2 0.8 %collective-permute-done.4.refs_5_ = bf16[32,1536]{1,0:T(8,128)(2,1)S(1)} collective-permute-done((bf16[32,1536]{1,0:T(8,128)(2,1)S(1)}, bf16[32,1536]{1,0:T(8,128)(2,1)S(1)}, u32[]{:S(2)}, u32[]{:S(2)}) %collective-permute-start.4) | collective-permute-done | bytes 98336 | tf_op jit(solution)/shard_map/ppermute | solution.py:306
  17.0 0.2 collective-permute-done.2.refs_3_
  17.1 0.0 collective-permute-done.7.refs_8_
  17.1 0.5 %cross.1.refs_10_ = bf16[16,256]{1,0:T(8,128)(2,1)S(1)} custom-call(bf16[32,1536]{1,0:T(8,128)(2,1)S(1)} %get-tuple-element.10.refs_0_, bf16[32,1536]{1,0:T(8,128)(2,1)S(1)} %collective-permute-done.refs_1_, bf16[32,1536]{1,0:T(8,128)(2,1)S(1)} %collective-permute-done.1.refs_2_, bf16[32,1536]{1,0:T(8,128)(2,1)S(1)} %collective-permute-done.2.refs_3_, ...), custom_call_target="tpu_custom_call" | custom-call | flops 100663296 | bytes 1179648 | tf_op jit(solution)/shard_map/cross/pallas_call | solution.py:250
  17.6 1.3 %collective-permute-start.8 = (bf16[16,256]{1,0:T(8,128)(2,1)S(1)}, bf16[16,256]{1,0:T(8,128)(2,1)S(1)}, u32[]{:S(2)}, u32[]{:S(2)}) collective-permute-start(bf16[16,256]{1,0:T(8,128)(2,1)S(1)} %cross.1.refs_10_), channel_id=1, source_target_pairs={{0,2},{1,3},{2,0},{3,1},{4,6},{5,7},{6,4},{7,5},{8,10},{9,11},{10,... | collective-permute-start | bytes 24584 | tf_op jit(solution)/shard_map/ppermute | solution.py:306
  18.9 0.0 copy-done
  18.9 1.4 %table_and_own.1 = (bf16[32,8192]{1,0:T(8,128)(2,1)S(1)}, bf16[256,32]{1,0:T(8,128)(2,1)S(1)}) custom-call(bf16[32,1536]{1,0:T(8,128)(2,1)S(1)} %get-tuple-element.10.refs_0_, bf16[32,1536]{1,0:T(8,128)(2,1)S(1)} %collective-permute-done.refs_1_, bf16[32,1536]{1,0:T(8,128)(2,1)S(1)} %collective-permute-done.1.refs_2_, ...), custom_call_target="tpu_custom_call" | custom-call | flops 2097152 | bytes 524288 | tf_op jit(solution)/shard_map/table_and_own/pallas_call | solution.py:178
  20.3 1.0 %collective-permute-done.8.got_ref = bf16[16,256]{1,0:T(8,128)(2,1)S(1)} collective-permute-done((bf16[16,256]{1,0:T(8,128)(2,1)S(1)}, bf16[16,256]{1,0:T(8,128)(2,1)S(1)}, u32[]{:S(2)}, u32[]{:S(2)}) %collective-permute-start.8) | collective-permute-done | bytes 8224 | tf_op jit(solution)/shard_map/ppermute | solution.py:306
  21.3 2.6 %synthesis.1 = bf16[256,8192]{1,0:T(8,128)(2,1)} custom-call(bf16[256,32]{1,0:T(8,128)(2,1)S(1)} %get-tuple-element.13.own_ref, bf16[16,256]{1,0:T(8,128)(2,1)S(1)} %collective-permute-done.8.got_ref, bf16[32,8192]{1,0:T(8,128)(2,1)S(1)} %get-tuple-element.14.table_ref), custom_call_target="tpu_custom_call" | custom-call | flops 134217728 | bytes 4718592 | tf_op jit(solution)/shard_map/synthesis/pallas_call | solution.py:289
  (1 shorter events, 0.0 us)
Async XLA Ops:
  2.4 8.2 %collective-permute-start.5 = (bf16[32,1536]{1,0:T(8,128)(2,1)S(1)}, bf16[32,1536]{1,0:T(8,128)(2,1)S(1)}, u32[]{:S(2)}, u32[]{:S(2)}) collective-permute-start(bf16[32,1536]{1,0:T(8,128)(2,1)S(1)} %get-tuple-element.10.refs_0_), channel_id=1, source_target_pairs={{0,4},{1,5},{2,6},{3,7},{4,8},{5,9},{6,10},{7,11},{8,12},{9,13},{1... | collective-permute-start | bytes 294920 | tf_op jit(solution)/shard_map/ppermute | solution.py:314
  5.1 13.8 %copy-start = (s32[16]{0:T(128)S(1)}, s32[16]{0:T(128)}, u32[]{:S(2)}) copy-start(s32[16]{0:T(128)} %refs_8_.1) | copy-start | bytes 196
  5.1 12.0 %collective-permute-start.7 = (bf16[128,1536]{1,0:T(8,128)(2,1)S(1)}, bf16[128,1536]{1,0:T(8,128)(2,1)S(1)}, u32[]{:S(2)}, u32[]{:S(2)}) collective-permute-start(bf16[128,1536]{1,0:T(8,128)(2,1)S(1)} %get-tuple-element.12), channel_id=1, source_target_pairs={{0,2},{1,3},{2,0},{3,1},{4,6},{5,7},{6,4},{7,5},{8,10},{9,11},{10,... | collective-permute-start | bytes 1179656 | tf_op jit(solution)/shard_map/ppermute | solution.py:306
  8.2 7.5 %collective-permute-start.3 = (bf16[32,1536]{1,0:T(8,128)(2,1)S(1)}, bf16[32,1536]{1,0:T(8,128)(2,1)S(1)}, u32[]{:S(2)}, u32[]{:S(2)}) collective-permute-start(bf16[32,1536]{1,0:T(8,128)(2,1)S(1)} %get-tuple-element.10.refs_0_), channel_id=1, source_target_pairs={{0,8},{1,9},{2,10},{3,11},{4,12},{5,13},{6,14},{7,15},{8,0},{9,1},... | collective-permute-start | bytes 294920 | tf_op jit(solution)/shard_map/ppermute | solution.py:314
  9.2 6.5 %collective-permute-start.1 = (bf16[32,1536]{1,0:T(8,128)(2,1)S(1)}, bf16[32,1536]{1,0:T(8,128)(2,1)S(1)}, u32[]{:S(2)}, u32[]{:S(2)}) collective-permute-start(bf16[32,1536]{1,0:T(8,128)(2,1)S(1)} %get-tuple-element.10.refs_0_), channel_id=1, source_target_pairs={{0,12},{1,13},{2,14},{3,15},{4,0},{5,1},{6,2},{7,3},{8,4},{9,5},{1... | collective-permute-start | bytes 294920 | tf_op jit(solution)/shard_map/ppermute | solution.py:314
  10.7 5.5 %collective-permute-start = (bf16[32,1536]{1,0:T(8,128)(2,1)S(1)}, bf16[32,1536]{1,0:T(8,128)(2,1)S(1)}, u32[]{:S(2)}, u32[]{:S(2)}) collective-permute-start(bf16[32,1536]{1,0:T(8,128)(2,1)S(1)} %get-tuple-element.10.refs_0_), channel_id=1, source_target_pairs={{0,1},{1,0},{2,3},{3,2},{4,5},{5,4},{6,7},{7,6},{8,9},{9,8},{10,11... | collective-permute-start | bytes 294920 | tf_op jit(solution)/shard_map/ppermute | solution.py:306
  10.7 5.5 %collective-permute-start.6 = (bf16[32,1536]{1,0:T(8,128)(2,1)S(1)}, bf16[32,1536]{1,0:T(8,128)(2,1)S(1)}, u32[]{:S(2)}, u32[]{:S(2)}) collective-permute-start(bf16[32,1536]{1,0:T(8,128)(2,1)S(1)} %relay.1.refs_6_), channel_id=1, source_target_pairs={{0,1},{1,0},{2,3},{3,2},{4,5},{5,4},{6,7},{7,6},{8,9},{9,8},{10,11... | collective-permute-start | bytes 294920 | tf_op jit(solution)/shard_map/ppermute | solution.py:306
  15.7 1.3 %collective-permute-start.4 = (bf16[32,1536]{1,0:T(8,128)(2,1)S(1)}, bf16[32,1536]{1,0:T(8,128)(2,1)S(1)}, u32[]{:S(2)}, u32[]{:S(2)}) collective-permute-start(bf16[32,1536]{1,0:T(8,128)(2,1)S(1)} %collective-permute-done.3.refs_4_), channel_id=1, source_target_pairs={{0,1},{1,0},{2,3},{3,2},{4,5},{5,4},{6,7},{7,6},{8,9},{9,8},{10,11... | collective-permute-start | bytes 294920 | tf_op jit(solution)/shard_map/ppermute | solution.py:306
  15.7 1.5 %collective-permute-start.2 = (bf16[32,1536]{1,0:T(8,128)(2,1)S(1)}, bf16[32,1536]{1,0:T(8,128)(2,1)S(1)}, u32[]{:S(2)}, u32[]{:S(2)}) collective-permute-start(bf16[32,1536]{1,0:T(8,128)(2,1)S(1)} %collective-permute-done.1.refs_2_), channel_id=1, source_target_pairs={{0,1},{1,0},{2,3},{3,2},{4,5},{5,4},{6,7},{7,6},{8,9},{9,8},{10,11... | collective-permute-start | bytes 294920 | tf_op jit(solution)/shard_map/ppermute | solution.py:306
  17.6 3.7 %collective-permute-start.8 = (bf16[16,256]{1,0:T(8,128)(2,1)S(1)}, bf16[16,256]{1,0:T(8,128)(2,1)S(1)}, u32[]{:S(2)}, u32[]{:S(2)}) collective-permute-start(bf16[16,256]{1,0:T(8,128)(2,1)S(1)} %cross.1.refs_10_), channel_id=1, source_target_pairs={{0,2},{1,3},{2,0},{3,1},{4,6},{5,7},{6,4},{7,5},{8,10},{9,11},{10,... | collective-permute-start | bytes 24584 | tf_op jit(solution)/shard_map/ppermute | solution.py:306

commit v20 on v11

--- a/solution.py
+++ b/solution.py
@@ -264,7 +264,7 @@
 
 
 def synthesize(own, got, table):
-    tiles = 16
+    tiles = 32
     out_rows = own.shape[0]
     return pl.pallas_call(
         functools.partial(synthesis_kernel, tiles),

time: 24 us -> 24.1 us (level)
  no operation moved by 1% of the time
where the time goes in v20:
time: 24.1 us; the launch traced here: 24 us
  starting transfers between devices  10.8 us (45%)
  Pallas kernels  7.28 us (30%)
  waiting for transfers between devices  5.91 us (25%)
    ppermute x3, starting transfers between devices, gather_shards(): shards[turn << at] = lax.ppermute(value, 'mset', pairs)  7.01 us
    ppermute x6, starting transfers between devices, exchange(): return lax.ppermute(value, 'mset', [(d, d ^ mask) for d in range(size)])  3.74 us
    ppermute x3, waiting for transfers between devices, gather_shards(): shards[turn << at] = lax.ppermute(value, 'mset', pairs)  3.53 us
    pallas_call x1, Pallas kernels, prepare(): pl.pallas_call(functools.partial(prepare_kernel, at), out_shape=[jax.Shap...  2.91 us
    pallas_call x1, Pallas kernels, synthesize(): pl.pallas_call(functools.partial(synthesis_kernel, tiles), out_shape=jax....  2.71 us
    ppermute x6, waiting for transfers between devices, exchange(): return lax.ppermute(value, 'mset', [(d, d ^ mask) for d in range(size)])  2.38 us
    pallas_call x1, Pallas kernels, table_and_own(): pl.pallas_call(functools.partial(table_kernel, at, line), out_shape=[jax....  1.1 us
    pallas_call x1, Pallas kernels, cross(): pl.pallas_call(functools.partial(cross_kernel, at, line, order, min(8, co...  0.55 us
  transfers between devices with their start and end apart: 9, of which 4 were waited for; matrix products, arithmetic and copies ran while one was open for 0% of the time, Pallas kernels for 5%

profile of v20, /device:TPU:0, one launch (start us, length us, event | category | flops | bytes accessed | tf_op | source)
XLA Modules:
  0.0 24.0 jit_solution(692103060922647455)
XLA Ops:
  0.0 2.9 %prepare.1 = (bf16[32,1536]{1,0:T(8,128)(2,1)S(1)}, bf16[128,1536]{1,0:T(8,128)(2,1)S(1)}, bf16[128,1536]{1,0:T(8,128)(2,1)S(1)}) custom-call(s32[16]{0:T(128)} %m_ref.3, bf16[32,1536]{1,0:T(8,128)(2,1)} %bitcast.6, bf16[1536,1536]{1,0:T(8,128)(2,1)} %bitcast.4, bf16[256,1536]{1,0:T(8,128)(2,1)} %bitcast.5), custom_call_target="tpu_custom_call" | custom-call | flops 352321536 | bytes 5505024 | tf_op jit(solution)/shard_map/prepare/pallas_call | solution.py:133
  2.9 3.1 %collective-permute-start.5 = (bf16[32,1536]{1,0:T(8,128)(2,1)S(1)}, bf16[32,1536]{1,0:T(8,128)(2,1)S(1)}, u32[]{:S(2)}, u32[]{:S(2)}) collective-permute-start(bf16[32,1536]{1,0:T(8,128)(2,1)S(1)} %get-tuple-element.12.refs_0_), channel_id=1, source_target_pairs={{0,4},{1,5},{2,6},{3,7},{4,8},{5,9},{6,10},{7,11},{8,12},{9,13},{1... | collective-permute-start | bytes 294920 | tf_op jit(solution)/shard_map/ppermute | solution.py:294
  6.0 0.0 copy-start
  6.0 1.5 %collective-permute-start.7 = (bf16[128,1536]{1,0:T(8,128)(2,1)S(1)}, bf16[128,1536]{1,0:T(8,128)(2,1)S(1)}, u32[]{:S(2)}, u32[]{:S(2)}) collective-permute-start(bf16[128,1536]{1,0:T(8,128)(2,1)S(1)} %get-tuple-element.14), channel_id=1, source_target_pairs={{0,2},{1,3},{2,0},{3,1},{4,6},{5,7},{6,4},{7,5},{8,10},{9,11},{10,... | collective-permute-start | bytes 1179656 | tf_op jit(solution)/shard_map/ppermute | solution.py:286
  7.5 2.6 %collective-permute-start.3 = (bf16[32,1536]{1,0:T(8,128)(2,1)S(1)}, bf16[32,1536]{1,0:T(8,128)(2,1)S(1)}, u32[]{:S(2)}, u32[]{:S(2)}) collective-permute-start(bf16[32,1536]{1,0:T(8,128)(2,1)S(1)} %get-tuple-element.12.refs_0_), channel_id=1, source_target_pairs={{0,8},{1,9},{2,10},{3,11},{4,12},{5,13},{6,14},{7,15},{8,0},{9,1},... | collective-permute-start | bytes 294920 | tf_op jit(solution)/shard_map/ppermute | solution.py:294
  10.1 1.3 %collective-permute-start.1 = (bf16[32,1536]{1,0:T(8,128)(2,1)S(1)}, bf16[32,1536]{1,0:T(8,128)(2,1)S(1)}, u32[]{:S(2)}, u32[]{:S(2)}) collective-permute-start(bf16[32,1536]{1,0:T(8,128)(2,1)S(1)} %get-tuple-element.12.refs_0_), channel_id=1, source_target_pairs={{0,12},{1,13},{2,14},{3,15},{4,0},{5,1},{6,2},{7,3},{8,4},{9,5},{1... | collective-permute-start | bytes 294920 | tf_op jit(solution)/shard_map/ppermute | solution.py:294
  11.5 0.0 collective-permute-start
  11.5 0.0 collective-permute-done.5.shard_ref
  11.5 0.6 %collective-permute-start.6 = (bf16[32,1536]{1,0:T(8,128)(2,1)S(1)}, bf16[32,1536]{1,0:T(8,128)(2,1)S(1)}, u32[]{:S(2)}, u32[]{:S(2)}) collective-permute-start(bf16[32,1536]{1,0:T(8,128)(2,1)S(1)} %relay.1.refs_6_), channel_id=1, source_target_pairs={{0,1},{1,0},{2,3},{3,2},{4,5},{5,4},{6,7},{7,6},{8,9},{9,8},{10,11... | collective-permute-start | bytes 294920 | tf_op jit(solution)/shard_map/ppermute | solution.py:286
  12.0 3.5 %collective-permute-done.3.refs_4_ = bf16[32,1536]{1,0:T(8,128)(2,1)S(1)} collective-permute-done((bf16[32,1536]{1,0:T(8,128)(2,1)S(1)}, bf16[32,1536]{1,0:T(8,128)(2,1)S(1)}, u32[]{:S(2)}, u32[]{:S(2)}) %collective-permute-start.3) | collective-permute-done | bytes 98336 | tf_op jit(solution)/shard_map/ppermute | solution.py:294
  15.6 0.0 collective-permute-start.4
  15.6 0.0 collective-permute-done.1.refs_2_
  15.6 0.5 %collective-permute-start.2 = (bf16[32,1536]{1,0:T(8,128)(2,1)S(1)}, bf16[32,1536]{1,0:T(8,128)(2,1)S(1)}, u32[]{:S(2)}, u32[]{:S(2)}) collective-permute-start(bf16[32,1536]{1,0:T(8,128)(2,1)S(1)} %collective-permute-done.1.refs_2_), channel_id=1, source_target_pairs={{0,1},{1,0},{2,3},{3,2},{4,5},{5,4},{6,7},{7,6},{8,9},{9,8},{10,11... | collective-permute-start | bytes 294920 | tf_op jit(solution)/shard_map/ppermute | solution.py:286
  16.1 0.0 collective-permute-done.refs_1_
  16.1 0.0 collective-permute-done.6.refs_7_
  16.1 0.8 %collective-permute-done.4.refs_5_ = bf16[32,1536]{1,0:T(8,128)(2,1)S(1)} collective-permute-done((bf16[32,1536]{1,0:T(8,128)(2,1)S(1)}, bf16[32,1536]{1,0:T(8,128)(2,1)S(1)}, u32[]{:S(2)}, u32[]{:S(2)}) %collective-permute-start.4) | collective-permute-done | bytes 98336 | tf_op jit(solution)/shard_map/ppermute | solution.py:286
  16.9 0.2 collective-permute-done.2.refs_3_
  17.0 0.0 collective-permute-done.7.refs_9_
  17.0 0.6 %cross.1 = (bf16[16,256]{1,0:T(8,128)(2,1)S(1)}, bf16[16,256]{1,0:T(8,128)(2,1)S(1)}) custom-call(bf16[32,1536]{1,0:T(8,128)(2,1)S(1)} %get-tuple-element.12.refs_0_, bf16[32,1536]{1,0:T(8,128)(2,1)S(1)} %collective-permute-done.refs_1_, bf16[32,1536]{1,0:T(8,128)(2,1)S(1)} %collective-permute-done.1.refs_2_, ...), custom_call_target="tpu_custom_call" | custom-call | flops 201326592 | bytes 1572864 | tf_op jit(solution)/shard_map/cross/pallas_call | solution.py:235
  17.6 1.1 %collective-permute-start.8 = (bf16[16,256]{1,0:T(8,128)(2,1)S(1)}, bf16[16,256]{1,0:T(8,128)(2,1)S(1)}, u32[]{:S(2)}, u32[]{:S(2)}) collective-permute-start(bf16[16,256]{1,0:T(8,128)(2,1)S(1)} %get-tuple-element.17), channel_id=1, source_target_pairs={{0,2},{1,3},{2,0},{3,1},{4,6},{5,7},{6,4},{7,5},{8,10},{9,11},{10,... | collective-permute-start | bytes 24584 | tf_op jit(solution)/shard_map/ppermute | solution.py:286
  18.7 0.0 copy-done
  18.7 1.1 %table_and_own.1 = (bf16[32,8192]{1,0:T(8,128)(2,1)S(1)}, bf16[256,32]{1,0:T(8,128)(2,1)S(1)}) custom-call(s32[16]{0:T(128)S(1)} %copy-done, bf16[16,256]{1,0:T(8,128)(2,1)S(1)} %get-tuple-element.15.own_ref), custom_call_target="tpu_custom_call" | custom-call | flops 2097152 | bytes 524288 | tf_op jit(solution)/shard_map/table_and_own/pallas_call | solution.py:167
  19.8 1.4 %collective-permute-done.8.got_ref = bf16[16,256]{1,0:T(8,128)(2,1)S(1)} collective-permute-done((bf16[16,256]{1,0:T(8,128)(2,1)S(1)}, bf16[16,256]{1,0:T(8,128)(2,1)S(1)}, u32[]{:S(2)}, u32[]{:S(2)}) %collective-permute-start.8) | collective-permute-done | bytes 8224 | tf_op jit(solution)/shard_map/ppermute | solution.py:286
  21.3 2.7 %synthesis.1 = bf16[256,8192]{1,0:T(8,128)(2,1)} custom-call(bf16[256,32]{1,0:T(8,128)(2,1)S(1)} %get-tuple-element.16.own_ref, bf16[16,256]{1,0:T(8,128)(2,1)S(1)} %collective-permute-done.8.got_ref, bf16[32,8192]{1,0:T(8,128)(2,1)S(1)} %get-tuple-element.18.table_ref), custom_call_target="tpu_custom_call" | custom-call | flops 134217728 | bytes 4718592 | tf_op jit(solution)/shard_map/synthesis/pallas_call | solution.py:269
  (1 shorter events, 0.0 us)
Async XLA Ops:
  2.9 8.5 %collective-permute-start.5 = (bf16[32,1536]{1,0:T(8,128)(2,1)S(1)}, bf16[32,1536]{1,0:T(8,128)(2,1)S(1)}, u32[]{:S(2)}, u32[]{:S(2)}) collective-permute-start(bf16[32,1536]{1,0:T(8,128)(2,1)S(1)} %get-tuple-element.12.refs_0_), channel_id=1, source_target_pairs={{0,4},{1,5},{2,6},{3,7},{4,8},{5,9},{6,10},{7,11},{8,12},{9,13},{1... | collective-permute-start | bytes 294920 | tf_op jit(solution)/shard_map/ppermute | solution.py:294
  6.0 12.7 %copy-start = (s32[16]{0:T(128)S(1)}, s32[16]{0:T(128)}, u32[]{:S(2)}) copy-start(s32[16]{0:T(128)} %m_ref.3) | copy-start | bytes 196
  6.0 11.0 %collective-permute-start.7 = (bf16[128,1536]{1,0:T(8,128)(2,1)S(1)}, bf16[128,1536]{1,0:T(8,128)(2,1)S(1)}, u32[]{:S(2)}, u32[]{:S(2)}) collective-permute-start(bf16[128,1536]{1,0:T(8,128)(2,1)S(1)} %get-tuple-element.14), channel_id=1, source_target_pairs={{0,2},{1,3},{2,0},{3,1},{4,6},{5,7},{6,4},{7,5},{8,10},{9,11},{10,... | collective-permute-start | bytes 1179656 | tf_op jit(solution)/shard_map/ppermute | solution.py:286
  7.5 8.1 %collective-permute-start.3 = (bf16[32,1536]{1,0:T(8,128)(2,1)S(1)}, bf16[32,1536]{1,0:T(8,128)(2,1)S(1)}, u32[]{:S(2)}, u32[]{:S(2)}) collective-permute-start(bf16[32,1536]{1,0:T(8,128)(2,1)S(1)} %get-tuple-element.12.refs_0_), channel_id=1, source_target_pairs={{0,8},{1,9},{2,10},{3,11},{4,12},{5,13},{6,14},{7,15},{8,0},{9,1},... | collective-permute-start | bytes 294920 | tf_op jit(solution)/shard_map/ppermute | solution.py:294
  10.1 5.5 %collective-permute-start.1 = (bf16[32,1536]{1,0:T(8,128)(2,1)S(1)}, bf16[32,1536]{1,0:T(8,128)(2,1)S(1)}, u32[]{:S(2)}, u32[]{:S(2)}) collective-permute-start(bf16[32,1536]{1,0:T(8,128)(2,1)S(1)} %get-tuple-element.12.refs_0_), channel_id=1, source_target_pairs={{0,12},{1,13},{2,14},{3,15},{4,0},{5,1},{6,2},{7,3},{8,4},{9,5},{1... | collective-permute-start | bytes 294920 | tf_op jit(solution)/shard_map/ppermute | solution.py:294
  11.5 4.6 %collective-permute-start = (bf16[32,1536]{1,0:T(8,128)(2,1)S(1)}, bf16[32,1536]{1,0:T(8,128)(2,1)S(1)}, u32[]{:S(2)}, u32[]{:S(2)}) collective-permute-start(bf16[32,1536]{1,0:T(8,128)(2,1)S(1)} %get-tuple-element.12.refs_0_), channel_id=1, source_target_pairs={{0,1},{1,0},{2,3},{3,2},{4,5},{5,4},{6,7},{7,6},{8,9},{9,8},{10,11... | collective-permute-start | bytes 294920 | tf_op jit(solution)/shard_map/ppermute | solution.py:286
  11.5 4.6 %collective-permute-start.6 = (bf16[32,1536]{1,0:T(8,128)(2,1)S(1)}, bf16[32,1536]{1,0:T(8,128)(2,1)S(1)}, u32[]{:S(2)}, u32[]{:S(2)}) collective-permute-start(bf16[32,1536]{1,0:T(8,128)(2,1)S(1)} %relay.1.refs_6_), channel_id=1, source_target_pairs={{0,1},{1,0},{2,3},{3,2},{4,5},{5,4},{6,7},{7,6},{8,9},{9,8},{10,11... | collective-permute-start | bytes 294920 | tf_op jit(solution)/shard_map/ppermute | solution.py:286
  15.6 1.3 %collective-permute-start.4 = (bf16[32,1536]{1,0:T(8,128)(2,1)S(1)}, bf16[32,1536]{1,0:T(8,128)(2,1)S(1)}, u32[]{:S(2)}, u32[]{:S(2)}) collective-permute-start(bf16[32,1536]{1,0:T(8,128)(2,1)S(1)} %collective-permute-done.3.refs_4_), channel_id=1, source_target_pairs={{0,1},{1,0},{2,3},{3,2},{4,5},{5,4},{6,7},{7,6},{8,9},{9,8},{10,11... | collective-permute-start | bytes 294920 | tf_op jit(solution)/shard_map/ppermute | solution.py:286
  15.6 1.5 %collective-permute-start.2 = (bf16[32,1536]{1,0:T(8,128)(2,1)S(1)}, bf16[32,1536]{1,0:T(8,128)(2,1)S(1)}, u32[]{:S(2)}, u32[]{:S(2)}) collective-permute-start(bf16[32,1536]{1,0:T(8,128)(2,1)S(1)} %collective-permute-done.1.refs_2_), channel_id=1, source_target_pairs={{0,1},{1,0},{2,3},{3,2},{4,5},{5,4},{6,7},{7,6},{8,9},{9,8},{10,11... | collective-permute-start | bytes 294920 | tf_op jit(solution)/shard_map/ppermute | solution.py:286
  17.6 3.7 %collective-permute-start.8 = (bf16[16,256]{1,0:T(8,128)(2,1)S(1)}, bf16[16,256]{1,0:T(8,128)(2,1)S(1)}, u32[]{:S(2)}, u32[]{:S(2)}) collective-permute-start(bf16[16,256]{1,0:T(8,128)(2,1)S(1)} %get-tuple-element.17), channel_id=1, source_target_pairs={{0,2},{1,3},{2,0},{3,1},{4,6},{5,7},{6,4},{7,5},{8,10},{9,11},{10,... | collective-permute-start | bytes 24584 | tf_op jit(solution)/shard_map/ppermute | solution.py:286
